TPU v7x, 512 devices: a whole 4x4x16 slice. The times are simulated.
512 devices in a mesh: section: 32 (over z, core), tensor: 8 (over x, y_lo), replica: 2 (over y_hi).
Axes of the slice: x: 4, y: 4 (y_hi: 2, y_lo: 2; y = y_hi * 2 + y_lo), z: 16, core: 2. Of those that a mesh axis runs over, the one named last changes fastest.
Arguments:
- pool_inputs: bfloat16 [32, 256, 2, 1408], P('section', 'replica', None, 'tensor'), may hold values from -6 to 6
- pool_mixed: bfloat16 [32, 256, 1408], P('section', 'replica'), may hold values from -6 to 6
- crop_ids: int32 [32, 8, 128], P('section', 'replica'), may hold values from 0 to 127
- incoming: bfloat16 [32, 256, 1408], P('section', 'replica', 'tensor'), may hold values from -6 to 6
- loss_grads: bfloat16 [3, 256, 1408], P(None, 'replica', 'tensor'), may hold values from -6 to 6
- w_proj: bfloat16 [32, 2, 1408, 1408], P('section', None, ('tensor', 'replica')), may hold values from -0.109375 to 0.109375
- w_up: bfloat16 [32, 1408, 3072], P('section', None, ('tensor', 'replica')), may hold values from -0.15625 to 0.15625
- w_down: bfloat16 [32, 3072, 1408], P('section', ('tensor', 'replica')), may hold values from -0.109375 to 0.109375
Outputs:
- grad_proj: bfloat16 [32, 2, 1408, 1408], P('section', None, ('tensor', 'replica'))
- grad_up: bfloat16 [32, 1408, 3072], P('section', None, ('tensor', 'replica'))
- grad_down: bfloat16 [32, 3072, 1408], P('section', ('tensor', 'replica'))
- outgoing: bfloat16 [32, 256, 2, 1408], P('section', 'replica', None, 'tensor')
All inputs are finite; a program needn't handle non-finite values.
Results may differ from a plain program's by a relative error of at most 0.02.
Values may be sent and summed in bfloat16 or wider, within the bound.
No kernel may reach another device: no remote copies, remote signals or barrier semaphores. Data moves between devices by JAX's collectives and lax.ppermute only.
A program may use at most 64 MiB of HBM per device.

v0:
```python
import jax
import jax.numpy as jnp
from jax import lax
from jax.sharding import PartitionSpec as P

gelu_scale = 0.7978845608
gelu_cubic = 0.044715


def from_partner(value, axis, bit):
    mask = 2**bit
    pairs = [(source, source ^ mask) for source in range(lax.axis_size(axis))]
    return lax.ppermute(value, axis, pairs)


def shifted(x, axis, by):
    devices = lax.axis_size(axis)
    pairs = [(i, i + by) for i in range(devices) if 0 <= i + by < devices]
    return lax.ppermute(x, axis, pairs)


def gelu_pair(pre_gelu):
    inner = gelu_scale * (pre_gelu + gelu_cubic * pre_gelu * pre_gelu * pre_gelu)
    tanh_part = jnp.tanh(inner)
    gelu_value = 0.5 * pre_gelu * (1.0 + tanh_part)
    gelu_slope = 0.5 * (1.0 + tanh_part) + 0.5 * pre_gelu * (
        1.0 - tanh_part * tanh_part
    ) * gelu_scale * (1.0 + 3.0 * gelu_cubic * pre_gelu * pre_gelu)
    return (gelu_value, gelu_slope)


def reflect(block, section_count):
    for bit_number in range(section_count.bit_length() - 1):
        block = from_partner(block, "section", bit_number)
    return block


def body(pool_inputs, pool_mixed, crop_ids, incoming, loss_grads, w_proj, w_up, w_down):
    section_index = lax.axis_index("section")
    section_count = lax.axis_size("section")
    proj_full, up_full, down_full = (
        lax.all_gather(w_proj, "replica", axis=2, tiled=True),
        lax.all_gather(w_up, "replica", axis=2, tiled=True),
        lax.all_gather(w_down, "replica", axis=1, tiled=True),
    )
    proj_local = proj_full[0]
    up_local = up_full[0]
    down_local = down_full[0]
    seed_full, loss_full = (
        lax.all_gather(incoming, "tensor", axis=2, tiled=True),
        lax.all_gather(loss_grads, "tensor", axis=2, tiled=True),
    )
    encoder = section_index < section_count // 2
    decoder_flag = jnp.where(encoder, 0.0, 1.0).astype(jnp.bfloat16)
    skip_mask = jnp.stack([jnp.ones((), jnp.bfloat16), decoder_flag])[None, :, None]
    encoder_weight = jnp.where(encoder, 1.0, 0.0).astype(jnp.float32)
    is_top = section_index == section_count - 1
    tick_count = crop_ids.shape[1]
    upstream = seed_full[0]
    kept_inputs, kept_mixed, kept_active, kept_hidden, kept_grads, kept_upstream = (
        [],
        [],
        [],
        [],
        [],
        [],
    )
    input_grad = None
    for tick_index in range(tick_count):
        picked_rows = crop_ids[0, tick_index]
        inputs = pool_inputs[0][picked_rows] * skip_mask
        mixed_rows = pool_mixed[0][picked_rows]
        pre_gelu = jnp.dot(mixed_rows, up_local, preferred_element_type=jnp.float32)
        gelu_value, gelu_slope = gelu_pair(pre_gelu)
        activated = gelu_value.astype(jnp.bfloat16)
        back_act = jnp.einsum("md,fd->mf", upstream, down_local, preferred_element_type=jnp.float32)
        back_hidden = (back_act * gelu_slope).astype(jnp.bfloat16)
        partial_back = jnp.einsum(
            "mf,df->md", back_hidden, up_local, preferred_element_type=jnp.float32
        )
        back_mixed = upstream.astype(jnp.float32) + lax.psum(partial_back, "tensor")
        mixed_grad = back_mixed.astype(jnp.bfloat16)
        input_grad = jnp.einsum(
            "mj,kij->mki", mixed_grad, proj_local, preferred_element_type=jnp.float32
        ).astype(jnp.bfloat16)
        kept_inputs.append(inputs)
        kept_mixed.append(mixed_rows)
        kept_active.append(activated)
        kept_hidden.append(back_hidden)
        kept_grads.append(mixed_grad)
        kept_upstream.append(upstream)
        if tick_index + 1 < tick_count:
            payload = lax.all_gather(input_grad, "tensor", axis=2, tiled=True)
            from_above = shifted(payload[:, 0], "section", -1)
            mirrored = reflect(payload[:, 1], section_count)
            summed = (
                from_above.astype(jnp.float32) + encoder_weight * mirrored.astype(jnp.float32)
            ).astype(jnp.bfloat16)
            upstream = jnp.where(is_top, loss_full[tick_index], summed)
    all_inputs = jnp.concatenate(kept_inputs, axis=0)
    all_mixed = jnp.concatenate(kept_mixed, axis=0)
    all_active = jnp.concatenate(kept_active, axis=0)
    all_hidden = jnp.concatenate(kept_hidden, axis=0)
    all_grads = jnp.concatenate(kept_grads, axis=0)
    all_upstream = jnp.concatenate(kept_upstream, axis=0)
    down_total = jnp.einsum(
        "mf,md->fd", all_active, all_upstream, preferred_element_type=jnp.float32
    )
    up_total = jnp.einsum("md,mf->df", all_mixed, all_hidden, preferred_element_type=jnp.float32)
    proj_total = jnp.einsum(
        "mki,mj->kij", all_inputs, all_grads, preferred_element_type=jnp.float32
    )
    reduced = (
        lax.psum_scatter(
            proj_total[None].astype(jnp.bfloat16), "replica", scatter_dimension=2, tiled=True
        ).astype(jnp.float32),
        lax.psum_scatter(
            up_total[None].astype(jnp.bfloat16), "replica", scatter_dimension=2, tiled=True
        ).astype(jnp.float32),
        lax.psum_scatter(
            down_total[None].astype(jnp.bfloat16), "replica", scatter_dimension=1, tiled=True
        ).astype(jnp.float32),
    )
    return (
        reduced[0].astype(jnp.bfloat16),
        reduced[1].astype(jnp.bfloat16),
        reduced[2].astype(jnp.bfloat16),
        input_grad[None],
    )


def solution(mesh):
    in_specs = (
        P("section", "replica", None, "tensor"),
        P("section", "replica", None),
        P("section", "replica", None),
        P("section", "replica", "tensor"),
        P(None, "replica", "tensor"),
        P("section", None, ("tensor", "replica"), None),
        P("section", None, ("tensor", "replica")),
        P("section", ("tensor", "replica"), None),
    )
    out_specs = (
        P("section", None, ("tensor", "replica"), None),
        P("section", None, ("tensor", "replica")),
        P("section", ("tensor", "replica"), None),
        P("section", "replica", None, "tensor"),
    )
    return jax.shard_map(body, mesh=mesh, in_specs=in_specs, out_specs=out_specs, check_vma=False)
```

profile of v0, /device:TPU:1, one launch (start us, length us, event | category | flops | bytes accessed | tf_op | source)
XLA Modules:
  0.0 1006.9 jit_solution(8471942278215179916)
XLA Ops:
  9.7 23.1 %all_gather.24 = bf16[1,128,1408]{1,2,0:T(8,128)(2,1)S(1)} all-gather(bf16[1,128,176]{1,2,0:T(8,128)(2,1)S(1)} %copy-done.36), channel_id=1, replica_groups=mesh['section'=32,'tensor'=8,'replica'=2] {'tensor'}, dimensions={2}, use_global_device_ids=true | all-gather | bytes 405504 | tf_op jit(solution)/shard_map/all_gather | solution.py:50
  32.8 16.5 %all-gather.6.cloned.1.call-done = bf16[1,1408,384]{1,2,0:T(8,128)(2,1)} async-done(((bf16[1,1408,192]{1,2,0:T(8,128)(2,1)}), bf16[1,1408,384]{1,2,0:T(8,128)(2,1)}) %all-gather.6.cloned.1.call-update) | async-done | bytes 1081360 | tf_op jit(solution)/shard_map/all_gather | solution.py:43
  51.7 33.1 %all-gather.4.cloned.1.call-done = bf16[1,384,1408]{2,1,0:T(8,128)(2,1)} async-done(((bf16[1,192,1408]{2,1,0:T(8,128)(2,1)}), bf16[1,384,1408]{2,1,0:T(8,128)(2,1)}) %all-gather.4.cloned.1.call-update) | async-done | bytes 1081360 | tf_op jit(solution)/shard_map/all_gather | solution.py:44
  89.5 14.4 %all_gather.28 = bf16[1,2,176,1408]{3,2,1,0:T(8,128)(2,1)S(1)} all-gather(bf16[1,2,88,1408]{3,2,1,0:T(8,128)(2,1)S(1)} %copy-done.23), channel_id=1, replica_groups=mesh['section'=32,'tensor'=8,'replica'=2] {'replica'}, dimensions={2}, use_global_device_ids=true | all-gather | bytes 1486848 | tf_op jit(solution)/shard_map/all_gather | solution.py:42
  103.8 70.2 %all-reduce.5.cloned.1.call-done = f32[128,1408]{1,0:T(8,128)} async-done(((f32[128,1408]{1,0:T(8,128)}), f32[128,1408]{1,0:T(8,128)}) %all-reduce.5.cloned.1.call-update) | async-done | bytes 720912 | tf_op jit(solution)/shard_map/psum | solution.py:81
  176.0 23.6 %all_gather.29 = bf16[128,2,1408]{0,1,2:T(2,128)(2,1)S(1)} all-gather(bf16[128,2,176]{0,1,2:T(2,128)(2,1)S(1)} %copy.36), channel_id=1, replica_groups=mesh['section'=32,'tensor'=8,'replica'=2] {'tensor'}, dimensions={2}, use_global_device_ids=true | all-gather | bytes 811008 | tf_op jit(solution)/shard_map/all_gather | solution.py:93
  201.4 2.8 copy.56
  204.3 14.3 %collective-permute-start.1 = (bf16[128,1408]{1,0:T(8,128)(2,1)}, bf16[128,1408]{1,0:T(8,128)(2,1)S(1)}, u32[]{:S(2)}, u32[]{:S(2)}) collective-permute-start(bf16[128,1408]{1,0:T(8,128)(2,1)} %bitcast.141), channel_id=1, source_target_pairs={{0,16},{16,0},{32,48},{48,32},{64,80},{80,64},{96,112},{112,96},{1... | collective-permute-start | bytes 1081352 | tf_op jit(solution)/shard_map/ppermute | solution.py:13
  220.1 3.2 collective-permute-start.2
  223.2 8.4 collective-permute-done.2
  231.7 4.6 collective-permute-start.3
  236.3 16.0 %collective-permute-done.3 = bf16[128,1408]{1,0:T(8,128)(2,1)} collective-permute-done((bf16[128,1408]{1,0:T(8,128)(2,1)}, bf16[128,1408]{1,0:T(8,128)(2,1)}, u32[]{:S(2)}, u32[]{:S(2)}) %collective-permute-start.3) | collective-permute-done | bytes 360480 | tf_op jit(solution)/shard_map/ppermute | solution.py:13
  252.3 7.1 collective-permute-start.4
  265.0 3.7 collective-permute-start
  268.7 22.2 %collective-permute-done.4 = bf16[128,1408]{1,0:T(8,128)(2,1)} collective-permute-done((bf16[128,1408]{1,0:T(8,128)(2,1)}, bf16[128,1408]{1,0:T(8,128)(2,1)}, u32[]{:S(2)}, u32[]{:S(2)}) %collective-permute-start.4) | collective-permute-done | bytes 360480 | tf_op jit(solution)/shard_map/ppermute | solution.py:13
  290.9 18.8 %collective-permute-start.5 = (bf16[128,1408]{1,0:T(8,128)(2,1)}, bf16[128,1408]{1,0:T(8,128)(2,1)}, u32[]{:S(2)}, u32[]{:S(2)}) collective-permute-start(bf16[128,1408]{1,0:T(8,128)(2,1)} %collective-permute-done.4), channel_id=1, source_target_pairs={{0,256},{16,272},{32,288},{48,304},{64,320},{80,336},{96,352},{112... | collective-permute-start | bytes 1081352 | tf_op jit(solution)/shard_map/ppermute | solution.py:13
  312.2 12.0 %collective-permute-done.5 = bf16[128,1408]{1,0:T(8,128)(2,1)} collective-permute-done((bf16[128,1408]{1,0:T(8,128)(2,1)}, bf16[128,1408]{1,0:T(8,128)(2,1)}, u32[]{:S(2)}, u32[]{:S(2)}) %collective-permute-start.5) | collective-permute-done | bytes 360480 | tf_op jit(solution)/shard_map/ppermute | solution.py:13
  327.9 87.0 %all-reduce.7.cloned.1.call-done = f32[128,1408]{1,0:T(8,128)} async-done(((f32[128,1408]{1,0:T(8,128)}), f32[128,1408]{1,0:T(8,128)}) %all-reduce.7.cloned.1.call-update) | async-done | bytes 720912 | tf_op jit(solution)/shard_map/psum | solution.py:81
  416.9 23.3 %all_gather.30 = bf16[128,2,1408]{0,1,2:T(2,128)(2,1)S(1)} all-gather(bf16[128,2,176]{0,1,2:T(2,128)(2,1)S(1)} %copy.40), channel_id=1, replica_groups=mesh['section'=32,'tensor'=8,'replica'=2] {'tensor'}, dimensions={2}, use_global_device_ids=true | all-gather | bytes 811008 | tf_op jit(solution)/shard_map/all_gather | solution.py:93
  442.0 2.8 copy.59
  444.8 13.9 %collective-permute-start.7 = (bf16[128,1408]{1,0:T(8,128)(2,1)}, bf16[128,1408]{1,0:T(8,128)(2,1)S(1)}, u32[]{:S(2)}, u32[]{:S(2)}) collective-permute-start(bf16[128,1408]{1,0:T(8,128)(2,1)} %bitcast.142), channel_id=1, source_target_pairs={{0,16},{16,0},{32,48},{48,32},{64,80},{80,64},{96,112},{112,96},{1... | collective-permute-start | bytes 1081352 | tf_op jit(solution)/shard_map/ppermute | solution.py:13
  460.2 3.0 collective-permute-start.8
  463.2 8.5 collective-permute-done.8
  471.7 4.0 collective-permute-start.9
  475.7 16.0 %collective-permute-done.9 = bf16[128,1408]{1,0:T(8,128)(2,1)} collective-permute-done((bf16[128,1408]{1,0:T(8,128)(2,1)S(1)}, bf16[128,1408]{1,0:T(8,128)(2,1)}, u32[]{:S(2)}, u32[]{:S(2)}) %collective-permute-start.9) | collective-permute-done | bytes 360480 | tf_op jit(solution)/shard_map/ppermute | solution.py:13
  491.8 7.0 collective-permute-start.10
  500.5 3.7 collective-permute-start.6
  504.2 26.1 %collective-permute-done.10 = bf16[128,1408]{1,0:T(8,128)(2,1)} collective-permute-done((bf16[128,1408]{1,0:T(8,128)(2,1)}, bf16[128,1408]{1,0:T(8,128)(2,1)}, u32[]{:S(2)}, u32[]{:S(2)}) %collective-permute-start.10) | collective-permute-done | bytes 360480 | tf_op jit(solution)/shard_map/ppermute | solution.py:13
  530.3 18.7 %collective-permute-start.11 = (bf16[128,1408]{1,0:T(8,128)(2,1)}, bf16[128,1408]{1,0:T(8,128)(2,1)}, u32[]{:S(2)}, u32[]{:S(2)}) collective-permute-start(bf16[128,1408]{1,0:T(8,128)(2,1)} %collective-permute-done.10), channel_id=1, source_target_pairs={{0,256},{16,272},{32,288},{48,304},{64,320},{80,336},{96,352},{112... | collective-permute-start | bytes 1081352 | tf_op jit(solution)/shard_map/ppermute | solution.py:13
  551.4 12.0 %collective-permute-done.11 = bf16[128,1408]{1,0:T(8,128)(2,1)} collective-permute-done((bf16[128,1408]{1,0:T(8,128)(2,1)}, bf16[128,1408]{1,0:T(8,128)(2,1)}, u32[]{:S(2)}, u32[]{:S(2)}) %collective-permute-start.11) | collective-permute-done | bytes 360480 | tf_op jit(solution)/shard_map/ppermute | solution.py:13
  566.5 86.1 %all-reduce.9.cloned.1.call-done = f32[128,1408]{1,0:T(8,128)} async-done(((f32[128,1408]{1,0:T(8,128)}), f32[128,1408]{1,0:T(8,128)}) %all-reduce.9.cloned.1.call-update) | async-done | bytes 720912 | tf_op jit(solution)/shard_map/psum | solution.py:81
  654.5 23.3 %all_gather.31 = bf16[128,2,1408]{0,1,2:T(2,128)(2,1)S(1)} all-gather(bf16[128,2,176]{0,1,2:T(2,128)(2,1)S(1)} %copy.44), channel_id=1, replica_groups=mesh['section'=32,'tensor'=8,'replica'=2] {'tensor'}, dimensions={2}, use_global_device_ids=true | all-gather | bytes 811008 | tf_op jit(solution)/shard_map/all_gather | solution.py:93
  682.4 13.9 %collective-permute-start.13 = (bf16[128,1408]{1,0:T(8,128)(2,1)}, bf16[128,1408]{1,0:T(8,128)(2,1)S(1)}, u32[]{:S(2)}, u32[]{:S(2)}) collective-permute-start(bf16[128,1408]{1,0:T(8,128)(2,1)} %bitcast.143), channel_id=1, source_target_pairs={{0,16},{16,0},{32,48},{48,32},{64,80},{80,64},{96,112},{112,96},{1... | collective-permute-start | bytes 1081352 | tf_op jit(solution)/shard_map/ppermute | solution.py:13
  697.8 3.0 collective-permute-start.14
  700.8 8.5 collective-permute-done.14
  709.3 4.0 collective-permute-start.15
  713.4 16.0 %collective-permute-done.15 = bf16[128,1408]{1,0:T(8,128)(2,1)} collective-permute-done((bf16[128,1408]{1,0:T(8,128)(2,1)S(1)}, bf16[128,1408]{1,0:T(8,128)(2,1)}, u32[]{:S(2)}, u32[]{:S(2)}) %collective-permute-start.15) | collective-permute-done | bytes 360480 | tf_op jit(solution)/shard_map/ppermute | solution.py:13
  729.4 7.2 collective-permute-start.16
  738.3 3.7 collective-permute-start.12
  742.0 25.9 %collective-permute-done.16 = bf16[128,1408]{1,0:T(8,128)(2,1)} collective-permute-done((bf16[128,1408]{1,0:T(8,128)(2,1)}, bf16[128,1408]{1,0:T(8,128)(2,1)}, u32[]{:S(2)}, u32[]{:S(2)}) %collective-permute-start.16) | collective-permute-done | bytes 360480 | tf_op jit(solution)/shard_map/ppermute | solution.py:13
  767.9 18.7 %collective-permute-start.17 = (bf16[128,1408]{1,0:T(8,128)(2,1)}, bf16[128,1408]{1,0:T(8,128)(2,1)}, u32[]{:S(2)}, u32[]{:S(2)}) collective-permute-start(bf16[128,1408]{1,0:T(8,128)(2,1)} %collective-permute-done.16), channel_id=1, source_target_pairs={{0,256},{16,272},{32,288},{48,304},{64,320},{80,336},{96,352},{112... | collective-permute-start | bytes 1081352 | tf_op jit(solution)/shard_map/ppermute | solution.py:13
  789.0 12.0 %collective-permute-done.17 = bf16[128,1408]{1,0:T(8,128)(2,1)} collective-permute-done((bf16[128,1408]{1,0:T(8,128)(2,1)}, bf16[128,1408]{1,0:T(8,128)(2,1)}, u32[]{:S(2)}, u32[]{:S(2)}) %collective-permute-start.17) | collective-permute-done | bytes 360480 | tf_op jit(solution)/shard_map/ppermute | solution.py:13
  807.6 4.8 copy.50
  822.8 68.8 %all-reduce.11.cloned.1.call-done = f32[128,1408]{1,0:T(8,128)} async-done(((f32[128,1408]{1,0:T(8,128)}), f32[128,1408]{1,0:T(8,128)}) %all-reduce.11.cloned.1.call-update) | async-done | bytes 720912 | tf_op jit(solution)/shard_map/psum | solution.py:81
  896.4 3.0 fusion.1
  901.5 29.7 %reduce-scatter.12.cloned.1.call-done = bf16[192,1408]{1,0:T(8,128)(2,1)} async-done(((bf16[384,1408]{1,0:T(8,128)(2,1)}), bf16[192,1408]{1,0:T(8,128)(2,1)}) %reduce-scatter.12.cloned.1.call-update) | async-done | bytes 540688
  933.6 31.3 %reduce-scatter.10.cloned.1.call-done = bf16[88,2816]{1,0:T(8,128)(2,1)} async-done(((bf16[176,2816]{1,0:T(8,128)(2,1)}), bf16[88,2816]{1,0:T(8,128)(2,1)}) %reduce-scatter.10.cloned.1.call-update) | async-done | bytes 495632
  966.9 33.1 %reduce-scatter.8.cloned.1.call-done = bf16[1,192,1408]{2,1,0:T(8,128)(2,1)} async-done(((bf16[1,384,1408]{2,1,0:T(8,128)(2,1)}), bf16[1,192,1408]{2,1,0:T(8,128)(2,1)}) %reduce-scatter.8.cloned.1.call-update) | async-done | bytes 540688 | tf_op jit(solution)/shard_map/reduce_scatter | solution.py:120
  (176 shorter events, 78.6 us)
Async XLA Ops:
  7.2 1.6 copy-start
  7.2 1.5 copy-start.37
  7.2 42.2 %all-gather.6.cloned.1.call-start = ((), (), s32[]{:S(2)}) async-start(), calls=%async_computation.4 | async-start | bytes 1622016 | tf_op jit(solution)/shard_map/all_gather | solution.py:43
  7.9 76.9 %all-gather.4.cloned.1.call-start = ((), (), s32[]{:S(2)}) async-start(), calls=%async_computation.3 | async-start | bytes 1622016 | tf_op jit(solution)/shard_map/all_gather | solution.py:44
  8.7 165.4 %all-reduce.5.cloned.1.call-start = ((), (), s32[]{:S(2)}) async-start(), calls=%async_computation.5 | async-start | bytes 1441792 | tf_op jit(solution)/shard_map/psum | solution.py:81
  9.7 76.9 %copy-start.6 = (bf16[128,1408]{1,0:T(8,128)(2,1)}, bf16[128,1408]{1,0:T(8,128)(2,1)S(1)}, u32[]{:S(2)}) copy-start(bf16[128,1408]{1,0:T(8,128)(2,1)S(1)} %gather_fusion.4) | copy-start | bytes 1081348
  51.7 35.5 %copy-start.1 = (bf16[1,1408,384]{1,2,0:T(8,128)(2,1)S(1)}, bf16[1,1408,384]{1,2,0:T(8,128)(2,1)}, u32[]{:S(2)}) copy-start(bf16[1,1408,384]{1,2,0:T(8,128)(2,1)} %all-gather.6.cloned.1.call-done) | copy-start | bytes 3244036
  88.5 221.3 %all-gather.8.cloned.1.call-start = ((), (), s32[]{:S(2)}) async-start(), calls=%async_computation.6 | async-start | bytes 1216512 | tf_op jit(solution)/shard_map/all_gather | solution.py:51
  89.1 325.9 %all-reduce.7.cloned.1.call-start = ((), (), s32[]{:S(2)}) async-start(), calls=%async_computation.7 | async-start | bytes 1441792 | tf_op jit(solution)/shard_map/psum | solution.py:81
  204.3 15.8 %collective-permute-start.1 = (bf16[128,1408]{1,0:T(8,128)(2,1)}, bf16[128,1408]{1,0:T(8,128)(2,1)S(1)}, u32[]{:S(2)}, u32[]{:S(2)}) collective-permute-start(bf16[128,1408]{1,0:T(8,128)(2,1)} %bitcast.141), channel_id=1, source_target_pairs={{0,16},{16,0},{32,48},{48,32},{64,80},{80,64},{96,112},{112,96},{1... | collective-permute-start | bytes 1081352 | tf_op jit(solution)/shard_map/ppermute | solution.py:13
  220.1 11.6 %collective-permute-start.2 = (bf16[128,1408]{1,0:T(8,128)(2,1)S(1)}, bf16[128,1408]{1,0:T(8,128)(2,1)}, u32[]{:S(2)}, u32[]{:S(2)}) collective-permute-start(bf16[128,1408]{1,0:T(8,128)(2,1)S(1)} %collective-permute-done.1), channel_id=1, source_target_pairs={{0,32},{16,48},{32,0},{48,16},{64,96},{80,112},{96,64},{112,80},{1... | collective-permute-start | bytes 1081352 | tf_op jit(solution)/shard_map/ppermute | solution.py:13
  231.7 20.6 %collective-permute-start.3 = (bf16[128,1408]{1,0:T(8,128)(2,1)}, bf16[128,1408]{1,0:T(8,128)(2,1)}, u32[]{:S(2)}, u32[]{:S(2)}) collective-permute-start(bf16[128,1408]{1,0:T(8,128)(2,1)} %collective-permute-done.2), channel_id=1, source_target_pairs={{0,64},{16,80},{32,96},{48,112},{64,0},{80,16},{96,32},{112,48},{1... | collective-permute-start | bytes 1081352 | tf_op jit(solution)/shard_map/ppermute | solution.py:13
  252.3 38.6 %collective-permute-start.4 = (bf16[128,1408]{1,0:T(8,128)(2,1)}, bf16[128,1408]{1,0:T(8,128)(2,1)}, u32[]{:S(2)}, u32[]{:S(2)}) collective-permute-start(bf16[128,1408]{1,0:T(8,128)(2,1)} %collective-permute-done.3), channel_id=1, source_target_pairs={{0,128},{16,144},{32,160},{48,176},{64,192},{80,208},{96,224},{112... | collective-permute-start | bytes 1081352 | tf_op jit(solution)/shard_map/ppermute | solution.py:13
  265.0 47.2 %collective-permute-start = (bf16[128,1408]{1,0:T(8,128)(2,1)}, bf16[128,1408]{1,0:T(8,128)(2,1)}, u32[]{:S(2)}, u32[]{:S(2)}) collective-permute-start(bf16[128,1408]{1,0:T(8,128)(2,1)} %bitcast.138), channel_id=1, source_target_pairs={{16,0},{32,16},{48,32},{64,48},{80,64},{96,80},{112,96},{128,112},... | collective-permute-start | bytes 1081352 | tf_op jit(solution)/shard_map/ppermute | solution.py:19
  290.9 33.2 %collective-permute-start.5 = (bf16[128,1408]{1,0:T(8,128)(2,1)}, bf16[128,1408]{1,0:T(8,128)(2,1)}, u32[]{:S(2)}, u32[]{:S(2)}) collective-permute-start(bf16[128,1408]{1,0:T(8,128)(2,1)} %collective-permute-done.4), channel_id=1, source_target_pairs={{0,256},{16,272},{32,288},{48,304},{64,320},{80,336},{96,352},{112... | collective-permute-start | bytes 1081352 | tf_op jit(solution)/shard_map/ppermute | solution.py:13
  312.2 13.3 %copy-start.24 = (f32[128,384]{1,0:T(8,128)S(1)}, f32[128,384]{1,0:T(8,128)}, u32[]{:S(2)}) copy-start(f32[128,384]{1,0:T(8,128)} %get-tuple-element.38) | copy-start | bytes 589828
  312.2 13.3 %copy-start.38 = (bf16[1,384,1408]{2,1,0:T(8,128)(2,1)S(1)}, bf16[1,384,1408]{2,1,0:T(8,128)(2,1)}, u32[]{:S(2)}) copy-start(bf16[1,384,1408]{2,1,0:T(8,128)(2,1)} %all-gather.4.cloned.1.call-done) | copy-start | bytes 3244036
  325.4 89.5 %copy-start.8 = (bf16[128,1408]{1,0:T(8,128)(2,1)}, bf16[128,1408]{1,0:T(8,128)(2,1)S(1)}, u32[]{:S(2)}) copy-start(bf16[128,1408]{1,0:T(8,128)(2,1)S(1)} %fusion.66) | copy-start | bytes 1081348
  327.9 324.7 %all-reduce.9.cloned.1.call-start = ((), (), s32[]{:S(2)}) async-start(), calls=%async_computation.8 | async-start | bytes 1441792 | tf_op jit(solution)/shard_map/psum | solution.py:81
  444.8 15.4 %collective-permute-start.7 = (bf16[128,1408]{1,0:T(8,128)(2,1)}, bf16[128,1408]{1,0:T(8,128)(2,1)S(1)}, u32[]{:S(2)}, u32[]{:S(2)}) collective-permute-start(bf16[128,1408]{1,0:T(8,128)(2,1)} %bitcast.142), channel_id=1, source_target_pairs={{0,16},{16,0},{32,48},{48,32},{64,80},{80,64},{96,112},{112,96},{1... | collective-permute-start | bytes 1081352 | tf_op jit(solution)/shard_map/ppermute | solution.py:13
  460.2 11.5 %collective-permute-start.8 = (bf16[128,1408]{1,0:T(8,128)(2,1)S(1)}, bf16[128,1408]{1,0:T(8,128)(2,1)S(1)}, u32[]{:S(2)}, u32[]{:S(2)}) collective-permute-start(bf16[128,1408]{1,0:T(8,128)(2,1)S(1)} %collective-permute-done.7), channel_id=1, source_target_pairs={{0,32},{16,48},{32,0},{48,16},{64,96},{80,112},{96,64},{112,80},{1... | collective-permute-start | bytes 1081352 | tf_op jit(solution)/shard_map/ppermute | solution.py:13
  471.7 20.1 %collective-permute-start.9 = (bf16[128,1408]{1,0:T(8,128)(2,1)S(1)}, bf16[128,1408]{1,0:T(8,128)(2,1)}, u32[]{:S(2)}, u32[]{:S(2)}) collective-permute-start(bf16[128,1408]{1,0:T(8,128)(2,1)S(1)} %collective-permute-done.8), channel_id=1, source_target_pairs={{0,64},{16,80},{32,96},{48,112},{64,0},{80,16},{96,32},{112,48},{1... | collective-permute-start | bytes 1081352 | tf_op jit(solution)/shard_map/ppermute | solution.py:13
  491.8 38.5 %collective-permute-start.10 = (bf16[128,1408]{1,0:T(8,128)(2,1)}, bf16[128,1408]{1,0:T(8,128)(2,1)}, u32[]{:S(2)}, u32[]{:S(2)}) collective-permute-start(bf16[128,1408]{1,0:T(8,128)(2,1)} %collective-permute-done.9), channel_id=1, source_target_pairs={{0,128},{16,144},{32,160},{48,176},{64,192},{80,208},{96,224},{112... | collective-permute-start | bytes 1081352 | tf_op jit(solution)/shard_map/ppermute | solution.py:13
  500.5 50.9 %collective-permute-start.6 = (bf16[128,1408]{1,0:T(8,128)(2,1)}, bf16[128,1408]{1,0:T(8,128)(2,1)}, u32[]{:S(2)}, u32[]{:S(2)}) collective-permute-start(bf16[128,1408]{1,0:T(8,128)(2,1)} %bitcast.140), channel_id=1, source_target_pairs={{16,0},{32,16},{48,32},{64,48},{80,64},{96,80},{112,96},{128,112},... | collective-permute-start | bytes 1081352 | tf_op jit(solution)/shard_map/ppermute | solution.py:19
  530.3 33.0 %collective-permute-start.11 = (bf16[128,1408]{1,0:T(8,128)(2,1)}, bf16[128,1408]{1,0:T(8,128)(2,1)}, u32[]{:S(2)}, u32[]{:S(2)}) collective-permute-start(bf16[128,1408]{1,0:T(8,128)(2,1)} %collective-permute-done.10), channel_id=1, source_target_pairs={{0,256},{16,272},{32,288},{48,304},{64,320},{80,336},{96,352},{112... | collective-permute-start | bytes 1081352 | tf_op jit(solution)/shard_map/ppermute | solution.py:13
  551.3 13.3 %copy-start.26 = (f32[128,384]{1,0:T(8,128)S(1)}, f32[128,384]{1,0:T(8,128)}, u32[]{:S(2)}) copy-start(f32[128,384]{1,0:T(8,128)} %get-tuple-element.36) | copy-start | bytes 589828
  551.4 13.3 %copy-start.39 = (bf16[1,384,1408]{2,1,0:T(8,128)(2,1)S(1)}, bf16[1,384,1408]{2,1,0:T(8,128)(2,1)}, u32[]{:S(2)}) copy-start(bf16[1,384,1408]{2,1,0:T(8,128)(2,1)} %all-gather.4.cloned.1.call-done) | copy-start | bytes 3244036
  564.6 88.0 %copy-start.13 = (bf16[128,1408]{1,0:T(8,128)(2,1)}, bf16[128,1408]{1,0:T(8,128)(2,1)S(1)}, u32[]{:S(2)}) copy-start(bf16[128,1408]{1,0:T(8,128)(2,1)S(1)} %fusion.67) | copy-start | bytes 1081348
  566.4 325.1 %all-reduce.11.cloned.1.call-start = ((), (), s32[]{:S(2)}) async-start(), calls=%async_computation.9 | async-start | bytes 1441792 | tf_op jit(solution)/shard_map/psum | solution.py:81
  682.4 15.4 %collective-permute-start.13 = (bf16[128,1408]{1,0:T(8,128)(2,1)}, bf16[128,1408]{1,0:T(8,128)(2,1)S(1)}, u32[]{:S(2)}, u32[]{:S(2)}) collective-permute-start(bf16[128,1408]{1,0:T(8,128)(2,1)} %bitcast.143), channel_id=1, source_target_pairs={{0,16},{16,0},{32,48},{48,32},{64,80},{80,64},{96,112},{112,96},{1... | collective-permute-start | bytes 1081352 | tf_op jit(solution)/shard_map/ppermute | solution.py:13
  697.8 11.5 %collective-permute-start.14 = (bf16[128,1408]{1,0:T(8,128)(2,1)S(1)}, bf16[128,1408]{1,0:T(8,128)(2,1)S(1)}, u32[]{:S(2)}, u32[]{:S(2)}) collective-permute-start(bf16[128,1408]{1,0:T(8,128)(2,1)S(1)} %collective-permute-done.13), channel_id=1, source_target_pairs={{0,32},{16,48},{32,0},{48,16},{64,96},{80,112},{96,64},{112,80},{1... | collective-permute-start | bytes 1081352 | tf_op jit(solution)/shard_map/ppermute | solution.py:13
  709.3 20.1 %collective-permute-start.15 = (bf16[128,1408]{1,0:T(8,128)(2,1)S(1)}, bf16[128,1408]{1,0:T(8,128)(2,1)}, u32[]{:S(2)}, u32[]{:S(2)}) collective-permute-start(bf16[128,1408]{1,0:T(8,128)(2,1)S(1)} %collective-permute-done.14), channel_id=1, source_target_pairs={{0,64},{16,80},{32,96},{48,112},{64,0},{80,16},{96,32},{112,48},{1... | collective-permute-start | bytes 1081352 | tf_op jit(solution)/shard_map/ppermute | solution.py:13
  729.4 38.5 %collective-permute-start.16 = (bf16[128,1408]{1,0:T(8,128)(2,1)}, bf16[128,1408]{1,0:T(8,128)(2,1)}, u32[]{:S(2)}, u32[]{:S(2)}) collective-permute-start(bf16[128,1408]{1,0:T(8,128)(2,1)} %collective-permute-done.15), channel_id=1, source_target_pairs={{0,128},{16,144},{32,160},{48,176},{64,192},{80,208},{96,224},{112... | collective-permute-start | bytes 1081352 | tf_op jit(solution)/shard_map/ppermute | solution.py:13
  738.3 50.7 %collective-permute-start.12 = (bf16[128,1408]{1,0:T(8,128)(2,1)}, bf16[128,1408]{1,0:T(8,128)(2,1)}, u32[]{:S(2)}, u32[]{:S(2)}) collective-permute-start(bf16[128,1408]{1,0:T(8,128)(2,1)} %bitcast.139), channel_id=1, source_target_pairs={{16,0},{32,16},{48,32},{64,48},{80,64},{96,80},{112,96},{128,112},... | collective-permute-start | bytes 1081352 | tf_op jit(solution)/shard_map/ppermute | solution.py:19
  767.9 33.0 %collective-permute-start.17 = (bf16[128,1408]{1,0:T(8,128)(2,1)}, bf16[128,1408]{1,0:T(8,128)(2,1)}, u32[]{:S(2)}, u32[]{:S(2)}) collective-permute-start(bf16[128,1408]{1,0:T(8,128)(2,1)} %collective-permute-done.16), channel_id=1, source_target_pairs={{0,256},{16,272},{32,288},{48,304},{64,320},{80,336},{96,352},{112... | collective-permute-start | bytes 1081352 | tf_op jit(solution)/shard_map/ppermute | solution.py:13
  789.0 14.0 %copy-start.25 = (f32[128,384]{1,0:T(8,128)S(1)}, f32[128,384]{1,0:T(8,128)}, u32[]{:S(2)}) copy-start(f32[128,384]{1,0:T(8,128)} %get-tuple-element.34) | copy-start | bytes 589828
  789.0 14.0 %copy-start.40 = (bf16[1,384,1408]{2,1,0:T(8,128)(2,1)S(1)}, bf16[1,384,1408]{2,1,0:T(8,128)(2,1)}, u32[]{:S(2)}) copy-start(bf16[1,384,1408]{2,1,0:T(8,128)(2,1)} %all-gather.4.cloned.1.call-done) | copy-start | bytes 3244036
  805.4 125.7 %reduce-scatter.12.cloned.1.call-start = ((), (), s32[]{:S(2)}) async-start(), calls=%async_computation.12 | async-start | bytes 1622016
  815.2 149.6 %reduce-scatter.10.cloned.1.call-start = ((), (), s32[]{:S(2)}) async-start(), calls=%async_computation.11 | async-start | bytes 1486848
  818.0 73.6 %copy-start.19 = (bf16[128,1408]{1,0:T(8,128)(2,1)S(1)}, bf16[128,1408]{1,0:T(8,128)(2,1)}, u32[]{:S(2)}) copy-start(bf16[128,1408]{1,0:T(8,128)(2,1)} %copy-done.18) | copy-start | bytes 1081348
  821.0 72.6 %copy-start.5 = (bf16[128,1408]{1,0:T(8,128)(2,1)S(1)}, bf16[128,1408]{1,0:T(8,128)(2,1)}, u32[]{:S(2)}) copy-start(bf16[128,1408]{1,0:T(8,128)(2,1)} %copy-done.4) | copy-start | bytes 1081348
  821.0 72.6 %copy-start.11 = (bf16[128,1408]{1,0:T(8,128)(2,1)S(1)}, bf16[128,1408]{1,0:T(8,128)(2,1)}, u32[]{:S(2)}) copy-start(bf16[128,1408]{1,0:T(8,128)(2,1)} %copy-done.10) | copy-start | bytes 1081348
  821.0 72.6 %copy-start.16 = (bf16[128,1408]{1,0:T(8,128)(2,1)S(1)}, bf16[128,1408]{1,0:T(8,128)(2,1)}, u32[]{:S(2)}) copy-start(bf16[128,1408]{1,0:T(8,128)(2,1)} %copy-done.15) | copy-start | bytes 1081348
  891.6 2.0 copy-start.31
  891.6 2.0 copy-start.32
  891.6 2.0 copy-start.33
  891.6 2.0 copy-start.34
  896.2 103.8 %reduce-scatter.8.cloned.1.call-start = ((), (), s32[]{:S(2)}) async-start(), calls=%async_computation.10 | async-start | bytes 1622016 | tf_op jit(solution)/shard_map/reduce_scatter | solution.py:120
  (21 other events, 20.8 us)
Sparse Core Ops, SparseCore 0:
  10.1 39.1 all-gather.5
  51.4 33.3 all-gather.3
  88.6 85.4 all-reduce.4
  176.0 49.4 all-gather.7
  328.0 86.9 all-reduce.6
  566.5 85.9 all-reduce.8
  805.5 86.0 all-reduce.10
  894.4 36.7 reduce-scatter.11
  934.0 30.8 reduce-scatter.9
  968.1 31.8 reduce-scatter.7
where the time goes:
time: 1010 us
  waiting for transfers between devices  646 us (64%)
  starting transfers between devices  153 us (15%)
  blocking collectives  108 us (11%)
  local copies, waits for them, and re-layouts  51.2 us (5%)
  matrix products  23.4 us (2%)
  between operations  14.9 us (1%)
  other arithmetic  10.5 us (1%)
    psum x4, waiting for transfers between devices, body(): back_mixed = upstream.astype(jnp.float32) + lax.psum(partial_back, 'tensor')  312 us
    ppermute x15, waiting for transfers between devices, from_partner(): return lax.ppermute(value, axis, pairs)  188 us
    ppermute x15, starting transfers between devices, from_partner(): return lax.ppermute(value, axis, pairs)  141 us
    all_gather x3, blocking collectives, body(): payload = lax.all_gather(input_grad, 'tensor', axis=2, tiled=True)  70.2 us
    unnamed x12, waiting for transfers between devices  63 us
    unnamed x100, local copies, waits for them, and re-layouts  34.3 us
    reduce_scatter x1, waiting for transfers between devices, body(): lax.psum_scatter(down_total[None].astype(jnp.bfloat16), 'replica', scatte...  33.1 us
    all_gather x1, waiting for transfers between devices, body(): lax.all_gather(w_down, 'replica', axis=1, tiled=True)  33.1 us
  transfers between devices with their start and end apart: 28, of which 24 were waited for; matrix products, arithmetic and copies ran while one was open for 5% of the time, Pallas kernels for 0%

commit v1 on v0

v1 whole, which is shorter than its diff:
```python
import jax
import jax.numpy as jnp
from jax import lax
from jax.sharding import PartitionSpec as P

gelu_scale = 0.7978845608
gelu_cubic = 0.044715
f32 = jnp.float32
bf16 = jnp.bfloat16


def gelu_pair(pre_gelu):
    inner = gelu_scale * (pre_gelu + gelu_cubic * pre_gelu * pre_gelu * pre_gelu)
    tanh_part = jnp.tanh(inner)
    gelu_value = 0.5 * pre_gelu * (1.0 + tanh_part)
    gelu_slope = 0.5 * (1.0 + tanh_part) + 0.5 * pre_gelu * (
        1.0 - tanh_part * tanh_part
    ) * gelu_scale * (1.0 + 3.0 * gelu_cubic * pre_gelu * pre_gelu)
    return (gelu_value, gelu_slope)


def dot(a, b, ca=1, cb=0):
    return lax.dot_general(a, b, (((ca,), (cb,)), ((), ())), preferred_element_type=f32)


def swap(x):
    return lax.ppermute(x, "replica", [(0, 1), (1, 0)])


def gather(chunk, axes="tensor"):
    count = lax.axis_size(axes)
    spread = jnp.broadcast_to(chunk[None], (count, *chunk.shape))
    return lax.all_to_all(spread, axes, 0, 0)


def body(pool_inputs, pool_mixed, crop_ids, incoming, loss_grads, w_proj, w_up, w_down):
    section = lax.axis_index("section")
    sections = lax.axis_size("section")
    replica = lax.axis_index("replica")
    parts = lax.axis_size("tensor")
    half = sections // 2
    first = replica == 0
    is_top = section == sections - 1
    ticks, rows = crop_ids.shape[1:]
    pool = pool_mixed.shape[1]
    width = pool_mixed.shape[2]
    units = w_down.shape[1]
    own_in = w_proj.shape[2]
    chunk_rows = incoming.shape[2]

    def by_replica(own, other):
        return jnp.where(first, own, other), jnp.where(first, other, own)

    up_other = swap(w_up[0])
    down_other = swap(w_down[0])
    proj_other = swap(w_proj[0])
    mixed_other = swap(pool_mixed[0])
    ids_other = swap(crop_ids[0, ticks - 1])

    chunk = incoming[0].T
    upstream = gather(chunk).reshape(width, rows)

    up = jnp.concatenate([w_up[0], up_other], axis=1)
    down = jnp.concatenate([w_down[0], down_other], axis=0)
    proj = jnp.concatenate(by_replica(w_proj[0], proj_other), axis=1).reshape(-1, width)

    places = jnp.arange(pool, dtype=jnp.int32)[:, None]
    pick = (crop_ids[0].reshape(1, -1) == places).astype(bf16)
    pick_other = (ids_other[None, :] == places).astype(bf16)

    def picked(t):
        return pick[:, t * rows : (t + 1) * rows]

    pre = dot(up, pool_mixed[0], 0, 1)
    value, slope = gelu_pair(pre)
    active = value.astype(bf16)
    high = slope.astype(bf16)
    low = (slope - high.astype(f32)).astype(bf16)
    slopes = dot(high, pick) + dot(low, pick)

    decoder = jnp.where(section < half, 0.0, 1.0).astype(bf16)
    mask = jnp.stack([jnp.ones((), bf16), decoder])[:, None, None]
    saved = pool_inputs[0].transpose(1, 2, 0) * mask
    saved_first, saved_second = saved[:, :own_in], saved[:, own_in:]
    saved_own = jnp.where(first, saved_first, saved_second).reshape(-1, pool)
    saved_sent = jnp.where(first, saved_second, saved_first).reshape(-1, pool)
    saved_other = swap(saved_sent)
    last_own = dot(saved_own, picked(ticks - 1)).astype(bf16)
    last_other = dot(saved_other, pick_other).astype(bf16)
    active_other = swap(active[units:])

    hiddens, grads, upstreams = [], [], []
    for t in range(ticks):
        upstreams.append(upstream)
        if t + 1 == ticks:
            seen = dot(jnp.concatenate(upstreams, axis=1), pick, 1, 1).astype(bf16)
            seen_other = swap(seen)
            early = dot(
                jnp.concatenate(grads, axis=1), pick[:, : t * rows], 1, 1
            ).astype(bf16)
            early_other = swap(early)
        slope_now = slopes[:, t * rows : (t + 1) * rows]
        hidden = (dot(down, upstream) * slope_now).astype(bf16)
        hiddens.append(hidden)
        partial = dot(up, hidden).astype(bf16)
        terms = lax.all_to_all(partial.reshape(parts, chunk_rows, rows), "tensor", 0, 0)
        mixed_chunk = (
            jnp.sum(terms.astype(f32), axis=0) + chunk.astype(f32)
        ).astype(bf16)
        if t + 1 < ticks:
            mixed_grad = gather(mixed_chunk).reshape(width, rows)
            grads.append(mixed_grad)
            input_grad = dot(proj, mixed_grad).astype(bf16).reshape(2, chunk_rows, rows)
            above = lax.ppermute(
                input_grad[0], "section", [(i, i - 1) for i in range(1, sections)]
            )
            mirrored = lax.ppermute(
                input_grad[1],
                "section",
                [(i, sections - 1 - i) for i in range(half, sections)],
            )
            summed = (above.astype(f32) + mirrored.astype(f32)).astype(bf16)
            chunk = jnp.where(is_top, loss_grads[t].T, summed)
            upstream = gather(chunk).reshape(width, rows)
        else:
            spread = dot(jnp.concatenate(hiddens, axis=1), pick, 1, 1).astype(bf16)
            spread_other = swap(spread[units:])
            both = gather(mixed_chunk, ("replica", "tensor")).reshape(2, width, rows)
            mixed_grad = jnp.where(first, both[0], both[1])
            input_grad = dot(proj, mixed_grad).astype(bf16).reshape(2, chunk_rows, rows)

    grad_up = dot(
        jnp.concatenate([pool_mixed[0], mixed_other], axis=0),
        jnp.concatenate([spread[:units], spread_other], axis=1),
        0,
        1,
    ).astype(bf16)
    grad_down = dot(
        jnp.concatenate([active[:units], active_other], axis=1),
        jnp.concatenate([seen, seen_other], axis=1),
        1,
        1,
    ).astype(bf16)
    grad_proj = dot(
        jnp.concatenate(
            [saved_own, saved_other, *by_replica(last_own, last_other)], axis=1
        ),
        jnp.concatenate([early, early_other, both[0], both[1]], axis=1),
        1,
        1,
    ).astype(bf16)
    return (
        grad_proj.reshape(1, 2, own_in, width),
        grad_up[None],
        grad_down[None],
        input_grad.transpose(2, 0, 1)[None],
    )


def solution(mesh):
    in_specs = (
        P("section", "replica", None, "tensor"),
        P("section", "replica", None),
        P("section", "replica", None),
        P("section", "replica", "tensor"),
        P(None, "replica", "tensor"),
        P("section", None, ("tensor", "replica"), None),
        P("section", None, ("tensor", "replica")),
        P("section", ("tensor", "replica"), None),
    )
    out_specs = (
        P("section", None, ("tensor", "replica"), None),
        P("section", None, ("tensor", "replica")),
        P("section", ("tensor", "replica"), None),
        P("section", "replica", None, "tensor"),
    )
    return jax.shard_map(body, mesh=mesh, in_specs=in_specs, out_specs=out_specs, check_vma=False)
```

time: 1010 us -> 247 us (0.24)
  the two profiles are of different devices: /device:TPU:1 before, /device:TPU:96 now
where the time goes in v1:
time: 247 us; the launch traced here: 245 us
  starting transfers between devices  87.7 us (36%)
  waiting for transfers between devices  85.1 us (34%)
  blocking collectives  33.2 us (13%)
  matrix products  27.8 us (11%)
  local copies, waits for them, and re-layouts  7.37 us (3%)
  other arithmetic  2.94 us (1%)
    ppermute x10, starting transfers between devices, swap(): return lax.ppermute(x, 'replica', [(0, 1), (1, 0)])  38.2 us
    ppermute x3, waiting for transfers between devices, body(): lax.ppermute(input_grad[1], 'section', [(i, sections - 1 - i) for i in ra...  31.5 us
    dot_general x23, matrix products, dot(): lax.dot_general(a, b, (((ca,), (cb,)), ((), ())), preferred_element_type=...  27.8 us
    all_to_all x6, starting transfers between devices, gather(): return lax.all_to_all(spread, axes, 0, 0)  27.8 us
    all_to_all x2, blocking collectives, gather(): return lax.all_to_all(spread, axes, 0, 0)  22.9 us
    all_to_all x6, waiting for transfers between devices, gather(): return lax.all_to_all(spread, axes, 0, 0)  22.7 us
    ppermute x10, waiting for transfers between devices, swap(): return lax.ppermute(x, 'replica', [(0, 1), (1, 0)])  20.2 us
    all_to_all x3, starting transfers between devices, body(): lax.all_to_all(partial.reshape(parts, chunk_rows, rows), 'tensor', 0, 0)  12.1 us
  transfers between devices with their start and end apart: 25, of which 15 were waited for; matrix products, arithmetic and copies ran while one was open for 12% of the time, Pallas kernels for 0%

profile of v1, /device:TPU:96, one launch (start us, length us, event | category | flops | bytes accessed | tf_op | source)
XLA Modules:
  0.0 245.5 jit_solution(8100702403613285950)
XLA Ops:
  0.7 5.2 %collective-permute-start.2 = (bf16[1408,192]{0,1:T(8,128)(2,1)}, bf16[1408,192]{0,1:T(8,128)(2,1)S(1)}, u32[]{:S(2)}, u32[]{:S(2)}) collective-permute-start(bf16[1408,192]{0,1:T(8,128)(2,1)} %bitcast.118), channel_id=1, source_target_pairs={{0,1},{1,0},{2,3},{3,2},{4,5},{5,4},{6,7},{7,6},{8,9},{9,8},{10,11... | collective-permute-start | bytes 1622024 | tf_op jit(solution)/shard_map/ppermute | solution.py:27
  5.9 2.2 collective-permute-start.3
  8.2 1.6 broadcast_in_dim.22
  9.7 5.3 %all-to-all-start = ((bf16[8,176,128]{2,1,0:T(8,128)(2,1)}), bf16[8,176,128]{2,1,0:T(8,128)(2,1)S(1)}, u32[]{:S(2)}, u32[]{:S(2)}) async-start(bf16[8,176,128]{2,1,0:T(8,128)(2,1)} %broadcast_in_dim.22), calls=%async_computation | async-start | bytes 720896 | tf_op jit(solution)/shard_map/all_to_all | solution.py:33
  15.0 6.7 %collective-permute-done.2 = bf16[1408,192]{0,1:T(8,128)(2,1)S(1)} collective-permute-done((bf16[1408,192]{0,1:T(8,128)(2,1)}, bf16[1408,192]{0,1:T(8,128)(2,1)S(1)}, u32[]{:S(2)}, u32[]{:S(2)}) %collective-permute-start.2) | collective-permute-done | bytes 540704 | tf_op jit(solution)/shard_map/ppermute | solution.py:27
  23.7 10.5 %all-to-all-done = bf16[8,176,128]{2,1,0:T(8,128)(2,1)S(1)} async-done(((bf16[8,176,128]{2,1,0:T(8,128)(2,1)}), bf16[8,176,128]{2,1,0:T(8,128)(2,1)S(1)}, u32[]{:S(2)}, u32[]{:S(2)}) %all-to-all-start) | async-done | bytes 360480 | tf_op jit(solution)/shard_map/all_to_all | solution.py:33
  34.2 1.6 fusion.16
  37.1 5.2 %all-to-all-start.1 = ((bf16[8,176,128]{2,1,0:T(8,128)(2,1)}), bf16[8,176,128]{2,1,0:T(8,128)(2,1)S(1)}, u32[]{:S(2)}, u32[]{:S(2)}) async-start(bf16[8,176,128]{2,1,0:T(8,128)(2,1)} %bitcast.13), calls=%async_computation.1 | async-start | bytes 720896 | tf_op jit(solution)/shard_map/all_to_all | solution.py:106
  42.3 4.3 %collective-permute-start.4 = (bf16[2,88,1408]{2,1,0:T(8,128)(2,1)S(1)}, bf16[2,88,1408]{2,1,0:T(8,128)(2,1)S(1)}, u32[]{:S(2)}, u32[]{:S(2)}) collective-permute-start(bf16[2,88,1408]{2,1,0:T(8,128)(2,1)S(1)} %bitcast.94), channel_id=1, source_target_pairs={{0,1},{1,0},{2,3},{3,2},{4,5},{5,4},{6,7},{7,6},{8,9},{9,8},{10,11... | collective-permute-start | bytes 1486856 | tf_op jit(solution)/shard_map/ppermute | solution.py:27
  46.6 3.0 %all-to-all-done.1 = bf16[8,176,128]{2,1,0:T(8,128)(2,1)S(1)} async-done(((bf16[8,176,128]{2,1,0:T(8,128)(2,1)}), bf16[8,176,128]{2,1,0:T(8,128)(2,1)S(1)}, u32[]{:S(2)}, u32[]{:S(2)}) %all-to-all-start.1) | async-done | bytes 360480 | tf_op jit(solution)/shard_map/all_to_all | solution.py:106
  50.5 3.4 %all-to-all-start.2 = ((bf16[8,176,128]{2,1,0:T(8,128)(2,1)}), bf16[8,176,128]{2,1,0:T(8,128)(2,1)S(1)}, u32[]{:S(2)}, u32[]{:S(2)}) async-start(bf16[8,176,128]{2,1,0:T(8,128)(2,1)} %broadcast_in_dim.23), calls=%async_computation.2 | async-start | bytes 720896 | tf_op jit(solution)/shard_map/all_to_all | solution.py:33
  54.0 9.2 %collective-permute-done.4 = bf16[2,88,1408]{2,1,0:T(8,128)(2,1)S(1)} collective-permute-done((bf16[2,88,1408]{2,1,0:T(8,128)(2,1)S(1)}, bf16[2,88,1408]{2,1,0:T(8,128)(2,1)S(1)}, u32[]{:S(2)}, u32[]{:S(2)}) %collective-permute-start.4) | collective-permute-done | bytes 495648 | tf_op jit(solution)/shard_map/ppermute | solution.py:27
  64.1 1.9 collective-permute-start.5
  66.0 1.3 collective-permute-start.6
  67.7 11.2 %collective-permute-done.6 = bf16[176,128]{1,0:T(8,128)(2,1)S(1)} collective-permute-done((bf16[176,128]{1,0:T(8,128)(2,1)S(1)}, bf16[176,128]{1,0:T(8,128)(2,1)S(1)}, u32[]{:S(2)}, u32[]{:S(2)}) %collective-permute-start.6) | collective-permute-done | bytes 45088 | tf_op jit(solution)/shard_map/ppermute | solution.py:117
  79.0 12.6 %all_to_all.60 = bf16[8,176,128]{2,1,0:T(8,128)(2,1)S(1)} all-to-all(bf16[8,176,128]{2,1,0:T(8,128)(2,1)S(1)} %broadcast_in_dim.24), channel_id=1, replica_groups=mesh['section'=32,'tensor'=8,'replica'=2] {'tensor'}, dimensions={0} | all-to-all | bytes 720896 | tf_op jit(solution)/shard_map/all_to_all | solution.py:33
  91.5 1.7 fusion.17
  93.9 10.3 %all_to_all.61 = bf16[8,176,128]{2,1,0:T(8,128)(2,1)S(1)} all-to-all(bf16[8,176,128]{2,1,0:T(8,128)(2,1)S(1)} %bitcast.103), channel_id=1, replica_groups=mesh['section'=32,'tensor'=8,'replica'=2] {'tensor'}, dimensions={0} | all-to-all | bytes 720896 | tf_op jit(solution)/shard_map/all_to_all | solution.py:106
  104.3 10.3 %all_to_all.62 = bf16[8,176,128]{2,1,0:T(8,128)(2,1)S(1)} all-to-all(bf16[8,176,128]{2,1,0:T(8,128)(2,1)S(1)} %broadcast_in_dim.25), channel_id=1, replica_groups=mesh['section'=32,'tensor'=8,'replica'=2] {'tensor'}, dimensions={0} | all-to-all | bytes 720896 | tf_op jit(solution)/shard_map/all_to_all | solution.py:33
  115.1 1.9 collective-permute-start.7
  117.1 1.3 collective-permute-start.8
  118.8 10.3 %collective-permute-done.8 = bf16[176,128]{1,0:T(8,128)(2,1)S(1)} collective-permute-done((bf16[176,128]{1,0:T(8,128)(2,1)S(1)}, bf16[176,128]{1,0:T(8,128)(2,1)S(1)}, u32[]{:S(2)}, u32[]{:S(2)}) %collective-permute-start.8) | collective-permute-done | bytes 45088 | tf_op jit(solution)/shard_map/ppermute | solution.py:117
  129.8 3.4 %all-to-all-start.6 = ((bf16[8,176,128]{2,1,0:T(8,128)(2,1)}), bf16[8,176,128]{2,1,0:T(8,128)(2,1)S(1)}, u32[]{:S(2)}, u32[]{:S(2)}) async-start(bf16[8,176,128]{2,1,0:T(8,128)(2,1)} %broadcast_in_dim.26), calls=%async_computation.6 | async-start | bytes 720896 | tf_op jit(solution)/shard_map/all_to_all | solution.py:33
  133.3 4.3 %collective-permute-start.12 = (bf16[128,1408]{1,0:T(8,128)(2,1)}, bf16[128,1408]{1,0:T(8,128)(2,1)}, u32[]{:S(2)}, u32[]{:S(2)}) collective-permute-start(bf16[128,1408]{1,0:T(8,128)(2,1)} %bitcast.124), channel_id=1, source_target_pairs={{0,1},{1,0},{2,3},{3,2},{4,5},{5,4},{6,7},{7,6},{8,9},{9,8},{10,11... | collective-permute-start | bytes 1081352 | tf_op jit(solution)/shard_map/ppermute | solution.py:27
  137.6 4.4 %all-to-all-done.6 = bf16[8,176,128]{2,1,0:T(8,128)(2,1)S(1)} async-done(((bf16[8,176,128]{2,1,0:T(8,128)(2,1)}), bf16[8,176,128]{2,1,0:T(8,128)(2,1)S(1)}, u32[]{:S(2)}, u32[]{:S(2)}) %all-to-all-start.6) | async-done | bytes 360480 | tf_op jit(solution)/shard_map/all_to_all | solution.py:33
  142.0 1.8 fusion.18
  145.1 3.4 %all-to-all-start.7 = ((bf16[8,176,128]{2,1,0:T(8,128)(2,1)}), bf16[8,176,128]{2,1,0:T(8,128)(2,1)S(1)}, u32[]{:S(2)}, u32[]{:S(2)}) async-start(bf16[8,176,128]{2,1,0:T(8,128)(2,1)} %bitcast.102), calls=%async_computation.7 | async-start | bytes 720896 | tf_op jit(solution)/shard_map/all_to_all | solution.py:106
  149.6 6.9 %all-to-all-done.7 = bf16[8,176,128]{2,1,0:T(8,128)(2,1)S(1)} async-done(((bf16[8,176,128]{2,1,0:T(8,128)(2,1)}), bf16[8,176,128]{2,1,0:T(8,128)(2,1)S(1)}, u32[]{:S(2)}, u32[]{:S(2)}) %all-to-all-start.7) | async-done | bytes 360480 | tf_op jit(solution)/shard_map/all_to_all | solution.py:106
  157.3 3.4 %all-to-all-start.8 = ((bf16[8,176,128]{2,1,0:T(8,128)(2,1)}), bf16[8,176,128]{2,1,0:T(8,128)(2,1)S(1)}, u32[]{:S(2)}, u32[]{:S(2)}) async-start(bf16[8,176,128]{2,1,0:T(8,128)(2,1)} %broadcast_in_dim.27), calls=%async_computation.8 | async-start | bytes 720896 | tf_op jit(solution)/shard_map/all_to_all | solution.py:33
  161.4 4.1 %collective-permute-start = (bf16[176,128]{1,0:T(8,128)(2,1)}, bf16[176,128]{1,0:T(8,128)(2,1)S(1)}, u32[]{:S(2)}, u32[]{:S(2)}) collective-permute-start(bf16[176,128]{1,0:T(8,128)(2,1)} %bitcast.4), channel_id=1, source_target_pairs={{0,1},{1,0},{2,3},{3,2},{4,5},{5,4},{6,7},{7,6},{8,9},{9,8},{10,11... | collective-permute-start | bytes 135176 | tf_op jit(solution)/shard_map/ppermute | solution.py:27
  165.6 3.2 %collective-permute-start.1 = (s32[128]{0:T(128)S(1)}, s32[128]{0:T(128)S(1)}, u32[]{:S(2)}, u32[]{:S(2)}) collective-permute-start(s32[128]{0:T(128)S(1)} %slice_bitcast_fusion), channel_id=1, source_target_pairs={{0,1},{1,0},{2,3},{3,2},{4,5},{5,4},{6,7},{7,6},{8,9},{9,8},{10,11... | collective-permute-start | bytes 1544 | tf_op jit(solution)/shard_map/ppermute | solution.py:27
  169.2 1.9 collective-permute-start.10
  171.2 1.3 collective-permute-start.11
  173.1 10.0 %collective-permute-done.11 = bf16[176,128]{1,0:T(8,128)(2,1)S(1)} collective-permute-done((bf16[176,128]{1,0:T(8,128)(2,1)S(1)}, bf16[176,128]{1,0:T(8,128)(2,1)S(1)}, u32[]{:S(2)}, u32[]{:S(2)}) %collective-permute-start.11) | collective-permute-done | bytes 45088 | tf_op jit(solution)/shard_map/ppermute | solution.py:117
  184.0 5.6 %all-to-all-start.9 = ((bf16[8,176,128]{2,1,0:T(8,128)(2,1)}), bf16[8,176,128]{2,1,0:T(8,128)(2,1)}, u32[]{:S(2)}, u32[]{:S(2)}) async-start(bf16[8,176,128]{2,1,0:T(8,128)(2,1)} %broadcast_in_dim.28), calls=%async_computation.9 | async-start | bytes 720896 | tf_op jit(solution)/shard_map/all_to_all | solution.py:33
  190.6 7.5 %all-to-all-done.9 = bf16[8,176,128]{2,1,0:T(8,128)(2,1)} async-done(((bf16[8,176,128]{2,1,0:T(8,128)(2,1)}), bf16[8,176,128]{2,1,0:T(8,128)(2,1)}, u32[]{:S(2)}, u32[]{:S(2)}) %all-to-all-start.9) | async-done | bytes 360480 | tf_op jit(solution)/shard_map/all_to_all | solution.py:33
  198.1 1.9 fusion.19
  201.3 3.4 %all-to-all-start.10 = ((bf16[8,176,128]{2,1,0:T(8,128)(2,1)}), bf16[8,176,128]{2,1,0:T(8,128)(2,1)S(1)}, u32[]{:S(2)}, u32[]{:S(2)}) async-start(bf16[8,176,128]{2,1,0:T(8,128)(2,1)} %bitcast.101), calls=%async_computation.10 | async-start | bytes 720896 | tf_op jit(solution)/shard_map/all_to_all | solution.py:106
  205.6 4.1 %collective-permute-start.14 = (bf16[192,128]{1,0:T(8,128)(2,1)S(1)}, bf16[192,128]{1,0:T(8,128)(2,1)}, u32[]{:S(2)}, u32[]{:S(2)}) collective-permute-start(bf16[192,128]{1,0:T(8,128)(2,1)S(1)} %get-tuple-element.10), channel_id=1, source_target_pairs={{0,1},{1,0},{2,3},{3,2},{4,5},{5,4},{6,7},{7,6},{8,9},{9,8},{10,11... | collective-permute-start | bytes 147464 | tf_op jit(solution)/shard_map/ppermute | solution.py:27
  209.7 2.5 convolution_convert_fusion.3
  212.2 3.2 %collective-permute-start.15 = (bf16[1408,128]{0,1:T(8,128)(2,1)}, bf16[1408,128]{0,1:T(8,128)(2,1)}, u32[]{:S(2)}, u32[]{:S(2)}) collective-permute-start(bf16[1408,128]{0,1:T(8,128)(2,1)} %convolution_convert_fusion.3), channel_id=1, source_target_pairs={{0,1},{1,0},{2,3},{3,2},{4,5},{5,4},{6,7},{7,6},{8,9},{9,8},{10,11... | collective-permute-start | bytes 1081352 | tf_op jit(solution)/shard_map/ppermute | solution.py:27
  216.5 6.5 %all-to-all-start.11 = ((bf16[16,176,128]{2,1,0:T(8,128)(2,1)}), bf16[16,176,128]{2,1,0:T(8,128)(2,1)S(1)}, u32[]{:S(2)}, u32[]{:S(2)}) async-start(bf16[16,176,128]{2,1,0:T(8,128)(2,1)} %broadcast_in_dim.29), calls=%async_computation.11 | async-start | bytes 1441792 | tf_op jit(solution)/shard_map/all_to_all | solution.py:33
  224.2 5.5 %collective-permute-start.13 = (bf16[192,128]{1,0:T(8,128)(2,1)S(1)}, bf16[192,128]{1,0:T(8,128)(2,1)S(1)}, u32[]{:S(2)}, u32[]{:S(2)}) collective-permute-start(bf16[192,128]{1,0:T(8,128)(2,1)S(1)} %get-tuple-element.12), channel_id=1, source_target_pairs={{0,1},{1,0},{2,3},{3,2},{4,5},{5,4},{6,7},{7,6},{8,9},{9,8},{10,11... | collective-permute-start | bytes 147464 | tf_op jit(solution)/shard_map/ppermute | solution.py:27
  230.9 2.0 collective-permute-start.9
  234.0 2.1 fusion.1
  236.1 2.3 fusion
  240.0 3.1 %collective-permute-done.9 = bf16[1408,128]{0,1:T(8,128)(2,1)} collective-permute-done((bf16[1408,128]{0,1:T(8,128)(2,1)}, bf16[1408,128]{0,1:T(8,128)(2,1)}, u32[]{:S(2)}, u32[]{:S(2)}) %collective-permute-start.9) | collective-permute-done | bytes 360480 | tf_op jit(solution)/shard_map/ppermute | solution.py:27
  243.1 2.3 convolution_convert_fusion.2
  (126 shorter events, 22.5 us)
Async XLA Ops:
  0.6 21.1 %copy-start.13 = (bf16[1,1408,192]{1,2,0:T(8,128)(2,1)S(1)}, bf16[1,1408,192]{1,2,0:T(8,128)(2,1)}, u32[]{:S(2)}) copy-start(bf16[1,1408,192]{1,2,0:T(8,128)(2,1)} %param.14) | copy-start | bytes 1622020
  0.6 21.1 %copy-start.23 = (bf16[1,128,1408]{2,1,0:T(8,128)(2,1)S(1)}, bf16[1,128,1408]{2,1,0:T(8,128)(2,1)}, u32[]{:S(2)}) copy-start(bf16[1,128,1408]{2,1,0:T(8,128)(2,1)} %param.9) | copy-start | bytes 1081348
  0.7 21.1 %collective-permute-start.2 = (bf16[1408,192]{0,1:T(8,128)(2,1)}, bf16[1408,192]{0,1:T(8,128)(2,1)S(1)}, u32[]{:S(2)}, u32[]{:S(2)}) collective-permute-start(bf16[1408,192]{0,1:T(8,128)(2,1)} %bitcast.118), channel_id=1, source_target_pairs={{0,1},{1,0},{2,3},{3,2},{4,5},{5,4},{6,7},{7,6},{8,9},{9,8},{10,11... | collective-permute-start | bytes 1622024 | tf_op jit(solution)/shard_map/ppermute | solution.py:27
  5.9 28.3 %collective-permute-start.3 = (bf16[192,1408]{1,0:T(8,128)(2,1)}, bf16[192,1408]{1,0:T(8,128)(2,1)}, u32[]{:S(2)}, u32[]{:S(2)}) collective-permute-start(bf16[192,1408]{1,0:T(8,128)(2,1)} %bitcast.113), channel_id=1, source_target_pairs={{0,1},{1,0},{2,3},{3,2},{4,5},{5,4},{6,7},{7,6},{8,9},{9,8},{10,11... | collective-permute-start | bytes 1622024 | tf_op jit(solution)/shard_map/ppermute | solution.py:27
  9.7 24.5 %all-to-all-start = ((bf16[8,176,128]{2,1,0:T(8,128)(2,1)}), bf16[8,176,128]{2,1,0:T(8,128)(2,1)S(1)}, u32[]{:S(2)}, u32[]{:S(2)}) async-start(bf16[8,176,128]{2,1,0:T(8,128)(2,1)} %broadcast_in_dim.22), calls=%async_computation | async-start | bytes 720896 | tf_op jit(solution)/shard_map/all_to_all | solution.py:33
  15.0 7.9 %copy-start.11 = (s32[1,4,128]{2,1,0:T(4,128)S(1)}, s32[1,4,128]{2,1,0:T(4,128)}, u32[]{:S(2)}) copy-start(s32[1,4,128]{2,1,0:T(4,128)} %param.10) | copy-start | bytes 6148
  23.3 10.9 %copy-start.12 = (bf16[1,192,1408]{2,1,0:T(8,128)(2,1)S(1)}, bf16[1,192,1408]{2,1,0:T(8,128)(2,1)}, u32[]{:S(2)}) copy-start(bf16[1,192,1408]{2,1,0:T(8,128)(2,1)} %param.15) | copy-start | bytes 1622020
  35.9 6.5 %copy-start = (bf16[1,2,88,1408]{3,2,1,0:T(8,128)(2,1)S(1)}, bf16[1,2,88,1408]{3,2,1,0:T(8,128)(2,1)}, u32[]{:S(2)}) copy-start(bf16[1,2,88,1408]{3,2,1,0:T(8,128)(2,1)} %param.13) | copy-start | bytes 1486852
  37.1 12.6 %copy-start.4 = (bf16[1,128,176]{1,2,0:T(8,128)(2,1)S(1)}, bf16[1,128,176]{1,2,0:T(8,128)(2,1)}, u32[]{:S(2)}) copy-start(bf16[1,128,176]{1,2,0:T(8,128)(2,1)} %param.11) | copy-start | bytes 135172
  37.1 12.6 %all-to-all-start.1 = ((bf16[8,176,128]{2,1,0:T(8,128)(2,1)}), bf16[8,176,128]{2,1,0:T(8,128)(2,1)S(1)}, u32[]{:S(2)}, u32[]{:S(2)}) async-start(bf16[8,176,128]{2,1,0:T(8,128)(2,1)} %bitcast.13), calls=%async_computation.1 | async-start | bytes 720896 | tf_op jit(solution)/shard_map/all_to_all | solution.py:106
  42.3 20.9 %collective-permute-start.4 = (bf16[2,88,1408]{2,1,0:T(8,128)(2,1)S(1)}, bf16[2,88,1408]{2,1,0:T(8,128)(2,1)S(1)}, u32[]{:S(2)}, u32[]{:S(2)}) collective-permute-start(bf16[2,88,1408]{2,1,0:T(8,128)(2,1)S(1)} %bitcast.94), channel_id=1, source_target_pairs={{0,1},{1,0},{2,3},{3,2},{4,5},{5,4},{6,7},{7,6},{8,9},{9,8},{10,11... | collective-permute-start | bytes 1486856 | tf_op jit(solution)/shard_map/ppermute | solution.py:27
  50.5 13.1 %all-to-all-start.2 = ((bf16[8,176,128]{2,1,0:T(8,128)(2,1)}), bf16[8,176,128]{2,1,0:T(8,128)(2,1)S(1)}, u32[]{:S(2)}, u32[]{:S(2)}) async-start(bf16[8,176,128]{2,1,0:T(8,128)(2,1)} %broadcast_in_dim.23), calls=%async_computation.2 | async-start | bytes 720896 | tf_op jit(solution)/shard_map/all_to_all | solution.py:33
  63.4 15.4 %copy-start.5 = (bf16[3,128,176]{1,2,0:T(8,128)(2,1)S(1)}, bf16[3,128,176]{1,2,0:T(8,128)(2,1)}, u32[]{:S(2)}) copy-start(bf16[3,128,176]{1,2,0:T(8,128)(2,1)} %param.12) | copy-start | bytes 405508
  64.1 3.6 %collective-permute-start.5 = (bf16[176,128]{1,0:T(8,128)(2,1)S(1)}, bf16[176,128]{1,0:T(8,128)(2,1)S(1)}, u32[]{:S(2)}, u32[]{:S(2)}) collective-permute-start(bf16[176,128]{1,0:T(8,128)(2,1)S(1)} %get-tuple-element.21), channel_id=1, source_target_pairs={{16,0},{32,16},{48,32},{64,48},{80,64},{96,80},{112,96},{128,112},... | collective-permute-start | bytes 135176 | tf_op jit(solution)/shard_map/ppermute | solution.py:114
  66.0 12.9 %collective-permute-start.6 = (bf16[176,128]{1,0:T(8,128)(2,1)S(1)}, bf16[176,128]{1,0:T(8,128)(2,1)S(1)}, u32[]{:S(2)}, u32[]{:S(2)}) collective-permute-start(bf16[176,128]{1,0:T(8,128)(2,1)S(1)} %get-tuple-element.22), channel_id=1, source_target_pairs={{256,240},{272,224},{288,208},{304,192},{320,176},{336,160},{352,1... | collective-permute-start | bytes 135176 | tf_op jit(solution)/shard_map/ppermute | solution.py:117
  91.5 1.7 copy-start.20
  115.1 3.6 %collective-permute-start.7 = (bf16[176,128]{1,0:T(8,128)(2,1)S(1)}, bf16[176,128]{1,0:T(8,128)(2,1)S(1)}, u32[]{:S(2)}, u32[]{:S(2)}) collective-permute-start(bf16[176,128]{1,0:T(8,128)(2,1)S(1)} %get-tuple-element.19), channel_id=1, source_target_pairs={{16,0},{32,16},{48,32},{64,48},{80,64},{96,80},{112,96},{128,112},... | collective-permute-start | bytes 135176 | tf_op jit(solution)/shard_map/ppermute | solution.py:114
  117.1 12.0 %collective-permute-start.8 = (bf16[176,128]{1,0:T(8,128)(2,1)S(1)}, bf16[176,128]{1,0:T(8,128)(2,1)S(1)}, u32[]{:S(2)}, u32[]{:S(2)}) collective-permute-start(bf16[176,128]{1,0:T(8,128)(2,1)S(1)} %get-tuple-element.20), channel_id=1, source_target_pairs={{256,240},{272,224},{288,208},{304,192},{320,176},{336,160},{352,1... | collective-permute-start | bytes 135176 | tf_op jit(solution)/shard_map/ppermute | solution.py:117
  129.8 12.1 %all-to-all-start.6 = ((bf16[8,176,128]{2,1,0:T(8,128)(2,1)}), bf16[8,176,128]{2,1,0:T(8,128)(2,1)S(1)}, u32[]{:S(2)}, u32[]{:S(2)}) async-start(bf16[8,176,128]{2,1,0:T(8,128)(2,1)} %broadcast_in_dim.26), calls=%async_computation.6 | async-start | bytes 720896 | tf_op jit(solution)/shard_map/all_to_all | solution.py:33
  133.3 99.6 %collective-permute-start.12 = (bf16[128,1408]{1,0:T(8,128)(2,1)}, bf16[128,1408]{1,0:T(8,128)(2,1)}, u32[]{:S(2)}, u32[]{:S(2)}) collective-permute-start(bf16[128,1408]{1,0:T(8,128)(2,1)} %bitcast.124), channel_id=1, source_target_pairs={{0,1},{1,0},{2,3},{3,2},{4,5},{5,4},{6,7},{7,6},{8,9},{9,8},{10,11... | collective-permute-start | bytes 1081352 | tf_op jit(solution)/shard_map/ppermute | solution.py:27
  142.0 1.9 copy-start.3
  142.0 1.9 copy-start.16
  142.0 1.9 copy-start.21
  145.1 11.4 %all-to-all-start.7 = ((bf16[8,176,128]{2,1,0:T(8,128)(2,1)}), bf16[8,176,128]{2,1,0:T(8,128)(2,1)S(1)}, u32[]{:S(2)}, u32[]{:S(2)}) async-start(bf16[8,176,128]{2,1,0:T(8,128)(2,1)} %bitcast.102), calls=%async_computation.7 | async-start | bytes 720896 | tf_op jit(solution)/shard_map/all_to_all | solution.py:106
  157.3 11.4 %all-to-all-start.8 = ((bf16[8,176,128]{2,1,0:T(8,128)(2,1)}), bf16[8,176,128]{2,1,0:T(8,128)(2,1)S(1)}, u32[]{:S(2)}, u32[]{:S(2)}) async-start(bf16[8,176,128]{2,1,0:T(8,128)(2,1)} %broadcast_in_dim.27), calls=%async_computation.8 | async-start | bytes 720896 | tf_op jit(solution)/shard_map/all_to_all | solution.py:33
  161.4 28.4 %collective-permute-start = (bf16[176,128]{1,0:T(8,128)(2,1)}, bf16[176,128]{1,0:T(8,128)(2,1)S(1)}, u32[]{:S(2)}, u32[]{:S(2)}) collective-permute-start(bf16[176,128]{1,0:T(8,128)(2,1)} %bitcast.4), channel_id=1, source_target_pairs={{0,1},{1,0},{2,3},{3,2},{4,5},{5,4},{6,7},{7,6},{8,9},{9,8},{10,11... | collective-permute-start | bytes 135176 | tf_op jit(solution)/shard_map/ppermute | solution.py:27
  165.6 24.2 %collective-permute-start.1 = (s32[128]{0:T(128)S(1)}, s32[128]{0:T(128)S(1)}, u32[]{:S(2)}, u32[]{:S(2)}) collective-permute-start(s32[128]{0:T(128)S(1)} %slice_bitcast_fusion), channel_id=1, source_target_pairs={{0,1},{1,0},{2,3},{3,2},{4,5},{5,4},{6,7},{7,6},{8,9},{9,8},{10,11... | collective-permute-start | bytes 1544 | tf_op jit(solution)/shard_map/ppermute | solution.py:27
  169.2 3.9 %collective-permute-start.10 = (bf16[176,128]{1,0:T(8,128)(2,1)S(1)}, bf16[176,128]{1,0:T(8,128)(2,1)S(1)}, u32[]{:S(2)}, u32[]{:S(2)}) collective-permute-start(bf16[176,128]{1,0:T(8,128)(2,1)S(1)} %get-tuple-element.17), channel_id=1, source_target_pairs={{16,0},{32,16},{48,32},{64,48},{80,64},{96,80},{112,96},{128,112},... | collective-permute-start | bytes 135176 | tf_op jit(solution)/shard_map/ppermute | solution.py:114
  171.2 12.0 %collective-permute-start.11 = (bf16[176,128]{1,0:T(8,128)(2,1)S(1)}, bf16[176,128]{1,0:T(8,128)(2,1)S(1)}, u32[]{:S(2)}, u32[]{:S(2)}) collective-permute-start(bf16[176,128]{1,0:T(8,128)(2,1)S(1)} %get-tuple-element.18), channel_id=1, source_target_pairs={{256,240},{272,224},{288,208},{304,192},{320,176},{336,160},{352,1... | collective-permute-start | bytes 135176 | tf_op jit(solution)/shard_map/ppermute | solution.py:117
  183.2 6.4 %copy-start.6 = (pred[128,512]{1,0:T(32,128)(4,1)S(1)}, pred[128,512]{1,0:T(32,128)(4,1)}, u32[]{:S(2)}) copy-start(pred[128,512]{1,0:T(32,128)(4,1)} %iota_compare_fusion) | copy-start | bytes 196612
  184.0 14.2 %all-to-all-start.9 = ((bf16[8,176,128]{2,1,0:T(8,128)(2,1)}), bf16[8,176,128]{2,1,0:T(8,128)(2,1)}, u32[]{:S(2)}, u32[]{:S(2)}) async-start(bf16[8,176,128]{2,1,0:T(8,128)(2,1)} %broadcast_in_dim.28), calls=%async_computation.9 | async-start | bytes 720896 | tf_op jit(solution)/shard_map/all_to_all | solution.py:33
  189.8 10.2 %copy-start.7 = (bf16[176,128]{1,0:T(8,128)(2,1)}, bf16[176,128]{1,0:T(8,128)(2,1)S(1)}, u32[]{:S(2)}) copy-start(bf16[176,128]{1,0:T(8,128)(2,1)S(1)} %collective-permute-done) | copy-start | bytes 135172
  198.1 1.9 copy-start.17
  198.1 1.9 copy-start.22
  200.0 9.7 %copy-start.2 = (bf16[8,176,128]{2,1,0:T(8,128)(2,1)S(1)}, bf16[8,176,128]{2,1,0:T(8,128)(2,1)}, u32[]{:S(2)}) copy-start(bf16[8,176,128]{2,1,0:T(8,128)(2,1)} %copy-done.1) | copy-start | bytes 1081348
  201.3 14.1 %all-to-all-start.10 = ((bf16[8,176,128]{2,1,0:T(8,128)(2,1)}), bf16[8,176,128]{2,1,0:T(8,128)(2,1)S(1)}, u32[]{:S(2)}, u32[]{:S(2)}) async-start(bf16[8,176,128]{2,1,0:T(8,128)(2,1)} %bitcast.101), calls=%async_computation.10 | async-start | bytes 720896 | tf_op jit(solution)/shard_map/all_to_all | solution.py:106
  205.6 30.6 %collective-permute-start.14 = (bf16[192,128]{1,0:T(8,128)(2,1)S(1)}, bf16[192,128]{1,0:T(8,128)(2,1)}, u32[]{:S(2)}, u32[]{:S(2)}) collective-permute-start(bf16[192,128]{1,0:T(8,128)(2,1)S(1)} %get-tuple-element.10), channel_id=1, source_target_pairs={{0,1},{1,0},{2,3},{3,2},{4,5},{5,4},{6,7},{7,6},{8,9},{9,8},{10,11... | collective-permute-start | bytes 147464 | tf_op jit(solution)/shard_map/ppermute | solution.py:27
  212.2 24.0 %collective-permute-start.15 = (bf16[1408,128]{0,1:T(8,128)(2,1)}, bf16[1408,128]{0,1:T(8,128)(2,1)}, u32[]{:S(2)}, u32[]{:S(2)}) collective-permute-start(bf16[1408,128]{0,1:T(8,128)(2,1)} %convolution_convert_fusion.3), channel_id=1, source_target_pairs={{0,1},{1,0},{2,3},{3,2},{4,5},{5,4},{6,7},{7,6},{8,9},{9,8},{10,11... | collective-permute-start | bytes 1081352 | tf_op jit(solution)/shard_map/ppermute | solution.py:27
  215.4 7.5 %copy-start.26 = (bf16[384,128]{0,1:T(8,128)(2,1)S(1)}, bf16[384,128]{0,1:T(8,128)(2,1)}, u32[]{:S(2)}) copy-start(bf16[384,128]{0,1:T(8,128)(2,1)} %copy-done.25) | copy-start | bytes 294916
  215.5 7.5 %copy-start.28 = (bf16[384,128]{0,1:T(8,128)(2,1)S(1)}, bf16[384,128]{0,1:T(8,128)(2,1)}, u32[]{:S(2)}) copy-start(bf16[384,128]{0,1:T(8,128)(2,1)} %copy-done.27) | copy-start | bytes 294916
  215.5 7.5 %copy-start.30 = (bf16[384,128]{0,1:T(8,128)(2,1)S(1)}, bf16[384,128]{0,1:T(8,128)(2,1)}, u32[]{:S(2)}) copy-start(bf16[384,128]{0,1:T(8,128)(2,1)} %copy-done.29) | copy-start | bytes 294916
  216.5 22.0 %all-to-all-start.11 = ((bf16[16,176,128]{2,1,0:T(8,128)(2,1)}), bf16[16,176,128]{2,1,0:T(8,128)(2,1)S(1)}, u32[]{:S(2)}, u32[]{:S(2)}) async-start(bf16[16,176,128]{2,1,0:T(8,128)(2,1)} %broadcast_in_dim.29), calls=%async_computation.11 | async-start | bytes 1441792 | tf_op jit(solution)/shard_map/all_to_all | solution.py:33
  224.2 9.8 %copy-start.24 = (bf16[1,128,1408]{2,1,0:T(8,128)(2,1)S(1)}, bf16[1,128,1408]{2,1,0:T(8,128)(2,1)}, u32[]{:S(2)}) copy-start(bf16[1,128,1408]{2,1,0:T(8,128)(2,1)} %param.9) | copy-start | bytes 1081348
  224.2 9.8 %collective-permute-start.13 = (bf16[192,128]{1,0:T(8,128)(2,1)S(1)}, bf16[192,128]{1,0:T(8,128)(2,1)S(1)}, u32[]{:S(2)}, u32[]{:S(2)}) collective-permute-start(bf16[192,128]{1,0:T(8,128)(2,1)S(1)} %get-tuple-element.12), channel_id=1, source_target_pairs={{0,1},{1,0},{2,3},{3,2},{4,5},{5,4},{6,7},{7,6},{8,9},{9,8},{10,11... | collective-permute-start | bytes 147464 | tf_op jit(solution)/shard_map/ppermute | solution.py:27
  230.9 12.2 %collective-permute-start.9 = (bf16[1408,128]{0,1:T(8,128)(2,1)}, bf16[1408,128]{0,1:T(8,128)(2,1)}, u32[]{:S(2)}, u32[]{:S(2)}) collective-permute-start(bf16[1408,128]{0,1:T(8,128)(2,1)} %convolution_convert_fusion.5), channel_id=1, source_target_pairs={{0,1},{1,0},{2,3},{3,2},{4,5},{5,4},{6,7},{7,6},{8,9},{9,8},{10,11... | collective-permute-start | bytes 1081352 | tf_op jit(solution)/shard_map/ppermute | solution.py:27
  238.7 4.4 %copy-start.8 = (bf16[176,128]{1,0:T(8,128)(2,1)S(1)}, bf16[176,128]{1,0:T(8,128)(2,1)}, u32[]{:S(2)}) copy-start(bf16[176,128]{1,0:T(8,128)(2,1)} %copy-done.7) | copy-start | bytes 135172
  238.7 4.4 %copy-start.9 = (bf16[176,128]{1,0:T(8,128)(2,1)S(1)}, bf16[176,128]{1,0:T(8,128)(2,1)}, u32[]{:S(2)}) copy-start(bf16[176,128]{1,0:T(8,128)(2,1)} %get-tuple-element.13) | copy-start | bytes 135172
  238.7 4.4 %copy-start.10 = (bf16[176,128]{1,0:T(8,128)(2,1)S(1)}, bf16[176,128]{1,0:T(8,128)(2,1)}, u32[]{:S(2)}) copy-start(bf16[176,128]{1,0:T(8,128)(2,1)} %get-tuple-element.14) | copy-start | bytes 135172
  (9 other events, 12.1 us)

commit v2 on v1

--- a/solution.py
+++ b/solution.py
@@ -51,32 +51,28 @@
     def by_replica(own, other):
         return jnp.where(first, own, other), jnp.where(first, other, own)
 
+    def tied(*values):
+        return lax.optimization_barrier(values)
+
     up_other = swap(w_up[0])
     down_other = swap(w_down[0])
-    proj_other = swap(w_proj[0])
-    mixed_other = swap(pool_mixed[0])
-    ids_other = swap(crop_ids[0, ticks - 1])
-
     chunk = incoming[0].T
     upstream = gather(chunk).reshape(width, rows)
+    upstream, proj_own = tied(upstream, w_proj[0])
+    proj_other = swap(proj_own)
 
     up = jnp.concatenate([w_up[0], up_other], axis=1)
     down = jnp.concatenate([w_down[0], down_other], axis=0)
-    proj = jnp.concatenate(by_replica(w_proj[0], proj_other), axis=1).reshape(-1, width)
+    proj = jnp.concatenate(by_replica(proj_own, proj_other), axis=1).reshape(-1, width)
 
     places = jnp.arange(pool, dtype=jnp.int32)[:, None]
-    pick = (crop_ids[0].reshape(1, -1) == places).astype(bf16)
-    pick_other = (ids_other[None, :] == places).astype(bf16)
-
-    def picked(t):
-        return pick[:, t * rows : (t + 1) * rows]
+    pick = [(ids[None, :] == places).astype(bf16) for ids in crop_ids[0]]
 
     pre = dot(up, pool_mixed[0], 0, 1)
     value, slope = gelu_pair(pre)
     active = value.astype(bf16)
     high = slope.astype(bf16)
     low = (slope - high.astype(f32)).astype(bf16)
-    slopes = dot(high, pick) + dot(low, pick)
 
     decoder = jnp.where(section < half, 0.0, 1.0).astype(bf16)
     mask = jnp.stack([jnp.ones((), bf16), decoder])[:, None, None]
@@ -84,32 +80,30 @@
     saved_first, saved_second = saved[:, :own_in], saved[:, own_in:]
     saved_own = jnp.where(first, saved_first, saved_second).reshape(-1, pool)
     saved_sent = jnp.where(first, saved_second, saved_first).reshape(-1, pool)
-    saved_other = swap(saved_sent)
-    last_own = dot(saved_own, picked(ticks - 1)).astype(bf16)
-    last_other = dot(saved_other, pick_other).astype(bf16)
-    active_other = swap(active[units:])
+    ids_sent = jnp.broadcast_to(crop_ids[0, ticks - 1].astype(bf16)[None], (16, rows))
+    small = jnp.concatenate([saved_sent, active[units:], ids_sent], axis=0)
 
-    hiddens, grads, upstreams = [], [], []
+    seen, spread, early = 0.0, 0.0, 0.0
     for t in range(ticks):
-        upstreams.append(upstream)
-        if t + 1 == ticks:
-            seen = dot(jnp.concatenate(upstreams, axis=1), pick, 1, 1).astype(bf16)
-            seen_other = swap(seen)
-            early = dot(
-                jnp.concatenate(grads, axis=1), pick[:, : t * rows], 1, 1
-            ).astype(bf16)
-            early_other = swap(early)
-        slope_now = slopes[:, t * rows : (t + 1) * rows]
+        slope_now = dot(high, pick[t]) + dot(low, pick[t])
         hidden = (dot(down, upstream) * slope_now).astype(bf16)
-        hiddens.append(hidden)
         partial = dot(up, hidden).astype(bf16)
         terms = lax.all_to_all(partial.reshape(parts, chunk_rows, rows), "tensor", 0, 0)
+        upstream_late, hidden_late, _ = tied(upstream, hidden, partial)
+        seen = seen + dot(upstream_late, pick[t], 1, 1)
+        spread = spread + dot(hidden_late, pick[t], 1, 1)
+        if t + 1 == ticks:
+            seen = seen.astype(bf16)
+            seen_other = swap(seen)
+            spread = spread.astype(bf16)
+            spread_other = swap(spread[units:])
+            terms, seen_other, spread_other = tied(terms, seen_other, spread_other)
         mixed_chunk = (
             jnp.sum(terms.astype(f32), axis=0) + chunk.astype(f32)
         ).astype(bf16)
         if t + 1 < ticks:
             mixed_grad = gather(mixed_chunk).reshape(width, rows)
-            grads.append(mixed_grad)
+            early = early + dot(mixed_grad, pick[t], 1, 1)
             input_grad = dot(proj, mixed_grad).astype(bf16).reshape(2, chunk_rows, rows)
             above = lax.ppermute(
                 input_grad[0], "section", [(i, i - 1) for i in range(1, sections)]
@@ -119,15 +113,35 @@
                 "section",
                 [(i, sections - 1 - i) for i in range(half, sections)],
             )
+            if t == 0:
+                mixed_own, _ = tied(pool_mixed[0], mixed_grad)
+                sent = swap(mixed_own)
+            elif t == 1:
+                small, _ = tied(small, mixed_grad)
+                sent = swap(small)
+            else:
+                early = early.astype(bf16)
+                sent = swap(early)
             summed = (above.astype(f32) + mirrored.astype(f32)).astype(bf16)
             chunk = jnp.where(is_top, loss_grads[t].T, summed)
             upstream = gather(chunk).reshape(width, rows)
+            upstream, sent = tied(upstream, sent)
+            if t == 0:
+                mixed_other = sent
+            elif t == 1:
+                count = saved_own.shape[0]
+                saved_other = sent[:count]
+                active_other = sent[count : count + units]
+                ids_other = sent[count + units].astype(jnp.int32)
+                pick_other = (ids_other[None, :] == places).astype(bf16)
+                last_own = dot(saved_own, pick[ticks - 1]).astype(bf16)
+                last_other = dot(saved_other, pick_other).astype(bf16)
+            else:
+                early_other = sent
         else:
-            spread = dot(jnp.concatenate(hiddens, axis=1), pick, 1, 1).astype(bf16)
-            spread_other = swap(spread[units:])
             both = gather(mixed_chunk, ("replica", "tensor")).reshape(2, width, rows)
-            mixed_grad = jnp.where(first, both[0], both[1])
-            input_grad = dot(proj, mixed_grad).astype(bf16).reshape(2, chunk_rows, rows)
+            input_grad = jnp.where(first, dot(proj, both[0]), dot(proj, both[1]))
+            input_grad = input_grad.astype(bf16).reshape(2, chunk_rows, rows)
 
     grad_up = dot(
         jnp.concatenate([pool_mixed[0], mixed_other], axis=0),

time: 247 us -> 251 us (1.016)
  blocking collectives: 33.2 us -> 0 us
  waiting for transfers between devices: 85.1 us -> 114 us
  matrix products: 27.8 us -> 33.1 us
  starting transfers between devices: 87.7 us -> 91.1 us
    all_to_all x3 -> x0, blocking collectives: 33.2 us -> none  [the longest x2 22.9 us: gather(): return lax.all_to_all(spread, axes, 0, 0)]
    all_to_all x6 -> x8, waiting for transfers between devices: 22.7 us -> 44.4 us  [gather(): return lax.all_to_all(spread, axes, 0, 0)]
    ppermute x10 -> x8, waiting for transfers between devices: 20.2 us -> 31.1 us  [swap(): return lax.ppermute(x, 'replica', [(0, 1), (1, 0)])]
    ppermute x3, waiting for transfers between devices: 31.5 us -> 22.7 us  [body(): lax.ppermute(input_grad[1], 'section', [(i, sections - 1 - i) for i in ra...]
    all_to_all x3 -> x4, waiting for transfers between devices: 9.96 us -> 15.4 us  [body(): lax.all_to_all(partial.reshape(parts, chunk_rows, rows), 'tensor', 0, 0)]
    dot_general x23 -> x38, matrix products: 27.8 us -> 33.1 us  [dot(): lax.dot_general(a, b, (((ca,), (cb,)), ((), ())), preferred_element_type=...]
    all_to_all x3 -> x4, starting transfers between devices: 12.1 us -> 16.6 us  [body(): lax.all_to_all(partial.reshape(parts, chunk_rows, rows), 'tensor', 0, 0)]
    ppermute x10 -> x8, starting transfers between devices: 38.2 us -> 34.1 us  [swap(): return lax.ppermute(x, 'replica', [(0, 1), (1, 0)])]
  transfers between devices with their start and end apart: 25 -> 26, of which waited for: 15 -> 17; matrix products, arithmetic and copies ran while one was open for 12% -> 9% of each run, Pallas kernels for 0% -> 0%
where the time goes in v2:
time: 251 us; the launch traced here: 249 us
  waiting for transfers between devices  114 us (45%)
  starting transfers between devices  91.1 us (36%)
  matrix products  33.1 us (13%)
  local copies, waits for them, and re-layouts  7.92 us (3%)
    all_to_all x8, waiting for transfers between devices, gather(): return lax.all_to_all(spread, axes, 0, 0)  44.4 us
    ppermute x8, starting transfers between devices, swap(): return lax.ppermute(x, 'replica', [(0, 1), (1, 0)])  34.1 us
    dot_general x38, matrix products, dot(): lax.dot_general(a, b, (((ca,), (cb,)), ((), ())), preferred_element_type=...  33.1 us
    ppermute x8, waiting for transfers between devices, swap(): return lax.ppermute(x, 'replica', [(0, 1), (1, 0)])  31.1 us
    all_to_all x8, starting transfers between devices, gather(): return lax.all_to_all(spread, axes, 0, 0)  30.8 us
    ppermute x3, waiting for transfers between devices, body(): lax.ppermute(input_grad[1], 'section', [(i, sections - 1 - i) for i in ra...  22.7 us
    all_to_all x4, starting transfers between devices, body(): lax.all_to_all(partial.reshape(parts, chunk_rows, rows), 'tensor', 0, 0)  16.6 us
    all_to_all x4, waiting for transfers between devices, body(): lax.all_to_all(partial.reshape(parts, chunk_rows, rows), 'tensor', 0, 0)  15.4 us
  transfers between devices with their start and end apart: 26, of which 17 were waited for; matrix products, arithmetic and copies ran while one was open for 9% of the time, Pallas kernels for 0%

profile of v2, /device:TPU:96, one launch (start us, length us, event | category | flops | bytes accessed | tf_op | source)
XLA Modules:
  0.0 248.9 jit_solution(9512888788149365502)
XLA Ops:
  0.7 5.2 %collective-permute-start.1 = (bf16[1408,192]{0,1:T(8,128)(2,1)}, bf16[1408,192]{0,1:T(8,128)(2,1)S(1)}, u32[]{:S(2)}, u32[]{:S(2)}) collective-permute-start(bf16[1408,192]{0,1:T(8,128)(2,1)} %bitcast.144), channel_id=1, source_target_pairs={{0,1},{1,0},{2,3},{3,2},{4,5},{5,4},{6,7},{7,6},{8,9},{9,8},{10,11... | collective-permute-start | bytes 1622024 | tf_op jit(solution)/shard_map/ppermute | solution.py:27
  5.9 1.6 broadcast_in_dim.24
  7.5 4.4 %all-to-all-start = ((bf16[8,176,128]{2,1,0:T(8,128)(2,1)}), bf16[8,176,128]{2,1,0:T(8,128)(2,1)S(1)}, u32[]{:S(2)}, u32[]{:S(2)}) async-start(bf16[8,176,128]{2,1,0:T(8,128)(2,1)} %broadcast_in_dim.24), calls=%async_computation | async-start | bytes 720896 | tf_op jit(solution)/shard_map/all_to_all | solution.py:33
  11.9 3.7 %collective-permute-start.2 = (bf16[192,1408]{1,0:T(8,128)(2,1)S(1)}, bf16[192,1408]{1,0:T(8,128)(2,1)}, u32[]{:S(2)}, u32[]{:S(2)}) collective-permute-start(bf16[192,1408]{1,0:T(8,128)(2,1)S(1)} %bitcast.142), channel_id=1, source_target_pairs={{0,1},{1,0},{2,3},{3,2},{4,5},{5,4},{6,7},{7,6},{8,9},{9,8},{10,11... | collective-permute-start | bytes 1622024 | tf_op jit(solution)/shard_map/ppermute | solution.py:27
  15.8 8.0 %all-to-all-done = bf16[8,176,128]{2,1,0:T(8,128)(2,1)S(1)} async-done(((bf16[8,176,128]{2,1,0:T(8,128)(2,1)}), bf16[8,176,128]{2,1,0:T(8,128)(2,1)S(1)}, u32[]{:S(2)}, u32[]{:S(2)}) %all-to-all-start) | async-done | bytes 360480 | tf_op jit(solution)/shard_map/all_to_all | solution.py:33
  23.8 1.7 subtract_convert_fusion
  25.9 8.1 %collective-permute-done.2 = bf16[192,1408]{1,0:T(8,128)(2,1)} collective-permute-done((bf16[192,1408]{1,0:T(8,128)(2,1)S(1)}, bf16[192,1408]{1,0:T(8,128)(2,1)}, u32[]{:S(2)}, u32[]{:S(2)}) %collective-permute-start.2) | collective-permute-done | bytes 540704 | tf_op jit(solution)/shard_map/ppermute | solution.py:27
  34.0 1.5 fusion.11
  36.7 5.4 %all-to-all-start.1 = ((bf16[8,176,128]{2,1,0:T(8,128)(2,1)}), bf16[8,176,128]{2,1,0:T(8,128)(2,1)S(1)}, u32[]{:S(2)}, u32[]{:S(2)}) async-start(bf16[8,176,128]{2,1,0:T(8,128)(2,1)} %bitcast.17), calls=%async_computation.1 | async-start | bytes 720896 | tf_op jit(solution)/shard_map/all_to_all | solution.py:91
  42.3 4.8 %collective-permute-start = (bf16[2,88,1408]{2,1,0:T(8,128)(2,1)S(1)}, bf16[2,88,1408]{2,1,0:T(8,128)(2,1)S(1)}, u32[]{:S(2)}, u32[]{:S(2)}) collective-permute-start(bf16[2,88,1408]{2,1,0:T(8,128)(2,1)S(1)} %bitcast.131), channel_id=1, source_target_pairs={{0,1},{1,0},{2,3},{3,2},{4,5},{5,4},{6,7},{7,6},{8,9},{9,8},{10,11... | collective-permute-start | bytes 1486856 | tf_op jit(solution)/shard_map/ppermute | solution.py:27
  47.1 2.4 all-to-all-done.1
  50.4 3.4 %all-to-all-start.2 = ((bf16[8,176,128]{2,1,0:T(8,128)(2,1)}), bf16[8,176,128]{2,1,0:T(8,128)(2,1)S(1)}, u32[]{:S(2)}, u32[]{:S(2)}) async-start(bf16[8,176,128]{2,1,0:T(8,128)(2,1)} %broadcast_in_dim.25), calls=%async_computation.2 | async-start | bytes 720896 | tf_op jit(solution)/shard_map/all_to_all | solution.py:33
  53.8 9.9 %collective-permute-done = bf16[2,88,1408]{2,1,0:T(8,128)(2,1)S(1)} collective-permute-done((bf16[2,88,1408]{2,1,0:T(8,128)(2,1)S(1)}, bf16[2,88,1408]{2,1,0:T(8,128)(2,1)S(1)}, u32[]{:S(2)}, u32[]{:S(2)}) %collective-permute-start) | collective-permute-done | bytes 495648 | tf_op jit(solution)/shard_map/ppermute | solution.py:27
  64.4 1.9 collective-permute-start.3
  67.8 4.3 %collective-permute-start.5 = (bf16[128,1408]{1,0:T(8,128)(2,1)}, bf16[128,1408]{1,0:T(8,128)(2,1)}, u32[]{:S(2)}, u32[]{:S(2)}) collective-permute-start(bf16[128,1408]{1,0:T(8,128)(2,1)} %bitcast.15), channel_id=1, source_target_pairs={{0,1},{1,0},{2,3},{3,2},{4,5},{5,4},{6,7},{7,6},{8,9},{9,8},{10,11... | collective-permute-start | bytes 1081352 | tf_op jit(solution)/shard_map/ppermute | solution.py:27
  72.1 7.1 %collective-permute-done.4 = bf16[176,128]{1,0:T(8,128)(2,1)S(1)} collective-permute-done((bf16[176,128]{1,0:T(8,128)(2,1)S(1)}, bf16[176,128]{1,0:T(8,128)(2,1)S(1)}, u32[]{:S(2)}, u32[]{:S(2)}) %collective-permute-start.4) | collective-permute-done | bytes 45088 | tf_op jit(solution)/shard_map/ppermute | solution.py:111
  80.0 4.1 %all-to-all-start.3 = ((bf16[8,176,128]{2,1,0:T(8,128)(2,1)}), bf16[8,176,128]{2,1,0:T(8,128)(2,1)S(1)}, u32[]{:S(2)}, u32[]{:S(2)}) async-start(bf16[8,176,128]{2,1,0:T(8,128)(2,1)} %broadcast_in_dim.26), calls=%async_computation.3 | async-start | bytes 720896 | tf_op jit(solution)/shard_map/all_to_all | solution.py:33
  84.5 8.0 %all-to-all-done.3 = bf16[8,176,128]{2,1,0:T(8,128)(2,1)S(1)} async-done(((bf16[8,176,128]{2,1,0:T(8,128)(2,1)}), bf16[8,176,128]{2,1,0:T(8,128)(2,1)S(1)}, u32[]{:S(2)}, u32[]{:S(2)}) %all-to-all-start.3) | async-done | bytes 360480 | tf_op jit(solution)/shard_map/all_to_all | solution.py:33
  92.5 1.8 fusion.12
  95.6 3.4 %all-to-all-start.4 = ((bf16[8,176,128]{2,1,0:T(8,128)(2,1)}), bf16[8,176,128]{2,1,0:T(8,128)(2,1)S(1)}, u32[]{:S(2)}, u32[]{:S(2)}) async-start(bf16[8,176,128]{2,1,0:T(8,128)(2,1)} %bitcast.22), calls=%async_computation.4 | async-start | bytes 720896 | tf_op jit(solution)/shard_map/all_to_all | solution.py:91
  99.4 7.4 %all-to-all-done.4 = bf16[8,176,128]{2,1,0:T(8,128)(2,1)S(1)} async-done(((bf16[8,176,128]{2,1,0:T(8,128)(2,1)}), bf16[8,176,128]{2,1,0:T(8,128)(2,1)S(1)}, u32[]{:S(2)}, u32[]{:S(2)}) %all-to-all-start.4) | async-done | bytes 360480 | tf_op jit(solution)/shard_map/all_to_all | solution.py:91
  107.6 3.4 %all-to-all-start.5 = ((bf16[8,176,128]{2,1,0:T(8,128)(2,1)}), bf16[8,176,128]{2,1,0:T(8,128)(2,1)S(1)}, u32[]{:S(2)}, u32[]{:S(2)}) async-start(bf16[8,176,128]{2,1,0:T(8,128)(2,1)} %broadcast_in_dim.27), calls=%async_computation.5 | async-start | bytes 720896 | tf_op jit(solution)/shard_map/all_to_all | solution.py:33
  112.2 6.2 %all-to-all-done.5 = bf16[8,176,128]{2,1,0:T(8,128)(2,1)S(1)} async-done(((bf16[8,176,128]{2,1,0:T(8,128)(2,1)}), bf16[8,176,128]{2,1,0:T(8,128)(2,1)S(1)}, u32[]{:S(2)}, u32[]{:S(2)}) %all-to-all-start.5) | async-done | bytes 360480 | tf_op jit(solution)/shard_map/all_to_all | solution.py:33
  118.8 1.9 collective-permute-start.6
  122.4 10.3 %collective-permute-done.7 = bf16[176,128]{1,0:T(8,128)(2,1)S(1)} collective-permute-done((bf16[176,128]{1,0:T(8,128)(2,1)S(1)}, bf16[176,128]{1,0:T(8,128)(2,1)S(1)}, u32[]{:S(2)}, u32[]{:S(2)}) %collective-permute-start.7) | collective-permute-done | bytes 45088 | tf_op jit(solution)/shard_map/ppermute | solution.py:111
  133.5 3.4 %all-to-all-start.6 = ((bf16[8,176,128]{2,1,0:T(8,128)(2,1)}), bf16[8,176,128]{2,1,0:T(8,128)(2,1)S(1)}, u32[]{:S(2)}, u32[]{:S(2)}) async-start(bf16[8,176,128]{2,1,0:T(8,128)(2,1)} %broadcast_in_dim.28), calls=%async_computation.6 | async-start | bytes 720896 | tf_op jit(solution)/shard_map/all_to_all | solution.py:33
  137.0 4.3 %collective-permute-start.8 = (bf16[384,128]{1,0:T(8,128)(2,1)S(1)}, bf16[384,128]{1,0:T(8,128)(2,1)S(1)}, u32[]{:S(2)}, u32[]{:S(2)}) collective-permute-start(bf16[384,128]{1,0:T(8,128)(2,1)S(1)} %pad_maximum_fusion.3), channel_id=1, source_target_pairs={{0,1},{1,0},{2,3},{3,2},{4,5},{5,4},{6,7},{7,6},{8,9},{9,8},{10,11... | collective-permute-start | bytes 294920 | tf_op jit(solution)/shard_map/ppermute | solution.py:27
  141.3 1.8 fusion.45
  143.0 4.3 %collective-permute-done.8 = bf16[384,128]{1,0:T(8,128)(2,1)S(1)} collective-permute-done((bf16[384,128]{1,0:T(8,128)(2,1)S(1)}, bf16[384,128]{1,0:T(8,128)(2,1)S(1)}, u32[]{:S(2)}, u32[]{:S(2)}) %collective-permute-start.8) | collective-permute-done | bytes 98336 | tf_op jit(solution)/shard_map/ppermute | solution.py:27
  147.3 1.8 fusion.13
  150.4 4.3 %all-to-all-start.7 = ((bf16[8,176,128]{2,1,0:T(8,128)(2,1)}), bf16[8,176,128]{2,1,0:T(8,128)(2,1)S(1)}, u32[]{:S(2)}, u32[]{:S(2)}) async-start(bf16[8,176,128]{2,1,0:T(8,128)(2,1)} %bitcast.133), calls=%async_computation.7 | async-start | bytes 720896 | tf_op jit(solution)/shard_map/all_to_all | solution.py:91
  157.2 5.6 %all-to-all-done.7 = bf16[8,176,128]{2,1,0:T(8,128)(2,1)S(1)} async-done(((bf16[8,176,128]{2,1,0:T(8,128)(2,1)}), bf16[8,176,128]{2,1,0:T(8,128)(2,1)S(1)}, u32[]{:S(2)}, u32[]{:S(2)}) %all-to-all-start.7) | async-done | bytes 360480 | tf_op jit(solution)/shard_map/all_to_all | solution.py:91
  163.6 3.4 %all-to-all-start.8 = ((bf16[8,176,128]{2,1,0:T(8,128)(2,1)}), bf16[8,176,128]{2,1,0:T(8,128)(2,1)S(1)}, u32[]{:S(2)}, u32[]{:S(2)}) async-start(bf16[8,176,128]{2,1,0:T(8,128)(2,1)} %broadcast_in_dim.30), calls=%async_computation.8 | async-start | bytes 720896 | tf_op jit(solution)/shard_map/all_to_all | solution.py:33
  169.4 5.1 %all-to-all-done.8 = bf16[8,176,128]{2,1,0:T(8,128)(2,1)S(1)} async-done(((bf16[8,176,128]{2,1,0:T(8,128)(2,1)}), bf16[8,176,128]{2,1,0:T(8,128)(2,1)S(1)}, u32[]{:S(2)}, u32[]{:S(2)}) %all-to-all-start.8) | async-done | bytes 360480 | tf_op jit(solution)/shard_map/all_to_all | solution.py:33
  174.9 1.9 collective-permute-start.9
  179.2 4.4 %collective-permute-start.11 = (bf16[1408,128]{0,1:T(8,128)(2,1)}, bf16[1408,128]{0,1:T(8,128)(2,1)}, u32[]{:S(2)}, u32[]{:S(2)}) collective-permute-start(bf16[1408,128]{0,1:T(8,128)(2,1)} %fusion.2), channel_id=1, source_target_pairs={{0,1},{1,0},{2,3},{3,2},{4,5},{5,4},{6,7},{7,6},{8,9},{9,8},{10,11... | collective-permute-start | bytes 1081352 | tf_op jit(solution)/shard_map/ppermute | solution.py:27
  183.6 5.2 %collective-permute-done.10 = bf16[176,128]{1,0:T(8,128)(2,1)S(1)} collective-permute-done((bf16[176,128]{1,0:T(8,128)(2,1)S(1)}, bf16[176,128]{1,0:T(8,128)(2,1)S(1)}, u32[]{:S(2)}, u32[]{:S(2)}) %collective-permute-start.10) | collective-permute-done | bytes 45088 | tf_op jit(solution)/shard_map/ppermute | solution.py:111
  190.4 3.4 %all-to-all-start.9 = ((bf16[8,176,128]{2,1,0:T(8,128)(2,1)}), bf16[8,176,128]{2,1,0:T(8,128)(2,1)S(1)}, u32[]{:S(2)}, u32[]{:S(2)}) async-start(bf16[8,176,128]{2,1,0:T(8,128)(2,1)} %broadcast_in_dim.31), calls=%async_computation.9 | async-start | bytes 720896 | tf_op jit(solution)/shard_map/all_to_all | solution.py:33
  194.4 8.1 %all-to-all-done.9 = bf16[8,176,128]{2,1,0:T(8,128)(2,1)S(1)} async-done(((bf16[8,176,128]{2,1,0:T(8,128)(2,1)}), bf16[8,176,128]{2,1,0:T(8,128)(2,1)S(1)}, u32[]{:S(2)}, u32[]{:S(2)}) %all-to-all-start.9) | async-done | bytes 360480 | tf_op jit(solution)/shard_map/all_to_all | solution.py:33
  202.5 1.8 fusion.14
  205.5 3.4 %all-to-all-start.10 = ((bf16[8,176,128]{2,1,0:T(8,128)(2,1)}), bf16[8,176,128]{2,1,0:T(8,128)(2,1)S(1)}, u32[]{:S(2)}, u32[]{:S(2)}) async-start(bf16[8,176,128]{2,1,0:T(8,128)(2,1)} %bitcast.34), calls=%async_computation.10 | async-start | bytes 720896 | tf_op jit(solution)/shard_map/all_to_all | solution.py:91
  209.2 4.3 %collective-permute-start.12 = (bf16[1408,128]{0,1:T(8,128)(2,1)S(1)}, bf16[1408,128]{0,1:T(8,128)(2,1)S(1)}, u32[]{:S(2)}, u32[]{:S(2)}) collective-permute-start(bf16[1408,128]{0,1:T(8,128)(2,1)S(1)} %fusion.3), channel_id=1, source_target_pairs={{0,1},{1,0},{2,3},{3,2},{4,5},{5,4},{6,7},{7,6},{8,9},{9,8},{10,11... | collective-permute-start | bytes 1081352 | tf_op jit(solution)/shard_map/ppermute | solution.py:27
  213.7 3.1 %collective-permute-start.13 = (bf16[192,128]{1,0:T(8,128)(2,1)S(1)}, bf16[192,128]{1,0:T(8,128)(2,1)S(1)}, u32[]{:S(2)}, u32[]{:S(2)}) collective-permute-start(bf16[192,128]{1,0:T(8,128)(2,1)S(1)} %get-tuple-element.56), channel_id=1, source_target_pairs={{0,1},{1,0},{2,3},{3,2},{4,5},{5,4},{6,7},{7,6},{8,9},{9,8},{10,11... | collective-permute-start | bytes 147464 | tf_op jit(solution)/shard_map/ppermute | solution.py:27
  216.8 8.8 %collective-permute-done.13 = bf16[192,128]{1,0:T(8,128)(2,1)S(1)} collective-permute-done((bf16[192,128]{1,0:T(8,128)(2,1)S(1)}, bf16[192,128]{1,0:T(8,128)(2,1)S(1)}, u32[]{:S(2)}, u32[]{:S(2)}) %collective-permute-start.13) | collective-permute-done | bytes 49184 | tf_op jit(solution)/shard_map/ppermute | solution.py:27
  226.7 5.1 %all-to-all-start.11 = ((bf16[16,176,128]{2,1,0:T(8,128)(2,1)}), bf16[16,176,128]{2,1,0:T(8,128)(2,1)S(1)}, u32[]{:S(2)}, u32[]{:S(2)}) async-start(bf16[16,176,128]{2,1,0:T(8,128)(2,1)} %broadcast_in_dim.32), calls=%async_computation.11 | async-start | bytes 1441792 | tf_op jit(solution)/shard_map/all_to_all | solution.py:33
  233.3 2.2 fusion.1
  235.5 9.1 %all-to-all-done.11 = bf16[16,176,128]{2,1,0:T(8,128)(2,1)S(1)} async-done(((bf16[16,176,128]{2,1,0:T(8,128)(2,1)}), bf16[16,176,128]{2,1,0:T(8,128)(2,1)S(1)}, u32[]{:S(2)}, u32[]{:S(2)}) %all-to-all-start.11) | async-done | bytes 720928 | tf_op jit(solution)/shard_map/all_to_all | solution.py:33
  246.5 2.3 convolution_convert_fusion.2
  (132 shorter events, 30.2 us)
Async XLA Ops:
  0.6 23.1 %copy-start.17 = (bf16[1,1408,192]{1,2,0:T(8,128)(2,1)S(1)}, bf16[1,1408,192]{1,2,0:T(8,128)(2,1)}, u32[]{:S(2)}) copy-start(bf16[1,1408,192]{1,2,0:T(8,128)(2,1)} %param.14) | copy-start | bytes 1622020
  0.6 11.3 %copy-start.16 = (bf16[1,192,1408]{2,1,0:T(8,128)(2,1)S(1)}, bf16[1,192,1408]{2,1,0:T(8,128)(2,1)}, u32[]{:S(2)}) copy-start(bf16[1,192,1408]{2,1,0:T(8,128)(2,1)} %param.15) | copy-start | bytes 1622020
  0.7 15.1 %copy-start.15 = (s32[1,4,128]{2,1,0:T(4,128)S(1)}, s32[1,4,128]{2,1,0:T(4,128)}, u32[]{:S(2)}) copy-start(s32[1,4,128]{2,1,0:T(4,128)} %param.10) | copy-start | bytes 6148
  0.7 23.1 %collective-permute-start.1 = (bf16[1408,192]{0,1:T(8,128)(2,1)}, bf16[1408,192]{0,1:T(8,128)(2,1)S(1)}, u32[]{:S(2)}, u32[]{:S(2)}) collective-permute-start(bf16[1408,192]{0,1:T(8,128)(2,1)} %bitcast.144), channel_id=1, source_target_pairs={{0,1},{1,0},{2,3},{3,2},{4,5},{5,4},{6,7},{7,6},{8,9},{9,8},{10,11... | collective-permute-start | bytes 1622024 | tf_op jit(solution)/shard_map/ppermute | solution.py:27
  7.5 16.3 %all-to-all-start = ((bf16[8,176,128]{2,1,0:T(8,128)(2,1)}), bf16[8,176,128]{2,1,0:T(8,128)(2,1)S(1)}, u32[]{:S(2)}, u32[]{:S(2)}) async-start(bf16[8,176,128]{2,1,0:T(8,128)(2,1)} %broadcast_in_dim.24), calls=%async_computation | async-start | bytes 720896 | tf_op jit(solution)/shard_map/all_to_all | solution.py:33
  11.9 22.1 %collective-permute-start.2 = (bf16[192,1408]{1,0:T(8,128)(2,1)S(1)}, bf16[192,1408]{1,0:T(8,128)(2,1)}, u32[]{:S(2)}, u32[]{:S(2)}) collective-permute-start(bf16[192,1408]{1,0:T(8,128)(2,1)S(1)} %bitcast.142), channel_id=1, source_target_pairs={{0,1},{1,0},{2,3},{3,2},{4,5},{5,4},{6,7},{7,6},{8,9},{9,8},{10,11... | collective-permute-start | bytes 1622024 | tf_op jit(solution)/shard_map/ppermute | solution.py:27
  23.8 11.7 %copy-start.21 = (bf16[1408,192]{0,1:T(8,128)(2,1)}, bf16[1408,192]{0,1:T(8,128)(2,1)S(1)}, u32[]{:S(2)}) copy-start(bf16[1408,192]{0,1:T(8,128)(2,1)S(1)} %collective-permute-done.1) | copy-start | bytes 1622020
  35.5 6.7 %copy-start.14 = (bf16[1,128,2,176]{1,3,2,0:T(8,128)(2,1)S(1)}, bf16[1,128,2,176]{1,3,2,0:T(8,128)(2,1)}, u32[]{:S(2)}) copy-start(bf16[1,128,2,176]{1,3,2,0:T(8,128)(2,1)} %param.8) | copy-start | bytes 270340
  35.5 6.8 %copy-start.5 = (bf16[1,2,88,1408]{3,2,1,0:T(8,128)(2,1)S(1)}, bf16[1,2,88,1408]{3,2,1,0:T(8,128)(2,1)}, u32[]{:S(2)}) copy-start(bf16[1,2,88,1408]{3,2,1,0:T(8,128)(2,1)} %param.13) | copy-start | bytes 1486852
  36.7 12.8 %copy-start.6 = (bf16[1,128,176]{1,2,0:T(8,128)(2,1)S(1)}, bf16[1,128,176]{1,2,0:T(8,128)(2,1)}, u32[]{:S(2)}) copy-start(bf16[1,128,176]{1,2,0:T(8,128)(2,1)} %param.11) | copy-start | bytes 135172
  36.7 12.8 %all-to-all-start.1 = ((bf16[8,176,128]{2,1,0:T(8,128)(2,1)}), bf16[8,176,128]{2,1,0:T(8,128)(2,1)S(1)}, u32[]{:S(2)}, u32[]{:S(2)}) async-start(bf16[8,176,128]{2,1,0:T(8,128)(2,1)} %bitcast.17), calls=%async_computation.1 | async-start | bytes 720896 | tf_op jit(solution)/shard_map/all_to_all | solution.py:91
  42.3 21.5 %collective-permute-start = (bf16[2,88,1408]{2,1,0:T(8,128)(2,1)S(1)}, bf16[2,88,1408]{2,1,0:T(8,128)(2,1)S(1)}, u32[]{:S(2)}, u32[]{:S(2)}) collective-permute-start(bf16[2,88,1408]{2,1,0:T(8,128)(2,1)S(1)} %bitcast.131), channel_id=1, source_target_pairs={{0,1},{1,0},{2,3},{3,2},{4,5},{5,4},{6,7},{7,6},{8,9},{9,8},{10,11... | collective-permute-start | bytes 1486856 | tf_op jit(solution)/shard_map/ppermute | solution.py:27
  50.4 13.6 %all-to-all-start.2 = ((bf16[8,176,128]{2,1,0:T(8,128)(2,1)}), bf16[8,176,128]{2,1,0:T(8,128)(2,1)S(1)}, u32[]{:S(2)}, u32[]{:S(2)}) async-start(bf16[8,176,128]{2,1,0:T(8,128)(2,1)} %broadcast_in_dim.25), calls=%async_computation.2 | async-start | bytes 720896 | tf_op jit(solution)/shard_map/all_to_all | solution.py:33
  63.9 15.3 %copy-start.7 = (bf16[3,128,176]{1,2,0:T(8,128)(2,1)S(1)}, bf16[3,128,176]{1,2,0:T(8,128)(2,1)}, u32[]{:S(2)}) copy-start(bf16[3,128,176]{1,2,0:T(8,128)(2,1)} %param.12) | copy-start | bytes 405508
  64.4 7.7 %collective-permute-start.3 = (bf16[176,128]{1,0:T(8,128)(2,1)S(1)}, bf16[176,128]{1,0:T(8,128)(2,1)S(1)}, u32[]{:S(2)}, u32[]{:S(2)}) collective-permute-start(bf16[176,128]{1,0:T(8,128)(2,1)S(1)} %get-tuple-element.65), channel_id=1, source_target_pairs={{16,0},{32,16},{48,32},{64,48},{80,64},{96,80},{112,96},{128,112},... | collective-permute-start | bytes 135176 | tf_op jit(solution)/shard_map/ppermute | solution.py:108
  66.3 12.9 %collective-permute-start.4 = (bf16[176,128]{1,0:T(8,128)(2,1)S(1)}, bf16[176,128]{1,0:T(8,128)(2,1)S(1)}, u32[]{:S(2)}, u32[]{:S(2)}) collective-permute-start(bf16[176,128]{1,0:T(8,128)(2,1)S(1)} %get-tuple-element.66), channel_id=1, source_target_pairs={{256,240},{272,224},{288,208},{304,192},{320,176},{336,160},{352,1... | collective-permute-start | bytes 135176 | tf_op jit(solution)/shard_map/ppermute | solution.py:111
  67.8 24.7 %collective-permute-start.5 = (bf16[128,1408]{1,0:T(8,128)(2,1)}, bf16[128,1408]{1,0:T(8,128)(2,1)}, u32[]{:S(2)}, u32[]{:S(2)}) collective-permute-start(bf16[128,1408]{1,0:T(8,128)(2,1)} %bitcast.15), channel_id=1, source_target_pairs={{0,1},{1,0},{2,3},{3,2},{4,5},{5,4},{6,7},{7,6},{8,9},{9,8},{10,11... | collective-permute-start | bytes 1081352 | tf_op jit(solution)/shard_map/ppermute | solution.py:27
  80.0 12.4 %all-to-all-start.3 = ((bf16[8,176,128]{2,1,0:T(8,128)(2,1)}), bf16[8,176,128]{2,1,0:T(8,128)(2,1)S(1)}, u32[]{:S(2)}, u32[]{:S(2)}) async-start(bf16[8,176,128]{2,1,0:T(8,128)(2,1)} %broadcast_in_dim.26), calls=%async_computation.3 | async-start | bytes 720896 | tf_op jit(solution)/shard_map/all_to_all | solution.py:33
  92.5 1.8 copy-start.2
  92.5 1.8 copy-start.18
  92.5 1.9 copy-start.22
  95.6 11.2 %all-to-all-start.4 = ((bf16[8,176,128]{2,1,0:T(8,128)(2,1)}), bf16[8,176,128]{2,1,0:T(8,128)(2,1)S(1)}, u32[]{:S(2)}, u32[]{:S(2)}) async-start(bf16[8,176,128]{2,1,0:T(8,128)(2,1)} %bitcast.22), calls=%async_computation.4 | async-start | bytes 720896 | tf_op jit(solution)/shard_map/all_to_all | solution.py:91
  107.6 10.7 %all-to-all-start.5 = ((bf16[8,176,128]{2,1,0:T(8,128)(2,1)}), bf16[8,176,128]{2,1,0:T(8,128)(2,1)S(1)}, u32[]{:S(2)}, u32[]{:S(2)}) async-start(bf16[8,176,128]{2,1,0:T(8,128)(2,1)} %broadcast_in_dim.27), calls=%async_computation.5 | async-start | bytes 720896 | tf_op jit(solution)/shard_map/all_to_all | solution.py:33
  118.8 3.6 %collective-permute-start.6 = (bf16[176,128]{1,0:T(8,128)(2,1)S(1)}, bf16[176,128]{1,0:T(8,128)(2,1)S(1)}, u32[]{:S(2)}, u32[]{:S(2)}) collective-permute-start(bf16[176,128]{1,0:T(8,128)(2,1)S(1)} %get-tuple-element.63), channel_id=1, source_target_pairs={{16,0},{32,16},{48,32},{64,48},{80,64},{96,80},{112,96},{128,112},... | collective-permute-start | bytes 135176 | tf_op jit(solution)/shard_map/ppermute | solution.py:108
  120.7 12.0 %collective-permute-start.7 = (bf16[176,128]{1,0:T(8,128)(2,1)S(1)}, bf16[176,128]{1,0:T(8,128)(2,1)S(1)}, u32[]{:S(2)}, u32[]{:S(2)}) collective-permute-start(bf16[176,128]{1,0:T(8,128)(2,1)S(1)} %get-tuple-element.64), channel_id=1, source_target_pairs={{256,240},{272,224},{288,208},{304,192},{320,176},{336,160},{352,1... | collective-permute-start | bytes 135176 | tf_op jit(solution)/shard_map/ppermute | solution.py:111
  133.5 13.8 %all-to-all-start.6 = ((bf16[8,176,128]{2,1,0:T(8,128)(2,1)}), bf16[8,176,128]{2,1,0:T(8,128)(2,1)S(1)}, u32[]{:S(2)}, u32[]{:S(2)}) async-start(bf16[8,176,128]{2,1,0:T(8,128)(2,1)} %broadcast_in_dim.28), calls=%async_computation.6 | async-start | bytes 720896 | tf_op jit(solution)/shard_map/all_to_all | solution.py:33
  137.0 10.3 %collective-permute-start.8 = (bf16[384,128]{1,0:T(8,128)(2,1)S(1)}, bf16[384,128]{1,0:T(8,128)(2,1)S(1)}, u32[]{:S(2)}, u32[]{:S(2)}) collective-permute-start(bf16[384,128]{1,0:T(8,128)(2,1)S(1)} %pad_maximum_fusion.3), channel_id=1, source_target_pairs={{0,1},{1,0},{2,3},{3,2},{4,5},{5,4},{6,7},{7,6},{8,9},{9,8},{10,11... | collective-permute-start | bytes 294920 | tf_op jit(solution)/shard_map/ppermute | solution.py:27
  147.3 1.9 copy-start.12
  147.3 1.9 copy-start.3
  147.3 1.9 copy-start.19
  147.3 1.9 copy-start.23
  150.4 12.3 %all-to-all-start.7 = ((bf16[8,176,128]{2,1,0:T(8,128)(2,1)}), bf16[8,176,128]{2,1,0:T(8,128)(2,1)S(1)}, u32[]{:S(2)}, u32[]{:S(2)}) async-start(bf16[8,176,128]{2,1,0:T(8,128)(2,1)} %bitcast.133), calls=%async_computation.7 | async-start | bytes 720896 | tf_op jit(solution)/shard_map/all_to_all | solution.py:91
  162.8 5.4 %copy-start = (f32[1408,128]{0,1:T(8,128)S(1)}, f32[1408,128]{0,1:T(8,128)}, u32[]{:S(2)}) copy-start(f32[1408,128]{0,1:T(8,128)} %fusion.47) | copy-start | bytes 2162692
  163.6 10.9 %all-to-all-start.8 = ((bf16[8,176,128]{2,1,0:T(8,128)(2,1)}), bf16[8,176,128]{2,1,0:T(8,128)(2,1)S(1)}, u32[]{:S(2)}, u32[]{:S(2)}) async-start(bf16[8,176,128]{2,1,0:T(8,128)(2,1)} %broadcast_in_dim.30), calls=%async_computation.8 | async-start | bytes 720896 | tf_op jit(solution)/shard_map/all_to_all | solution.py:33
  169.4 8.8 %copy-start.1 = (f32[1408,128]{0,1:T(8,128)S(1)}, f32[1408,128]{0,1:T(8,128)}, u32[]{:S(2)}) copy-start(f32[1408,128]{0,1:T(8,128)} %convolution_add_fusion.4) | copy-start | bytes 2162692
  174.9 8.7 %collective-permute-start.9 = (bf16[176,128]{1,0:T(8,128)(2,1)S(1)}, bf16[176,128]{1,0:T(8,128)(2,1)S(1)}, u32[]{:S(2)}, u32[]{:S(2)}) collective-permute-start(bf16[176,128]{1,0:T(8,128)(2,1)S(1)} %get-tuple-element.61), channel_id=1, source_target_pairs={{16,0},{32,16},{48,32},{64,48},{80,64},{96,80},{112,96},{128,112},... | collective-permute-start | bytes 135176 | tf_op jit(solution)/shard_map/ppermute | solution.py:108
  176.9 12.0 %collective-permute-start.10 = (bf16[176,128]{1,0:T(8,128)(2,1)S(1)}, bf16[176,128]{1,0:T(8,128)(2,1)S(1)}, u32[]{:S(2)}, u32[]{:S(2)}) collective-permute-start(bf16[176,128]{1,0:T(8,128)(2,1)S(1)} %get-tuple-element.62), channel_id=1, source_target_pairs={{256,240},{272,224},{288,208},{304,192},{320,176},{336,160},{352,1... | collective-permute-start | bytes 135176 | tf_op jit(solution)/shard_map/ppermute | solution.py:111
  179.2 14.7 %copy-start.11 = (bf16[384,128]{1,0:T(8,128)(2,1)S(1)}, bf16[384,128]{1,0:T(8,128)(2,1)}, u32[]{:S(2)}) copy-start(bf16[384,128]{1,0:T(8,128)(2,1)} %copy-done.10) | copy-start | bytes 294916
  179.2 14.9 %copy-start.4 = (bf16[8,176,128]{2,1,0:T(8,128)(2,1)S(1)}, bf16[8,176,128]{2,1,0:T(8,128)(2,1)}, u32[]{:S(2)}) copy-start(bf16[8,176,128]{2,1,0:T(8,128)(2,1)} %copy-done.3) | copy-start | bytes 1081348
  179.2 23.3 %collective-permute-start.11 = (bf16[1408,128]{0,1:T(8,128)(2,1)}, bf16[1408,128]{0,1:T(8,128)(2,1)}, u32[]{:S(2)}, u32[]{:S(2)}) collective-permute-start(bf16[1408,128]{0,1:T(8,128)(2,1)} %fusion.2), channel_id=1, source_target_pairs={{0,1},{1,0},{2,3},{3,2},{4,5},{5,4},{6,7},{7,6},{8,9},{9,8},{10,11... | collective-permute-start | bytes 1081352 | tf_op jit(solution)/shard_map/ppermute | solution.py:27
  190.4 12.0 %all-to-all-start.9 = ((bf16[8,176,128]{2,1,0:T(8,128)(2,1)}), bf16[8,176,128]{2,1,0:T(8,128)(2,1)S(1)}, u32[]{:S(2)}, u32[]{:S(2)}) async-start(bf16[8,176,128]{2,1,0:T(8,128)(2,1)} %broadcast_in_dim.31), calls=%async_computation.9 | async-start | bytes 720896 | tf_op jit(solution)/shard_map/all_to_all | solution.py:33
  202.5 1.8 copy-start.24
  205.5 20.1 %all-to-all-start.10 = ((bf16[8,176,128]{2,1,0:T(8,128)(2,1)}), bf16[8,176,128]{2,1,0:T(8,128)(2,1)S(1)}, u32[]{:S(2)}, u32[]{:S(2)}) async-start(bf16[8,176,128]{2,1,0:T(8,128)(2,1)} %bitcast.34), calls=%async_computation.10 | async-start | bytes 720896 | tf_op jit(solution)/shard_map/all_to_all | solution.py:91
  209.2 16.4 %collective-permute-start.12 = (bf16[1408,128]{0,1:T(8,128)(2,1)S(1)}, bf16[1408,128]{0,1:T(8,128)(2,1)S(1)}, u32[]{:S(2)}, u32[]{:S(2)}) collective-permute-start(bf16[1408,128]{0,1:T(8,128)(2,1)S(1)} %fusion.3), channel_id=1, source_target_pairs={{0,1},{1,0},{2,3},{3,2},{4,5},{5,4},{6,7},{7,6},{8,9},{9,8},{10,11... | collective-permute-start | bytes 1081352 | tf_op jit(solution)/shard_map/ppermute | solution.py:27
  213.7 11.9 %collective-permute-start.13 = (bf16[192,128]{1,0:T(8,128)(2,1)S(1)}, bf16[192,128]{1,0:T(8,128)(2,1)S(1)}, u32[]{:S(2)}, u32[]{:S(2)}) collective-permute-start(bf16[192,128]{1,0:T(8,128)(2,1)S(1)} %get-tuple-element.56), channel_id=1, source_target_pairs={{0,1},{1,0},{2,3},{3,2},{4,5},{5,4},{6,7},{7,6},{8,9},{9,8},{10,11... | collective-permute-start | bytes 147464 | tf_op jit(solution)/shard_map/ppermute | solution.py:27
  226.7 5.3 %copy-start.13 = (bf16[384,128]{1,0:T(8,128)(2,1)S(1)}, bf16[384,128]{1,0:T(8,128)(2,1)}, u32[]{:S(2)}) copy-start(bf16[384,128]{1,0:T(8,128)(2,1)} %copy-done.12) | copy-start | bytes 294916
  226.7 5.4 %slice-start.1 = ((bf16[384,128]{1,0:T(8,128)(2,1)}), bf16[192,128]{1,0:T(8,128)(2,1)S(1)}, s32[]{:S(2)}) async-start(bf16[384,128]{1,0:T(8,128)(2,1)} %copy-done.12), calls=%async_computation.13 | async-start | bytes 98304 | tf_op jit(solution)/shard_map/slice | solution.py:134
  226.7 17.8 %all-to-all-start.11 = ((bf16[16,176,128]{2,1,0:T(8,128)(2,1)}), bf16[16,176,128]{2,1,0:T(8,128)(2,1)S(1)}, u32[]{:S(2)}, u32[]{:S(2)}) async-start(bf16[16,176,128]{2,1,0:T(8,128)(2,1)} %broadcast_in_dim.32), calls=%async_computation.11 | async-start | bytes 1441792 | tf_op jit(solution)/shard_map/all_to_all | solution.py:33
  (5 other events, 6.8 us)

commit v3 on v1

v3 whole, which is shorter than its diff:
```python
import jax
import jax.numpy as jnp
from jax import lax
from jax.sharding import PartitionSpec as P

gelu_scale = 0.7978845608
gelu_cubic = 0.044715
f32 = jnp.float32
bf16 = jnp.bfloat16


def gelu_pair(pre_gelu):
    inner = gelu_scale * (pre_gelu + gelu_cubic * pre_gelu * pre_gelu * pre_gelu)
    tanh_part = jnp.tanh(inner)
    gelu_value = 0.5 * pre_gelu * (1.0 + tanh_part)
    gelu_slope = 0.5 * (1.0 + tanh_part) + 0.5 * pre_gelu * (
        1.0 - tanh_part * tanh_part
    ) * gelu_scale * (1.0 + 3.0 * gelu_cubic * pre_gelu * pre_gelu)
    return (gelu_value, gelu_slope)


def dot(a, b, ca=1, cb=0):
    return lax.dot_general(a, b, (((ca,), (cb,)), ((), ())), preferred_element_type=f32)


def swap(x):
    return lax.ppermute(x, "replica", [(0, 1), (1, 0)])


def gather(chunk, axes="tensor"):
    count = lax.axis_size(axes)
    spread = jnp.broadcast_to(chunk[None], (count, *chunk.shape))
    return lax.all_to_all(spread, axes, 0, 0)


def body(pool_inputs, pool_mixed, crop_ids, incoming, loss_grads, w_proj, w_up, w_down):
    section = lax.axis_index("section")
    sections = lax.axis_size("section")
    replica = lax.axis_index("replica")
    parts = lax.axis_size("tensor")
    half = sections // 2
    first = replica == 0
    is_top = section == sections - 1
    ticks, rows = crop_ids.shape[1:]
    pool = pool_mixed.shape[1]
    width = pool_mixed.shape[2]
    units = w_down.shape[1]
    own_in = w_proj.shape[2]
    chunk_rows = incoming.shape[2]

    def by_replica(own, other):
        return jnp.where(first, own, other), jnp.where(first, other, own)

    def tied(*values):
        return lax.optimization_barrier(values)

    up_other = swap(w_up[0])
    down_other = swap(w_down[0])
    proj_other = swap(w_proj[0])

    chunk = incoming[0].T
    upstream = gather(chunk).reshape(width, rows)

    up = jnp.concatenate([w_up[0], up_other], axis=1)
    down = jnp.concatenate([w_down[0], down_other], axis=0)
    proj = jnp.concatenate(by_replica(w_proj[0], proj_other), axis=1).reshape(-1, width)

    places = jnp.arange(pool, dtype=jnp.int32)[:, None]
    pick = [(ids[None, :] == places).astype(bf16) for ids in crop_ids[0]]

    pre = dot(up, pool_mixed[0], 0, 1)
    value, slope = gelu_pair(pre)
    active = value.astype(bf16)
    high = slope.astype(bf16)
    low = (slope - high.astype(f32)).astype(bf16)

    decoder = jnp.where(section < half, 0.0, 1.0).astype(bf16)
    mask = jnp.stack([jnp.ones((), bf16), decoder])[:, None, None]
    saved = pool_inputs[0].transpose(1, 2, 0) * mask
    saved_first, saved_second = saved[:, :own_in], saved[:, own_in:]
    saved_own = jnp.where(first, saved_first, saved_second).reshape(-1, pool)
    saved_sent = jnp.where(first, saved_second, saved_first).reshape(-1, pool)
    ids_sent = jnp.broadcast_to(crop_ids[0, ticks - 1].astype(bf16)[None], (16, rows))
    mixed_sent = lax.dynamic_slice_in_dim(
        pool_mixed[0], lax.axis_index("tensor") * chunk_rows, chunk_rows, 1
    ).T
    side = jnp.concatenate([mixed_sent, saved_sent, active[units:], ids_sent], axis=0)

    def scatter(x, t):
        return dot(x, pick[t], 1, 1)

    def split(arrived):
        return (
            arrived[:, :chunk_rows].reshape(width, rows),
            arrived[:, chunk_rows:].reshape(width, pool),
        )

    seen, spread, early, seen_chunk, early_chunk = 0.0, 0.0, 0.0, 0.0, 0.0
    for t in range(ticks):
        last = t + 1 == ticks
        slope_now = dot(high, pick[t]) + dot(low, pick[t])
        hidden = (dot(down, upstream) * slope_now).astype(bf16)
        partial = dot(up, hidden).astype(bf16)
        sent = partial.reshape(parts, chunk_rows, rows)
        if last:
            rider = jnp.broadcast_to(seen_rider[None], (parts, chunk_rows, pool))
            sent = jnp.concatenate([sent, rider], axis=1)
        terms = lax.all_to_all(sent, "tensor", 0, 0)
        upstream_late, hidden_late, chunk_late, _ = tied(upstream, hidden, chunk, partial)
        seen = seen + scatter(upstream_late, t)
        spread = spread + scatter(hidden_late, t)
        seen_chunk = seen_chunk + scatter(chunk_late, t)
        if last:
            seen = seen.astype(bf16)
            spread = spread.astype(bf16)
            spread_other = swap(spread[units:])
            terms, seen_other = terms[:, :chunk_rows], terms[:, chunk_rows:]
            seen_other = seen_other.reshape(width, pool)
        mixed_chunk = (
            jnp.sum(terms.astype(f32), axis=0) + chunk.astype(f32)
        ).astype(bf16)
        if last:
            break
        early_chunk = early_chunk + scatter(mixed_chunk, t)
        mixed_grad = gather(mixed_chunk).reshape(width, rows)
        if t + 2 == ticks:
            early_rider = swap(early_chunk.astype(bf16))
            mixed_grad, early_rider = tied(mixed_grad, early_rider)
        early = early + scatter(mixed_grad, t)
        input_grad = dot(proj, mixed_grad).astype(bf16).reshape(2, chunk_rows, rows)
        above = lax.ppermute(
            input_grad[0], "section", [(i, i - 1) for i in range(1, sections)]
        )
        mirrored = lax.ppermute(
            input_grad[1],
            "section",
            [(i, sections - 1 - i) for i in range(half, sections)],
        )
        if t == 0:
            side, _ = tied(side, mixed_grad)
            side_other = swap(side)
        summed = (above.astype(f32) + mirrored.astype(f32)).astype(bf16)
        chunk = jnp.where(is_top, loss_grads[t].T, summed)
        if t == 1:
            upstream, mixed_other = split(
                gather(jnp.concatenate([chunk, side_other[:chunk_rows]], axis=0))
            )
        elif t + 2 == ticks:
            upstream, early_other = split(
                gather(jnp.concatenate([chunk, early_rider], axis=0))
            )
            seen_rider = swap((seen_chunk + scatter(chunk, t + 1)).astype(bf16))
        else:
            upstream = gather(chunk).reshape(width, rows)
            upstream, side_other = tied(upstream, side_other)

    both = gather(mixed_chunk, ("replica", "tensor")).reshape(2, width, rows)
    input_grad = jnp.where(first, dot(proj, both[0]), dot(proj, both[1]))
    input_grad = input_grad.astype(bf16).reshape(2, chunk_rows, rows)

    start = chunk_rows + saved_own.shape[0]
    saved_other = side_other[chunk_rows:start]
    active_other = side_other[start : start + units]
    ids_other = side_other[start + units].astype(jnp.int32)
    pick_other = (ids_other[None, :] == places).astype(bf16)
    last_own = dot(saved_own, pick[ticks - 1]).astype(bf16)
    last_other = dot(saved_other, pick_other).astype(bf16)
    grad_up = dot(pool_mixed[0], spread[:units], 0, 1) + dot(
        mixed_other, spread_other, 1, 1
    )
    grad_down = dot(
        jnp.concatenate([active[:units], active_other], axis=1),
        jnp.concatenate([seen, seen_other], axis=1),
        1,
        1,
    ).astype(bf16)
    grad_up = grad_up.astype(bf16)
    grad_proj = dot(
        jnp.concatenate(
            [saved_own, saved_other, *by_replica(last_own, last_other)], axis=1
        ),
        jnp.concatenate([early.astype(bf16), early_other, both[0], both[1]], axis=1),
        1,
        1,
    ).astype(bf16)
    return (
        grad_proj.reshape(1, 2, own_in, width),
        grad_up[None],
        grad_down[None],
        input_grad.transpose(2, 0, 1)[None],
    )


def solution(mesh):
    in_specs = (
        P("section", "replica", None, "tensor"),
        P("section", "replica", None),
        P("section", "replica", None),
        P("section", "replica", "tensor"),
        P(None, "replica", "tensor"),
        P("section", None, ("tensor", "replica"), None),
        P("section", None, ("tensor", "replica")),
        P("section", ("tensor", "replica"), None),
    )
    out_specs = (
        P("section", None, ("tensor", "replica"), None),
        P("section", None, ("tensor", "replica")),
        P("section", ("tensor", "replica"), None),
        P("section", "replica", None, "tensor"),
    )
    return jax.shard_map(body, mesh=mesh, in_specs=in_specs, out_specs=out_specs, check_vma=False)
```

time: 247 us -> 282 us (1.14)
  waiting for transfers between devices: 85.1 us -> 121 us
  blocking collectives: 33.2 us -> 0 us
  matrix products: 27.8 us -> 44.1 us
  local copies, waits for them, and re-layouts: 7.37 us -> 14.3 us
  other arithmetic: 2.94 us -> 7.05 us
  starting transfers between devices: 87.7 us -> 91.5 us
    all_to_all x3 -> x0, blocking collectives: 33.2 us -> none  [the longest x2 22.9 us: gather(): return lax.all_to_all(spread, axes, 0, 0)]
    dot_general x23 -> x46, matrix products: 27.8 us -> 44.1 us  [dot(): lax.dot_general(a, b, (((ca,), (cb,)), ((), ())), preferred_element_type=...]
    ppermute x10 -> x7, waiting for transfers between devices: 20.2 us -> 32.9 us  [swap(): return lax.ppermute(x, 'replica', [(0, 1), (1, 0)])]
    all_to_all x6 -> x8, waiting for transfers between devices: 22.7 us -> 35.2 us  [gather(): return lax.all_to_all(spread, axes, 0, 0)]
    all_to_all x3 -> x4, waiting for transfers between devices: 9.96 us -> 22.2 us  [body(): terms = lax.all_to_all(sent, 'tensor', 0, 0)]
    all_to_all x6 -> x8, starting transfers between devices: 27.8 us -> 34.8 us  [gather(): return lax.all_to_all(spread, axes, 0, 0)]
    ppermute x10 -> x7, starting transfers between devices: 38.2 us -> 31.3 us  [swap(): return lax.ppermute(x, 'replica', [(0, 1), (1, 0)])]
    all_to_all x3 -> x4, starting transfers between devices: 12.1 us -> 15.5 us  [body(): terms = lax.all_to_all(sent, 'tensor', 0, 0)]
  transfers between devices with their start and end apart: 25 -> 25, of which waited for: 15 -> 17; matrix products, arithmetic and copies ran while one was open for 12% -> 12% of each run, Pallas kernels for 0% -> 0%
where the time goes in v3:
time: 282 us; the launch traced here: 280 us
  waiting for transfers between devices  121 us (43%)
  starting transfers between devices  91.5 us (32%)
  matrix products  44.1 us (16%)
  local copies, waits for them, and re-layouts  14.3 us (5%)
  other arithmetic  7.05 us (2%)
    dot_general x46, matrix products, dot(): lax.dot_general(a, b, (((ca,), (cb,)), ((), ())), preferred_element_type=...  44.1 us
    all_to_all x8, waiting for transfers between devices, gather(): return lax.all_to_all(spread, axes, 0, 0)  35.2 us
    all_to_all x8, starting transfers between devices, gather(): return lax.all_to_all(spread, axes, 0, 0)  34.8 us
    ppermute x7, waiting for transfers between devices, swap(): return lax.ppermute(x, 'replica', [(0, 1), (1, 0)])  32.9 us
    ppermute x7, starting transfers between devices, swap(): return lax.ppermute(x, 'replica', [(0, 1), (1, 0)])  31.3 us
    ppermute x3, waiting for transfers between devices, body(): lax.ppermute(input_grad[1], 'section', [(i, sections - 1 - i) for i in ra...  30.8 us
    all_to_all x4, waiting for transfers between devices, body(): terms = lax.all_to_all(sent, 'tensor', 0, 0)  22.2 us
    all_to_all x4, starting transfers between devices, body(): terms = lax.all_to_all(sent, 'tensor', 0, 0)  15.5 us
  transfers between devices with their start and end apart: 25, of which 17 were waited for; matrix products, arithmetic and copies ran while one was open for 12% of the time, Pallas kernels for 0%

profile of v3, /device:TPU:96, one launch (start us, length us, event | category | flops | bytes accessed | tf_op | source)
XLA Modules:
  0.0 279.6 jit_solution(13574045657784149471)
XLA Ops:
  0.7 1.7 broadcast_in_dim.26
  2.4 5.3 %all-to-all-start = ((bf16[8,176,128]{2,1,0:T(8,128)(2,1)}), bf16[8,176,128]{2,1,0:T(8,128)(2,1)S(1)}, u32[]{:S(2)}, u32[]{:S(2)}) async-start(bf16[8,176,128]{2,1,0:T(8,128)(2,1)} %broadcast_in_dim.26), calls=%async_computation | async-start | bytes 720896 | tf_op jit(solution)/shard_map/all_to_all | solution.py:33
  7.7 4.8 %collective-permute-start = (bf16[2,88,1408]{2,1,0:T(8,128)(2,1)S(1)}, bf16[2,88,1408]{2,1,0:T(8,128)(2,1)S(1)}, u32[]{:S(2)}, u32[]{:S(2)}) collective-permute-start(bf16[2,88,1408]{2,1,0:T(8,128)(2,1)S(1)} %bitcast.153), channel_id=1, source_target_pairs={{0,1},{1,0},{2,3},{3,2},{4,5},{5,4},{6,7},{7,6},{8,9},{9,8},{10,11... | collective-permute-start | bytes 1486856 | tf_op jit(solution)/shard_map/ppermute | solution.py:27
  12.5 2.5 collective-permute-start.1
  15.1 4.8 %collective-permute-start.2 = (bf16[192,1408]{1,0:T(8,128)(2,1)S(1)}, bf16[192,1408]{1,0:T(8,128)(2,1)}, u32[]{:S(2)}, u32[]{:S(2)}) collective-permute-start(bf16[192,1408]{1,0:T(8,128)(2,1)S(1)} %bitcast.168), channel_id=1, source_target_pairs={{0,1},{1,0},{2,3},{3,2},{4,5},{5,4},{6,7},{7,6},{8,9},{9,8},{10,11... | collective-permute-start | bytes 1622024 | tf_op jit(solution)/shard_map/ppermute | solution.py:27
  21.1 5.7 %collective-permute-done = bf16[2,88,1408]{2,1,0:T(8,128)(2,1)S(1)} collective-permute-done((bf16[2,88,1408]{2,1,0:T(8,128)(2,1)S(1)}, bf16[2,88,1408]{2,1,0:T(8,128)(2,1)S(1)}, u32[]{:S(2)}, u32[]{:S(2)}) %collective-permute-start) | collective-permute-done | bytes 495648 | tf_op jit(solution)/shard_map/ppermute | solution.py:27
  27.1 11.5 %collective-permute-done.1 = bf16[1408,192]{0,1:T(8,128)(2,1)} collective-permute-done((bf16[1408,192]{0,1:T(8,128)(2,1)}, bf16[1408,192]{0,1:T(8,128)(2,1)}, u32[]{:S(2)}, u32[]{:S(2)}) %collective-permute-start.1) | collective-permute-done | bytes 540704 | tf_op jit(solution)/shard_map/ppermute | solution.py:27
  41.5 8.1 %collective-permute-done.2 = bf16[192,1408]{1,0:T(8,128)(2,1)} collective-permute-done((bf16[192,1408]{1,0:T(8,128)(2,1)S(1)}, bf16[192,1408]{1,0:T(8,128)(2,1)}, u32[]{:S(2)}, u32[]{:S(2)}) %collective-permute-start.2) | collective-permute-done | bytes 540704 | tf_op jit(solution)/shard_map/ppermute | solution.py:27
  51.2 2.3 convolution_convert_fusion.5
  53.4 4.3 %all-to-all-start.1 = ((bf16[8,176,128]{2,1,0:T(8,128)(2,1)}), bf16[8,176,128]{2,1,0:T(8,128)(2,1)S(1)}, u32[]{:S(2)}, u32[]{:S(2)}) async-start(bf16[8,176,128]{2,1,0:T(8,128)(2,1)} %bitcast.15), calls=%async_computation.1 | async-start | bytes 720896 | tf_op jit(solution)/shard_map/all_to_all | solution.py:108
  58.8 6.8 %all-to-all-done.1 = bf16[8,176,128]{2,1,0:T(8,128)(2,1)S(1)} async-done(((bf16[8,176,128]{2,1,0:T(8,128)(2,1)}), bf16[8,176,128]{2,1,0:T(8,128)(2,1)S(1)}, u32[]{:S(2)}, u32[]{:S(2)}) %all-to-all-start.1) | async-done | bytes 360480 | tf_op jit(solution)/shard_map/all_to_all | solution.py:108
  66.4 3.4 %all-to-all-start.2 = ((bf16[8,176,128]{2,1,0:T(8,128)(2,1)}), bf16[8,176,128]{2,1,0:T(8,128)(2,1)S(1)}, u32[]{:S(2)}, u32[]{:S(2)}) async-start(bf16[8,176,128]{2,1,0:T(8,128)(2,1)} %broadcast_in_dim.27), calls=%async_computation.2 | async-start | bytes 720896 | tf_op jit(solution)/shard_map/all_to_all | solution.py:33
  70.9 6.3 %all-to-all-done.2 = bf16[8,176,128]{2,1,0:T(8,128)(2,1)S(1)} async-done(((bf16[8,176,128]{2,1,0:T(8,128)(2,1)}), bf16[8,176,128]{2,1,0:T(8,128)(2,1)S(1)}, u32[]{:S(2)}, u32[]{:S(2)}) %all-to-all-start.2) | async-done | bytes 360480 | tf_op jit(solution)/shard_map/all_to_all | solution.py:33
  77.6 2.1 collective-permute-start.3
  81.6 11.2 %collective-permute-done.4 = bf16[176,128]{1,0:T(8,128)(2,1)S(1)} collective-permute-done((bf16[176,128]{1,0:T(8,128)(2,1)S(1)}, bf16[176,128]{1,0:T(8,128)(2,1)S(1)}, u32[]{:S(2)}, u32[]{:S(2)}) %collective-permute-start.4) | collective-permute-done | bytes 45088 | tf_op jit(solution)/shard_map/ppermute | solution.py:134
  94.5 3.4 %all-to-all-start.3 = ((bf16[8,176,128]{2,1,0:T(8,128)(2,1)}), bf16[8,176,128]{2,1,0:T(8,128)(2,1)S(1)}, u32[]{:S(2)}, u32[]{:S(2)}) async-start(bf16[8,176,128]{2,1,0:T(8,128)(2,1)} %broadcast_in_dim.28), calls=%async_computation.3 | async-start | bytes 720896 | tf_op jit(solution)/shard_map/all_to_all | solution.py:33
  97.9 3.3 %collective-permute-start.5 = (bf16[560,128]{1,0:T(8,128)(2,1)S(1)}, bf16[560,128]{1,0:T(8,128)(2,1)S(1)}, u32[]{:S(2)}, u32[]{:S(2)}) collective-permute-start(bf16[560,128]{1,0:T(8,128)(2,1)S(1)} %pad_maximum_fusion.4), channel_id=1, source_target_pairs={{0,1},{1,0},{2,3},{3,2},{4,5},{5,4},{6,7},{7,6},{8,9},{9,8},{10,11... | collective-permute-start | bytes 430088 | tf_op jit(solution)/shard_map/ppermute | solution.py:27
  101.5 6.8 %collective-permute-done.5 = bf16[560,128]{1,0:T(8,128)(2,1)S(1)} collective-permute-done((bf16[560,128]{1,0:T(8,128)(2,1)S(1)}, bf16[560,128]{1,0:T(8,128)(2,1)S(1)}, u32[]{:S(2)}, u32[]{:S(2)}) %collective-permute-start.5) | collective-permute-done | bytes 143392 | tf_op jit(solution)/shard_map/ppermute | solution.py:27
  108.3 1.7 fusion.13
  110.0 2.3 convolution_convert_fusion.4
  112.3 4.1 %all-to-all-start.4 = ((bf16[8,176,128]{2,1,0:T(8,128)(2,1)}), bf16[8,176,128]{2,1,0:T(8,128)(2,1)S(1)}, u32[]{:S(2)}, u32[]{:S(2)}) async-start(bf16[8,176,128]{2,1,0:T(8,128)(2,1)} %bitcast.157), calls=%async_computation.4 | async-start | bytes 720896 | tf_op jit(solution)/shard_map/all_to_all | solution.py:108
  117.8 6.3 %all-to-all-done.4 = bf16[8,176,128]{2,1,0:T(8,128)(2,1)S(1)} async-done(((bf16[8,176,128]{2,1,0:T(8,128)(2,1)}), bf16[8,176,128]{2,1,0:T(8,128)(2,1)S(1)}, u32[]{:S(2)}, u32[]{:S(2)}) %all-to-all-start.4) | async-done | bytes 360480 | tf_op jit(solution)/shard_map/all_to_all | solution.py:108
  125.0 3.4 %all-to-all-start.5 = ((bf16[8,176,128]{2,1,0:T(8,128)(2,1)}), bf16[8,176,128]{2,1,0:T(8,128)(2,1)S(1)}, u32[]{:S(2)}, u32[]{:S(2)}) async-start(bf16[8,176,128]{2,1,0:T(8,128)(2,1)} %broadcast_in_dim.30), calls=%async_computation.5 | async-start | bytes 720896 | tf_op jit(solution)/shard_map/all_to_all | solution.py:33
  129.5 6.2 %all-to-all-done.5 = bf16[8,176,128]{2,1,0:T(8,128)(2,1)S(1)} async-done(((bf16[8,176,128]{2,1,0:T(8,128)(2,1)}), bf16[8,176,128]{2,1,0:T(8,128)(2,1)S(1)}, u32[]{:S(2)}, u32[]{:S(2)}) %all-to-all-start.5) | async-done | bytes 360480 | tf_op jit(solution)/shard_map/all_to_all | solution.py:33
  136.2 1.9 collective-permute-start.6
  140.0 10.0 %collective-permute-done.7 = bf16[176,128]{1,0:T(8,128)(2,1)S(1)} collective-permute-done((bf16[176,128]{1,0:T(8,128)(2,1)S(1)}, bf16[176,128]{1,0:T(8,128)(2,1)S(1)}, u32[]{:S(2)}, u32[]{:S(2)}) %collective-permute-start.7) | collective-permute-done | bytes 45088 | tf_op jit(solution)/shard_map/ppermute | solution.py:134
  151.9 4.2 %all-to-all-start.6 = ((bf16[8,352,128]{2,1,0:T(8,128)(2,1)}), bf16[8,352,128]{2,1,0:T(8,128)(2,1)}, u32[]{:S(2)}, u32[]{:S(2)}) async-start(bf16[8,352,128]{2,1,0:T(8,128)(2,1)} %broadcast_in_dim.31), calls=%async_computation.6 | async-start | bytes 1441792 | tf_op jit(solution)/shard_map/all_to_all | solution.py:33
  159.2 10.1 %all-to-all-done.6 = bf16[8,352,128]{2,1,0:T(8,128)(2,1)} async-done(((bf16[8,352,128]{2,1,0:T(8,128)(2,1)}), bf16[8,352,128]{2,1,0:T(8,128)(2,1)}, u32[]{:S(2)}, u32[]{:S(2)}) %all-to-all-start.6) | async-done | bytes 720928 | tf_op jit(solution)/shard_map/all_to_all | solution.py:33
  169.2 1.9 fusion.89
  171.2 1.6 fusion.14
  172.9 2.3 convolution_convert_fusion.3
  175.2 3.4 %all-to-all-start.7 = ((bf16[8,176,128]{2,1,0:T(8,128)(2,1)}), bf16[8,176,128]{2,1,0:T(8,128)(2,1)S(1)}, u32[]{:S(2)}, u32[]{:S(2)}) async-start(bf16[8,176,128]{2,1,0:T(8,128)(2,1)} %bitcast.156), calls=%async_computation.7 | async-start | bytes 720896 | tf_op jit(solution)/shard_map/all_to_all | solution.py:108
  179.3 1.7 convolution_add_fusion.17
  181.1 5.5 %all-to-all-done.7 = bf16[8,176,128]{2,1,0:T(8,128)(2,1)S(1)} async-done(((bf16[8,176,128]{2,1,0:T(8,128)(2,1)}), bf16[8,176,128]{2,1,0:T(8,128)(2,1)S(1)}, u32[]{:S(2)}, u32[]{:S(2)}) %all-to-all-start.7) | async-done | bytes 360480 | tf_op jit(solution)/shard_map/all_to_all | solution.py:108
  188.2 3.4 %all-to-all-start.8 = ((bf16[8,176,128]{2,1,0:T(8,128)(2,1)}), bf16[8,176,128]{2,1,0:T(8,128)(2,1)S(1)}, u32[]{:S(2)}, u32[]{:S(2)}) async-start(bf16[8,176,128]{2,1,0:T(8,128)(2,1)} %broadcast_in_dim.32), calls=%async_computation.8 | async-start | bytes 720896 | tf_op jit(solution)/shard_map/all_to_all | solution.py:33
  192.8 5.3 %collective-permute-start.8 = (bf16[176,128]{1,0:T(8,128)(2,1)S(1)}, bf16[176,128]{1,0:T(8,128)(2,1)}, u32[]{:S(2)}, u32[]{:S(2)}) collective-permute-start(bf16[176,128]{1,0:T(8,128)(2,1)S(1)} %fusion.18), channel_id=1, source_target_pairs={{0,1},{1,0},{2,3},{3,2},{4,5},{5,4},{6,7},{7,6},{8,9},{9,8},{10,11... | collective-permute-start | bytes 135176 | tf_op jit(solution)/shard_map/ppermute | solution.py:27
  198.1 1.6 broadcast_select_fusion.3
  201.0 1.9 collective-permute-start.9
  205.4 9.5 %collective-permute-done.10 = bf16[176,128]{1,0:T(8,128)(2,1)S(1)} collective-permute-done((bf16[176,128]{1,0:T(8,128)(2,1)S(1)}, bf16[176,128]{1,0:T(8,128)(2,1)S(1)}, u32[]{:S(2)}, u32[]{:S(2)}) %collective-permute-start.10) | collective-permute-done | bytes 45088 | tf_op jit(solution)/shard_map/ppermute | solution.py:134
  218.1 5.4 %all-to-all-start.9 = ((bf16[8,352,128]{2,1,0:T(8,128)(2,1)}), bf16[8,352,128]{2,1,0:T(8,128)(2,1)S(1)}, u32[]{:S(2)}, u32[]{:S(2)}) async-start(bf16[8,352,128]{2,1,0:T(8,128)(2,1)} %broadcast_in_dim.33), calls=%async_computation.9 | async-start | bytes 1441792 | tf_op jit(solution)/shard_map/all_to_all | solution.py:33
  225.9 5.3 %collective-permute-start.11 = (bf16[176,128]{1,0:T(8,128)(2,1)S(1)}, bf16[176,128]{1,0:T(8,128)(2,1)S(1)}, u32[]{:S(2)}, u32[]{:S(2)}) collective-permute-start(bf16[176,128]{1,0:T(8,128)(2,1)S(1)} %fusion.19), channel_id=1, source_target_pairs={{0,1},{1,0},{2,3},{3,2},{4,5},{5,4},{6,7},{7,6},{8,9},{9,8},{10,11... | collective-permute-start | bytes 135176 | tf_op jit(solution)/shard_map/ppermute | solution.py:27
  231.2 4.8 %all-to-all-done.9 = bf16[8,352,128]{2,1,0:T(8,128)(2,1)S(1)} async-done(((bf16[8,352,128]{2,1,0:T(8,128)(2,1)}), bf16[8,352,128]{2,1,0:T(8,128)(2,1)S(1)}, u32[]{:S(2)}, u32[]{:S(2)}) %all-to-all-start.9) | async-done | bytes 720928 | tf_op jit(solution)/shard_map/all_to_all | solution.py:33
  236.8 1.7 fusion.15
  241.1 3.7 %all-to-all-start.10 = ((bf16[8,352,128]{2,1,0:T(8,128)(2,1)}), bf16[8,352,128]{2,1,0:T(8,128)(2,1)S(1)}, u32[]{:S(2)}, u32[]{:S(2)}) async-start(bf16[8,352,128]{2,1,0:T(8,128)(2,1)} %pad_maximum_fusion.3), calls=%async_computation.10 | async-start | bytes 1441792 | tf_op jit(solution)/shard_map/all_to_all | solution.py:108
  247.3 5.3 %collective-permute-start.12 = (bf16[192,128]{1,0:T(8,128)(2,1)S(1)}, bf16[192,128]{1,0:T(8,128)(2,1)S(1)}, u32[]{:S(2)}, u32[]{:S(2)}) collective-permute-start(bf16[192,128]{1,0:T(8,128)(2,1)S(1)} %slice.143), channel_id=1, source_target_pairs={{0,1},{1,0},{2,3},{3,2},{4,5},{5,4},{6,7},{7,6},{8,9},{9,8},{10,11... | collective-permute-start | bytes 147464 | tf_op jit(solution)/shard_map/ppermute | solution.py:27
  252.6 3.6 %all-to-all-done.10 = bf16[8,352,128]{2,1,0:T(8,128)(2,1)S(1)} async-done(((bf16[8,352,128]{2,1,0:T(8,128)(2,1)}), bf16[8,352,128]{2,1,0:T(8,128)(2,1)S(1)}, u32[]{:S(2)}, u32[]{:S(2)}) %all-to-all-start.10) | async-done | bytes 720928 | tf_op jit(solution)/shard_map/all_to_all | solution.py:108
  258.0 6.1 %all-to-all-start.11 = ((bf16[16,176,128]{2,1,0:T(8,128)(2,1)}), bf16[16,176,128]{2,1,0:T(8,128)(2,1)S(1)}, u32[]{:S(2)}, u32[]{:S(2)}) async-start(bf16[16,176,128]{2,1,0:T(8,128)(2,1)} %broadcast_in_dim.35), calls=%async_computation.11 | async-start | bytes 1441792 | tf_op jit(solution)/shard_map/all_to_all | solution.py:33
  268.6 7.9 %all-to-all-done.11 = bf16[16,176,128]{2,1,0:T(8,128)(2,1)S(1)} async-done(((bf16[16,176,128]{2,1,0:T(8,128)(2,1)}), bf16[16,176,128]{2,1,0:T(8,128)(2,1)S(1)}, u32[]{:S(2)}, u32[]{:S(2)}) %all-to-all-start.11) | async-done | bytes 720928 | tf_op jit(solution)/shard_map/all_to_all | solution.py:33
  (174 shorter events, 51.3 us)
Async XLA Ops:
  0.6 19.5 %copy-start = (bf16[1,128,1408]{2,1,0:T(8,128)(2,1)S(1)}, bf16[1,128,1408]{2,1,0:T(8,128)(2,1)}, u32[]{:S(2)}) copy-start(bf16[1,128,1408]{2,1,0:T(8,128)(2,1)} %param.9) | copy-start | bytes 1081348
  0.6 7.0 %copy-start.9 = (bf16[1,2,88,1408]{3,2,1,0:T(8,128)(2,1)S(1)}, bf16[1,2,88,1408]{3,2,1,0:T(8,128)(2,1)}, u32[]{:S(2)}) copy-start(bf16[1,2,88,1408]{3,2,1,0:T(8,128)(2,1)} %param.13) | copy-start | bytes 1486852
  0.7 14.4 %copy-start.31 = (bf16[1,192,1408]{2,1,0:T(8,128)(2,1)S(1)}, bf16[1,192,1408]{2,1,0:T(8,128)(2,1)}, u32[]{:S(2)}) copy-start(bf16[1,192,1408]{2,1,0:T(8,128)(2,1)} %param.15) | copy-start | bytes 1622020
  0.7 19.2 %copy-start.30 = (s32[1,4,128]{2,1,0:T(4,128)S(1)}, s32[1,4,128]{2,1,0:T(4,128)}, u32[]{:S(2)}) copy-start(s32[1,4,128]{2,1,0:T(4,128)} %param.10) | copy-start | bytes 6148
  0.7 19.3 %copy-start.27 = (bf16[1,128,2,176]{1,3,2,0:T(8,128)(2,1)S(1)}, bf16[1,128,2,176]{1,3,2,0:T(8,128)(2,1)}, u32[]{:S(2)}) copy-start(bf16[1,128,2,176]{1,3,2,0:T(8,128)(2,1)} %param.8) | copy-start | bytes 270340
  2.4 39.1 %all-to-all-start = ((bf16[8,176,128]{2,1,0:T(8,128)(2,1)}), bf16[8,176,128]{2,1,0:T(8,128)(2,1)S(1)}, u32[]{:S(2)}, u32[]{:S(2)}) async-start(bf16[8,176,128]{2,1,0:T(8,128)(2,1)} %broadcast_in_dim.26), calls=%async_computation | async-start | bytes 720896 | tf_op jit(solution)/shard_map/all_to_all | solution.py:33
  7.7 19.2 %collective-permute-start = (bf16[2,88,1408]{2,1,0:T(8,128)(2,1)S(1)}, bf16[2,88,1408]{2,1,0:T(8,128)(2,1)S(1)}, u32[]{:S(2)}, u32[]{:S(2)}) collective-permute-start(bf16[2,88,1408]{2,1,0:T(8,128)(2,1)S(1)} %bitcast.153), channel_id=1, source_target_pairs={{0,1},{1,0},{2,3},{3,2},{4,5},{5,4},{6,7},{7,6},{8,9},{9,8},{10,11... | collective-permute-start | bytes 1486856 | tf_op jit(solution)/shard_map/ppermute | solution.py:27
  12.5 26.0 %collective-permute-start.1 = (bf16[1408,192]{0,1:T(8,128)(2,1)}, bf16[1408,192]{0,1:T(8,128)(2,1)}, u32[]{:S(2)}, u32[]{:S(2)}) collective-permute-start(bf16[1408,192]{0,1:T(8,128)(2,1)} %bitcast.171), channel_id=1, source_target_pairs={{0,1},{1,0},{2,3},{3,2},{4,5},{5,4},{6,7},{7,6},{8,9},{9,8},{10,11... | collective-permute-start | bytes 1622024 | tf_op jit(solution)/shard_map/ppermute | solution.py:27
  15.1 34.5 %collective-permute-start.2 = (bf16[192,1408]{1,0:T(8,128)(2,1)S(1)}, bf16[192,1408]{1,0:T(8,128)(2,1)}, u32[]{:S(2)}, u32[]{:S(2)}) collective-permute-start(bf16[192,1408]{1,0:T(8,128)(2,1)S(1)} %bitcast.168), channel_id=1, source_target_pairs={{0,1},{1,0},{2,3},{3,2},{4,5},{5,4},{6,7},{7,6},{8,9},{9,8},{10,11... | collective-permute-start | bytes 1622024 | tf_op jit(solution)/shard_map/ppermute | solution.py:27
  20.3 6.7 %copy-start.18 = (bf16[2,88,128]{2,1,0:T(8,128)(2,1)}, bf16[2,88,128]{2,1,0:T(8,128)(2,1)S(1)}, u32[]{:S(2)}) copy-start(bf16[2,88,128]{2,1,0:T(8,128)(2,1)S(1)} %get-tuple-element.53) | copy-start | bytes 135172
  27.0 11.6 %copy-start.33 = (bf16[1,1408,192]{1,2,0:T(8,128)(2,1)S(1)}, bf16[1,1408,192]{1,2,0:T(8,128)(2,1)}, u32[]{:S(2)}) copy-start(bf16[1,1408,192]{1,2,0:T(8,128)(2,1)} %param.14) | copy-start | bytes 1622020
  53.4 12.2 %copy-start.10 = (bf16[1,128,176]{1,2,0:T(8,128)(2,1)S(1)}, bf16[1,128,176]{1,2,0:T(8,128)(2,1)}, u32[]{:S(2)}) copy-start(bf16[1,128,176]{1,2,0:T(8,128)(2,1)} %param.11) | copy-start | bytes 135172
  53.4 12.1 %all-to-all-start.1 = ((bf16[8,176,128]{2,1,0:T(8,128)(2,1)}), bf16[8,176,128]{2,1,0:T(8,128)(2,1)S(1)}, u32[]{:S(2)}, u32[]{:S(2)}) async-start(bf16[8,176,128]{2,1,0:T(8,128)(2,1)} %bitcast.15), calls=%async_computation.1 | async-start | bytes 720896 | tf_op jit(solution)/shard_map/all_to_all | solution.py:108
  66.4 10.8 %all-to-all-start.2 = ((bf16[8,176,128]{2,1,0:T(8,128)(2,1)}), bf16[8,176,128]{2,1,0:T(8,128)(2,1)S(1)}, u32[]{:S(2)}, u32[]{:S(2)}) async-start(bf16[8,176,128]{2,1,0:T(8,128)(2,1)} %broadcast_in_dim.27), calls=%async_computation.2 | async-start | bytes 720896 | tf_op jit(solution)/shard_map/all_to_all | solution.py:33
  77.6 30.6 %copy-start.17 = (f32[384,128]{1,0:T(8,128)S(1)}, f32[384,128]{1,0:T(8,128)}, u32[]{:S(2)}) copy-start(f32[384,128]{1,0:T(8,128)} %convolution_add_fusion.11) | copy-start | bytes 589828
  77.6 4.0 %collective-permute-start.3 = (bf16[176,128]{1,0:T(8,128)(2,1)S(1)}, bf16[176,128]{1,0:T(8,128)(2,1)S(1)}, u32[]{:S(2)}, u32[]{:S(2)}) collective-permute-start(bf16[176,128]{1,0:T(8,128)(2,1)S(1)} %get-tuple-element.59), channel_id=1, source_target_pairs={{16,0},{32,16},{48,32},{64,48},{80,64},{96,80},{112,96},{128,112},... | collective-permute-start | bytes 135176 | tf_op jit(solution)/shard_map/ppermute | solution.py:131
  79.7 13.2 %collective-permute-start.4 = (bf16[176,128]{1,0:T(8,128)(2,1)S(1)}, bf16[176,128]{1,0:T(8,128)(2,1)S(1)}, u32[]{:S(2)}, u32[]{:S(2)}) collective-permute-start(bf16[176,128]{1,0:T(8,128)(2,1)S(1)} %get-tuple-element.60), channel_id=1, source_target_pairs={{256,240},{272,224},{288,208},{304,192},{320,176},{336,160},{352,1... | collective-permute-start | bytes 135176 | tf_op jit(solution)/shard_map/ppermute | solution.py:134
  94.5 13.8 %all-to-all-start.3 = ((bf16[8,176,128]{2,1,0:T(8,128)(2,1)}), bf16[8,176,128]{2,1,0:T(8,128)(2,1)S(1)}, u32[]{:S(2)}, u32[]{:S(2)}) async-start(bf16[8,176,128]{2,1,0:T(8,128)(2,1)} %broadcast_in_dim.28), calls=%async_computation.3 | async-start | bytes 720896 | tf_op jit(solution)/shard_map/all_to_all | solution.py:33
  97.9 10.3 %collective-permute-start.5 = (bf16[560,128]{1,0:T(8,128)(2,1)S(1)}, bf16[560,128]{1,0:T(8,128)(2,1)S(1)}, u32[]{:S(2)}, u32[]{:S(2)}) collective-permute-start(bf16[560,128]{1,0:T(8,128)(2,1)S(1)} %pad_maximum_fusion.4), channel_id=1, source_target_pairs={{0,1},{1,0},{2,3},{3,2},{4,5},{5,4},{6,7},{7,6},{8,9},{9,8},{10,11... | collective-permute-start | bytes 430088 | tf_op jit(solution)/shard_map/ppermute | solution.py:27
  108.2 1.8 copy-start.20
  108.2 1.8 copy-start.35
  110.0 2.3 copy-start.23
  112.3 11.8 %all-to-all-start.4 = ((bf16[8,176,128]{2,1,0:T(8,128)(2,1)}), bf16[8,176,128]{2,1,0:T(8,128)(2,1)S(1)}, u32[]{:S(2)}, u32[]{:S(2)}) async-start(bf16[8,176,128]{2,1,0:T(8,128)(2,1)} %bitcast.157), calls=%async_computation.4 | async-start | bytes 720896 | tf_op jit(solution)/shard_map/all_to_all | solution.py:108
  124.2 4.2 %copy-start.11 = (bf16[176,128]{1,0:T(8,128)(2,1)}, bf16[176,128]{1,0:T(8,128)(2,1)S(1)}, u32[]{:S(2)}) copy-start(bf16[176,128]{1,0:T(8,128)(2,1)S(1)} %add_convert_fusion.4) | copy-start | bytes 135172
  125.0 10.7 %all-to-all-start.5 = ((bf16[8,176,128]{2,1,0:T(8,128)(2,1)}), bf16[8,176,128]{2,1,0:T(8,128)(2,1)S(1)}, u32[]{:S(2)}, u32[]{:S(2)}) async-start(bf16[8,176,128]{2,1,0:T(8,128)(2,1)} %broadcast_in_dim.30), calls=%async_computation.5 | async-start | bytes 720896 | tf_op jit(solution)/shard_map/all_to_all | solution.py:33
  129.5 9.9 %copy-start.21 = (bf16[560,128]{1,0:T(8,128)(2,1)S(1)}, bf16[560,128]{1,0:T(8,128)(2,1)}, u32[]{:S(2)}) copy-start(bf16[560,128]{1,0:T(8,128)(2,1)} %copy-done.20) | copy-start | bytes 430084
  136.2 3.9 %collective-permute-start.6 = (bf16[176,128]{1,0:T(8,128)(2,1)S(1)}, bf16[176,128]{1,0:T(8,128)(2,1)S(1)}, u32[]{:S(2)}, u32[]{:S(2)}) collective-permute-start(bf16[176,128]{1,0:T(8,128)(2,1)S(1)} %get-tuple-element.57), channel_id=1, source_target_pairs={{16,0},{32,16},{48,32},{64,48},{80,64},{96,80},{112,96},{128,112},... | collective-permute-start | bytes 135176 | tf_op jit(solution)/shard_map/ppermute | solution.py:131
  138.1 12.0 %collective-permute-start.7 = (bf16[176,128]{1,0:T(8,128)(2,1)S(1)}, bf16[176,128]{1,0:T(8,128)(2,1)S(1)}, u32[]{:S(2)}, u32[]{:S(2)}) collective-permute-start(bf16[176,128]{1,0:T(8,128)(2,1)S(1)} %get-tuple-element.58), channel_id=1, source_target_pairs={{256,240},{272,224},{288,208},{304,192},{320,176},{336,160},{352,1... | collective-permute-start | bytes 135176 | tf_op jit(solution)/shard_map/ppermute | solution.py:134
  150.9 6.0 %copy-start.24 = (bf16[384,128]{1,0:T(8,128)(2,1)S(1)}, bf16[384,128]{1,0:T(8,128)(2,1)}, u32[]{:S(2)}) copy-start(bf16[384,128]{1,0:T(8,128)(2,1)} %copy-done.23) | copy-start | bytes 294916
  151.9 17.4 %all-to-all-start.6 = ((bf16[8,352,128]{2,1,0:T(8,128)(2,1)}), bf16[8,352,128]{2,1,0:T(8,128)(2,1)}, u32[]{:S(2)}, u32[]{:S(2)}) async-start(bf16[8,352,128]{2,1,0:T(8,128)(2,1)} %broadcast_in_dim.31), calls=%async_computation.6 | async-start | bytes 1441792 | tf_op jit(solution)/shard_map/all_to_all | solution.py:33
  169.2 2.0 copy-start.16
  169.2 2.0 copy-start.32
  172.9 2.3 copy-start.22
  175.2 11.4 %all-to-all-start.7 = ((bf16[8,176,128]{2,1,0:T(8,128)(2,1)}), bf16[8,176,128]{2,1,0:T(8,128)(2,1)S(1)}, u32[]{:S(2)}, u32[]{:S(2)}) async-start(bf16[8,176,128]{2,1,0:T(8,128)(2,1)} %bitcast.156), calls=%async_computation.7 | async-start | bytes 720896 | tf_op jit(solution)/shard_map/all_to_all | solution.py:108
  188.2 12.3 %all-to-all-start.8 = ((bf16[8,176,128]{2,1,0:T(8,128)(2,1)}), bf16[8,176,128]{2,1,0:T(8,128)(2,1)S(1)}, u32[]{:S(2)}, u32[]{:S(2)}) async-start(bf16[8,176,128]{2,1,0:T(8,128)(2,1)} %broadcast_in_dim.32), calls=%async_computation.8 | async-start | bytes 720896 | tf_op jit(solution)/shard_map/all_to_all | solution.py:33
  192.8 7.8 %collective-permute-start.8 = (bf16[176,128]{1,0:T(8,128)(2,1)S(1)}, bf16[176,128]{1,0:T(8,128)(2,1)}, u32[]{:S(2)}, u32[]{:S(2)}) collective-permute-start(bf16[176,128]{1,0:T(8,128)(2,1)S(1)} %fusion.18), channel_id=1, source_target_pairs={{0,1},{1,0},{2,3},{3,2},{4,5},{5,4},{6,7},{7,6},{8,9},{9,8},{10,11... | collective-permute-start | bytes 135176 | tf_op jit(solution)/shard_map/ppermute | solution.py:27
  201.0 4.4 %collective-permute-start.9 = (bf16[176,128]{1,0:T(8,128)(2,1)S(1)}, bf16[176,128]{1,0:T(8,128)(2,1)S(1)}, u32[]{:S(2)}, u32[]{:S(2)}) collective-permute-start(bf16[176,128]{1,0:T(8,128)(2,1)S(1)} %get-tuple-element.55), channel_id=1, source_target_pairs={{16,0},{32,16},{48,32},{64,48},{80,64},{96,80},{112,96},{128,112},... | collective-permute-start | bytes 135176 | tf_op jit(solution)/shard_map/ppermute | solution.py:131
  203.0 12.0 %collective-permute-start.10 = (bf16[176,128]{1,0:T(8,128)(2,1)S(1)}, bf16[176,128]{1,0:T(8,128)(2,1)S(1)}, u32[]{:S(2)}, u32[]{:S(2)}) collective-permute-start(bf16[176,128]{1,0:T(8,128)(2,1)S(1)} %get-tuple-element.56), channel_id=1, source_target_pairs={{256,240},{272,224},{288,208},{304,192},{320,176},{336,160},{352,1... | collective-permute-start | bytes 135176 | tf_op jit(solution)/shard_map/ppermute | solution.py:134
  217.2 7.5 %copy-start.5 = (bf16[8,176,128]{2,1,0:T(8,128)(2,1)S(1)}, bf16[8,176,128]{2,1,0:T(8,128)(2,1)}, u32[]{:S(2)}) copy-start(bf16[8,176,128]{2,1,0:T(8,128)(2,1)} %copy-done.4) | copy-start | bytes 1081348
  218.1 17.9 %all-to-all-start.9 = ((bf16[8,352,128]{2,1,0:T(8,128)(2,1)}), bf16[8,352,128]{2,1,0:T(8,128)(2,1)S(1)}, u32[]{:S(2)}, u32[]{:S(2)}) async-start(bf16[8,352,128]{2,1,0:T(8,128)(2,1)} %broadcast_in_dim.33), calls=%async_computation.9 | async-start | bytes 1441792 | tf_op jit(solution)/shard_map/all_to_all | solution.py:33
  223.5 2.3 copy-start.8
  225.8 11.1 %copy-start.15 = (f32[384,128]{1,0:T(8,128)S(1)}, f32[384,128]{1,0:T(8,128)}, u32[]{:S(2)}) copy-start(f32[384,128]{1,0:T(8,128)} %convolution_add_fusion.9) | copy-start | bytes 589828
  225.9 14.2 %collective-permute-start.11 = (bf16[176,128]{1,0:T(8,128)(2,1)S(1)}, bf16[176,128]{1,0:T(8,128)(2,1)S(1)}, u32[]{:S(2)}, u32[]{:S(2)}) collective-permute-start(bf16[176,128]{1,0:T(8,128)(2,1)S(1)} %fusion.19), channel_id=1, source_target_pairs={{0,1},{1,0},{2,3},{3,2},{4,5},{5,4},{6,7},{7,6},{8,9},{9,8},{10,11... | collective-permute-start | bytes 135176 | tf_op jit(solution)/shard_map/ppermute | solution.py:27
  241.1 4.9 %copy-start.2 = (f32[1408,128]{1,0:T(8,128)S(1)}, f32[1408,128]{1,0:T(8,128)}, u32[]{:S(2)}) copy-start(f32[1408,128]{1,0:T(8,128)} %convolution_add_fusion.5) | copy-start | bytes 2162692
  241.1 15.0 %all-to-all-start.10 = ((bf16[8,352,128]{2,1,0:T(8,128)(2,1)}), bf16[8,352,128]{2,1,0:T(8,128)(2,1)S(1)}, u32[]{:S(2)}, u32[]{:S(2)}) async-start(bf16[8,352,128]{2,1,0:T(8,128)(2,1)} %pad_maximum_fusion.3), calls=%async_computation.10 | async-start | bytes 1441792 | tf_op jit(solution)/shard_map/all_to_all | solution.py:108
  244.8 2.2 copy-start.26
  247.3 18.3 %collective-permute-start.12 = (bf16[192,128]{1,0:T(8,128)(2,1)S(1)}, bf16[192,128]{1,0:T(8,128)(2,1)S(1)}, u32[]{:S(2)}, u32[]{:S(2)}) collective-permute-start(bf16[192,128]{1,0:T(8,128)(2,1)S(1)} %slice.143), channel_id=1, source_target_pairs={{0,1},{1,0},{2,3},{3,2},{4,5},{5,4},{6,7},{7,6},{8,9},{9,8},{10,11... | collective-permute-start | bytes 147464 | tf_op jit(solution)/shard_map/ppermute | solution.py:27
  258.0 18.5 %all-to-all-start.11 = ((bf16[16,176,128]{2,1,0:T(8,128)(2,1)}), bf16[16,176,128]{2,1,0:T(8,128)(2,1)S(1)}, u32[]{:S(2)}, u32[]{:S(2)}) async-start(bf16[16,176,128]{2,1,0:T(8,128)(2,1)} %broadcast_in_dim.35), calls=%async_computation.11 | async-start | bytes 1441792 | tf_op jit(solution)/shard_map/all_to_all | solution.py:33
  (18 other events, 21.7 us)

commit v4 on v3

v4 whole, which is shorter than its diff:
```python
import jax
import jax.numpy as jnp
from jax import lax
from jax.sharding import PartitionSpec as P

gelu_scale = 0.7978845608
gelu_cubic = 0.044715
f32 = jnp.float32
bf16 = jnp.bfloat16


def gelu_pair(pre_gelu):
    inner = gelu_scale * (pre_gelu + gelu_cubic * pre_gelu * pre_gelu * pre_gelu)
    tanh_part = jnp.tanh(inner)
    gelu_value = 0.5 * pre_gelu * (1.0 + tanh_part)
    gelu_slope = 0.5 * (1.0 + tanh_part) + 0.5 * pre_gelu * (
        1.0 - tanh_part * tanh_part
    ) * gelu_scale * (1.0 + 3.0 * gelu_cubic * pre_gelu * pre_gelu)
    return (gelu_value, gelu_slope)


def dot(a, b, ca=1, cb=0):
    return lax.dot_general(a, b, (((ca,), (cb,)), ((), ())), preferred_element_type=f32)


def swap(x):
    return lax.ppermute(x, "replica", [(0, 1), (1, 0)])


def gather(chunk, axes="tensor"):
    count = lax.axis_size(axes)
    spread = jnp.broadcast_to(chunk[None], (count, *chunk.shape))
    return lax.all_to_all(spread, axes, 0, 0)


def body(pool_inputs, pool_mixed, crop_ids, incoming, loss_grads, w_proj, w_up, w_down):
    section = lax.axis_index("section")
    sections = lax.axis_size("section")
    replica = lax.axis_index("replica")
    parts = lax.axis_size("tensor")
    half = sections // 2
    first = replica == 0
    is_top = section == sections - 1
    ticks, rows = crop_ids.shape[1:]
    pool = pool_mixed.shape[1]
    width = pool_mixed.shape[2]
    units = w_down.shape[1]
    own_in = w_proj.shape[2]
    chunk_rows = incoming.shape[2]

    def by_replica(own, other):
        return jnp.where(first, own, other), jnp.where(first, other, own)

    def tied(*values):
        return lax.optimization_barrier(values)

    def pick_of(ids):
        places = jnp.arange(pool, dtype=jnp.int32)[:, None]
        return (ids[None, :] == places).astype(bf16)

    def other_of(pair):
        return jnp.where(first, pair[1], pair[0])

    up_other = swap(w_up[0])
    down_other = swap(w_down[0])
    proj_rows = 2 * own_in
    flat_inputs = pool_inputs[0].transpose(1, 2, 0).reshape(-1, width)
    ids_row = jnp.pad(crop_ids[0, ticks - 1].astype(bf16), (0, width - rows))
    ids_rows = jnp.broadcast_to(ids_row[None], (16, width))
    pairs = lax.all_gather(
        jnp.concatenate(
            [w_proj[0].reshape(proj_rows, width), pool_mixed[0], flat_inputs, ids_rows],
            axis=0,
        ),
        "replica",
    )
    proj = pairs[:, :proj_rows].reshape(2, 2, own_in, width).transpose(1, 0, 2, 3)
    proj = proj.reshape(-1, width)
    mixed_pair = pairs[:, proj_rows : proj_rows + pool]
    inputs_pair = pairs[:, proj_rows + pool : -16].reshape(2, 2, -1, pool)
    ids_pair = pairs[:, -1, :rows].astype(jnp.int32)

    chunk = incoming[0].T
    upstream = gather(chunk).reshape(width, rows)

    up = jnp.concatenate([w_up[0], up_other], axis=1)
    down = jnp.concatenate([w_down[0], down_other], axis=0)
    pick = [pick_of(ids) for ids in crop_ids[0]]

    def hidden_parts(weight, mixed):
        value, slope = gelu_pair(dot(weight, mixed, 0, 1))
        high = slope.astype(bf16)
        low = (slope - high.astype(f32)).astype(bf16)
        return value.astype(bf16), high, low

    active, high, low = hidden_parts(up, pool_mixed[0])

    def scatter(x, t):
        return dot(x, pick[t], 1, 1)

    seen, spread, early = 0.0, 0.0, 0.0
    for t in range(ticks):
        last = t + 1 == ticks
        slope_now = dot(high, pick[t]) + dot(low, pick[t])
        if last:
            backs = dot(down, upstreams[0]), dot(down, upstreams[1])
            back = jnp.where(first, *backs)
        else:
            back = dot(down, upstream)
        hidden = (back * slope_now).astype(bf16)
        partial = dot(up, hidden).astype(bf16)
        terms = lax.all_to_all(partial.reshape(parts, chunk_rows, rows), "tensor", 0, 0)
        mixed_chunk = (
            jnp.sum(terms.astype(f32), axis=0) + chunk.astype(f32)
        ).astype(bf16)
        if last:
            break
        upstream_late, hidden_late, _ = tied(upstream, hidden, partial)
        seen = seen + scatter(upstream_late, t)
        spread = spread + scatter(hidden_late, t)
        mixed_grad = gather(mixed_chunk).reshape(width, rows)
        early = early + scatter(mixed_grad, t)
        input_grad = dot(proj, mixed_grad).astype(bf16).reshape(2, chunk_rows, rows)
        above = lax.ppermute(
            input_grad[0], "section", [(i, i - 1) for i in range(1, sections)]
        )
        mirrored = lax.ppermute(
            input_grad[1],
            "section",
            [(i, sections - 1 - i) for i in range(half, sections)],
        )
        summed = (above.astype(f32) + mirrored.astype(f32)).astype(bf16)
        chunk = jnp.where(is_top, loss_grads[t].T, summed)
        if t + 2 == ticks:
            factors = jnp.concatenate([seen, early, spread[units:]], axis=0)
            factors = lax.all_gather(factors.astype(bf16), "replica")
            upstreams = gather(chunk, ("replica", "tensor")).reshape(2, width, rows)
        else:
            upstream = gather(chunk).reshape(width, rows)

    mixed_grads = gather(mixed_chunk, ("replica", "tensor")).reshape(2, width, rows)
    input_grad = jnp.where(first, dot(proj, mixed_grads[0]), dot(proj, mixed_grads[1]))
    input_grad = input_grad.astype(bf16).reshape(2, chunk_rows, rows)

    pick_other = pick_of(other_of(ids_pair))
    mixed_other = other_of(mixed_pair)
    active_other, high, low = hidden_parts(w_up[0], mixed_other)
    slope_other = dot(high, pick_other) + dot(low, pick_other)
    back_other = jnp.where(first, backs[1], backs[0])[:units]
    hidden_other = (back_other * slope_other).astype(bf16)
    spread_own = spread[:units] + scatter(hidden[:units], ticks - 1)
    spread_other = other_of(factors[:, 2 * width :]).astype(f32)
    spread_other = spread_other + dot(hidden_other, pick_other, 1, 1)
    grad_up = dot(
        jnp.concatenate([pool_mixed[0], mixed_other], axis=0),
        jnp.concatenate([spread_own, spread_other], axis=1).astype(bf16),
        0,
        1,
    ).astype(bf16)

    picks = by_replica(pick[ticks - 1], pick_other)
    actives = by_replica(active[:units], active_other)
    seens = [
        (factors[r, :width].astype(f32) + dot(upstreams[r], picks[r], 1, 1)).astype(bf16)
        for r in range(2)
    ]
    grad_down = dot(
        jnp.concatenate(actives, axis=1), jnp.concatenate(seens, axis=1), 1, 1
    ).astype(bf16)

    decoder = jnp.where(section < half, 0.0, 1.0).astype(bf16)
    mask = jnp.stack([jnp.ones((), bf16), decoder])[:, None, None]
    saved = inputs_pair * mask
    saved = jnp.where(first, saved[:, :, :own_in], saved[:, :, own_in:])
    saved = saved.reshape(2, 2 * own_in, pool)
    lasts = [dot(saved[r], picks[r]).astype(bf16) for r in range(2)]
    grad_proj = dot(
        jnp.concatenate([saved[0], saved[1], *lasts], axis=1),
        jnp.concatenate(
            [factors[0, width : 2 * width], factors[1, width : 2 * width], *mixed_grads],
            axis=1,
        ),
        1,
        1,
    ).astype(bf16)
    return (
        grad_proj.reshape(1, 2, own_in, width),
        grad_up[None],
        grad_down[None],
        input_grad.transpose(2, 0, 1)[None],
    )


def solution(mesh):
    in_specs = (
        P("section", "replica", None, "tensor"),
        P("section", "replica", None),
        P("section", "replica", None),
        P("section", "replica", "tensor"),
        P(None, "replica", "tensor"),
        P("section", None, ("tensor", "replica"), None),
        P("section", None, ("tensor", "replica")),
        P("section", ("tensor", "replica"), None),
    )
    out_specs = (
        P("section", None, ("tensor", "replica"), None),
        P("section", None, ("tensor", "replica")),
        P("section", ("tensor", "replica"), None),
        P("section", "replica", None, "tensor"),
    )
    return jax.shard_map(body, mesh=mesh, in_specs=in_specs, out_specs=out_specs, check_vma=False)
```

time: 282 us -> 286 us (1.014)
  the two profiles are of different devices: /device:TPU:96 before, /device:TPU:98 now
where the time goes in v4:
time: 286 us; the launch traced here: 284 us
  waiting for transfers between devices  120 us (42%)
  starting transfers between devices  80.3 us (28%)
  matrix products  41.3 us (14%)
  local copies, waits for them, and re-layouts  16.9 us (6%)
  between operations  14.9 us (5%)
  other arithmetic  9.97 us (3%)
    dot_general x43, matrix products, dot(): lax.dot_general(a, b, (((ca,), (cb,)), ((), ())), preferred_element_type=...  41.3 us
    all_to_all x8, starting transfers between devices, gather(): return lax.all_to_all(spread, axes, 0, 0)  40.6 us
    ppermute x3, waiting for transfers between devices, body(): lax.ppermute(input_grad[1], 'section', [(i, sections - 1 - i) for i in ra...  30 us
    all_to_all x8, waiting for transfers between devices, gather(): return lax.all_to_all(spread, axes, 0, 0)  26.4 us
    all_to_all x4, starting transfers between devices, body(): lax.all_to_all(partial.reshape(parts, chunk_rows, rows), 'tensor', 0, 0)  22.6 us
    ppermute x2, waiting for transfers between devices, swap(): return lax.ppermute(x, 'replica', [(0, 1), (1, 0)])  19.7 us
    all_to_all x4, waiting for transfers between devices, body(): lax.all_to_all(partial.reshape(parts, chunk_rows, rows), 'tensor', 0, 0)  18 us
    all_gather x1, waiting for transfers between devices, body(): factors = lax.all_gather(factors.astype(bf16), 'replica')  14.7 us
  transfers between devices with their start and end apart: 22, of which 16 were waited for; matrix products, arithmetic and copies ran while one was open for 16% of the time, Pallas kernels for 0%

profile of v4, /device:TPU:98, one launch (start us, length us, event | category | flops | bytes accessed | tf_op | source)
XLA Modules:
  0.0 283.6 jit_solution(3140205218035250164)
XLA Ops:
  7.2 1.6 broadcast_in_dim.25
  8.8 5.8 %all-to-all-start = ((bf16[8,176,128]{2,1,0:T(8,128)(2,1)}), bf16[8,176,128]{2,1,0:T(8,128)(2,1)S(1)}, u32[]{:S(2)}, u32[]{:S(2)}) async-start(bf16[8,176,128]{2,1,0:T(8,128)(2,1)} %broadcast_in_dim.25), calls=%async_computation | async-start | bytes 720896 | tf_op jit(solution)/shard_map/all_to_all | solution.py:33
  14.7 4.8 %collective-permute-start = (bf16[192,1408]{1,0:T(8,128)(2,1)}, bf16[192,1408]{1,0:T(8,128)(2,1)}, u32[]{:S(2)}, u32[]{:S(2)}) collective-permute-start(bf16[192,1408]{1,0:T(8,128)(2,1)} %bitcast.188), channel_id=1, source_target_pairs={{0,1},{1,0},{2,3},{3,2},{4,5},{5,4},{6,7},{7,6},{8,9},{9,8},{10,11... | collective-permute-start | bytes 1622024 | tf_op jit(solution)/shard_map/ppermute | solution.py:27
  19.5 2.5 collective-permute-start.1
  25.1 19.7 %collective-permute-done.1 = bf16[1408,192]{0,1:T(8,128)(2,1)S(1)} collective-permute-done((bf16[1408,192]{0,1:T(8,128)(2,1)}, bf16[1408,192]{0,1:T(8,128)(2,1)S(1)}, u32[]{:S(2)}, u32[]{:S(2)}) %collective-permute-start.1) | collective-permute-done | bytes 540704 | tf_op jit(solution)/shard_map/ppermute | solution.py:27
  46.5 1.5 fusion.15
  49.3 5.3 %all-to-all-start.1 = ((bf16[8,176,128]{2,1,0:T(8,128)(2,1)}), bf16[8,176,128]{2,1,0:T(8,128)(2,1)S(1)}, u32[]{:S(2)}, u32[]{:S(2)}) async-start(bf16[8,176,128]{2,1,0:T(8,128)(2,1)} %bitcast.21), calls=%async_computation.1 | async-start | bytes 720896 | tf_op jit(solution)/shard_map/all_to_all | solution.py:112
  57.5 4.3 %all-to-all-done.1 = bf16[8,176,128]{2,1,0:T(8,128)(2,1)S(1)} async-done(((bf16[8,176,128]{2,1,0:T(8,128)(2,1)}), bf16[8,176,128]{2,1,0:T(8,128)(2,1)S(1)}, u32[]{:S(2)}, u32[]{:S(2)}) %all-to-all-start.1) | async-done | bytes 360480 | tf_op jit(solution)/shard_map/all_to_all | solution.py:112
  62.6 4.5 %all-to-all-start.2 = ((bf16[8,176,128]{2,1,0:T(8,128)(2,1)}), bf16[8,176,128]{2,1,0:T(8,128)(2,1)S(1)}, u32[]{:S(2)}, u32[]{:S(2)}) async-start(bf16[8,176,128]{2,1,0:T(8,128)(2,1)} %broadcast_in_dim.26), calls=%async_computation.2 | async-start | bytes 720896 | tf_op jit(solution)/shard_map/all_to_all | solution.py:33
  68.2 11.3 %all-gather.6.cloned.1.call-done = bf16[704,1408]{1,0:T(8,128)(2,1)} async-done(((bf16[352,1408]{1,0:T(8,128)(2,1)}), bf16[704,1408]{1,0:T(8,128)(2,1)}) %all-gather.6.cloned.1.call-update) | async-done | bytes 1982480 | tf_op jit(solution)/shard_map/all_gather | solution.py:70
  79.5 1.3 slice.175
  81.3 1.9 collective-permute-start.2
  83.3 1.3 collective-permute-start.3
  85.0 10.3 %collective-permute-done.3 = bf16[176,128]{1,0:T(8,128)(2,1)S(1)} collective-permute-done((bf16[176,128]{1,0:T(8,128)(2,1)S(1)}, bf16[176,128]{1,0:T(8,128)(2,1)S(1)}, u32[]{:S(2)}, u32[]{:S(2)}) %collective-permute-start.3) | collective-permute-done | bytes 45088 | tf_op jit(solution)/shard_map/ppermute | solution.py:127
  97.5 4.8 %all-to-all-start.3 = ((bf16[8,176,128]{2,1,0:T(8,128)(2,1)}), bf16[8,176,128]{2,1,0:T(8,128)(2,1)S(1)}, u32[]{:S(2)}, u32[]{:S(2)}) async-start(bf16[8,176,128]{2,1,0:T(8,128)(2,1)} %broadcast_in_dim.27), calls=%async_computation.3 | async-start | bytes 720896 | tf_op jit(solution)/shard_map/all_to_all | solution.py:33
  104.8 4.4 %all-to-all-done.3 = bf16[8,176,128]{2,1,0:T(8,128)(2,1)S(1)} async-done(((bf16[8,176,128]{2,1,0:T(8,128)(2,1)}), bf16[8,176,128]{2,1,0:T(8,128)(2,1)S(1)}, u32[]{:S(2)}, u32[]{:S(2)}) %all-to-all-start.3) | async-done | bytes 360480 | tf_op jit(solution)/shard_map/all_to_all | solution.py:33
  109.2 1.9 fusion.16
  112.3 5.0 %all-to-all-start.4 = ((bf16[8,176,128]{2,1,0:T(8,128)(2,1)}), bf16[8,176,128]{2,1,0:T(8,128)(2,1)S(1)}, u32[]{:S(2)}, u32[]{:S(2)}) async-start(bf16[8,176,128]{2,1,0:T(8,128)(2,1)} %bitcast.178), calls=%async_computation.4 | async-start | bytes 720896 | tf_op jit(solution)/shard_map/all_to_all | solution.py:112
  117.4 2.1 broadcast_select_fusion.1
  119.5 4.0 %all-to-all-done.4 = bf16[8,176,128]{2,1,0:T(8,128)(2,1)S(1)} async-done(((bf16[8,176,128]{2,1,0:T(8,128)(2,1)}), bf16[8,176,128]{2,1,0:T(8,128)(2,1)S(1)}, u32[]{:S(2)}, u32[]{:S(2)}) %all-to-all-start.4) | async-done | bytes 360480 | tf_op jit(solution)/shard_map/all_to_all | solution.py:112
  124.4 5.1 %all-to-all-start.5 = ((bf16[8,176,128]{2,1,0:T(8,128)(2,1)}), bf16[8,176,128]{2,1,0:T(8,128)(2,1)S(1)}, u32[]{:S(2)}, u32[]{:S(2)}) async-start(bf16[8,176,128]{2,1,0:T(8,128)(2,1)} %broadcast_in_dim.28), calls=%async_computation.5 | async-start | bytes 720896 | tf_op jit(solution)/shard_map/all_to_all | solution.py:33
  130.7 4.6 %all-to-all-done.5 = bf16[8,176,128]{2,1,0:T(8,128)(2,1)S(1)} async-done(((bf16[8,176,128]{2,1,0:T(8,128)(2,1)}), bf16[8,176,128]{2,1,0:T(8,128)(2,1)S(1)}, u32[]{:S(2)}, u32[]{:S(2)}) %all-to-all-start.5) | async-done | bytes 360480 | tf_op jit(solution)/shard_map/all_to_all | solution.py:33
  135.8 1.9 collective-permute-start.4
  137.7 1.3 collective-permute-start.5
  139.7 10.0 %collective-permute-done.5 = bf16[176,128]{1,0:T(8,128)(2,1)S(1)} collective-permute-done((bf16[176,128]{1,0:T(8,128)(2,1)S(1)}, bf16[176,128]{1,0:T(8,128)(2,1)S(1)}, u32[]{:S(2)}, u32[]{:S(2)}) %collective-permute-start.5) | collective-permute-done | bytes 45088 | tf_op jit(solution)/shard_map/ppermute | solution.py:127
  151.9 4.8 %all-to-all-start.6 = ((bf16[8,176,128]{2,1,0:T(8,128)(2,1)}), bf16[8,176,128]{2,1,0:T(8,128)(2,1)S(1)}, u32[]{:S(2)}, u32[]{:S(2)}) async-start(bf16[8,176,128]{2,1,0:T(8,128)(2,1)} %broadcast_in_dim.29), calls=%async_computation.6 | async-start | bytes 720896 | tf_op jit(solution)/shard_map/all_to_all | solution.py:33
  157.5 6.4 %all-to-all-done.6 = bf16[8,176,128]{2,1,0:T(8,128)(2,1)S(1)} async-done(((bf16[8,176,128]{2,1,0:T(8,128)(2,1)}), bf16[8,176,128]{2,1,0:T(8,128)(2,1)S(1)}, u32[]{:S(2)}, u32[]{:S(2)}) %all-to-all-start.6) | async-done | bytes 360480 | tf_op jit(solution)/shard_map/all_to_all | solution.py:33
  163.9 1.8 fusion.17
  167.0 5.4 %all-to-all-start.7 = ((bf16[8,176,128]{2,1,0:T(8,128)(2,1)}), bf16[8,176,128]{2,1,0:T(8,128)(2,1)}, u32[]{:S(2)}, u32[]{:S(2)}) async-start(bf16[8,176,128]{2,1,0:T(8,128)(2,1)} %bitcast.33), calls=%async_computation.7 | async-start | bytes 720896 | tf_op jit(solution)/shard_map/all_to_all | solution.py:112
  174.5 4.5 %all-to-all-done.7 = bf16[8,176,128]{2,1,0:T(8,128)(2,1)} async-done(((bf16[8,176,128]{2,1,0:T(8,128)(2,1)}), bf16[8,176,128]{2,1,0:T(8,128)(2,1)}, u32[]{:S(2)}, u32[]{:S(2)}) %all-to-all-start.7) | async-done | bytes 360480 | tf_op jit(solution)/shard_map/all_to_all | solution.py:112
  181.6 4.9 %all-to-all-start.8 = ((bf16[8,176,128]{2,1,0:T(8,128)(2,1)}), bf16[8,176,128]{2,1,0:T(8,128)(2,1)S(1)}, u32[]{:S(2)}, u32[]{:S(2)}) async-start(bf16[8,176,128]{2,1,0:T(8,128)(2,1)} %broadcast_in_dim.30), calls=%async_computation.8 | async-start | bytes 720896 | tf_op jit(solution)/shard_map/all_to_all | solution.py:33
  186.6 1.8 convolution_add_fusion.8
  189.5 3.1 %all-to-all-done.8 = bf16[8,176,128]{2,1,0:T(8,128)(2,1)S(1)} async-done(((bf16[8,176,128]{2,1,0:T(8,128)(2,1)}), bf16[8,176,128]{2,1,0:T(8,128)(2,1)S(1)}, u32[]{:S(2)}, u32[]{:S(2)}) %all-to-all-start.8) | async-done | bytes 360480 | tf_op jit(solution)/shard_map/all_to_all | solution.py:33
  193.0 1.9 collective-permute-start.6
  195.0 1.3 collective-permute-start.7
  197.2 9.8 %collective-permute-done.7 = bf16[176,128]{1,0:T(8,128)(2,1)S(1)} collective-permute-done((bf16[176,128]{1,0:T(8,128)(2,1)S(1)}, bf16[176,128]{1,0:T(8,128)(2,1)S(1)}, u32[]{:S(2)}, u32[]{:S(2)}) %collective-permute-start.7) | collective-permute-done | bytes 45088 | tf_op jit(solution)/shard_map/ppermute | solution.py:127
  208.7 5.7 %all-to-all-start.9 = ((bf16[16,176,128]{2,1,0:T(8,128)(2,1)}), bf16[16,176,128]{2,1,0:T(8,128)(2,1)S(1)}, u32[]{:S(2)}, u32[]{:S(2)}) async-start(bf16[16,176,128]{2,1,0:T(8,128)(2,1)} %broadcast_in_dim.31), calls=%async_computation.9 | async-start | bytes 1441792 | tf_op jit(solution)/shard_map/all_to_all | solution.py:33
  217.8 8.0 %all-to-all-done.9 = bf16[16,176,128]{2,1,0:T(8,128)(2,1)S(1)} async-done(((bf16[16,176,128]{2,1,0:T(8,128)(2,1)}), bf16[16,176,128]{2,1,0:T(8,128)(2,1)S(1)}, u32[]{:S(2)}, u32[]{:S(2)}) %all-to-all-start.9) | async-done | bytes 720928 | tf_op jit(solution)/shard_map/all_to_all | solution.py:33
  225.9 1.7 fusion.127
  227.7 1.6 fusion.126
  230.8 6.9 %all-to-all-start.10 = ((bf16[8,176,128]{2,1,0:T(8,128)(2,1)}), bf16[8,176,128]{2,1,0:T(8,128)(2,1)S(1)}, u32[]{:S(2)}, u32[]{:S(2)}) async-start(bf16[8,176,128]{2,1,0:T(8,128)(2,1)} %bitcast.43), calls=%async_computation.10 | async-start | bytes 720896 | tf_op jit(solution)/shard_map/all_to_all | solution.py:112
  239.3 5.2 %all-to-all-done.10 = bf16[8,176,128]{2,1,0:T(8,128)(2,1)S(1)} async-done(((bf16[8,176,128]{2,1,0:T(8,128)(2,1)}), bf16[8,176,128]{2,1,0:T(8,128)(2,1)S(1)}, u32[]{:S(2)}, u32[]{:S(2)}) %all-to-all-start.10) | async-done | bytes 360480 | tf_op jit(solution)/shard_map/all_to_all | solution.py:112
  245.5 4.9 %all-to-all-start.11 = ((bf16[16,176,128]{2,1,0:T(8,128)(2,1)}), bf16[16,176,128]{2,1,0:T(8,128)(2,1)S(1)}, u32[]{:S(2)}, u32[]{:S(2)}) async-start(bf16[16,176,128]{2,1,0:T(8,128)(2,1)} %broadcast_in_dim.32), calls=%async_computation.11 | async-start | bytes 1441792 | tf_op jit(solution)/shard_map/all_to_all | solution.py:33
  250.4 14.7 %all-gather.4.cloned.1.call-done = bf16[2,3008,128]{2,1,0:T(8,128)(2,1)} async-done(((bf16[1,3008,128]{2,1,0:T(8,128)(2,1)}), bf16[2,3008,128]{2,1,0:T(8,128)(2,1)}) %all-gather.4.cloned.1.call-update) | async-done | bytes 1540112 | tf_op jit(solution)/shard_map/all_gather | solution.py:136
  265.0 2.3 fusion.130
  267.3 1.9 fusion.20
  269.7 2.3 fusion.1
  275.3 1.4 convolution_convert_fusion.2
  (181 shorter events, 45.2 us)
Async XLA Ops:
  7.2 16.8 %copy-start.24 = (bf16[1,128,1408]{2,1,0:T(8,128)(2,1)S(1)}, bf16[1,128,1408]{2,1,0:T(8,128)(2,1)}, u32[]{:S(2)}) copy-start(bf16[1,128,1408]{2,1,0:T(8,128)(2,1)} %param.9) | copy-start | bytes 1081348
  7.2 16.8 %copy-start.14 = (bf16[1,2,88,1408]{3,2,1,0:T(8,128)(2,1)S(1)}, bf16[1,2,88,1408]{3,2,1,0:T(8,128)(2,1)}, u32[]{:S(2)}) copy-start(bf16[1,2,88,1408]{3,2,1,0:T(8,128)(2,1)} %param.13) | copy-start | bytes 1486852
  8.8 37.7 %all-to-all-start = ((bf16[8,176,128]{2,1,0:T(8,128)(2,1)}), bf16[8,176,128]{2,1,0:T(8,128)(2,1)S(1)}, u32[]{:S(2)}, u32[]{:S(2)}) async-start(bf16[8,176,128]{2,1,0:T(8,128)(2,1)} %broadcast_in_dim.25), calls=%async_computation | async-start | bytes 720896 | tf_op jit(solution)/shard_map/all_to_all | solution.py:33
  14.7 64.8 %all-gather.6.cloned.1.call-start = ((), (), s32[]{:S(2)}) async-start(), calls=%async_computation.13 | async-start | bytes 2973696 | tf_op jit(solution)/shard_map/all_gather | solution.py:70
  14.7 31.8 %collective-permute-start = (bf16[192,1408]{1,0:T(8,128)(2,1)}, bf16[192,1408]{1,0:T(8,128)(2,1)}, u32[]{:S(2)}, u32[]{:S(2)}) collective-permute-start(bf16[192,1408]{1,0:T(8,128)(2,1)} %bitcast.188), channel_id=1, source_target_pairs={{0,1},{1,0},{2,3},{3,2},{4,5},{5,4},{6,7},{7,6},{8,9},{9,8},{10,11... | collective-permute-start | bytes 1622024 | tf_op jit(solution)/shard_map/ppermute | solution.py:27
  19.5 25.4 %collective-permute-start.1 = (bf16[1408,192]{0,1:T(8,128)(2,1)}, bf16[1408,192]{0,1:T(8,128)(2,1)S(1)}, u32[]{:S(2)}, u32[]{:S(2)}) collective-permute-start(bf16[1408,192]{0,1:T(8,128)(2,1)} %bitcast.171), channel_id=1, source_target_pairs={{0,1},{1,0},{2,3},{3,2},{4,5},{5,4},{6,7},{7,6},{8,9},{9,8},{10,11... | collective-permute-start | bytes 1622024 | tf_op jit(solution)/shard_map/ppermute | solution.py:27
  23.1 21.8 %copy-start.10 = (bf16[1,1408,192]{1,2,0:T(8,128)(2,1)S(1)}, bf16[1,1408,192]{1,2,0:T(8,128)(2,1)}, u32[]{:S(2)}) copy-start(bf16[1,1408,192]{1,2,0:T(8,128)(2,1)} %param.14) | copy-start | bytes 1622020
  25.1 21.4 %copy-start.39 = (bf16[1,192,1408]{2,1,0:T(8,128)(2,1)S(1)}, bf16[1,192,1408]{2,1,0:T(8,128)(2,1)}, u32[]{:S(2)}) copy-start(bf16[1,192,1408]{2,1,0:T(8,128)(2,1)} %param.15) | copy-start | bytes 1622020
  44.9 3.2 %copy-start.41 = (bf16[1408,192]{0,1:T(8,128)(2,1)}, bf16[1408,192]{0,1:T(8,128)(2,1)S(1)}, u32[]{:S(2)}) copy-start(bf16[1408,192]{0,1:T(8,128)(2,1)S(1)} %collective-permute-done.1) | copy-start | bytes 1622020
  46.1 10.5 %copy-start.1 = (bf16[384,128]{1,0:T(8,128)(2,1)}, bf16[384,128]{1,0:T(8,128)(2,1)S(1)}, u32[]{:S(2)}) copy-start(bf16[384,128]{1,0:T(8,128)(2,1)S(1)} %get-tuple-element.18) | copy-start | bytes 294916
  49.3 12.5 %copy-start.29 = (bf16[1,128,176]{1,2,0:T(8,128)(2,1)S(1)}, bf16[1,128,176]{1,2,0:T(8,128)(2,1)}, u32[]{:S(2)}) copy-start(bf16[1,128,176]{1,2,0:T(8,128)(2,1)} %param.11) | copy-start | bytes 135172
  49.3 12.5 %all-to-all-start.1 = ((bf16[8,176,128]{2,1,0:T(8,128)(2,1)}), bf16[8,176,128]{2,1,0:T(8,128)(2,1)S(1)}, u32[]{:S(2)}, u32[]{:S(2)}) async-start(bf16[8,176,128]{2,1,0:T(8,128)(2,1)} %bitcast.21), calls=%async_computation.1 | async-start | bytes 720896 | tf_op jit(solution)/shard_map/all_to_all | solution.py:112
  62.6 18.3 %all-to-all-start.2 = ((bf16[8,176,128]{2,1,0:T(8,128)(2,1)}), bf16[8,176,128]{2,1,0:T(8,128)(2,1)S(1)}, u32[]{:S(2)}, u32[]{:S(2)}) async-start(bf16[8,176,128]{2,1,0:T(8,128)(2,1)} %broadcast_in_dim.26), calls=%async_computation.2 | async-start | bytes 720896 | tf_op jit(solution)/shard_map/all_to_all | solution.py:33
  81.3 3.6 %collective-permute-start.2 = (bf16[176,128]{1,0:T(8,128)(2,1)S(1)}, bf16[176,128]{1,0:T(8,128)(2,1)S(1)}, u32[]{:S(2)}, u32[]{:S(2)}) collective-permute-start(bf16[176,128]{1,0:T(8,128)(2,1)S(1)} %get-tuple-element.36), channel_id=1, source_target_pairs={{16,0},{32,16},{48,32},{64,48},{80,64},{96,80},{112,96},{128,112},... | collective-permute-start | bytes 135176 | tf_op jit(solution)/shard_map/ppermute | solution.py:124
  83.3 12.0 %collective-permute-start.3 = (bf16[176,128]{1,0:T(8,128)(2,1)S(1)}, bf16[176,128]{1,0:T(8,128)(2,1)S(1)}, u32[]{:S(2)}, u32[]{:S(2)}) collective-permute-start(bf16[176,128]{1,0:T(8,128)(2,1)S(1)} %get-tuple-element.37), channel_id=1, source_target_pairs={{256,240},{272,224},{288,208},{304,192},{320,176},{336,160},{352,1... | collective-permute-start | bytes 135176 | tf_op jit(solution)/shard_map/ppermute | solution.py:127
  97.5 11.8 %all-to-all-start.3 = ((bf16[8,176,128]{2,1,0:T(8,128)(2,1)}), bf16[8,176,128]{2,1,0:T(8,128)(2,1)S(1)}, u32[]{:S(2)}, u32[]{:S(2)}) async-start(bf16[8,176,128]{2,1,0:T(8,128)(2,1)} %broadcast_in_dim.27), calls=%async_computation.3 | async-start | bytes 720896 | tf_op jit(solution)/shard_map/all_to_all | solution.py:33
  103.4 13.9 %copy-start.5 = (bf16[128,1408]{1,0:T(8,128)(2,1)}, bf16[128,1408]{1,0:T(8,128)(2,1)S(1)}, u32[]{:S(2)}) copy-start(bf16[128,1408]{1,0:T(8,128)(2,1)S(1)} %fusion.27) | copy-start | bytes 1081348
  109.2 3.1 %copy-start.3 = (bf16[8,176,128]{2,1,0:T(8,128)(2,1)}, bf16[8,176,128]{2,1,0:T(8,128)(2,1)S(1)}, u32[]{:S(2)}) copy-start(bf16[8,176,128]{2,1,0:T(8,128)(2,1)S(1)} %all-to-all-done.3) | copy-start | bytes 1081348
  112.3 11.2 %copy-start.16 = (bf16[176,128]{1,0:T(8,128)(2,1)S(1)}, bf16[176,128]{1,0:T(8,128)(2,1)}, u32[]{:S(2)}) copy-start(bf16[176,128]{1,0:T(8,128)(2,1)} %copy-done.15) | copy-start | bytes 135172
  112.3 11.1 %all-to-all-start.4 = ((bf16[8,176,128]{2,1,0:T(8,128)(2,1)}), bf16[8,176,128]{2,1,0:T(8,128)(2,1)S(1)}, u32[]{:S(2)}, u32[]{:S(2)}) async-start(bf16[8,176,128]{2,1,0:T(8,128)(2,1)} %bitcast.178), calls=%async_computation.4 | async-start | bytes 720896 | tf_op jit(solution)/shard_map/all_to_all | solution.py:112
  119.4 37.3 %copy-start.20 = (f32[192,128]{1,0:T(8,128)}, f32[192,128]{1,0:T(8,128)S(1)}, u32[]{:S(2)}) copy-start(f32[192,128]{1,0:T(8,128)S(1)} %get-tuple-element.43) | copy-start | bytes 294916
  124.4 11.0 %all-to-all-start.5 = ((bf16[8,176,128]{2,1,0:T(8,128)(2,1)}), bf16[8,176,128]{2,1,0:T(8,128)(2,1)S(1)}, u32[]{:S(2)}, u32[]{:S(2)}) async-start(bf16[8,176,128]{2,1,0:T(8,128)(2,1)} %broadcast_in_dim.28), calls=%async_computation.5 | async-start | bytes 720896 | tf_op jit(solution)/shard_map/all_to_all | solution.py:33
  130.0 42.4 %copy-start.37 = (bf16[1,2,88,128]{3,2,1,0:T(8,128)(2,1)}, bf16[1,2,88,128]{3,2,1,0:T(8,128)(2,1)S(1)}, u32[]{:S(2)}) copy-start(bf16[1,2,88,128]{3,2,1,0:T(8,128)(2,1)S(1)} %get-tuple-element.31) | copy-start | bytes 135172
  135.3 28.6 %copy-start.25 = (f32[384,128]{1,0:T(8,128)S(1)}, f32[384,128]{1,0:T(8,128)}, u32[]{:S(2)}) copy-start(f32[384,128]{1,0:T(8,128)} %convolution_add_fusion.9) | copy-start | bytes 589828
  135.8 3.9 %collective-permute-start.4 = (bf16[176,128]{1,0:T(8,128)(2,1)S(1)}, bf16[176,128]{1,0:T(8,128)(2,1)S(1)}, u32[]{:S(2)}, u32[]{:S(2)}) collective-permute-start(bf16[176,128]{1,0:T(8,128)(2,1)S(1)} %get-tuple-element.34), channel_id=1, source_target_pairs={{16,0},{32,16},{48,32},{64,48},{80,64},{96,80},{112,96},{128,112},... | collective-permute-start | bytes 135176 | tf_op jit(solution)/shard_map/ppermute | solution.py:124
  137.7 12.0 %collective-permute-start.5 = (bf16[176,128]{1,0:T(8,128)(2,1)S(1)}, bf16[176,128]{1,0:T(8,128)(2,1)S(1)}, u32[]{:S(2)}, u32[]{:S(2)}) collective-permute-start(bf16[176,128]{1,0:T(8,128)(2,1)S(1)} %get-tuple-element.35), channel_id=1, source_target_pairs={{256,240},{272,224},{288,208},{304,192},{320,176},{336,160},{352,1... | collective-permute-start | bytes 135176 | tf_op jit(solution)/shard_map/ppermute | solution.py:127
  151.9 12.1 %all-to-all-start.6 = ((bf16[8,176,128]{2,1,0:T(8,128)(2,1)}), bf16[8,176,128]{2,1,0:T(8,128)(2,1)S(1)}, u32[]{:S(2)}, u32[]{:S(2)}) async-start(bf16[8,176,128]{2,1,0:T(8,128)(2,1)} %broadcast_in_dim.29), calls=%async_computation.6 | async-start | bytes 720896 | tf_op jit(solution)/shard_map/all_to_all | solution.py:33
  163.9 3.1 %copy-start.4 = (bf16[8,176,128]{2,1,0:T(8,128)(2,1)}, bf16[8,176,128]{2,1,0:T(8,128)(2,1)S(1)}, u32[]{:S(2)}) copy-start(bf16[8,176,128]{2,1,0:T(8,128)(2,1)S(1)} %all-to-all-done.6) | copy-start | bytes 1081348
  165.8 6.7 %copy-start.31 = (bf16[384,128]{1,0:T(8,128)(2,1)}, bf16[384,128]{1,0:T(8,128)(2,1)S(1)}, u32[]{:S(2)}) copy-start(bf16[384,128]{1,0:T(8,128)(2,1)S(1)} %fusion.17) | copy-start | bytes 294916
  167.0 12.0 %all-to-all-start.7 = ((bf16[8,176,128]{2,1,0:T(8,128)(2,1)}), bf16[8,176,128]{2,1,0:T(8,128)(2,1)}, u32[]{:S(2)}, u32[]{:S(2)}) async-start(bf16[8,176,128]{2,1,0:T(8,128)(2,1)} %bitcast.33), calls=%async_computation.7 | async-start | bytes 720896 | tf_op jit(solution)/shard_map/all_to_all | solution.py:112
  174.5 12.1 %copy-start.6 = (f32[384,128]{1,0:T(8,128)S(1)}, f32[384,128]{1,0:T(8,128)}, u32[]{:S(2)}) copy-start(f32[384,128]{1,0:T(8,128)} %fusion.57) | copy-start | bytes 589828
  181.6 11.0 %all-to-all-start.8 = ((bf16[8,176,128]{2,1,0:T(8,128)(2,1)}), bf16[8,176,128]{2,1,0:T(8,128)(2,1)S(1)}, u32[]{:S(2)}, u32[]{:S(2)}) async-start(bf16[8,176,128]{2,1,0:T(8,128)(2,1)} %broadcast_in_dim.30), calls=%async_computation.8 | async-start | bytes 720896 | tf_op jit(solution)/shard_map/all_to_all | solution.py:33
  188.3 7.9 %copy-start.7 = (f32[384,128]{1,0:T(8,128)S(1)}, f32[384,128]{1,0:T(8,128)}, u32[]{:S(2)}) copy-start(f32[384,128]{1,0:T(8,128)} %convolution_add_fusion.8) | copy-start | bytes 589828
  189.5 6.8 %copy-start.32 = (bf16[384,128]{1,0:T(8,128)(2,1)S(1)}, bf16[384,128]{1,0:T(8,128)(2,1)}, u32[]{:S(2)}) copy-start(bf16[384,128]{1,0:T(8,128)(2,1)} %copy-done.31) | copy-start | bytes 294916
  193.0 4.1 %collective-permute-start.6 = (bf16[176,128]{1,0:T(8,128)(2,1)S(1)}, bf16[176,128]{1,0:T(8,128)(2,1)S(1)}, u32[]{:S(2)}, u32[]{:S(2)}) collective-permute-start(bf16[176,128]{1,0:T(8,128)(2,1)S(1)} %get-tuple-element.32), channel_id=1, source_target_pairs={{16,0},{32,16},{48,32},{64,48},{80,64},{96,80},{112,96},{128,112},... | collective-permute-start | bytes 135176 | tf_op jit(solution)/shard_map/ppermute | solution.py:124
  195.0 12.0 %collective-permute-start.7 = (bf16[176,128]{1,0:T(8,128)(2,1)S(1)}, bf16[176,128]{1,0:T(8,128)(2,1)S(1)}, u32[]{:S(2)}, u32[]{:S(2)}) collective-permute-start(bf16[176,128]{1,0:T(8,128)(2,1)S(1)} %get-tuple-element.33), channel_id=1, source_target_pairs={{256,240},{272,224},{288,208},{304,192},{320,176},{336,160},{352,1... | collective-permute-start | bytes 135176 | tf_op jit(solution)/shard_map/ppermute | solution.py:127
  208.7 7.9 %copy-start = (f32[1408,128]{1,0:T(8,128)S(1)}, f32[1408,128]{1,0:T(8,128)}, u32[]{:S(2)}) copy-start(f32[1408,128]{1,0:T(8,128)} %convolution_add_fusion.3) | copy-start | bytes 2162692
  208.7 17.1 %all-to-all-start.9 = ((bf16[16,176,128]{2,1,0:T(8,128)(2,1)}), bf16[16,176,128]{2,1,0:T(8,128)(2,1)S(1)}, u32[]{:S(2)}, u32[]{:S(2)}) async-start(bf16[16,176,128]{2,1,0:T(8,128)(2,1)} %broadcast_in_dim.31), calls=%async_computation.9 | async-start | bytes 1441792 | tf_op jit(solution)/shard_map/all_to_all | solution.py:33
  214.4 50.6 %all-gather.4.cloned.1.call-start = ((), (), s32[]{:S(2)}) async-start(), calls=%async_computation.12 | async-start | bytes 2310144 | tf_op jit(solution)/shard_map/all_gather | solution.py:136
  229.6 8.1 %copy-start.35 = (bf16[1,2,88,128]{3,2,1,0:T(8,128)(2,1)S(1)}, bf16[1,2,88,128]{3,2,1,0:T(8,128)(2,1)}, u32[]{:S(2)}) copy-start(bf16[1,2,88,128]{3,2,1,0:T(8,128)(2,1)} %get-tuple-element.30) | copy-start | bytes 135172
  229.6 8.9 %copy-start.9 = (f32[384,128]{1,0:T(8,128)S(1)}, f32[384,128]{1,0:T(8,128)}, u32[]{:S(2)}) copy-start(f32[384,128]{1,0:T(8,128)} %convolution_add_fusion.7) | copy-start | bytes 589828
  229.6 14.9 %copy-start.19 = (bf16[176,128]{1,0:T(8,128)(2,1)S(1)}, bf16[176,128]{1,0:T(8,128)(2,1)}, u32[]{:S(2)}) copy-start(bf16[176,128]{1,0:T(8,128)(2,1)} %copy-done.18) | copy-start | bytes 135172
  230.8 13.6 %all-to-all-start.10 = ((bf16[8,176,128]{2,1,0:T(8,128)(2,1)}), bf16[8,176,128]{2,1,0:T(8,128)(2,1)S(1)}, u32[]{:S(2)}, u32[]{:S(2)}) async-start(bf16[8,176,128]{2,1,0:T(8,128)(2,1)} %bitcast.43), calls=%async_computation.10 | async-start | bytes 720896 | tf_op jit(solution)/shard_map/all_to_all | solution.py:112
  245.5 28.2 %all-to-all-start.11 = ((bf16[16,176,128]{2,1,0:T(8,128)(2,1)}), bf16[16,176,128]{2,1,0:T(8,128)(2,1)S(1)}, u32[]{:S(2)}, u32[]{:S(2)}) async-start(bf16[16,176,128]{2,1,0:T(8,128)(2,1)} %broadcast_in_dim.32), calls=%async_computation.11 | async-start | bytes 1441792 | tf_op jit(solution)/shard_map/all_to_all | solution.py:33
  250.4 16.9 %copy-start.21 = (f32[192,128]{1,0:T(8,128)S(1)}, f32[192,128]{1,0:T(8,128)}, u32[]{:S(2)}) copy-start(f32[192,128]{1,0:T(8,128)} %copy-done.20) | copy-start | bytes 294916
  250.4 16.9 %copy-start.27 = (f32[384,128]{1,0:T(8,128)S(1)}, f32[384,128]{1,0:T(8,128)}, u32[]{:S(2)}) copy-start(f32[384,128]{1,0:T(8,128)} %copy-done.26) | copy-start | bytes 589828
  269.6 2.9 %copy-start.33 = (bf16[192,128]{1,0:T(8,128)(2,1)S(1)}, bf16[192,128]{1,0:T(8,128)(2,1)}, u32[]{:S(2)}) copy-start(bf16[192,128]{1,0:T(8,128)(2,1)} %get-tuple-element.16) | copy-start | bytes 147460
  269.7 2.9 %copy-start.34 = (bf16[192,128]{1,0:T(8,128)(2,1)S(1)}, bf16[192,128]{1,0:T(8,128)(2,1)}, u32[]{:S(2)}) copy-start(bf16[192,128]{1,0:T(8,128)(2,1)} %broadcast_select_fusion) | copy-start | bytes 147460
  (21 other events, 32.6 us)
Sparse Core Ops, SparseCore 0:
  25.2 54.3 all-gather.5
  218.0 47.0 all-gather.3

commit v5 on v2

--- a/solution.py
+++ b/solution.py
@@ -61,8 +61,8 @@
     upstream, proj_own = tied(upstream, w_proj[0])
     proj_other = swap(proj_own)
 
-    up = jnp.concatenate([w_up[0], up_other], axis=1)
-    down = jnp.concatenate([w_down[0], down_other], axis=0)
+    (up,) = tied(jnp.concatenate([w_up[0], up_other], axis=1))
+    (down,) = tied(jnp.concatenate([w_down[0], down_other], axis=0))
     proj = jnp.concatenate(by_replica(proj_own, proj_other), axis=1).reshape(-1, width)
 
     places = jnp.arange(pool, dtype=jnp.int32)[:, None]
@@ -97,7 +97,6 @@
             seen_other = swap(seen)
             spread = spread.astype(bf16)
             spread_other = swap(spread[units:])
-            terms, seen_other, spread_other = tied(terms, seen_other, spread_other)
         mixed_chunk = (
             jnp.sum(terms.astype(f32), axis=0) + chunk.astype(f32)
         ).astype(bf16)

time: 251 us -> 268 us (1.068)
  the two profiles are of different devices: /device:TPU:96 before, /device:TPU:98 now
where the time goes in v5:
time: 268 us; the launch traced here: 264 us
  starting transfers between devices  106 us (40%)
  waiting for transfers between devices  76.3 us (28%)
  matrix products  55.2 us (21%)
  local copies, waits for them, and re-layouts  13.2 us (5%)
  other arithmetic  11.9 us (4%)
    dot_general x38, matrix products, dot(): lax.dot_general(a, b, (((ca,), (cb,)), ((), ())), preferred_element_type=...  55.2 us
    all_to_all x8, starting transfers between devices, gather(): return lax.all_to_all(spread, axes, 0, 0)  44 us
    ppermute x8, waiting for transfers between devices, swap(): return lax.ppermute(x, 'replica', [(0, 1), (1, 0)])  36.9 us
    ppermute x8, starting transfers between devices, swap(): return lax.ppermute(x, 'replica', [(0, 1), (1, 0)])  32.2 us
    ppermute x3, waiting for transfers between devices, body(): lax.ppermute(input_grad[1], 'section', [(i, sections - 1 - i) for i in ra...  22.1 us
    all_to_all x4, starting transfers between devices, body(): lax.all_to_all(partial.reshape(parts, chunk_rows, rows), 'tensor', 0, 0)  20.5 us
    all_to_all x8, waiting for transfers between devices, gather(): return lax.all_to_all(spread, axes, 0, 0)  11.5 us
    broadcast_in_dim x8, local copies, waits for them, and re-layouts, gather(): spread = jnp.broadcast_to(chunk[None], (count, *chunk.shape))  7.33 us
  transfers between devices with their start and end apart: 26, of which 15 were waited for; matrix products, arithmetic and copies ran while one was open for 18% of the time, Pallas kernels for 0%

profile of v5, /device:TPU:98, one launch (start us, length us, event | category | flops | bytes accessed | tf_op | source)
XLA Modules:
  0.0 264.3 jit_solution(10982202045677285211)
XLA Ops:
  2.3 5.8 %all-to-all-start = ((bf16[8,176,128]{2,1,0:T(8,128)(2,1)}), bf16[8,176,128]{2,1,0:T(8,128)(2,1)S(1)}, u32[]{:S(2)}, u32[]{:S(2)}) async-start(bf16[8,176,128]{2,1,0:T(8,128)(2,1)} %broadcast_in_dim.24), calls=%async_computation | async-start | bytes 720896 | tf_op jit(solution)/shard_map/all_to_all | solution.py:33
  8.2 4.8 %collective-permute-start.1 = (bf16[1408,192]{0,1:T(8,128)(2,1)S(1)}, bf16[1408,192]{0,1:T(8,128)(2,1)S(1)}, u32[]{:S(2)}, u32[]{:S(2)}) collective-permute-start(bf16[1408,192]{0,1:T(8,128)(2,1)S(1)} %bitcast.132), channel_id=1, source_target_pairs={{0,1},{1,0},{2,3},{3,2},{4,5},{5,4},{6,7},{7,6},{8,9},{9,8},{10,11... | collective-permute-start | bytes 1622024 | tf_op jit(solution)/shard_map/ppermute | solution.py:27
  13.0 2.5 collective-permute-start.2
  16.6 10.6 %collective-permute-done.1 = bf16[1408,192]{0,1:T(8,128)(2,1)S(1)} collective-permute-done((bf16[1408,192]{0,1:T(8,128)(2,1)S(1)}, bf16[1408,192]{0,1:T(8,128)(2,1)S(1)}, u32[]{:S(2)}, u32[]{:S(2)}) %collective-permute-start.1) | collective-permute-done | bytes 540704 | tf_op jit(solution)/shard_map/ppermute | solution.py:27
  27.3 11.1 %collective-permute-done.2 = bf16[192,1408]{1,0:T(8,128)(2,1)} collective-permute-done((bf16[192,1408]{1,0:T(8,128)(2,1)S(1)}, bf16[192,1408]{1,0:T(8,128)(2,1)}, u32[]{:S(2)}, u32[]{:S(2)}) %collective-permute-start.2) | collective-permute-done | bytes 540704 | tf_op jit(solution)/shard_map/ppermute | solution.py:27
  39.6 2.2 subtract_convert_fusion
  43.8 5.3 %all-to-all-start.1 = ((bf16[8,176,128]{2,1,0:T(8,128)(2,1)}), bf16[8,176,128]{2,1,0:T(8,128)(2,1)S(1)}, u32[]{:S(2)}, u32[]{:S(2)}) async-start(bf16[8,176,128]{2,1,0:T(8,128)(2,1)} %bitcast.17), calls=%async_computation.1 | async-start | bytes 720896 | tf_op jit(solution)/shard_map/all_to_all | solution.py:91
  49.8 3.9 %collective-permute-start = (bf16[2,88,1408]{2,1,0:T(8,128)(2,1)S(1)}, bf16[2,88,1408]{2,1,0:T(8,128)(2,1)}, u32[]{:S(2)}, u32[]{:S(2)}) collective-permute-start(bf16[2,88,1408]{2,1,0:T(8,128)(2,1)S(1)} %bitcast.136), channel_id=1, source_target_pairs={{0,1},{1,0},{2,3},{3,2},{4,5},{5,4},{6,7},{7,6},{8,9},{9,8},{10,11... | collective-permute-start | bytes 1486856 | tf_op jit(solution)/shard_map/ppermute | solution.py:27
  56.4 5.4 %all-to-all-start.2 = ((bf16[8,176,128]{2,1,0:T(8,128)(2,1)}), bf16[8,176,128]{2,1,0:T(8,128)(2,1)}, u32[]{:S(2)}, u32[]{:S(2)}) async-start(bf16[8,176,128]{2,1,0:T(8,128)(2,1)} %broadcast_in_dim.25), calls=%async_computation.2 | async-start | bytes 720896 | tf_op jit(solution)/shard_map/all_to_all | solution.py:33
  61.8 7.7 %collective-permute-done = bf16[2,88,1408]{2,1,0:T(8,128)(2,1)} collective-permute-done((bf16[2,88,1408]{2,1,0:T(8,128)(2,1)S(1)}, bf16[2,88,1408]{2,1,0:T(8,128)(2,1)}, u32[]{:S(2)}, u32[]{:S(2)}) %collective-permute-start) | collective-permute-done | bytes 495648 | tf_op jit(solution)/shard_map/ppermute | solution.py:27
  72.2 1.9 collective-permute-start.3
  76.3 3.3 %collective-permute-start.5 = (bf16[128,1408]{1,0:T(8,128)(2,1)}, bf16[128,1408]{1,0:T(8,128)(2,1)}, u32[]{:S(2)}, u32[]{:S(2)}) collective-permute-start(bf16[128,1408]{1,0:T(8,128)(2,1)} %bitcast.15), channel_id=1, source_target_pairs={{0,1},{1,0},{2,3},{3,2},{4,5},{5,4},{6,7},{7,6},{8,9},{9,8},{10,11... | collective-permute-start | bytes 1081352 | tf_op jit(solution)/shard_map/ppermute | solution.py:27
  79.6 7.7 %collective-permute-done.4 = bf16[176,128]{1,0:T(8,128)(2,1)S(1)} collective-permute-done((bf16[176,128]{1,0:T(8,128)(2,1)S(1)}, bf16[176,128]{1,0:T(8,128)(2,1)S(1)}, u32[]{:S(2)}, u32[]{:S(2)}) %collective-permute-start.4) | collective-permute-done | bytes 45088 | tf_op jit(solution)/shard_map/ppermute | solution.py:110
  89.5 5.2 %all-to-all-start.3 = ((bf16[8,176,128]{2,1,0:T(8,128)(2,1)}), bf16[8,176,128]{2,1,0:T(8,128)(2,1)}, u32[]{:S(2)}, u32[]{:S(2)}) async-start(bf16[8,176,128]{2,1,0:T(8,128)(2,1)} %broadcast_in_dim.26), calls=%async_computation.3 | async-start | bytes 720896 | tf_op jit(solution)/shard_map/all_to_all | solution.py:33
  97.5 3.7 %all-to-all-done.3 = bf16[8,176,128]{2,1,0:T(8,128)(2,1)} async-done(((bf16[8,176,128]{2,1,0:T(8,128)(2,1)}), bf16[8,176,128]{2,1,0:T(8,128)(2,1)}, u32[]{:S(2)}, u32[]{:S(2)}) %all-to-all-start.3) | async-done | bytes 360480 | tf_op jit(solution)/shard_map/all_to_all | solution.py:33
  104.6 5.6 %all-to-all-start.4 = ((bf16[8,176,128]{2,1,0:T(8,128)(2,1)}), bf16[8,176,128]{2,1,0:T(8,128)(2,1)}, u32[]{:S(2)}, u32[]{:S(2)}) async-start(bf16[8,176,128]{2,1,0:T(8,128)(2,1)} %bitcast.131), calls=%async_computation.4 | async-start | bytes 720896 | tf_op jit(solution)/shard_map/all_to_all | solution.py:91
  113.0 3.2 %all-to-all-done.4 = bf16[8,176,128]{2,1,0:T(8,128)(2,1)} async-done(((bf16[8,176,128]{2,1,0:T(8,128)(2,1)}), bf16[8,176,128]{2,1,0:T(8,128)(2,1)}, u32[]{:S(2)}, u32[]{:S(2)}) %all-to-all-start.4) | async-done | bytes 360480 | tf_op jit(solution)/shard_map/all_to_all | solution.py:91
  118.8 5.5 %all-to-all-start.5 = ((bf16[8,176,128]{2,1,0:T(8,128)(2,1)}), bf16[8,176,128]{2,1,0:T(8,128)(2,1)}, u32[]{:S(2)}, u32[]{:S(2)}) async-start(bf16[8,176,128]{2,1,0:T(8,128)(2,1)} %broadcast_in_dim.27), calls=%async_computation.5 | async-start | bytes 720896 | tf_op jit(solution)/shard_map/all_to_all | solution.py:33
  127.2 2.9 %all-to-all-done.5 = bf16[8,176,128]{2,1,0:T(8,128)(2,1)} async-done(((bf16[8,176,128]{2,1,0:T(8,128)(2,1)}), bf16[8,176,128]{2,1,0:T(8,128)(2,1)}, u32[]{:S(2)}, u32[]{:S(2)}) %all-to-all-start.5) | async-done | bytes 360480 | tf_op jit(solution)/shard_map/all_to_all | solution.py:33
  131.6 1.9 collective-permute-start.6
  135.4 10.0 %collective-permute-done.7 = bf16[176,128]{1,0:T(8,128)(2,1)S(1)} collective-permute-done((bf16[176,128]{1,0:T(8,128)(2,1)S(1)}, bf16[176,128]{1,0:T(8,128)(2,1)S(1)}, u32[]{:S(2)}, u32[]{:S(2)}) %collective-permute-start.7) | collective-permute-done | bytes 45088 | tf_op jit(solution)/shard_map/ppermute | solution.py:110
  147.7 4.9 %all-to-all-start.6 = ((bf16[8,176,128]{2,1,0:T(8,128)(2,1)}), bf16[8,176,128]{2,1,0:T(8,128)(2,1)S(1)}, u32[]{:S(2)}, u32[]{:S(2)}) async-start(bf16[8,176,128]{2,1,0:T(8,128)(2,1)} %broadcast_in_dim.28), calls=%async_computation.6 | async-start | bytes 720896 | tf_op jit(solution)/shard_map/all_to_all | solution.py:33
  153.4 4.4 %collective-permute-start.8 = (bf16[384,128]{1,0:T(8,128)(2,1)S(1)}, bf16[384,128]{1,0:T(8,128)(2,1)}, u32[]{:S(2)}, u32[]{:S(2)}) collective-permute-start(bf16[384,128]{1,0:T(8,128)(2,1)S(1)} %pad_maximum_fusion.3), channel_id=1, source_target_pairs={{0,1},{1,0},{2,3},{3,2},{4,5},{5,4},{6,7},{7,6},{8,9},{9,8},{10,11... | collective-permute-start | bytes 294920 | tf_op jit(solution)/shard_map/ppermute | solution.py:27
  159.6 3.1 %collective-permute-done.8 = bf16[384,128]{1,0:T(8,128)(2,1)} collective-permute-done((bf16[384,128]{1,0:T(8,128)(2,1)S(1)}, bf16[384,128]{1,0:T(8,128)(2,1)}, u32[]{:S(2)}, u32[]{:S(2)}) %collective-permute-start.8) | collective-permute-done | bytes 98336 | tf_op jit(solution)/shard_map/ppermute | solution.py:27
  166.0 4.9 %all-to-all-start.7 = ((bf16[8,176,128]{2,1,0:T(8,128)(2,1)}), bf16[8,176,128]{2,1,0:T(8,128)(2,1)}, u32[]{:S(2)}, u32[]{:S(2)}) async-start(bf16[8,176,128]{2,1,0:T(8,128)(2,1)} %bitcast.130), calls=%async_computation.7 | async-start | bytes 720896 | tf_op jit(solution)/shard_map/all_to_all | solution.py:91
  170.8 2.2 fusion.47
  173.1 2.1 convolution_add_fusion.2
  175.2 2.3 all-to-all-done.7
  180.2 5.4 %all-to-all-start.8 = ((bf16[8,176,128]{2,1,0:T(8,128)(2,1)}), bf16[8,176,128]{2,1,0:T(8,128)(2,1)}, u32[]{:S(2)}, u32[]{:S(2)}) async-start(bf16[8,176,128]{2,1,0:T(8,128)(2,1)} %broadcast_in_dim.30), calls=%async_computation.8 | async-start | bytes 720896 | tf_op jit(solution)/shard_map/all_to_all | solution.py:33
  185.5 1.8 convolution_add_fusion.7
  187.4 2.4 convolution_add_fusion.4
  192.9 1.9 collective-permute-start.9
  196.1 2.0 fusion.2
  198.1 4.2 %collective-permute-start.11 = (bf16[1408,128]{0,1:T(8,128)(2,1)}, bf16[1408,128]{0,1:T(8,128)(2,1)}, u32[]{:S(2)}, u32[]{:S(2)}) collective-permute-start(bf16[1408,128]{0,1:T(8,128)(2,1)} %fusion.2), channel_id=1, source_target_pairs={{0,1},{1,0},{2,3},{3,2},{4,5},{5,4},{6,7},{7,6},{8,9},{9,8},{10,11... | collective-permute-start | bytes 1081352 | tf_op jit(solution)/shard_map/ppermute | solution.py:27
  202.4 4.4 %collective-permute-done.10 = bf16[176,128]{1,0:T(8,128)(2,1)S(1)} collective-permute-done((bf16[176,128]{1,0:T(8,128)(2,1)S(1)}, bf16[176,128]{1,0:T(8,128)(2,1)S(1)}, u32[]{:S(2)}, u32[]{:S(2)}) %collective-permute-start.10) | collective-permute-done | bytes 45088 | tf_op jit(solution)/shard_map/ppermute | solution.py:110
  209.0 5.6 %all-to-all-start.9 = ((bf16[8,176,128]{2,1,0:T(8,128)(2,1)}), bf16[8,176,128]{2,1,0:T(8,128)(2,1)}, u32[]{:S(2)}, u32[]{:S(2)}) async-start(bf16[8,176,128]{2,1,0:T(8,128)(2,1)} %broadcast_in_dim.31), calls=%async_computation.9 | async-start | bytes 720896 | tf_op jit(solution)/shard_map/all_to_all | solution.py:33
  214.6 1.8 convolution_add_fusion.6
  216.4 2.3 convolution_add_fusion.1
  218.7 3.2 %all-to-all-done.9 = bf16[8,176,128]{2,1,0:T(8,128)(2,1)} async-done(((bf16[8,176,128]{2,1,0:T(8,128)(2,1)}), bf16[8,176,128]{2,1,0:T(8,128)(2,1)}, u32[]{:S(2)}, u32[]{:S(2)}) %all-to-all-start.9) | async-done | bytes 360480 | tf_op jit(solution)/shard_map/all_to_all | solution.py:33
  224.6 4.8 %all-to-all-start.10 = ((bf16[8,176,128]{2,1,0:T(8,128)(2,1)}), bf16[8,176,128]{2,1,0:T(8,128)(2,1)S(1)}, u32[]{:S(2)}, u32[]{:S(2)}) async-start(bf16[8,176,128]{2,1,0:T(8,128)(2,1)} %bitcast.34), calls=%async_computation.10 | async-start | bytes 720896 | tf_op jit(solution)/shard_map/all_to_all | solution.py:91
  230.1 2.0 fusion.3
  232.1 4.2 %collective-permute-start.13 = (bf16[1408,128]{0,1:T(8,128)(2,1)}, bf16[1408,128]{0,1:T(8,128)(2,1)S(1)}, u32[]{:S(2)}, u32[]{:S(2)}) collective-permute-start(bf16[1408,128]{0,1:T(8,128)(2,1)} %fusion.3), channel_id=1, source_target_pairs={{0,1},{1,0},{2,3},{3,2},{4,5},{5,4},{6,7},{7,6},{8,9},{9,8},{10,11... | collective-permute-start | bytes 1081352 | tf_op jit(solution)/shard_map/ppermute | solution.py:27
  237.5 6.2 %all-to-all-start.11 = ((bf16[16,176,128]{2,1,0:T(8,128)(2,1)}), bf16[16,176,128]{2,1,0:T(8,128)(2,1)S(1)}, u32[]{:S(2)}, u32[]{:S(2)}) async-start(bf16[16,176,128]{2,1,0:T(8,128)(2,1)} %broadcast_in_dim.32), calls=%async_computation.11 | async-start | bytes 1441792 | tf_op jit(solution)/shard_map/all_to_all | solution.py:33
  243.9 4.9 %collective-permute-start.12 = (bf16[192,128]{1,0:T(8,128)(2,1)S(1)}, bf16[192,128]{1,0:T(8,128)(2,1)S(1)}, u32[]{:S(2)}, u32[]{:S(2)}) collective-permute-start(bf16[192,128]{1,0:T(8,128)(2,1)S(1)} %get-tuple-element.50), channel_id=1, source_target_pairs={{0,1},{1,0},{2,3},{3,2},{4,5},{5,4},{6,7},{7,6},{8,9},{9,8},{10,11... | collective-permute-start | bytes 147464 | tf_op jit(solution)/shard_map/ppermute | solution.py:27
  251.3 4.3 %collective-permute-done.12 = bf16[192,128]{1,0:T(8,128)(2,1)S(1)} collective-permute-done((bf16[192,128]{1,0:T(8,128)(2,1)S(1)}, bf16[192,128]{1,0:T(8,128)(2,1)S(1)}, u32[]{:S(2)}, u32[]{:S(2)}) %collective-permute-start.12) | collective-permute-done | bytes 49184 | tf_op jit(solution)/shard_map/ppermute | solution.py:27
  255.6 2.2 fusion.1
  257.9 2.1 fusion
  262.0 2.3 convolution_convert_fusion.2
  (130 shorter events, 60.7 us)
Async XLA Ops:
  0.6 7.5 %copy-start.10 = (bf16[1,1408,192]{1,2,0:T(8,128)(2,1)S(1)}, bf16[1,1408,192]{1,2,0:T(8,128)(2,1)}, u32[]{:S(2)}) copy-start(bf16[1,1408,192]{1,2,0:T(8,128)(2,1)} %param.14) | copy-start | bytes 1622020
  0.6 12.3 %copy-start.11 = (bf16[1,192,1408]{2,1,0:T(8,128)(2,1)S(1)}, bf16[1,192,1408]{2,1,0:T(8,128)(2,1)}, u32[]{:S(2)}) copy-start(bf16[1,192,1408]{2,1,0:T(8,128)(2,1)} %param.15) | copy-start | bytes 1622020
  0.7 14.9 %copy-start.23 = (s32[1,4,128]{2,1,0:T(4,128)S(1)}, s32[1,4,128]{2,1,0:T(4,128)}, u32[]{:S(2)}) copy-start(s32[1,4,128]{2,1,0:T(4,128)} %param.10) | copy-start | bytes 6148
  2.3 14.3 %all-to-all-start = ((bf16[8,176,128]{2,1,0:T(8,128)(2,1)}), bf16[8,176,128]{2,1,0:T(8,128)(2,1)S(1)}, u32[]{:S(2)}, u32[]{:S(2)}) async-start(bf16[8,176,128]{2,1,0:T(8,128)(2,1)} %broadcast_in_dim.24), calls=%async_computation | async-start | bytes 720896 | tf_op jit(solution)/shard_map/all_to_all | solution.py:33
  8.2 19.1 %collective-permute-start.1 = (bf16[1408,192]{0,1:T(8,128)(2,1)S(1)}, bf16[1408,192]{0,1:T(8,128)(2,1)S(1)}, u32[]{:S(2)}, u32[]{:S(2)}) collective-permute-start(bf16[1408,192]{0,1:T(8,128)(2,1)S(1)} %bitcast.132), channel_id=1, source_target_pairs={{0,1},{1,0},{2,3},{3,2},{4,5},{5,4},{6,7},{7,6},{8,9},{9,8},{10,11... | collective-permute-start | bytes 1622024 | tf_op jit(solution)/shard_map/ppermute | solution.py:27
  13.0 25.5 %collective-permute-start.2 = (bf16[192,1408]{1,0:T(8,128)(2,1)S(1)}, bf16[192,1408]{1,0:T(8,128)(2,1)}, u32[]{:S(2)}, u32[]{:S(2)}) collective-permute-start(bf16[192,1408]{1,0:T(8,128)(2,1)S(1)} %bitcast.134), channel_id=1, source_target_pairs={{0,1},{1,0},{2,3},{3,2},{4,5},{5,4},{6,7},{7,6},{8,9},{9,8},{10,11... | collective-permute-start | bytes 1622024 | tf_op jit(solution)/shard_map/ppermute | solution.py:27
  16.6 21.8 %copy-start.12 = (bf16[1,192,1408]{2,1,0:T(8,128)(2,1)S(1)}, bf16[1,192,1408]{2,1,0:T(8,128)(2,1)}, u32[]{:S(2)}) copy-start(bf16[1,192,1408]{2,1,0:T(8,128)(2,1)} %param.15) | copy-start | bytes 1622020
  41.8 0.8 copy-start.3
  41.8 0.8 copy-start.4
  42.6 1.2 copy-start.6
  42.6 7.2 %copy-start.13 = (bf16[1,2,88,1408]{3,2,1,0:T(8,128)(2,1)S(1)}, bf16[1,2,88,1408]{3,2,1,0:T(8,128)(2,1)}, u32[]{:S(2)}) copy-start(bf16[1,2,88,1408]{3,2,1,0:T(8,128)(2,1)} %param.13) | copy-start | bytes 1486852
  43.8 11.8 %copy-start.18 = (bf16[1,128,176]{1,2,0:T(8,128)(2,1)S(1)}, bf16[1,128,176]{1,2,0:T(8,128)(2,1)}, u32[]{:S(2)}) copy-start(bf16[1,128,176]{1,2,0:T(8,128)(2,1)} %param.11) | copy-start | bytes 135172
  43.8 11.7 %all-to-all-start.1 = ((bf16[8,176,128]{2,1,0:T(8,128)(2,1)}), bf16[8,176,128]{2,1,0:T(8,128)(2,1)S(1)}, u32[]{:S(2)}, u32[]{:S(2)}) async-start(bf16[8,176,128]{2,1,0:T(8,128)(2,1)} %bitcast.17), calls=%async_computation.1 | async-start | bytes 720896 | tf_op jit(solution)/shard_map/all_to_all | solution.py:91
  49.8 19.7 %collective-permute-start = (bf16[2,88,1408]{2,1,0:T(8,128)(2,1)S(1)}, bf16[2,88,1408]{2,1,0:T(8,128)(2,1)}, u32[]{:S(2)}, u32[]{:S(2)}) collective-permute-start(bf16[2,88,1408]{2,1,0:T(8,128)(2,1)S(1)} %bitcast.136), channel_id=1, source_target_pairs={{0,1},{1,0},{2,3},{3,2},{4,5},{5,4},{6,7},{7,6},{8,9},{9,8},{10,11... | collective-permute-start | bytes 1486856 | tf_op jit(solution)/shard_map/ppermute | solution.py:27
  56.4 14.3 %all-to-all-start.2 = ((bf16[8,176,128]{2,1,0:T(8,128)(2,1)}), bf16[8,176,128]{2,1,0:T(8,128)(2,1)}, u32[]{:S(2)}, u32[]{:S(2)}) async-start(bf16[8,176,128]{2,1,0:T(8,128)(2,1)} %broadcast_in_dim.25), calls=%async_computation.2 | async-start | bytes 720896 | tf_op jit(solution)/shard_map/all_to_all | solution.py:33
  70.7 4.7 %copy-start.5 = (bf16[384,128]{1,0:T(8,128)(2,1)S(1)}, bf16[384,128]{1,0:T(8,128)(2,1)}, u32[]{:S(2)}) copy-start(bf16[384,128]{1,0:T(8,128)(2,1)} %copy-done.4) | copy-start | bytes 294916
  72.2 7.4 %collective-permute-start.3 = (bf16[176,128]{1,0:T(8,128)(2,1)S(1)}, bf16[176,128]{1,0:T(8,128)(2,1)S(1)}, u32[]{:S(2)}, u32[]{:S(2)}) collective-permute-start(bf16[176,128]{1,0:T(8,128)(2,1)S(1)} %get-tuple-element.59), channel_id=1, source_target_pairs={{16,0},{32,16},{48,32},{64,48},{80,64},{96,80},{112,96},{128,112},... | collective-permute-start | bytes 135176 | tf_op jit(solution)/shard_map/ppermute | solution.py:107
  74.1 13.2 %collective-permute-start.4 = (bf16[176,128]{1,0:T(8,128)(2,1)S(1)}, bf16[176,128]{1,0:T(8,128)(2,1)S(1)}, u32[]{:S(2)}, u32[]{:S(2)}) collective-permute-start(bf16[176,128]{1,0:T(8,128)(2,1)S(1)} %get-tuple-element.60), channel_id=1, source_target_pairs={{256,240},{272,224},{288,208},{304,192},{320,176},{336,160},{352,1... | collective-permute-start | bytes 135176 | tf_op jit(solution)/shard_map/ppermute | solution.py:110
  76.3 25.0 %collective-permute-start.5 = (bf16[128,1408]{1,0:T(8,128)(2,1)}, bf16[128,1408]{1,0:T(8,128)(2,1)}, u32[]{:S(2)}, u32[]{:S(2)}) collective-permute-start(bf16[128,1408]{1,0:T(8,128)(2,1)} %bitcast.15), channel_id=1, source_target_pairs={{0,1},{1,0},{2,3},{3,2},{4,5},{5,4},{6,7},{7,6},{8,9},{9,8},{10,11... | collective-permute-start | bytes 1081352 | tf_op jit(solution)/shard_map/ppermute | solution.py:27
  88.1 0.6 copy-start.17
  89.5 11.8 %all-to-all-start.3 = ((bf16[8,176,128]{2,1,0:T(8,128)(2,1)}), bf16[8,176,128]{2,1,0:T(8,128)(2,1)}, u32[]{:S(2)}, u32[]{:S(2)}) async-start(bf16[8,176,128]{2,1,0:T(8,128)(2,1)} %broadcast_in_dim.26), calls=%async_computation.3 | async-start | bytes 720896 | tf_op jit(solution)/shard_map/all_to_all | solution.py:33
  102.8 0.6 copy-start.7
  104.6 11.5 %all-to-all-start.4 = ((bf16[8,176,128]{2,1,0:T(8,128)(2,1)}), bf16[8,176,128]{2,1,0:T(8,128)(2,1)}, u32[]{:S(2)}, u32[]{:S(2)}) async-start(bf16[8,176,128]{2,1,0:T(8,128)(2,1)} %bitcast.131), calls=%async_computation.4 | async-start | bytes 720896 | tf_op jit(solution)/shard_map/all_to_all | solution.py:91
  118.8 11.3 %all-to-all-start.5 = ((bf16[8,176,128]{2,1,0:T(8,128)(2,1)}), bf16[8,176,128]{2,1,0:T(8,128)(2,1)}, u32[]{:S(2)}, u32[]{:S(2)}) async-start(bf16[8,176,128]{2,1,0:T(8,128)(2,1)} %broadcast_in_dim.27), calls=%async_computation.5 | async-start | bytes 720896 | tf_op jit(solution)/shard_map/all_to_all | solution.py:33
  127.2 7.6 %copy-start.20 = (bf16[384,128]{1,0:T(8,128)(2,1)S(1)}, bf16[384,128]{1,0:T(8,128)(2,1)}, u32[]{:S(2)}) copy-start(bf16[384,128]{1,0:T(8,128)(2,1)} %get-tuple-element.46) | copy-start | bytes 294916
  131.6 3.9 %collective-permute-start.6 = (bf16[176,128]{1,0:T(8,128)(2,1)S(1)}, bf16[176,128]{1,0:T(8,128)(2,1)S(1)}, u32[]{:S(2)}, u32[]{:S(2)}) collective-permute-start(bf16[176,128]{1,0:T(8,128)(2,1)S(1)} %get-tuple-element.57), channel_id=1, source_target_pairs={{16,0},{32,16},{48,32},{64,48},{80,64},{96,80},{112,96},{128,112},... | collective-permute-start | bytes 135176 | tf_op jit(solution)/shard_map/ppermute | solution.py:107
  133.5 12.0 %collective-permute-start.7 = (bf16[176,128]{1,0:T(8,128)(2,1)S(1)}, bf16[176,128]{1,0:T(8,128)(2,1)S(1)}, u32[]{:S(2)}, u32[]{:S(2)}) collective-permute-start(bf16[176,128]{1,0:T(8,128)(2,1)S(1)} %get-tuple-element.58), channel_id=1, source_target_pairs={{256,240},{272,224},{288,208},{304,192},{320,176},{336,160},{352,1... | collective-permute-start | bytes 135176 | tf_op jit(solution)/shard_map/ppermute | solution.py:110
  147.7 15.1 %all-to-all-start.6 = ((bf16[8,176,128]{2,1,0:T(8,128)(2,1)}), bf16[8,176,128]{2,1,0:T(8,128)(2,1)S(1)}, u32[]{:S(2)}, u32[]{:S(2)}) async-start(bf16[8,176,128]{2,1,0:T(8,128)(2,1)} %broadcast_in_dim.28), calls=%async_computation.6 | async-start | bytes 720896 | tf_op jit(solution)/shard_map/all_to_all | solution.py:33
  153.4 9.3 %collective-permute-start.8 = (bf16[384,128]{1,0:T(8,128)(2,1)S(1)}, bf16[384,128]{1,0:T(8,128)(2,1)}, u32[]{:S(2)}, u32[]{:S(2)}) collective-permute-start(bf16[384,128]{1,0:T(8,128)(2,1)S(1)} %pad_maximum_fusion.3), channel_id=1, source_target_pairs={{0,1},{1,0},{2,3},{3,2},{4,5},{5,4},{6,7},{7,6},{8,9},{9,8},{10,11... | collective-permute-start | bytes 294920 | tf_op jit(solution)/shard_map/ppermute | solution.py:27
  164.1 0.6 copy-start.8
  166.0 11.6 %all-to-all-start.7 = ((bf16[8,176,128]{2,1,0:T(8,128)(2,1)}), bf16[8,176,128]{2,1,0:T(8,128)(2,1)}, u32[]{:S(2)}, u32[]{:S(2)}) async-start(bf16[8,176,128]{2,1,0:T(8,128)(2,1)} %bitcast.130), calls=%async_computation.7 | async-start | bytes 720896 | tf_op jit(solution)/shard_map/all_to_all | solution.py:91
  170.8 2.2 copy-start
  180.2 11.2 %all-to-all-start.8 = ((bf16[8,176,128]{2,1,0:T(8,128)(2,1)}), bf16[8,176,128]{2,1,0:T(8,128)(2,1)}, u32[]{:S(2)}, u32[]{:S(2)}) async-start(bf16[8,176,128]{2,1,0:T(8,128)(2,1)} %broadcast_in_dim.30), calls=%async_computation.8 | async-start | bytes 720896 | tf_op jit(solution)/shard_map/all_to_all | solution.py:33
  191.4 4.7 %copy-start.1 = (f32[1408,128]{0,1:T(8,128)S(1)}, f32[1408,128]{0,1:T(8,128)}, u32[]{:S(2)}) copy-start(f32[1408,128]{0,1:T(8,128)} %convolution_add_fusion.4) | copy-start | bytes 2162692
  192.9 9.5 %collective-permute-start.9 = (bf16[176,128]{1,0:T(8,128)(2,1)S(1)}, bf16[176,128]{1,0:T(8,128)(2,1)S(1)}, u32[]{:S(2)}, u32[]{:S(2)}) collective-permute-start(bf16[176,128]{1,0:T(8,128)(2,1)S(1)} %get-tuple-element.55), channel_id=1, source_target_pairs={{16,0},{32,16},{48,32},{64,48},{80,64},{96,80},{112,96},{128,112},... | collective-permute-start | bytes 135176 | tf_op jit(solution)/shard_map/ppermute | solution.py:107
  194.8 12.0 %collective-permute-start.10 = (bf16[176,128]{1,0:T(8,128)(2,1)S(1)}, bf16[176,128]{1,0:T(8,128)(2,1)S(1)}, u32[]{:S(2)}, u32[]{:S(2)}) collective-permute-start(bf16[176,128]{1,0:T(8,128)(2,1)S(1)} %get-tuple-element.56), channel_id=1, source_target_pairs={{256,240},{272,224},{288,208},{304,192},{320,176},{336,160},{352,1... | collective-permute-start | bytes 135176 | tf_op jit(solution)/shard_map/ppermute | solution.py:110
  198.1 23.8 %collective-permute-start.11 = (bf16[1408,128]{0,1:T(8,128)(2,1)}, bf16[1408,128]{0,1:T(8,128)(2,1)}, u32[]{:S(2)}, u32[]{:S(2)}) collective-permute-start(bf16[1408,128]{0,1:T(8,128)(2,1)} %fusion.2), channel_id=1, source_target_pairs={{0,1},{1,0},{2,3},{3,2},{4,5},{5,4},{6,7},{7,6},{8,9},{9,8},{10,11... | collective-permute-start | bytes 1081352 | tf_op jit(solution)/shard_map/ppermute | solution.py:27
  209.0 12.9 %all-to-all-start.9 = ((bf16[8,176,128]{2,1,0:T(8,128)(2,1)}), bf16[8,176,128]{2,1,0:T(8,128)(2,1)}, u32[]{:S(2)}, u32[]{:S(2)}) async-start(bf16[8,176,128]{2,1,0:T(8,128)(2,1)} %broadcast_in_dim.31), calls=%async_computation.9 | async-start | bytes 720896 | tf_op jit(solution)/shard_map/all_to_all | solution.py:33
  223.4 6.7 %copy-start.2 = (f32[1408,128]{0,1:T(8,128)S(1)}, f32[1408,128]{0,1:T(8,128)}, u32[]{:S(2)}) copy-start(f32[1408,128]{0,1:T(8,128)} %convolution_add_fusion.1) | copy-start | bytes 2162692
  224.6 11.7 %all-to-all-start.10 = ((bf16[8,176,128]{2,1,0:T(8,128)(2,1)}), bf16[8,176,128]{2,1,0:T(8,128)(2,1)S(1)}, u32[]{:S(2)}, u32[]{:S(2)}) async-start(bf16[8,176,128]{2,1,0:T(8,128)(2,1)} %bitcast.34), calls=%async_computation.10 | async-start | bytes 720896 | tf_op jit(solution)/shard_map/all_to_all | solution.py:91
  229.4 7.0 %copy-start.16 = (bf16[176,128]{1,0:T(8,128)(2,1)S(1)}, bf16[176,128]{1,0:T(8,128)(2,1)}, u32[]{:S(2)}) copy-start(bf16[176,128]{1,0:T(8,128)(2,1)} %copy-done.15) | copy-start | bytes 135172
  232.1 25.7 %collective-permute-start.13 = (bf16[1408,128]{0,1:T(8,128)(2,1)}, bf16[1408,128]{0,1:T(8,128)(2,1)S(1)}, u32[]{:S(2)}, u32[]{:S(2)}) collective-permute-start(bf16[1408,128]{0,1:T(8,128)(2,1)} %fusion.3), channel_id=1, source_target_pairs={{0,1},{1,0},{2,3},{3,2},{4,5},{5,4},{6,7},{7,6},{8,9},{9,8},{10,11... | collective-permute-start | bytes 1081352 | tf_op jit(solution)/shard_map/ppermute | solution.py:27
  236.5 7.2 %copy-start.9 = (f32[384,128]{1,0:T(8,128)S(1)}, f32[384,128]{1,0:T(8,128)}, u32[]{:S(2)}) copy-start(f32[384,128]{1,0:T(8,128)} %convolution_add_fusion.6) | copy-start | bytes 589828
  237.5 11.3 %copy-start.22 = (bf16[176,128]{1,0:T(8,128)(2,1)S(1)}, bf16[176,128]{1,0:T(8,128)(2,1)}, u32[]{:S(2)}) copy-start(bf16[176,128]{1,0:T(8,128)(2,1)} %convolution_convert_fusion.11) | copy-start | bytes 135172
  237.5 22.5 %all-to-all-start.11 = ((bf16[16,176,128]{2,1,0:T(8,128)(2,1)}), bf16[16,176,128]{2,1,0:T(8,128)(2,1)S(1)}, u32[]{:S(2)}, u32[]{:S(2)}) async-start(bf16[16,176,128]{2,1,0:T(8,128)(2,1)} %broadcast_in_dim.32), calls=%async_computation.11 | async-start | bytes 1441792 | tf_op jit(solution)/shard_map/all_to_all | solution.py:33
  243.9 14.0 %copy-start.21 = (bf16[192,128]{1,0:T(8,128)(2,1)S(1)}, bf16[192,128]{1,0:T(8,128)(2,1)}, u32[]{:S(2)}) copy-start(bf16[192,128]{1,0:T(8,128)(2,1)} %get-tuple-element.47) | copy-start | bytes 147460
  243.9 11.8 %collective-permute-start.12 = (bf16[192,128]{1,0:T(8,128)(2,1)S(1)}, bf16[192,128]{1,0:T(8,128)(2,1)S(1)}, u32[]{:S(2)}, u32[]{:S(2)}) collective-permute-start(bf16[192,128]{1,0:T(8,128)(2,1)S(1)} %get-tuple-element.50), channel_id=1, source_target_pairs={{0,1},{1,0},{2,3},{3,2},{4,5},{5,4},{6,7},{7,6},{8,9},{9,8},{10,11... | collective-permute-start | bytes 147464 | tf_op jit(solution)/shard_map/ppermute | solution.py:27
  260.7 1.3 copy-start.19
  (2 other events, 1.2 us)

commit v6 on v1

--- a/solution.py
+++ b/solution.py
@@ -25,6 +25,10 @@
 
 def swap(x):
     return lax.ppermute(x, "replica", [(0, 1), (1, 0)])
+
+
+def tied(*values):
+    return lax.optimization_barrier(values)
 
 
 def gather(chunk, axes="tensor"):
@@ -87,22 +91,17 @@
     saved_other = swap(saved_sent)
     last_own = dot(saved_own, picked(ticks - 1)).astype(bf16)
     last_other = dot(saved_other, pick_other).astype(bf16)
-    active_other = swap(active[units:])
 
     hiddens, grads, upstreams = [], [], []
     for t in range(ticks):
         upstreams.append(upstream)
-        if t + 1 == ticks:
-            seen = dot(jnp.concatenate(upstreams, axis=1), pick, 1, 1).astype(bf16)
-            seen_other = swap(seen)
-            early = dot(
-                jnp.concatenate(grads, axis=1), pick[:, : t * rows], 1, 1
-            ).astype(bf16)
-            early_other = swap(early)
         slope_now = slopes[:, t * rows : (t + 1) * rows]
         hidden = (dot(down, upstream) * slope_now).astype(bf16)
         hiddens.append(hidden)
         partial = dot(up, hidden).astype(bf16)
+        if t + 1 == ticks:
+            seen = dot(jnp.concatenate(upstreams, axis=1), pick, 1, 1).astype(bf16)
+            seen_other = swap(seen)
         terms = lax.all_to_all(partial.reshape(parts, chunk_rows, rows), "tensor", 0, 0)
         mixed_chunk = (
             jnp.sum(terms.astype(f32), axis=0) + chunk.astype(f32)
@@ -110,18 +109,32 @@
         if t + 1 < ticks:
             mixed_grad = gather(mixed_chunk).reshape(width, rows)
             grads.append(mixed_grad)
-            input_grad = dot(proj, mixed_grad).astype(bf16).reshape(2, chunk_rows, rows)
-            above = lax.ppermute(
-                input_grad[0], "section", [(i, i - 1) for i in range(1, sections)]
-            )
+            skip_grad = dot(proj[chunk_rows:], mixed_grad).astype(bf16)
             mirrored = lax.ppermute(
-                input_grad[1],
+                skip_grad,
                 "section",
                 [(i, sections - 1 - i) for i in range(half, sections)],
             )
+            later_grad, _ = tied(mixed_grad, skip_grad)
+            above = lax.ppermute(
+                dot(proj[:chunk_rows], later_grad).astype(bf16),
+                "section",
+                [(i, i - 1) for i in range(1, sections)],
+            )
+            if t + 3 == ticks:
+                active_sent, _ = tied(active[units:], skip_grad)
+                sent = swap(active_sent)
+            elif t + 2 == ticks:
+                early = dot(jnp.concatenate(grads, axis=1), pick[:, : (t + 1) * rows], 1, 1)
+                early = early.astype(bf16)
+                sent = swap(early)
             summed = (above.astype(f32) + mirrored.astype(f32)).astype(bf16)
             chunk = jnp.where(is_top, loss_grads[t].T, summed)
             upstream = gather(chunk).reshape(width, rows)
+            if t + 3 == ticks:
+                upstream, active_other = tied(upstream, sent)
+            elif t + 2 == ticks:
+                upstream, early_other = tied(upstream, sent)
         else:
             spread = dot(jnp.concatenate(hiddens, axis=1), pick, 1, 1).astype(bf16)
             spread_other = swap(spread[units:])

time: 247 us -> 235 us (0.951)
  the two profiles are of different devices: /device:TPU:96 before, /device:TPU:354 now
where the time goes in v6:
time: 235 us; the launch traced here: 234 us
  starting transfers between devices  118 us (50%)
  waiting for transfers between devices  50 us (21%)
  blocking collectives  32 us (14%)
  matrix products  24.6 us (10%)
  local copies, waits for them, and re-layouts  7.06 us (3%)
    ppermute x10, starting transfers between devices, swap(): return lax.ppermute(x, 'replica', [(0, 1), (1, 0)])  40.1 us
    all_to_all x6, starting transfers between devices, gather(): return lax.all_to_all(spread, axes, 0, 0)  31.4 us
    ppermute x10, waiting for transfers between devices, swap(): return lax.ppermute(x, 'replica', [(0, 1), (1, 0)])  25.9 us
    dot_general x26, matrix products, dot(): lax.dot_general(a, b, (((ca,), (cb,)), ((), ())), preferred_element_type=...  24.6 us
    ppermute x3, starting transfers between devices, body(): lax.ppermute(skip_grad, 'section', [(i, sections - 1 - i) for i in range(...  22.7 us
    all_to_all x2, blocking collectives, gather(): return lax.all_to_all(spread, axes, 0, 0)  21.7 us
    all_to_all x3, starting transfers between devices, body(): lax.all_to_all(partial.reshape(parts, chunk_rows, rows), 'tensor', 0, 0)  16 us
    all_to_all x6, waiting for transfers between devices, gather(): return lax.all_to_all(spread, axes, 0, 0)  12.5 us
  transfers between devices with their start and end apart: 25, of which 13 were waited for; matrix products, arithmetic and copies ran while one was open for 9% of the time, Pallas kernels for 0%

profile of v6, /device:TPU:354, one launch (start us, length us, event | category | flops | bytes accessed | tf_op | source)
XLA Modules:
  0.0 233.7 jit_solution(15587602448540541161)
XLA Ops:
  0.7 5.2 %collective-permute-start.2 = (bf16[1408,192]{0,1:T(8,128)(2,1)}, bf16[1408,192]{0,1:T(8,128)(2,1)S(1)}, u32[]{:S(2)}, u32[]{:S(2)}) collective-permute-start(bf16[1408,192]{0,1:T(8,128)(2,1)} %bitcast.129), channel_id=1, source_target_pairs={{0,1},{1,0},{2,3},{3,2},{4,5},{5,4},{6,7},{7,6},{8,9},{9,8},{10,11... | collective-permute-start | bytes 1622024 | tf_op jit(solution)/shard_map/ppermute | solution.py:27
  5.9 2.2 collective-permute-start.3
  8.2 1.6 broadcast_in_dim.22
  9.7 5.8 %all-to-all-start = ((bf16[8,176,128]{2,1,0:T(8,128)(2,1)}), bf16[8,176,128]{2,1,0:T(8,128)(2,1)S(1)}, u32[]{:S(2)}, u32[]{:S(2)}) async-start(bf16[8,176,128]{2,1,0:T(8,128)(2,1)} %broadcast_in_dim.22), calls=%async_computation | async-start | bytes 720896 | tf_op jit(solution)/shard_map/all_to_all | solution.py:37
  15.6 6.2 %collective-permute-done.2 = bf16[1408,192]{0,1:T(8,128)(2,1)S(1)} collective-permute-done((bf16[1408,192]{0,1:T(8,128)(2,1)}, bf16[1408,192]{0,1:T(8,128)(2,1)S(1)}, u32[]{:S(2)}, u32[]{:S(2)}) %collective-permute-start.2) | collective-permute-done | bytes 540704 | tf_op jit(solution)/shard_map/ppermute | solution.py:27
  23.3 10.9 %all-to-all-done = bf16[8,176,128]{2,1,0:T(8,128)(2,1)S(1)} async-done(((bf16[8,176,128]{2,1,0:T(8,128)(2,1)}), bf16[8,176,128]{2,1,0:T(8,128)(2,1)S(1)}, u32[]{:S(2)}, u32[]{:S(2)}) %all-to-all-start) | async-done | bytes 360480 | tf_op jit(solution)/shard_map/all_to_all | solution.py:37
  34.2 1.6 fusion.16
  37.1 5.7 %all-to-all-start.1 = ((bf16[8,176,128]{2,1,0:T(8,128)(2,1)}), bf16[8,176,128]{2,1,0:T(8,128)(2,1)S(1)}, u32[]{:S(2)}, u32[]{:S(2)}) async-start(bf16[8,176,128]{2,1,0:T(8,128)(2,1)} %bitcast.13), calls=%async_computation.1 | async-start | bytes 720896 | tf_op jit(solution)/shard_map/all_to_all | solution.py:105
  42.9 4.2 %collective-permute-start.4 = (bf16[2,88,1408]{2,1,0:T(8,128)(2,1)S(1)}, bf16[2,88,1408]{2,1,0:T(8,128)(2,1)S(1)}, u32[]{:S(2)}, u32[]{:S(2)}) collective-permute-start(bf16[2,88,1408]{2,1,0:T(8,128)(2,1)S(1)} %bitcast.95), channel_id=1, source_target_pairs={{0,1},{1,0},{2,3},{3,2},{4,5},{5,4},{6,7},{7,6},{8,9},{9,8},{10,11... | collective-permute-start | bytes 1486856 | tf_op jit(solution)/shard_map/ppermute | solution.py:27
  47.1 1.7 all-to-all-done.1
  49.7 4.8 %all-to-all-start.2 = ((bf16[8,176,128]{2,1,0:T(8,128)(2,1)}), bf16[8,176,128]{2,1,0:T(8,128)(2,1)S(1)}, u32[]{:S(2)}, u32[]{:S(2)}) async-start(bf16[8,176,128]{2,1,0:T(8,128)(2,1)} %broadcast_in_dim.23), calls=%async_computation.2 | async-start | bytes 720896 | tf_op jit(solution)/shard_map/all_to_all | solution.py:37
  54.5 8.3 %collective-permute-done.4 = bf16[2,88,1408]{2,1,0:T(8,128)(2,1)S(1)} collective-permute-done((bf16[2,88,1408]{2,1,0:T(8,128)(2,1)S(1)}, bf16[2,88,1408]{2,1,0:T(8,128)(2,1)S(1)}, u32[]{:S(2)}, u32[]{:S(2)}) %collective-permute-start.4) | collective-permute-done | bytes 495648 | tf_op jit(solution)/shard_map/ppermute | solution.py:27
  63.7 1.9 collective-permute-start.5
  65.6 2.2 collective-permute-start.6
  67.8 1.7 collective-permute-done.6
  69.6 11.3 %all_to_all.60 = bf16[8,176,128]{2,1,0:T(8,128)(2,1)S(1)} all-to-all(bf16[8,176,128]{2,1,0:T(8,128)(2,1)S(1)} %broadcast_in_dim.24), channel_id=1, replica_groups=mesh['section'=32,'tensor'=8,'replica'=2] {'tensor'}, dimensions={0} | all-to-all | bytes 720896 | tf_op jit(solution)/shard_map/all_to_all | solution.py:37
  80.9 1.6 fusion.17
  83.2 10.3 %all_to_all.61 = bf16[8,176,128]{2,1,0:T(8,128)(2,1)S(1)} all-to-all(bf16[8,176,128]{2,1,0:T(8,128)(2,1)S(1)} %bitcast.113), channel_id=1, replica_groups=mesh['section'=32,'tensor'=8,'replica'=2] {'tensor'}, dimensions={0} | all-to-all | bytes 720896 | tf_op jit(solution)/shard_map/all_to_all | solution.py:105
  93.7 10.3 %all_to_all.62 = bf16[8,176,128]{2,1,0:T(8,128)(2,1)S(1)} all-to-all(bf16[8,176,128]{2,1,0:T(8,128)(2,1)S(1)} %broadcast_in_dim.25), channel_id=1, replica_groups=mesh['section'=32,'tensor'=8,'replica'=2] {'tensor'}, dimensions={0} | all-to-all | bytes 720896 | tf_op jit(solution)/shard_map/all_to_all | solution.py:37
  104.7 1.9 collective-permute-start.7
  106.7 11.6 %collective-permute-start.8 = (bf16[176,128]{1,0:T(8,128)(2,1)S(1)}, bf16[176,128]{1,0:T(8,128)(2,1)S(1)}, u32[]{:S(2)}, u32[]{:S(2)}) collective-permute-start(bf16[176,128]{1,0:T(8,128)(2,1)S(1)} %convolution_convert_fusion.14), channel_id=1, source_target_pairs={{256,240},{272,224},{288,208},{304,192},{320,176},{336,160},{352,1... | collective-permute-start | bytes 135176 | tf_op jit(solution)/shard_map/ppermute | solution.py:113
  118.3 1.7 collective-permute-done.8
  120.7 4.8 %all-to-all-start.6 = ((bf16[8,176,128]{2,1,0:T(8,128)(2,1)}), bf16[8,176,128]{2,1,0:T(8,128)(2,1)S(1)}, u32[]{:S(2)}, u32[]{:S(2)}) async-start(bf16[8,176,128]{2,1,0:T(8,128)(2,1)} %broadcast_in_dim.26), calls=%async_computation.6 | async-start | bytes 720896 | tf_op jit(solution)/shard_map/all_to_all | solution.py:37
  125.6 4.4 %collective-permute-start.9 = (bf16[192,128]{1,0:T(8,128)(2,1)S(1)}, bf16[192,128]{1,0:T(8,128)(2,1)S(1)}, u32[]{:S(2)}, u32[]{:S(2)}) collective-permute-start(bf16[192,128]{1,0:T(8,128)(2,1)S(1)} %get-tuple-element.14), channel_id=1, source_target_pairs={{0,1},{1,0},{2,3},{3,2},{4,5},{5,4},{6,7},{7,6},{8,9},{9,8},{10,11... | collective-permute-start | bytes 147464 | tf_op jit(solution)/shard_map/ppermute | solution.py:27
  129.9 3.0 %collective-permute-start.13 = (bf16[128,1408]{1,0:T(8,128)(2,1)}, bf16[128,1408]{1,0:T(8,128)(2,1)}, u32[]{:S(2)}, u32[]{:S(2)}) collective-permute-start(bf16[128,1408]{1,0:T(8,128)(2,1)} %bitcast.135), channel_id=1, source_target_pairs={{0,1},{1,0},{2,3},{3,2},{4,5},{5,4},{6,7},{7,6},{8,9},{9,8},{10,11... | collective-permute-start | bytes 1081352 | tf_op jit(solution)/shard_map/ppermute | solution.py:27
  133.5 1.6 fusion.18
  136.4 5.2 %all-to-all-start.7 = ((bf16[8,176,128]{2,1,0:T(8,128)(2,1)}), bf16[8,176,128]{2,1,0:T(8,128)(2,1)S(1)}, u32[]{:S(2)}, u32[]{:S(2)}) async-start(bf16[8,176,128]{2,1,0:T(8,128)(2,1)} %bitcast.27), calls=%async_computation.7 | async-start | bytes 720896 | tf_op jit(solution)/shard_map/all_to_all | solution.py:105
  141.8 5.6 %all-to-all-done.7 = bf16[8,176,128]{2,1,0:T(8,128)(2,1)S(1)} async-done(((bf16[8,176,128]{2,1,0:T(8,128)(2,1)}), bf16[8,176,128]{2,1,0:T(8,128)(2,1)S(1)}, u32[]{:S(2)}, u32[]{:S(2)}) %all-to-all-start.7) | async-done | bytes 360480 | tf_op jit(solution)/shard_map/all_to_all | solution.py:105
  148.2 4.9 %all-to-all-start.8 = ((bf16[8,176,128]{2,1,0:T(8,128)(2,1)}), bf16[8,176,128]{2,1,0:T(8,128)(2,1)S(1)}, u32[]{:S(2)}, u32[]{:S(2)}) async-start(bf16[8,176,128]{2,1,0:T(8,128)(2,1)} %broadcast_in_dim.27), calls=%async_computation.8 | async-start | bytes 720896 | tf_op jit(solution)/shard_map/all_to_all | solution.py:37
  153.2 4.4 %collective-permute-start = (bf16[176,128]{1,0:T(8,128)(2,1)S(1)}, bf16[176,128]{1,0:T(8,128)(2,1)S(1)}, u32[]{:S(2)}, u32[]{:S(2)}) collective-permute-start(bf16[176,128]{1,0:T(8,128)(2,1)S(1)} %bitcast.118), channel_id=1, source_target_pairs={{0,1},{1,0},{2,3},{3,2},{4,5},{5,4},{6,7},{7,6},{8,9},{9,8},{10,11... | collective-permute-start | bytes 135176 | tf_op jit(solution)/shard_map/ppermute | solution.py:27
  157.6 1.3 all-to-all-done.8
  159.3 8.9 %collective-permute-start.11 = (bf16[176,128]{1,0:T(8,128)(2,1)S(1)}, bf16[176,128]{1,0:T(8,128)(2,1)S(1)}, u32[]{:S(2)}, u32[]{:S(2)}) collective-permute-start(bf16[176,128]{1,0:T(8,128)(2,1)S(1)} %convolution_convert_fusion.12), channel_id=1, source_target_pairs={{256,240},{272,224},{288,208},{304,192},{320,176},{336,160},{352,1... | collective-permute-start | bytes 135176 | tf_op jit(solution)/shard_map/ppermute | solution.py:113
  168.5 3.8 %collective-permute-start.10 = (bf16[176,128]{1,0:T(8,128)(2,1)S(1)}, bf16[176,128]{1,0:T(8,128)(2,1)S(1)}, u32[]{:S(2)}, u32[]{:S(2)}) collective-permute-start(bf16[176,128]{1,0:T(8,128)(2,1)S(1)} %convolution_convert_fusion.11), channel_id=1, source_target_pairs={{16,0},{32,16},{48,32},{64,48},{80,64},{96,80},{112,96},{128,112},... | collective-permute-start | bytes 135176 | tf_op jit(solution)/shard_map/ppermute | solution.py:119
  173.6 4.2 %collective-permute-start.12 = (bf16[1408,128]{0,1:T(8,128)(2,1)}, bf16[1408,128]{0,1:T(8,128)(2,1)}, u32[]{:S(2)}, u32[]{:S(2)}) collective-permute-start(bf16[1408,128]{0,1:T(8,128)(2,1)} %convolution_convert_fusion.5), channel_id=1, source_target_pairs={{0,1},{1,0},{2,3},{3,2},{4,5},{5,4},{6,7},{7,6},{8,9},{9,8},{10,11... | collective-permute-start | bytes 1081352 | tf_op jit(solution)/shard_map/ppermute | solution.py:27
  178.6 4.8 %all-to-all-start.9 = ((bf16[8,176,128]{2,1,0:T(8,128)(2,1)}), bf16[8,176,128]{2,1,0:T(8,128)(2,1)S(1)}, u32[]{:S(2)}, u32[]{:S(2)}) async-start(bf16[8,176,128]{2,1,0:T(8,128)(2,1)} %broadcast_in_dim.28), calls=%async_computation.9 | async-start | bytes 720896 | tf_op jit(solution)/shard_map/all_to_all | solution.py:37
  183.4 3.4 %collective-permute-start.1 = (s32[128]{0:T(128)S(1)}, s32[128]{0:T(128)S(1)}, u32[]{:S(2)}, u32[]{:S(2)}) collective-permute-start(s32[128]{0:T(128)S(1)} %slice_bitcast_fusion), channel_id=1, source_target_pairs={{0,1},{1,0},{2,3},{3,2},{4,5},{5,4},{6,7},{7,6},{8,9},{9,8},{10,11... | collective-permute-start | bytes 1544 | tf_op jit(solution)/shard_map/ppermute | solution.py:27
  187.0 4.4 %collective-permute-done.12 = bf16[1408,128]{0,1:T(8,128)(2,1)} collective-permute-done((bf16[1408,128]{0,1:T(8,128)(2,1)}, bf16[1408,128]{0,1:T(8,128)(2,1)}, u32[]{:S(2)}, u32[]{:S(2)}) %collective-permute-start.12) | collective-permute-done | bytes 360480 | tf_op jit(solution)/shard_map/ppermute | solution.py:27
  191.6 1.8 fusion.19
  193.4 1.2 convolution_convert_fusion.4
  194.6 5.0 %all-to-all-start.10 = ((bf16[8,176,128]{2,1,0:T(8,128)(2,1)}), bf16[8,176,128]{2,1,0:T(8,128)(2,1)S(1)}, u32[]{:S(2)}, u32[]{:S(2)}) async-start(bf16[8,176,128]{2,1,0:T(8,128)(2,1)} %bitcast.32), calls=%async_computation.10 | async-start | bytes 720896 | tf_op jit(solution)/shard_map/all_to_all | solution.py:105
  199.9 1.4 convolution_convert_fusion.3
  201.2 4.0 %collective-permute-start.15 = (bf16[1408,128]{0,1:T(8,128)(2,1)}, bf16[1408,128]{0,1:T(8,128)(2,1)}, u32[]{:S(2)}, u32[]{:S(2)}) collective-permute-start(bf16[1408,128]{0,1:T(8,128)(2,1)} %convolution_convert_fusion.3), channel_id=1, source_target_pairs={{0,1},{1,0},{2,3},{3,2},{4,5},{5,4},{6,7},{7,6},{8,9},{9,8},{10,11... | collective-permute-start | bytes 1081352 | tf_op jit(solution)/shard_map/ppermute | solution.py:27
  207.3 6.2 %all-to-all-start.11 = ((bf16[16,176,128]{2,1,0:T(8,128)(2,1)}), bf16[16,176,128]{2,1,0:T(8,128)(2,1)S(1)}, u32[]{:S(2)}, u32[]{:S(2)}) async-start(bf16[16,176,128]{2,1,0:T(8,128)(2,1)} %broadcast_in_dim.29), calls=%async_computation.11 | async-start | bytes 1441792 | tf_op jit(solution)/shard_map/all_to_all | solution.py:37
  213.9 5.0 %collective-permute-start.14 = (bf16[192,128]{1,0:T(8,128)(2,1)S(1)}, bf16[192,128]{1,0:T(8,128)(2,1)S(1)}, u32[]{:S(2)}, u32[]{:S(2)}) collective-permute-start(bf16[192,128]{1,0:T(8,128)(2,1)S(1)} %get-tuple-element.28), channel_id=1, source_target_pairs={{0,1},{1,0},{2,3},{3,2},{4,5},{5,4},{6,7},{7,6},{8,9},{9,8},{10,11... | collective-permute-start | bytes 147464 | tf_op jit(solution)/shard_map/ppermute | solution.py:27
  219.0 6.4 %collective-permute-done.14 = bf16[192,128]{1,0:T(8,128)(2,1)S(1)} collective-permute-done((bf16[192,128]{1,0:T(8,128)(2,1)S(1)}, bf16[192,128]{1,0:T(8,128)(2,1)S(1)}, u32[]{:S(2)}, u32[]{:S(2)}) %collective-permute-start.14) | collective-permute-done | bytes 49184 | tf_op jit(solution)/shard_map/ppermute | solution.py:27
  225.5 2.1 fusion.1
  227.6 2.2 fusion
  231.4 2.3 convolution_convert_fusion.2
  (122 shorter events, 16.9 us)
Async XLA Ops:
  0.6 21.1 %copy-start.13 = (bf16[1,1408,192]{1,2,0:T(8,128)(2,1)S(1)}, bf16[1,1408,192]{1,2,0:T(8,128)(2,1)}, u32[]{:S(2)}) copy-start(bf16[1,1408,192]{1,2,0:T(8,128)(2,1)} %param.14) | copy-start | bytes 1622020
  0.6 21.1 %copy-start.22 = (bf16[1,128,1408]{2,1,0:T(8,128)(2,1)S(1)}, bf16[1,128,1408]{2,1,0:T(8,128)(2,1)}, u32[]{:S(2)}) copy-start(bf16[1,128,1408]{2,1,0:T(8,128)(2,1)} %param.9) | copy-start | bytes 1081348
  0.7 21.1 %collective-permute-start.2 = (bf16[1408,192]{0,1:T(8,128)(2,1)}, bf16[1408,192]{0,1:T(8,128)(2,1)S(1)}, u32[]{:S(2)}, u32[]{:S(2)}) collective-permute-start(bf16[1408,192]{0,1:T(8,128)(2,1)} %bitcast.129), channel_id=1, source_target_pairs={{0,1},{1,0},{2,3},{3,2},{4,5},{5,4},{6,7},{7,6},{8,9},{9,8},{10,11... | collective-permute-start | bytes 1622024 | tf_op jit(solution)/shard_map/ppermute | solution.py:27
  5.9 28.3 %collective-permute-start.3 = (bf16[192,1408]{1,0:T(8,128)(2,1)}, bf16[192,1408]{1,0:T(8,128)(2,1)}, u32[]{:S(2)}, u32[]{:S(2)}) collective-permute-start(bf16[192,1408]{1,0:T(8,128)(2,1)} %bitcast.124), channel_id=1, source_target_pairs={{0,1},{1,0},{2,3},{3,2},{4,5},{5,4},{6,7},{7,6},{8,9},{9,8},{10,11... | collective-permute-start | bytes 1622024 | tf_op jit(solution)/shard_map/ppermute | solution.py:27
  9.7 24.5 %all-to-all-start = ((bf16[8,176,128]{2,1,0:T(8,128)(2,1)}), bf16[8,176,128]{2,1,0:T(8,128)(2,1)S(1)}, u32[]{:S(2)}, u32[]{:S(2)}) async-start(bf16[8,176,128]{2,1,0:T(8,128)(2,1)} %broadcast_in_dim.22), calls=%async_computation | async-start | bytes 720896 | tf_op jit(solution)/shard_map/all_to_all | solution.py:37
  15.6 7.0 %copy-start.10 = (s32[1,4,128]{2,1,0:T(4,128)S(1)}, s32[1,4,128]{2,1,0:T(4,128)}, u32[]{:S(2)}) copy-start(s32[1,4,128]{2,1,0:T(4,128)} %param.10) | copy-start | bytes 6148
  22.9 11.3 %copy-start.11 = (bf16[1,192,1408]{2,1,0:T(8,128)(2,1)S(1)}, bf16[1,192,1408]{2,1,0:T(8,128)(2,1)}, u32[]{:S(2)}) copy-start(bf16[1,192,1408]{2,1,0:T(8,128)(2,1)} %param.15) | copy-start | bytes 1622020
  34.2 1.7 copy-start.1
  34.2 1.7 copy-start.18
  35.9 7.0 %copy-start = (bf16[1,2,88,1408]{3,2,1,0:T(8,128)(2,1)S(1)}, bf16[1,2,88,1408]{3,2,1,0:T(8,128)(2,1)}, u32[]{:S(2)}) copy-start(bf16[1,2,88,1408]{3,2,1,0:T(8,128)(2,1)} %param.13) | copy-start | bytes 1486852
  37.1 11.7 %copy-start.7 = (bf16[1,128,176]{1,2,0:T(8,128)(2,1)S(1)}, bf16[1,128,176]{1,2,0:T(8,128)(2,1)}, u32[]{:S(2)}) copy-start(bf16[1,128,176]{1,2,0:T(8,128)(2,1)} %param.11) | copy-start | bytes 135172
  37.1 11.7 %all-to-all-start.1 = ((bf16[8,176,128]{2,1,0:T(8,128)(2,1)}), bf16[8,176,128]{2,1,0:T(8,128)(2,1)S(1)}, u32[]{:S(2)}, u32[]{:S(2)}) async-start(bf16[8,176,128]{2,1,0:T(8,128)(2,1)} %bitcast.13), calls=%async_computation.1 | async-start | bytes 720896 | tf_op jit(solution)/shard_map/all_to_all | solution.py:105
  42.9 19.9 %collective-permute-start.4 = (bf16[2,88,1408]{2,1,0:T(8,128)(2,1)S(1)}, bf16[2,88,1408]{2,1,0:T(8,128)(2,1)S(1)}, u32[]{:S(2)}, u32[]{:S(2)}) collective-permute-start(bf16[2,88,1408]{2,1,0:T(8,128)(2,1)S(1)} %bitcast.95), channel_id=1, source_target_pairs={{0,1},{1,0},{2,3},{3,2},{4,5},{5,4},{6,7},{7,6},{8,9},{9,8},{10,11... | collective-permute-start | bytes 1486856 | tf_op jit(solution)/shard_map/ppermute | solution.py:27
  49.7 13.2 %all-to-all-start.2 = ((bf16[8,176,128]{2,1,0:T(8,128)(2,1)}), bf16[8,176,128]{2,1,0:T(8,128)(2,1)S(1)}, u32[]{:S(2)}, u32[]{:S(2)}) async-start(bf16[8,176,128]{2,1,0:T(8,128)(2,1)} %broadcast_in_dim.23), calls=%async_computation.2 | async-start | bytes 720896 | tf_op jit(solution)/shard_map/all_to_all | solution.py:37
  63.2 6.3 %copy-start.8 = (bf16[3,128,176]{1,2,0:T(8,128)(2,1)S(1)}, bf16[3,128,176]{1,2,0:T(8,128)(2,1)}, u32[]{:S(2)}) copy-start(bf16[3,128,176]{1,2,0:T(8,128)(2,1)} %param.12) | copy-start | bytes 405508
  63.7 4.2 %collective-permute-start.5 = (bf16[176,128]{1,0:T(8,128)(2,1)S(1)}, bf16[176,128]{1,0:T(8,128)(2,1)S(1)}, u32[]{:S(2)}, u32[]{:S(2)}) collective-permute-start(bf16[176,128]{1,0:T(8,128)(2,1)S(1)} %convolution_convert_fusion.15), channel_id=1, source_target_pairs={{16,0},{32,16},{48,32},{64,48},{80,64},{96,80},{112,96},{128,112},... | collective-permute-start | bytes 135176 | tf_op jit(solution)/shard_map/ppermute | solution.py:119
  65.6 15.4 %copy-start.12 = (bf16[1,192,1408]{2,1,0:T(8,128)(2,1)S(1)}, bf16[1,192,1408]{2,1,0:T(8,128)(2,1)}, u32[]{:S(2)}) copy-start(bf16[1,192,1408]{2,1,0:T(8,128)(2,1)} %param.15) | copy-start | bytes 1622020
  65.6 3.9 %collective-permute-start.6 = (bf16[176,128]{1,0:T(8,128)(2,1)S(1)}, bf16[176,128]{1,0:T(8,128)(2,1)S(1)}, u32[]{:S(2)}, u32[]{:S(2)}) collective-permute-start(bf16[176,128]{1,0:T(8,128)(2,1)S(1)} %convolution_convert_fusion.16), channel_id=1, source_target_pairs={{256,240},{272,224},{288,208},{304,192},{320,176},{336,160},{352,1... | collective-permute-start | bytes 135176 | tf_op jit(solution)/shard_map/ppermute | solution.py:113
  80.9 1.6 copy-start.14
  80.9 1.6 copy-start.19
  104.7 13.5 %collective-permute-start.7 = (bf16[176,128]{1,0:T(8,128)(2,1)S(1)}, bf16[176,128]{1,0:T(8,128)(2,1)S(1)}, u32[]{:S(2)}, u32[]{:S(2)}) collective-permute-start(bf16[176,128]{1,0:T(8,128)(2,1)S(1)} %convolution_convert_fusion.13), channel_id=1, source_target_pairs={{16,0},{32,16},{48,32},{64,48},{80,64},{96,80},{112,96},{128,112},... | collective-permute-start | bytes 135176 | tf_op jit(solution)/shard_map/ppermute | solution.py:119
  106.7 13.3 %collective-permute-start.8 = (bf16[176,128]{1,0:T(8,128)(2,1)S(1)}, bf16[176,128]{1,0:T(8,128)(2,1)S(1)}, u32[]{:S(2)}, u32[]{:S(2)}) collective-permute-start(bf16[176,128]{1,0:T(8,128)(2,1)S(1)} %convolution_convert_fusion.14), channel_id=1, source_target_pairs={{256,240},{272,224},{288,208},{304,192},{320,176},{336,160},{352,1... | collective-permute-start | bytes 135176 | tf_op jit(solution)/shard_map/ppermute | solution.py:113
  120.7 12.8 %all-to-all-start.6 = ((bf16[8,176,128]{2,1,0:T(8,128)(2,1)}), bf16[8,176,128]{2,1,0:T(8,128)(2,1)S(1)}, u32[]{:S(2)}, u32[]{:S(2)}) async-start(bf16[8,176,128]{2,1,0:T(8,128)(2,1)} %broadcast_in_dim.26), calls=%async_computation.6 | async-start | bytes 720896 | tf_op jit(solution)/shard_map/all_to_all | solution.py:37
  125.6 8.0 %collective-permute-start.9 = (bf16[192,128]{1,0:T(8,128)(2,1)S(1)}, bf16[192,128]{1,0:T(8,128)(2,1)S(1)}, u32[]{:S(2)}, u32[]{:S(2)}) collective-permute-start(bf16[192,128]{1,0:T(8,128)(2,1)S(1)} %get-tuple-element.14), channel_id=1, source_target_pairs={{0,1},{1,0},{2,3},{3,2},{4,5},{5,4},{6,7},{7,6},{8,9},{9,8},{10,11... | collective-permute-start | bytes 147464 | tf_op jit(solution)/shard_map/ppermute | solution.py:27
  129.9 89.1 %collective-permute-start.13 = (bf16[128,1408]{1,0:T(8,128)(2,1)}, bf16[128,1408]{1,0:T(8,128)(2,1)}, u32[]{:S(2)}, u32[]{:S(2)}) collective-permute-start(bf16[128,1408]{1,0:T(8,128)(2,1)} %bitcast.135), channel_id=1, source_target_pairs={{0,1},{1,0},{2,3},{3,2},{4,5},{5,4},{6,7},{7,6},{8,9},{9,8},{10,11... | collective-permute-start | bytes 1081352 | tf_op jit(solution)/shard_map/ppermute | solution.py:27
  133.5 1.6 copy-start.20
  135.2 6.5 %copy-start.9 = (bf16[1,128,2,176]{1,3,2,0:T(8,128)(2,1)S(1)}, bf16[1,128,2,176]{1,3,2,0:T(8,128)(2,1)}, u32[]{:S(2)}) copy-start(bf16[1,128,2,176]{1,3,2,0:T(8,128)(2,1)} %param.8) | copy-start | bytes 270340
  136.4 11.0 %all-to-all-start.7 = ((bf16[8,176,128]{2,1,0:T(8,128)(2,1)}), bf16[8,176,128]{2,1,0:T(8,128)(2,1)S(1)}, u32[]{:S(2)}, u32[]{:S(2)}) async-start(bf16[8,176,128]{2,1,0:T(8,128)(2,1)} %bitcast.27), calls=%async_computation.7 | async-start | bytes 720896 | tf_op jit(solution)/shard_map/all_to_all | solution.py:105
  148.2 10.7 %all-to-all-start.8 = ((bf16[8,176,128]{2,1,0:T(8,128)(2,1)}), bf16[8,176,128]{2,1,0:T(8,128)(2,1)S(1)}, u32[]{:S(2)}, u32[]{:S(2)}) async-start(bf16[8,176,128]{2,1,0:T(8,128)(2,1)} %broadcast_in_dim.27), calls=%async_computation.8 | async-start | bytes 720896 | tf_op jit(solution)/shard_map/all_to_all | solution.py:37
  153.2 46.5 %collective-permute-start = (bf16[176,128]{1,0:T(8,128)(2,1)S(1)}, bf16[176,128]{1,0:T(8,128)(2,1)S(1)}, u32[]{:S(2)}, u32[]{:S(2)}) collective-permute-start(bf16[176,128]{1,0:T(8,128)(2,1)S(1)} %bitcast.118), channel_id=1, source_target_pairs={{0,1},{1,0},{2,3},{3,2},{4,5},{5,4},{6,7},{7,6},{8,9},{9,8},{10,11... | collective-permute-start | bytes 135176 | tf_op jit(solution)/shard_map/ppermute | solution.py:27
  159.3 13.1 %copy-start.4 = (bf16[8,176,128]{2,1,0:T(8,128)(2,1)S(1)}, bf16[8,176,128]{2,1,0:T(8,128)(2,1)}, u32[]{:S(2)}) copy-start(bf16[8,176,128]{2,1,0:T(8,128)(2,1)} %copy-done.3) | copy-start | bytes 1081348
  159.3 13.1 %copy-start.6 = (bf16[8,176,128]{2,1,0:T(8,128)(2,1)S(1)}, bf16[8,176,128]{2,1,0:T(8,128)(2,1)}, u32[]{:S(2)}) copy-start(bf16[8,176,128]{2,1,0:T(8,128)(2,1)} %copy-done.5) | copy-start | bytes 1081348
  159.3 18.5 %collective-permute-start.11 = (bf16[176,128]{1,0:T(8,128)(2,1)S(1)}, bf16[176,128]{1,0:T(8,128)(2,1)S(1)}, u32[]{:S(2)}, u32[]{:S(2)}) collective-permute-start(bf16[176,128]{1,0:T(8,128)(2,1)S(1)} %convolution_convert_fusion.12), channel_id=1, source_target_pairs={{256,240},{272,224},{288,208},{304,192},{320,176},{336,160},{352,1... | collective-permute-start | bytes 135176 | tf_op jit(solution)/shard_map/ppermute | solution.py:113
  168.5 9.3 %collective-permute-start.10 = (bf16[176,128]{1,0:T(8,128)(2,1)S(1)}, bf16[176,128]{1,0:T(8,128)(2,1)S(1)}, u32[]{:S(2)}, u32[]{:S(2)}) collective-permute-start(bf16[176,128]{1,0:T(8,128)(2,1)S(1)} %convolution_convert_fusion.11), channel_id=1, source_target_pairs={{16,0},{32,16},{48,32},{64,48},{80,64},{96,80},{112,96},{128,112},... | collective-permute-start | bytes 135176 | tf_op jit(solution)/shard_map/ppermute | solution.py:119
  173.6 17.8 %collective-permute-start.12 = (bf16[1408,128]{0,1:T(8,128)(2,1)}, bf16[1408,128]{0,1:T(8,128)(2,1)}, u32[]{:S(2)}, u32[]{:S(2)}) collective-permute-start(bf16[1408,128]{0,1:T(8,128)(2,1)} %convolution_convert_fusion.5), channel_id=1, source_target_pairs={{0,1},{1,0},{2,3},{3,2},{4,5},{5,4},{6,7},{7,6},{8,9},{9,8},{10,11... | collective-permute-start | bytes 1081352 | tf_op jit(solution)/shard_map/ppermute | solution.py:27
  178.6 13.0 %all-to-all-start.9 = ((bf16[8,176,128]{2,1,0:T(8,128)(2,1)}), bf16[8,176,128]{2,1,0:T(8,128)(2,1)S(1)}, u32[]{:S(2)}, u32[]{:S(2)}) async-start(bf16[8,176,128]{2,1,0:T(8,128)(2,1)} %broadcast_in_dim.28), calls=%async_computation.9 | async-start | bytes 720896 | tf_op jit(solution)/shard_map/all_to_all | solution.py:37
  183.4 16.3 %collective-permute-start.1 = (s32[128]{0:T(128)S(1)}, s32[128]{0:T(128)S(1)}, u32[]{:S(2)}, u32[]{:S(2)}) collective-permute-start(s32[128]{0:T(128)S(1)} %slice_bitcast_fusion), channel_id=1, source_target_pairs={{0,1},{1,0},{2,3},{3,2},{4,5},{5,4},{6,7},{7,6},{8,9},{9,8},{10,11... | collective-permute-start | bytes 1544 | tf_op jit(solution)/shard_map/ppermute | solution.py:27
  191.6 1.8 copy-start.16
  191.6 1.8 copy-start.21
  193.4 6.5 %copy-start.2 = (bf16[8,176,128]{2,1,0:T(8,128)(2,1)S(1)}, bf16[8,176,128]{2,1,0:T(8,128)(2,1)}, u32[]{:S(2)}) copy-start(bf16[8,176,128]{2,1,0:T(8,128)(2,1)} %copy-done.1) | copy-start | bytes 1081348
  194.6 11.6 %all-to-all-start.10 = ((bf16[8,176,128]{2,1,0:T(8,128)(2,1)}), bf16[8,176,128]{2,1,0:T(8,128)(2,1)S(1)}, u32[]{:S(2)}, u32[]{:S(2)}) async-start(bf16[8,176,128]{2,1,0:T(8,128)(2,1)} %bitcast.32), calls=%async_computation.10 | async-start | bytes 720896 | tf_op jit(solution)/shard_map/all_to_all | solution.py:105
  201.2 26.3 %collective-permute-start.15 = (bf16[1408,128]{0,1:T(8,128)(2,1)}, bf16[1408,128]{0,1:T(8,128)(2,1)}, u32[]{:S(2)}, u32[]{:S(2)}) collective-permute-start(bf16[1408,128]{0,1:T(8,128)(2,1)} %convolution_convert_fusion.3), channel_id=1, source_target_pairs={{0,1},{1,0},{2,3},{3,2},{4,5},{5,4},{6,7},{7,6},{8,9},{9,8},{10,11... | collective-permute-start | bytes 1081352 | tf_op jit(solution)/shard_map/ppermute | solution.py:27
  206.3 7.2 %copy-start.25 = (bf16[384,128]{0,1:T(8,128)(2,1)S(1)}, bf16[384,128]{0,1:T(8,128)(2,1)}, u32[]{:S(2)}) copy-start(bf16[384,128]{0,1:T(8,128)(2,1)} %copy-done.24) | copy-start | bytes 294916
  206.3 7.2 %copy-start.27 = (bf16[384,128]{0,1:T(8,128)(2,1)S(1)}, bf16[384,128]{0,1:T(8,128)(2,1)}, u32[]{:S(2)}) copy-start(bf16[384,128]{0,1:T(8,128)(2,1)} %copy-done.26) | copy-start | bytes 294916
  206.3 7.2 %copy-start.29 = (bf16[384,128]{0,1:T(8,128)(2,1)S(1)}, bf16[384,128]{0,1:T(8,128)(2,1)}, u32[]{:S(2)}) copy-start(bf16[384,128]{0,1:T(8,128)(2,1)} %copy-done.28) | copy-start | bytes 294916
  207.3 22.5 %all-to-all-start.11 = ((bf16[16,176,128]{2,1,0:T(8,128)(2,1)}), bf16[16,176,128]{2,1,0:T(8,128)(2,1)S(1)}, u32[]{:S(2)}, u32[]{:S(2)}) async-start(bf16[16,176,128]{2,1,0:T(8,128)(2,1)} %broadcast_in_dim.29), calls=%async_computation.11 | async-start | bytes 1441792 | tf_op jit(solution)/shard_map/all_to_all | solution.py:37
  213.9 11.6 %copy-start.23 = (bf16[1,128,1408]{2,1,0:T(8,128)(2,1)S(1)}, bf16[1,128,1408]{2,1,0:T(8,128)(2,1)}, u32[]{:S(2)}) copy-start(bf16[1,128,1408]{2,1,0:T(8,128)(2,1)} %param.9) | copy-start | bytes 1081348
  213.9 11.6 %collective-permute-start.14 = (bf16[192,128]{1,0:T(8,128)(2,1)S(1)}, bf16[192,128]{1,0:T(8,128)(2,1)S(1)}, u32[]{:S(2)}, u32[]{:S(2)}) collective-permute-start(bf16[192,128]{1,0:T(8,128)(2,1)S(1)} %get-tuple-element.28), channel_id=1, source_target_pairs={{0,1},{1,0},{2,3},{3,2},{4,5},{5,4},{6,7},{7,6},{8,9},{9,8},{10,11... | collective-permute-start | bytes 147464 | tf_op jit(solution)/shard_map/ppermute | solution.py:27
  (7 other events, 7.0 us)

commit v7 on v6

--- a/solution.py
+++ b/solution.py
@@ -65,7 +65,7 @@
     upstream = gather(chunk).reshape(width, rows)
 
     up = jnp.concatenate([w_up[0], up_other], axis=1)
-    down = jnp.concatenate([w_down[0], down_other], axis=0)
+    (down,) = tied(jnp.concatenate([w_down[0], down_other], axis=0))
     proj = jnp.concatenate(by_replica(w_proj[0], proj_other), axis=1).reshape(-1, width)
 
     places = jnp.arange(pool, dtype=jnp.int32)[:, None]
@@ -139,8 +139,8 @@
             spread = dot(jnp.concatenate(hiddens, axis=1), pick, 1, 1).astype(bf16)
             spread_other = swap(spread[units:])
             both = gather(mixed_chunk, ("replica", "tensor")).reshape(2, width, rows)
-            mixed_grad = jnp.where(first, both[0], both[1])
-            input_grad = dot(proj, mixed_grad).astype(bf16).reshape(2, chunk_rows, rows)
+            input_grad = jnp.where(first, dot(proj, both[0]), dot(proj, both[1]))
+            input_grad = input_grad.astype(bf16).reshape(2, chunk_rows, rows)
 
     grad_up = dot(
         jnp.concatenate([pool_mixed[0], mixed_other], axis=0),

time: 235 us -> 240 us (1.021)
  waiting for transfers between devices: 50 us -> 46.7 us
  local copies, waits for them, and re-layouts: 7.06 us -> 9.78 us
  other arithmetic: 0.8 us -> 3.35 us
    all_to_all x6, waiting for transfers between devices: 12.5 us -> 1.23 us  [gather(): return lax.all_to_all(spread, axes, 0, 0)]
    ppermute x10, waiting for transfers between devices: 25.9 us -> 36.5 us  [swap(): return lax.ppermute(x, 'replica', [(0, 1), (1, 0)])]
    all_to_all x3, waiting for transfers between devices: 8.23 us -> 5.63 us  [body(): lax.all_to_all(partial.reshape(parts, chunk_rows, rows), 'tensor', 0, 0)]
    dot_general x26 -> x27, matrix products: 24.6 us -> 26.1 us  [dot(): lax.dot_general(a, b, (((ca,), (cb,)), ((), ())), preferred_element_type=...]
  transfers between devices with their start and end apart: 25 -> 25, of which waited for: 13 -> 11; matrix products, arithmetic and copies ran while one was open for 9% -> 11% of each run, Pallas kernels for 0% -> 0%
where the time goes in v7:
time: 240 us; the launch traced here: 238 us
  starting transfers between devices  119 us (50%)
  waiting for transfers between devices  46.7 us (19%)
  blocking collectives  32.2 us (13%)
  matrix products  26.1 us (11%)
  local copies, waits for them, and re-layouts  9.78 us (4%)
  other arithmetic  3.35 us (1%)
    ppermute x10, starting transfers between devices, swap(): return lax.ppermute(x, 'replica', [(0, 1), (1, 0)])  40.6 us
    ppermute x10, waiting for transfers between devices, swap(): return lax.ppermute(x, 'replica', [(0, 1), (1, 0)])  36.5 us
    all_to_all x6, starting transfers between devices, gather(): return lax.all_to_all(spread, axes, 0, 0)  31.8 us
    dot_general x27, matrix products, dot(): lax.dot_general(a, b, (((ca,), (cb,)), ((), ())), preferred_element_type=...  26.1 us
    all_to_all x2, blocking collectives, gather(): return lax.all_to_all(spread, axes, 0, 0)  21.9 us
    ppermute x3, starting transfers between devices, body(): lax.ppermute(skip_grad, 'section', [(i, sections - 1 - i) for i in range(...  20.5 us
    all_to_all x3, starting transfers between devices, body(): lax.all_to_all(partial.reshape(parts, chunk_rows, rows), 'tensor', 0, 0)  16.6 us
    all_to_all x1, blocking collectives, body(): lax.all_to_all(partial.reshape(parts, chunk_rows, rows), 'tensor', 0, 0)  10.3 us
  transfers between devices with their start and end apart: 25, of which 11 were waited for; matrix products, arithmetic and copies ran while one was open for 11% of the time, Pallas kernels for 0%

profile of v7, /device:TPU:354, one launch (start us, length us, event | category | flops | bytes accessed | tf_op | source)
XLA Modules:
  0.0 238.0 jit_solution(12760762924907261242)
XLA Ops:
  0.6 5.2 %collective-permute-start.3 = (bf16[192,1408]{1,0:T(8,128)(2,1)}, bf16[192,1408]{1,0:T(8,128)(2,1)S(1)}, u32[]{:S(2)}, u32[]{:S(2)}) collective-permute-start(bf16[192,1408]{1,0:T(8,128)(2,1)} %bitcast.110), channel_id=1, source_target_pairs={{0,1},{1,0},{2,3},{3,2},{4,5},{5,4},{6,7},{7,6},{8,9},{9,8},{10,11... | collective-permute-start | bytes 1622024 | tf_op jit(solution)/shard_map/ppermute | solution.py:27
  5.9 2.2 collective-permute-start.2
  8.1 1.6 broadcast_in_dim.22
  9.7 5.8 %all-to-all-start = ((bf16[8,176,128]{2,1,0:T(8,128)(2,1)}), bf16[8,176,128]{2,1,0:T(8,128)(2,1)S(1)}, u32[]{:S(2)}, u32[]{:S(2)}) async-start(bf16[8,176,128]{2,1,0:T(8,128)(2,1)} %broadcast_in_dim.22), calls=%async_computation | async-start | bytes 720896 | tf_op jit(solution)/shard_map/all_to_all | solution.py:37
  15.6 6.2 %collective-permute-done.3 = bf16[192,1408]{1,0:T(8,128)(2,1)S(1)} collective-permute-done((bf16[192,1408]{1,0:T(8,128)(2,1)}, bf16[192,1408]{1,0:T(8,128)(2,1)S(1)}, u32[]{:S(2)}, u32[]{:S(2)}) %collective-permute-start.3) | collective-permute-done | bytes 540704 | tf_op jit(solution)/shard_map/ppermute | solution.py:27
  21.9 11.5 %collective-permute-done.2 = bf16[1408,192]{0,1:T(8,128)(2,1)S(1)} collective-permute-done((bf16[1408,192]{0,1:T(8,128)(2,1)}, bf16[1408,192]{0,1:T(8,128)(2,1)S(1)}, u32[]{:S(2)}, u32[]{:S(2)}) %collective-permute-start.2) | collective-permute-done | bytes 540704 | tf_op jit(solution)/shard_map/ppermute | solution.py:27
  36.6 1.2 convolution_convert_fusion.8
  37.9 6.0 %all-to-all-start.1 = ((bf16[8,176,128]{2,1,0:T(8,128)(2,1)}), bf16[8,176,128]{2,1,0:T(8,128)(2,1)S(1)}, u32[]{:S(2)}, u32[]{:S(2)}) async-start(bf16[8,176,128]{2,1,0:T(8,128)(2,1)} %bitcast.13), calls=%async_computation.1 | async-start | bytes 720896 | tf_op jit(solution)/shard_map/all_to_all | solution.py:105
  43.8 4.8 %collective-permute-start.4 = (bf16[2,88,1408]{2,1,0:T(8,128)(2,1)S(1)}, bf16[2,88,1408]{2,1,0:T(8,128)(2,1)}, u32[]{:S(2)}, u32[]{:S(2)}) collective-permute-start(bf16[2,88,1408]{2,1,0:T(8,128)(2,1)S(1)} %bitcast.112), channel_id=1, source_target_pairs={{0,1},{1,0},{2,3},{3,2},{4,5},{5,4},{6,7},{7,6},{8,9},{9,8},{10,11... | collective-permute-start | bytes 1486856 | tf_op jit(solution)/shard_map/ppermute | solution.py:27
  50.4 5.5 %all-to-all-start.2 = ((bf16[8,176,128]{2,1,0:T(8,128)(2,1)}), bf16[8,176,128]{2,1,0:T(8,128)(2,1)}, u32[]{:S(2)}, u32[]{:S(2)}) async-start(bf16[8,176,128]{2,1,0:T(8,128)(2,1)} %broadcast_in_dim.23), calls=%async_computation.2 | async-start | bytes 720896 | tf_op jit(solution)/shard_map/all_to_all | solution.py:37
  56.0 8.3 %collective-permute-done.4 = bf16[2,88,1408]{2,1,0:T(8,128)(2,1)} collective-permute-done((bf16[2,88,1408]{2,1,0:T(8,128)(2,1)S(1)}, bf16[2,88,1408]{2,1,0:T(8,128)(2,1)}, u32[]{:S(2)}, u32[]{:S(2)}) %collective-permute-start.4) | collective-permute-done | bytes 495648 | tf_op jit(solution)/shard_map/ppermute | solution.py:27
  65.4 1.3 convolution_convert_fusion.15
  66.7 1.3 convolution_convert_fusion.14
  68.0 1.9 collective-permute-start.5
  70.0 2.1 collective-permute-start.6
  72.1 1.7 collective-permute-done.6
  73.9 11.5 %all_to_all.60 = bf16[8,176,128]{2,1,0:T(8,128)(2,1)S(1)} all-to-all(bf16[8,176,128]{2,1,0:T(8,128)(2,1)S(1)} %broadcast_in_dim.24), channel_id=1, replica_groups=mesh['section'=32,'tensor'=8,'replica'=2] {'tensor'}, dimensions={0} | all-to-all | bytes 720896 | tf_op jit(solution)/shard_map/all_to_all | solution.py:37
  86.5 10.3 %all_to_all.61 = bf16[8,176,128]{2,1,0:T(8,128)(2,1)S(1)} all-to-all(bf16[8,176,128]{2,1,0:T(8,128)(2,1)S(1)} %bitcast.120), channel_id=1, replica_groups=mesh['section'=32,'tensor'=8,'replica'=2] {'tensor'}, dimensions={0} | all-to-all | bytes 720896 | tf_op jit(solution)/shard_map/all_to_all | solution.py:105
  97.0 10.3 %all_to_all.62 = bf16[8,176,128]{2,1,0:T(8,128)(2,1)S(1)} all-to-all(bf16[8,176,128]{2,1,0:T(8,128)(2,1)S(1)} %broadcast_in_dim.25), channel_id=1, replica_groups=mesh['section'=32,'tensor'=8,'replica'=2] {'tensor'}, dimensions={0} | all-to-all | bytes 720896 | tf_op jit(solution)/shard_map/all_to_all | solution.py:37
  108.1 1.9 collective-permute-start.7
  110.0 11.6 %collective-permute-start.8 = (bf16[176,128]{1,0:T(8,128)(2,1)S(1)}, bf16[176,128]{1,0:T(8,128)(2,1)S(1)}, u32[]{:S(2)}, u32[]{:S(2)}) collective-permute-start(bf16[176,128]{1,0:T(8,128)(2,1)S(1)} %convolution_convert_fusion.13), channel_id=1, source_target_pairs={{256,240},{272,224},{288,208},{304,192},{320,176},{336,160},{352,1... | collective-permute-start | bytes 135176 | tf_op jit(solution)/shard_map/ppermute | solution.py:113
  121.6 1.7 collective-permute-done.8
  124.1 4.8 %all-to-all-start.6 = ((bf16[8,176,128]{2,1,0:T(8,128)(2,1)}), bf16[8,176,128]{2,1,0:T(8,128)(2,1)S(1)}, u32[]{:S(2)}, u32[]{:S(2)}) async-start(bf16[8,176,128]{2,1,0:T(8,128)(2,1)} %broadcast_in_dim.26), calls=%async_computation.6 | async-start | bytes 720896 | tf_op jit(solution)/shard_map/all_to_all | solution.py:37
  129.5 3.9 %collective-permute-start.9 = (bf16[192,128]{1,0:T(8,128)(2,1)}, bf16[192,128]{1,0:T(8,128)(2,1)S(1)}, u32[]{:S(2)}, u32[]{:S(2)}) collective-permute-start(bf16[192,128]{1,0:T(8,128)(2,1)} %get-tuple-element.14), channel_id=1, source_target_pairs={{0,1},{1,0},{2,3},{3,2},{4,5},{5,4},{6,7},{7,6},{8,9},{9,8},{10,11... | collective-permute-start | bytes 147464 | tf_op jit(solution)/shard_map/ppermute | solution.py:27
  133.4 3.5 %collective-permute-start.13 = (bf16[128,1408]{1,0:T(8,128)(2,1)}, bf16[128,1408]{1,0:T(8,128)(2,1)}, u32[]{:S(2)}, u32[]{:S(2)}) collective-permute-start(bf16[128,1408]{1,0:T(8,128)(2,1)} %bitcast.136), channel_id=1, source_target_pairs={{0,1},{1,0},{2,3},{3,2},{4,5},{5,4},{6,7},{7,6},{8,9},{9,8},{10,11... | collective-permute-start | bytes 1081352 | tf_op jit(solution)/shard_map/ppermute | solution.py:27
  138.6 1.2 convolution_convert_fusion.6
  139.8 5.7 %all-to-all-start.7 = ((bf16[8,176,128]{2,1,0:T(8,128)(2,1)}), bf16[8,176,128]{2,1,0:T(8,128)(2,1)S(1)}, u32[]{:S(2)}, u32[]{:S(2)}) async-start(bf16[8,176,128]{2,1,0:T(8,128)(2,1)} %bitcast.119), calls=%async_computation.7 | async-start | bytes 720896 | tf_op jit(solution)/shard_map/all_to_all | solution.py:105
  146.6 4.7 %all-to-all-done.7 = bf16[8,176,128]{2,1,0:T(8,128)(2,1)S(1)} async-done(((bf16[8,176,128]{2,1,0:T(8,128)(2,1)}), bf16[8,176,128]{2,1,0:T(8,128)(2,1)S(1)}, u32[]{:S(2)}, u32[]{:S(2)}) %all-to-all-start.7) | async-done | bytes 360480 | tf_op jit(solution)/shard_map/all_to_all | solution.py:105
  152.1 4.9 %all-to-all-start.8 = ((bf16[8,176,128]{2,1,0:T(8,128)(2,1)}), bf16[8,176,128]{2,1,0:T(8,128)(2,1)S(1)}, u32[]{:S(2)}, u32[]{:S(2)}) async-start(bf16[8,176,128]{2,1,0:T(8,128)(2,1)} %broadcast_in_dim.27), calls=%async_computation.8 | async-start | bytes 720896 | tf_op jit(solution)/shard_map/all_to_all | solution.py:37
  157.7 3.9 %collective-permute-start = (bf16[176,128]{1,0:T(8,128)(2,1)}, bf16[176,128]{1,0:T(8,128)(2,1)}, u32[]{:S(2)}, u32[]{:S(2)}) collective-permute-start(bf16[176,128]{1,0:T(8,128)(2,1)} %bitcast.4), channel_id=1, source_target_pairs={{0,1},{1,0},{2,3},{3,2},{4,5},{5,4},{6,7},{7,6},{8,9},{9,8},{10,11... | collective-permute-start | bytes 135176 | tf_op jit(solution)/shard_map/ppermute | solution.py:27
  163.2 6.8 %collective-permute-start.11 = (bf16[176,128]{1,0:T(8,128)(2,1)S(1)}, bf16[176,128]{1,0:T(8,128)(2,1)S(1)}, u32[]{:S(2)}, u32[]{:S(2)}) collective-permute-start(bf16[176,128]{1,0:T(8,128)(2,1)S(1)} %convolution_convert_fusion.11), channel_id=1, source_target_pairs={{256,240},{272,224},{288,208},{304,192},{320,176},{336,160},{352,1... | collective-permute-start | bytes 135176 | tf_op jit(solution)/shard_map/ppermute | solution.py:113
  170.2 5.3 %collective-permute-start.10 = (bf16[176,128]{1,0:T(8,128)(2,1)S(1)}, bf16[176,128]{1,0:T(8,128)(2,1)S(1)}, u32[]{:S(2)}, u32[]{:S(2)}) collective-permute-start(bf16[176,128]{1,0:T(8,128)(2,1)S(1)} %convolution_convert_fusion.10), channel_id=1, source_target_pairs={{16,0},{32,16},{48,32},{64,48},{80,64},{96,80},{112,96},{128,112},... | collective-permute-start | bytes 135176 | tf_op jit(solution)/shard_map/ppermute | solution.py:119
  175.6 2.2 convolution_convert_fusion.5
  177.8 4.0 %collective-permute-start.12 = (bf16[1408,128]{0,1:T(8,128)(2,1)}, bf16[1408,128]{0,1:T(8,128)(2,1)}, u32[]{:S(2)}, u32[]{:S(2)}) collective-permute-start(bf16[1408,128]{0,1:T(8,128)(2,1)} %convolution_convert_fusion.5), channel_id=1, source_target_pairs={{0,1},{1,0},{2,3},{3,2},{4,5},{5,4},{6,7},{7,6},{8,9},{9,8},{10,11... | collective-permute-start | bytes 1081352 | tf_op jit(solution)/shard_map/ppermute | solution.py:27
  182.6 4.7 %all-to-all-start.9 = ((bf16[8,176,128]{2,1,0:T(8,128)(2,1)}), bf16[8,176,128]{2,1,0:T(8,128)(2,1)S(1)}, u32[]{:S(2)}, u32[]{:S(2)}) async-start(bf16[8,176,128]{2,1,0:T(8,128)(2,1)} %broadcast_in_dim.28), calls=%async_computation.9 | async-start | bytes 720896 | tf_op jit(solution)/shard_map/all_to_all | solution.py:37
  187.4 3.7 %collective-permute-start.1 = (s32[128]{0:T(128)S(1)}, s32[128]{0:T(128)S(1)}, u32[]{:S(2)}, u32[]{:S(2)}) collective-permute-start(s32[128]{0:T(128)S(1)} %slice_bitcast_fusion), channel_id=1, source_target_pairs={{0,1},{1,0},{2,3},{3,2},{4,5},{5,4},{6,7},{7,6},{8,9},{9,8},{10,11... | collective-permute-start | bytes 1544 | tf_op jit(solution)/shard_map/ppermute | solution.py:27
  191.9 3.6 %collective-permute-done.12 = bf16[1408,128]{0,1:T(8,128)(2,1)} collective-permute-done((bf16[1408,128]{0,1:T(8,128)(2,1)}, bf16[1408,128]{0,1:T(8,128)(2,1)}, u32[]{:S(2)}, u32[]{:S(2)}) %collective-permute-start.12) | collective-permute-done | bytes 360480 | tf_op jit(solution)/shard_map/ppermute | solution.py:27
  196.8 1.2 convolution_convert_fusion.4
  198.0 4.9 %all-to-all-start.10 = ((bf16[8,176,128]{2,1,0:T(8,128)(2,1)}), bf16[8,176,128]{2,1,0:T(8,128)(2,1)S(1)}, u32[]{:S(2)}, u32[]{:S(2)}) async-start(bf16[8,176,128]{2,1,0:T(8,128)(2,1)} %bitcast.32), calls=%async_computation.10 | async-start | bytes 720896 | tf_op jit(solution)/shard_map/all_to_all | solution.py:105
  202.9 1.6 broadcast_select_fusion.3
  204.5 1.4 convolution_convert_fusion.3
  205.9 4.4 %collective-permute-start.15 = (bf16[1408,128]{0,1:T(8,128)(2,1)}, bf16[1408,128]{0,1:T(8,128)(2,1)S(1)}, u32[]{:S(2)}, u32[]{:S(2)}) collective-permute-start(bf16[1408,128]{0,1:T(8,128)(2,1)} %convolution_convert_fusion.3), channel_id=1, source_target_pairs={{0,1},{1,0},{2,3},{3,2},{4,5},{5,4},{6,7},{7,6},{8,9},{9,8},{10,11... | collective-permute-start | bytes 1081352 | tf_op jit(solution)/shard_map/ppermute | solution.py:27
  211.4 5.9 %all-to-all-start.11 = ((bf16[16,176,128]{2,1,0:T(8,128)(2,1)}), bf16[16,176,128]{2,1,0:T(8,128)(2,1)S(1)}, u32[]{:S(2)}, u32[]{:S(2)}) async-start(bf16[16,176,128]{2,1,0:T(8,128)(2,1)} %broadcast_in_dim.29), calls=%async_computation.11 | async-start | bytes 1441792 | tf_op jit(solution)/shard_map/all_to_all | solution.py:37
  217.7 5.0 %collective-permute-start.14 = (bf16[192,128]{1,0:T(8,128)(2,1)S(1)}, bf16[192,128]{1,0:T(8,128)(2,1)S(1)}, u32[]{:S(2)}, u32[]{:S(2)}) collective-permute-start(bf16[192,128]{1,0:T(8,128)(2,1)S(1)} %get-tuple-element.27), channel_id=1, source_target_pairs={{0,1},{1,0},{2,3},{3,2},{4,5},{5,4},{6,7},{7,6},{8,9},{9,8},{10,11... | collective-permute-start | bytes 147464 | tf_op jit(solution)/shard_map/ppermute | solution.py:27
  222.8 6.6 %collective-permute-done.14 = bf16[192,128]{1,0:T(8,128)(2,1)S(1)} collective-permute-done((bf16[192,128]{1,0:T(8,128)(2,1)S(1)}, bf16[192,128]{1,0:T(8,128)(2,1)S(1)}, u32[]{:S(2)}, u32[]{:S(2)}) %collective-permute-start.14) | collective-permute-done | bytes 49184 | tf_op jit(solution)/shard_map/ppermute | solution.py:27
  229.4 2.1 fusion.1
  231.5 2.1 fusion
  235.6 2.4 convolution_convert_fusion.2
  (138 shorter events, 22.2 us)
Async XLA Ops:
  0.6 21.1 %copy-start.6 = (bf16[1,192,1408]{2,1,0:T(8,128)(2,1)S(1)}, bf16[1,192,1408]{2,1,0:T(8,128)(2,1)}, u32[]{:S(2)}) copy-start(bf16[1,192,1408]{2,1,0:T(8,128)(2,1)} %param.15) | copy-start | bytes 1622020
  0.6 21.1 %collective-permute-start.3 = (bf16[192,1408]{1,0:T(8,128)(2,1)}, bf16[192,1408]{1,0:T(8,128)(2,1)S(1)}, u32[]{:S(2)}, u32[]{:S(2)}) collective-permute-start(bf16[192,1408]{1,0:T(8,128)(2,1)} %bitcast.110), channel_id=1, source_target_pairs={{0,1},{1,0},{2,3},{3,2},{4,5},{5,4},{6,7},{7,6},{8,9},{9,8},{10,11... | collective-permute-start | bytes 1622024 | tf_op jit(solution)/shard_map/ppermute | solution.py:27
  5.9 27.5 %collective-permute-start.2 = (bf16[1408,192]{0,1:T(8,128)(2,1)}, bf16[1408,192]{0,1:T(8,128)(2,1)S(1)}, u32[]{:S(2)}, u32[]{:S(2)}) collective-permute-start(bf16[1408,192]{0,1:T(8,128)(2,1)} %bitcast.130), channel_id=1, source_target_pairs={{0,1},{1,0},{2,3},{3,2},{4,5},{5,4},{6,7},{7,6},{8,9},{9,8},{10,11... | collective-permute-start | bytes 1622024 | tf_op jit(solution)/shard_map/ppermute | solution.py:27
  9.7 25.6 %all-to-all-start = ((bf16[8,176,128]{2,1,0:T(8,128)(2,1)}), bf16[8,176,128]{2,1,0:T(8,128)(2,1)S(1)}, u32[]{:S(2)}, u32[]{:S(2)}) async-start(bf16[8,176,128]{2,1,0:T(8,128)(2,1)} %broadcast_in_dim.22), calls=%async_computation | async-start | bytes 720896 | tf_op jit(solution)/shard_map/all_to_all | solution.py:37
  15.6 17.8 %copy-start.23 = (bf16[1,1408,192]{1,2,0:T(8,128)(2,1)S(1)}, bf16[1,1408,192]{1,2,0:T(8,128)(2,1)}, u32[]{:S(2)}) copy-start(bf16[1,1408,192]{1,2,0:T(8,128)(2,1)} %param.14) | copy-start | bytes 1622020
  15.6 17.8 %copy-start.33 = (bf16[1,128,1408]{2,1,0:T(8,128)(2,1)S(1)}, bf16[1,128,1408]{2,1,0:T(8,128)(2,1)}, u32[]{:S(2)}) copy-start(bf16[1,128,1408]{2,1,0:T(8,128)(2,1)} %param.9) | copy-start | bytes 1081348
  21.8 12.7 %copy-start.22 = (s32[1,4,128]{2,1,0:T(4,128)S(1)}, s32[1,4,128]{2,1,0:T(4,128)}, u32[]{:S(2)}) copy-start(s32[1,4,128]{2,1,0:T(4,128)} %param.10) | copy-start | bytes 6148
  35.3 2.6 %copy-start = (bf16[8,176,128]{2,1,0:T(8,128)(2,1)}, bf16[8,176,128]{2,1,0:T(8,128)(2,1)S(1)}, u32[]{:S(2)}) copy-start(bf16[8,176,128]{2,1,0:T(8,128)(2,1)S(1)} %all-to-all-done) | copy-start | bytes 1081348
  36.6 7.2 %copy-start.7 = (bf16[1,2,88,1408]{3,2,1,0:T(8,128)(2,1)S(1)}, bf16[1,2,88,1408]{3,2,1,0:T(8,128)(2,1)}, u32[]{:S(2)}) copy-start(bf16[1,2,88,1408]{3,2,1,0:T(8,128)(2,1)} %param.13) | copy-start | bytes 1486852
  37.9 11.8 %copy-start.10 = (bf16[1,128,176]{1,2,0:T(8,128)(2,1)S(1)}, bf16[1,128,176]{1,2,0:T(8,128)(2,1)}, u32[]{:S(2)}) copy-start(bf16[1,128,176]{1,2,0:T(8,128)(2,1)} %param.11) | copy-start | bytes 135172
  37.9 11.7 %all-to-all-start.1 = ((bf16[8,176,128]{2,1,0:T(8,128)(2,1)}), bf16[8,176,128]{2,1,0:T(8,128)(2,1)S(1)}, u32[]{:S(2)}, u32[]{:S(2)}) async-start(bf16[8,176,128]{2,1,0:T(8,128)(2,1)} %bitcast.13), calls=%async_computation.1 | async-start | bytes 720896 | tf_op jit(solution)/shard_map/all_to_all | solution.py:105
  43.8 20.4 %collective-permute-start.4 = (bf16[2,88,1408]{2,1,0:T(8,128)(2,1)S(1)}, bf16[2,88,1408]{2,1,0:T(8,128)(2,1)}, u32[]{:S(2)}, u32[]{:S(2)}) collective-permute-start(bf16[2,88,1408]{2,1,0:T(8,128)(2,1)S(1)} %bitcast.112), channel_id=1, source_target_pairs={{0,1},{1,0},{2,3},{3,2},{4,5},{5,4},{6,7},{7,6},{8,9},{9,8},{10,11... | collective-permute-start | bytes 1486856 | tf_op jit(solution)/shard_map/ppermute | solution.py:27
  50.4 15.0 %all-to-all-start.2 = ((bf16[8,176,128]{2,1,0:T(8,128)(2,1)}), bf16[8,176,128]{2,1,0:T(8,128)(2,1)}, u32[]{:S(2)}, u32[]{:S(2)}) async-start(bf16[8,176,128]{2,1,0:T(8,128)(2,1)} %broadcast_in_dim.23), calls=%async_computation.2 | async-start | bytes 720896 | tf_op jit(solution)/shard_map/all_to_all | solution.py:37
  66.7 7.1 %copy-start.11 = (bf16[3,128,176]{1,2,0:T(8,128)(2,1)S(1)}, bf16[3,128,176]{1,2,0:T(8,128)(2,1)}, u32[]{:S(2)}) copy-start(bf16[3,128,176]{1,2,0:T(8,128)(2,1)} %param.12) | copy-start | bytes 405508
  68.0 4.0 %collective-permute-start.5 = (bf16[176,128]{1,0:T(8,128)(2,1)S(1)}, bf16[176,128]{1,0:T(8,128)(2,1)S(1)}, u32[]{:S(2)}, u32[]{:S(2)}) collective-permute-start(bf16[176,128]{1,0:T(8,128)(2,1)S(1)} %convolution_convert_fusion.14), channel_id=1, source_target_pairs={{16,0},{32,16},{48,32},{64,48},{80,64},{96,80},{112,96},{128,112},... | collective-permute-start | bytes 135176 | tf_op jit(solution)/shard_map/ppermute | solution.py:119
  70.0 3.8 %collective-permute-start.6 = (bf16[176,128]{1,0:T(8,128)(2,1)S(1)}, bf16[176,128]{1,0:T(8,128)(2,1)S(1)}, u32[]{:S(2)}, u32[]{:S(2)}) collective-permute-start(bf16[176,128]{1,0:T(8,128)(2,1)S(1)} %convolution_convert_fusion.15), channel_id=1, source_target_pairs={{256,240},{272,224},{288,208},{304,192},{320,176},{336,160},{352,1... | collective-permute-start | bytes 135176 | tf_op jit(solution)/shard_map/ppermute | solution.py:113
  73.8 12.0 %copy-start.25 = (bf16[1,1408,192]{1,2,0:T(8,128)(2,1)S(1)}, bf16[1,1408,192]{1,2,0:T(8,128)(2,1)}, u32[]{:S(2)}) copy-start(bf16[1,1408,192]{1,2,0:T(8,128)(2,1)} %param.14) | copy-start | bytes 1622020
  73.9 12.0 %copy-start.30 = (bf16[1408,192]{0,1:T(8,128)(2,1)S(1)}, bf16[1408,192]{0,1:T(8,128)(2,1)}, u32[]{:S(2)}) copy-start(bf16[1408,192]{0,1:T(8,128)(2,1)} %copy-done.28) | copy-start | bytes 1622020
  107.6 21.3 %copy-start.13 = (bf16[384,128]{1,0:T(8,128)(2,1)S(1)}, bf16[384,128]{1,0:T(8,128)(2,1)}, u32[]{:S(2)}) copy-start(bf16[384,128]{1,0:T(8,128)(2,1)} %get-tuple-element.32) | copy-start | bytes 294916
  108.1 13.5 %collective-permute-start.7 = (bf16[176,128]{1,0:T(8,128)(2,1)S(1)}, bf16[176,128]{1,0:T(8,128)(2,1)S(1)}, u32[]{:S(2)}, u32[]{:S(2)}) collective-permute-start(bf16[176,128]{1,0:T(8,128)(2,1)S(1)} %convolution_convert_fusion.12), channel_id=1, source_target_pairs={{16,0},{32,16},{48,32},{64,48},{80,64},{96,80},{112,96},{128,112},... | collective-permute-start | bytes 135176 | tf_op jit(solution)/shard_map/ppermute | solution.py:119
  110.0 13.3 %collective-permute-start.8 = (bf16[176,128]{1,0:T(8,128)(2,1)S(1)}, bf16[176,128]{1,0:T(8,128)(2,1)S(1)}, u32[]{:S(2)}, u32[]{:S(2)}) collective-permute-start(bf16[176,128]{1,0:T(8,128)(2,1)S(1)} %convolution_convert_fusion.13), channel_id=1, source_target_pairs={{256,240},{272,224},{288,208},{304,192},{320,176},{336,160},{352,1... | collective-permute-start | bytes 135176 | tf_op jit(solution)/shard_map/ppermute | solution.py:113
  124.1 13.1 %all-to-all-start.6 = ((bf16[8,176,128]{2,1,0:T(8,128)(2,1)}), bf16[8,176,128]{2,1,0:T(8,128)(2,1)S(1)}, u32[]{:S(2)}, u32[]{:S(2)}) async-start(bf16[8,176,128]{2,1,0:T(8,128)(2,1)} %broadcast_in_dim.26), calls=%async_computation.6 | async-start | bytes 720896 | tf_op jit(solution)/shard_map/all_to_all | solution.py:37
  129.5 7.7 %collective-permute-start.9 = (bf16[192,128]{1,0:T(8,128)(2,1)}, bf16[192,128]{1,0:T(8,128)(2,1)S(1)}, u32[]{:S(2)}, u32[]{:S(2)}) collective-permute-start(bf16[192,128]{1,0:T(8,128)(2,1)} %get-tuple-element.14), channel_id=1, source_target_pairs={{0,1},{1,0},{2,3},{3,2},{4,5},{5,4},{6,7},{7,6},{8,9},{9,8},{10,11... | collective-permute-start | bytes 147464 | tf_op jit(solution)/shard_map/ppermute | solution.py:27
  133.4 89.4 %collective-permute-start.13 = (bf16[128,1408]{1,0:T(8,128)(2,1)}, bf16[128,1408]{1,0:T(8,128)(2,1)}, u32[]{:S(2)}, u32[]{:S(2)}) collective-permute-start(bf16[128,1408]{1,0:T(8,128)(2,1)} %bitcast.136), channel_id=1, source_target_pairs={{0,1},{1,0},{2,3},{3,2},{4,5},{5,4},{6,7},{7,6},{8,9},{9,8},{10,11... | collective-permute-start | bytes 1081352 | tf_op jit(solution)/shard_map/ppermute | solution.py:27
  137.2 2.6 %copy-start.35 = (bf16[192,128]{1,0:T(8,128)(2,1)}, bf16[192,128]{1,0:T(8,128)(2,1)S(1)}, u32[]{:S(2)}) copy-start(bf16[192,128]{1,0:T(8,128)(2,1)S(1)} %collective-permute-done.9) | copy-start | bytes 147460
  137.2 2.6 %copy-start.4 = (bf16[8,176,128]{2,1,0:T(8,128)(2,1)}, bf16[8,176,128]{2,1,0:T(8,128)(2,1)S(1)}, u32[]{:S(2)}) copy-start(bf16[8,176,128]{2,1,0:T(8,128)(2,1)S(1)} %all-to-all-done.6) | copy-start | bytes 1081348
  139.8 11.5 %all-to-all-start.7 = ((bf16[8,176,128]{2,1,0:T(8,128)(2,1)}), bf16[8,176,128]{2,1,0:T(8,128)(2,1)S(1)}, u32[]{:S(2)}, u32[]{:S(2)}) async-start(bf16[8,176,128]{2,1,0:T(8,128)(2,1)} %bitcast.119), calls=%async_computation.7 | async-start | bytes 720896 | tf_op jit(solution)/shard_map/all_to_all | solution.py:105
  152.1 10.7 %all-to-all-start.8 = ((bf16[8,176,128]{2,1,0:T(8,128)(2,1)}), bf16[8,176,128]{2,1,0:T(8,128)(2,1)S(1)}, u32[]{:S(2)}, u32[]{:S(2)}) async-start(bf16[8,176,128]{2,1,0:T(8,128)(2,1)} %broadcast_in_dim.27), calls=%async_computation.8 | async-start | bytes 720896 | tf_op jit(solution)/shard_map/all_to_all | solution.py:37
  157.7 45.2 %collective-permute-start = (bf16[176,128]{1,0:T(8,128)(2,1)}, bf16[176,128]{1,0:T(8,128)(2,1)}, u32[]{:S(2)}, u32[]{:S(2)}) collective-permute-start(bf16[176,128]{1,0:T(8,128)(2,1)} %bitcast.4), channel_id=1, source_target_pairs={{0,1},{1,0},{2,3},{3,2},{4,5},{5,4},{6,7},{7,6},{8,9},{9,8},{10,11... | collective-permute-start | bytes 135176 | tf_op jit(solution)/shard_map/ppermute | solution.py:27
  161.6 14.0 %copy-start.12 = (pred[128,512]{1,0:T(32,128)(4,1)}, pred[128,512]{1,0:T(32,128)(4,1)S(1)}, u32[]{:S(2)}) copy-start(pred[128,512]{1,0:T(32,128)(4,1)S(1)} %iota_compare_fusion) | copy-start | bytes 196612
  163.1 12.4 %copy-start.9 = (bf16[8,176,128]{2,1,0:T(8,128)(2,1)S(1)}, bf16[8,176,128]{2,1,0:T(8,128)(2,1)}, u32[]{:S(2)}) copy-start(bf16[8,176,128]{2,1,0:T(8,128)(2,1)} %copy-done.8) | copy-start | bytes 1081348
  163.2 18.6 %collective-permute-start.11 = (bf16[176,128]{1,0:T(8,128)(2,1)S(1)}, bf16[176,128]{1,0:T(8,128)(2,1)S(1)}, u32[]{:S(2)}, u32[]{:S(2)}) collective-permute-start(bf16[176,128]{1,0:T(8,128)(2,1)S(1)} %convolution_convert_fusion.11), channel_id=1, source_target_pairs={{256,240},{272,224},{288,208},{304,192},{320,176},{336,160},{352,1... | collective-permute-start | bytes 135176 | tf_op jit(solution)/shard_map/ppermute | solution.py:113
  170.2 11.6 %collective-permute-start.10 = (bf16[176,128]{1,0:T(8,128)(2,1)S(1)}, bf16[176,128]{1,0:T(8,128)(2,1)S(1)}, u32[]{:S(2)}, u32[]{:S(2)}) collective-permute-start(bf16[176,128]{1,0:T(8,128)(2,1)S(1)} %convolution_convert_fusion.10), channel_id=1, source_target_pairs={{16,0},{32,16},{48,32},{64,48},{80,64},{96,80},{112,96},{128,112},... | collective-permute-start | bytes 135176 | tf_op jit(solution)/shard_map/ppermute | solution.py:119
  177.8 17.8 %collective-permute-start.12 = (bf16[1408,128]{0,1:T(8,128)(2,1)}, bf16[1408,128]{0,1:T(8,128)(2,1)}, u32[]{:S(2)}, u32[]{:S(2)}) collective-permute-start(bf16[1408,128]{0,1:T(8,128)(2,1)} %convolution_convert_fusion.5), channel_id=1, source_target_pairs={{0,1},{1,0},{2,3},{3,2},{4,5},{5,4},{6,7},{7,6},{8,9},{9,8},{10,11... | collective-permute-start | bytes 1081352 | tf_op jit(solution)/shard_map/ppermute | solution.py:27
  182.6 12.9 %all-to-all-start.9 = ((bf16[8,176,128]{2,1,0:T(8,128)(2,1)}), bf16[8,176,128]{2,1,0:T(8,128)(2,1)S(1)}, u32[]{:S(2)}, u32[]{:S(2)}) async-start(bf16[8,176,128]{2,1,0:T(8,128)(2,1)} %broadcast_in_dim.28), calls=%async_computation.9 | async-start | bytes 720896 | tf_op jit(solution)/shard_map/all_to_all | solution.py:37
  187.4 15.5 %collective-permute-start.1 = (s32[128]{0:T(128)S(1)}, s32[128]{0:T(128)S(1)}, u32[]{:S(2)}, u32[]{:S(2)}) collective-permute-start(s32[128]{0:T(128)S(1)} %slice_bitcast_fusion), channel_id=1, source_target_pairs={{0,1},{1,0},{2,3},{3,2},{4,5},{5,4},{6,7},{7,6},{8,9},{9,8},{10,11... | collective-permute-start | bytes 1544 | tf_op jit(solution)/shard_map/ppermute | solution.py:27
  196.8 7.7 %copy-start.1 = (bf16[8,176,128]{2,1,0:T(8,128)(2,1)S(1)}, bf16[8,176,128]{2,1,0:T(8,128)(2,1)}, u32[]{:S(2)}) copy-start(bf16[8,176,128]{2,1,0:T(8,128)(2,1)} %copy-done) | copy-start | bytes 1081348
  196.8 7.7 %copy-start.3 = (bf16[8,176,128]{2,1,0:T(8,128)(2,1)S(1)}, bf16[8,176,128]{2,1,0:T(8,128)(2,1)}, u32[]{:S(2)}) copy-start(bf16[8,176,128]{2,1,0:T(8,128)(2,1)} %copy-done.2) | copy-start | bytes 1081348
  196.8 7.7 %copy-start.5 = (bf16[8,176,128]{2,1,0:T(8,128)(2,1)S(1)}, bf16[8,176,128]{2,1,0:T(8,128)(2,1)}, u32[]{:S(2)}) copy-start(bf16[8,176,128]{2,1,0:T(8,128)(2,1)} %copy-done.4) | copy-start | bytes 1081348
  198.0 12.3 %all-to-all-start.10 = ((bf16[8,176,128]{2,1,0:T(8,128)(2,1)}), bf16[8,176,128]{2,1,0:T(8,128)(2,1)S(1)}, u32[]{:S(2)}, u32[]{:S(2)}) async-start(bf16[8,176,128]{2,1,0:T(8,128)(2,1)} %bitcast.32), calls=%async_computation.10 | async-start | bytes 720896 | tf_op jit(solution)/shard_map/all_to_all | solution.py:105
  205.9 25.6 %collective-permute-start.15 = (bf16[1408,128]{0,1:T(8,128)(2,1)}, bf16[1408,128]{0,1:T(8,128)(2,1)S(1)}, u32[]{:S(2)}, u32[]{:S(2)}) collective-permute-start(bf16[1408,128]{0,1:T(8,128)(2,1)} %convolution_convert_fusion.3), channel_id=1, source_target_pairs={{0,1},{1,0},{2,3},{3,2},{4,5},{5,4},{6,7},{7,6},{8,9},{9,8},{10,11... | collective-permute-start | bytes 1081352 | tf_op jit(solution)/shard_map/ppermute | solution.py:27
  210.4 6.9 %copy-start.15 = (bf16[384,128]{0,1:T(8,128)(2,1)S(1)}, bf16[384,128]{0,1:T(8,128)(2,1)}, u32[]{:S(2)}) copy-start(bf16[384,128]{0,1:T(8,128)(2,1)} %copy-done.14) | copy-start | bytes 294916
  210.4 6.9 %copy-start.17 = (bf16[384,128]{0,1:T(8,128)(2,1)S(1)}, bf16[384,128]{0,1:T(8,128)(2,1)}, u32[]{:S(2)}) copy-start(bf16[384,128]{0,1:T(8,128)(2,1)} %copy-done.16) | copy-start | bytes 294916
  210.4 6.9 %copy-start.19 = (bf16[384,128]{0,1:T(8,128)(2,1)S(1)}, bf16[384,128]{0,1:T(8,128)(2,1)}, u32[]{:S(2)}) copy-start(bf16[384,128]{0,1:T(8,128)(2,1)} %copy-done.18) | copy-start | bytes 294916
  211.4 22.2 %all-to-all-start.11 = ((bf16[16,176,128]{2,1,0:T(8,128)(2,1)}), bf16[16,176,128]{2,1,0:T(8,128)(2,1)S(1)}, u32[]{:S(2)}, u32[]{:S(2)}) async-start(bf16[16,176,128]{2,1,0:T(8,128)(2,1)} %broadcast_in_dim.29), calls=%async_computation.11 | async-start | bytes 1441792 | tf_op jit(solution)/shard_map/all_to_all | solution.py:37
  217.7 11.7 %copy-start.34 = (bf16[1,128,1408]{2,1,0:T(8,128)(2,1)S(1)}, bf16[1,128,1408]{2,1,0:T(8,128)(2,1)}, u32[]{:S(2)}) copy-start(bf16[1,128,1408]{2,1,0:T(8,128)(2,1)} %param.9) | copy-start | bytes 1081348
  217.7 11.7 %collective-permute-start.14 = (bf16[192,128]{1,0:T(8,128)(2,1)S(1)}, bf16[192,128]{1,0:T(8,128)(2,1)S(1)}, u32[]{:S(2)}, u32[]{:S(2)}) collective-permute-start(bf16[192,128]{1,0:T(8,128)(2,1)S(1)} %get-tuple-element.27), channel_id=1, source_target_pairs={{0,1},{1,0},{2,3},{3,2},{4,5},{5,4},{6,7},{7,6},{8,9},{9,8},{10,11... | collective-permute-start | bytes 147464 | tf_op jit(solution)/shard_map/ppermute | solution.py:27
  222.8 8.7 %copy-start.36 = (bf16[192,128]{1,0:T(8,128)(2,1)S(1)}, bf16[192,128]{1,0:T(8,128)(2,1)}, u32[]{:S(2)}) copy-start(bf16[192,128]{1,0:T(8,128)(2,1)} %copy-done.35) | copy-start | bytes 147460
  (14 other events, 15.3 us)

commit v8 on v7

--- a/solution.py
+++ b/solution.py
@@ -58,19 +58,15 @@
     up_other = swap(w_up[0])
     down_other = swap(w_down[0])
     proj_other = swap(w_proj[0])
-    mixed_other = swap(pool_mixed[0])
-    ids_other = swap(crop_ids[0, ticks - 1])
 
     chunk = incoming[0].T
     upstream = gather(chunk).reshape(width, rows)
 
     up = jnp.concatenate([w_up[0], up_other], axis=1)
-    (down,) = tied(jnp.concatenate([w_down[0], down_other], axis=0))
     proj = jnp.concatenate(by_replica(w_proj[0], proj_other), axis=1).reshape(-1, width)
 
     places = jnp.arange(pool, dtype=jnp.int32)[:, None]
     pick = (crop_ids[0].reshape(1, -1) == places).astype(bf16)
-    pick_other = (ids_other[None, :] == places).astype(bf16)
 
     def picked(t):
         return pick[:, t * rows : (t + 1) * rows]
@@ -81,16 +77,18 @@
     high = slope.astype(bf16)
     low = (slope - high.astype(f32)).astype(bf16)
     slopes = dot(high, pick) + dot(low, pick)
-
-    decoder = jnp.where(section < half, 0.0, 1.0).astype(bf16)
-    mask = jnp.stack([jnp.ones((), bf16), decoder])[:, None, None]
-    saved = pool_inputs[0].transpose(1, 2, 0) * mask
-    saved_first, saved_second = saved[:, :own_in], saved[:, own_in:]
-    saved_own = jnp.where(first, saved_first, saved_second).reshape(-1, pool)
-    saved_sent = jnp.where(first, saved_second, saved_first).reshape(-1, pool)
-    saved_other = swap(saved_sent)
-    last_own = dot(saved_own, picked(ticks - 1)).astype(bf16)
-    last_other = dot(saved_other, pick_other).astype(bf16)
+    down_own, down_other, slopes = tied(w_down[0], down_other, slopes)
+    (down,) = tied(jnp.concatenate([down_own, down_other], axis=0))
+
+    def small_of(inputs, active_sent, ids_sent):
+        decoder = jnp.where(section < half, 0.0, 1.0).astype(bf16)
+        mask = jnp.stack([jnp.ones((), bf16), decoder])[:, None, None]
+        saved = inputs.transpose(1, 2, 0) * mask
+        saved_first, saved_second = saved[:, :own_in], saved[:, own_in:]
+        saved_own = jnp.where(first, saved_first, saved_second).reshape(-1, pool)
+        saved_sent = jnp.where(first, saved_second, saved_first).reshape(-1, pool)
+        ids = jnp.broadcast_to(ids_sent.astype(bf16)[None], (16, rows))
+        return saved_own, jnp.concatenate([saved_sent, active_sent, ids], axis=0)
 
     hiddens, grads, upstreams = [], [], []
     for t in range(ticks):
@@ -100,6 +98,7 @@
         hiddens.append(hidden)
         partial = dot(up, hidden).astype(bf16)
         if t + 1 == ticks:
+            upstreams[-1], _ = tied(upstream, partial)
             seen = dot(jnp.concatenate(upstreams, axis=1), pick, 1, 1).astype(bf16)
             seen_other = swap(seen)
         terms = lax.all_to_all(partial.reshape(parts, chunk_rows, rows), "tensor", 0, 0)
@@ -121,20 +120,40 @@
                 "section",
                 [(i, i - 1) for i in range(1, sections)],
             )
-            if t + 3 == ticks:
-                active_sent, _ = tied(active[units:], skip_grad)
-                sent = swap(active_sent)
+            if t == 0:
+                mixed_sent, _ = tied(pool_mixed[0], skip_grad)
+                sent = swap(mixed_sent)
+            elif t + 3 == ticks:
+                inputs, active_late, ids_late, _ = tied(
+                    pool_inputs[0], active, crop_ids, skip_grad
+                )
+                saved_own, small = small_of(
+                    inputs, active_late[units:], ids_late[0, ticks - 1]
+                )
+                small_other = swap(small)
             elif t + 2 == ticks:
-                early = dot(jnp.concatenate(grads, axis=1), pick[:, : (t + 1) * rows], 1, 1)
+                ids_late, _ = tied(crop_ids, skip_grad)
+                picks = (ids_late[0, : t + 1].reshape(1, -1) == places).astype(bf16)
+                early = dot(jnp.concatenate(grads, axis=1), picks, 1, 1)
                 early = early.astype(bf16)
                 sent = swap(early)
             summed = (above.astype(f32) + mirrored.astype(f32)).astype(bf16)
             chunk = jnp.where(is_top, loss_grads[t].T, summed)
+            if t + 3 == ticks:
+                chunk, small_other = tied(chunk, small_other)
             upstream = gather(chunk).reshape(width, rows)
-            if t + 3 == ticks:
-                upstream, active_other = tied(upstream, sent)
+            if t == 0:
+                upstream, mixed_other = tied(upstream, sent)
             elif t + 2 == ticks:
                 upstream, early_other = tied(upstream, sent)
+                upstream, saved_own, small_other = tied(upstream, saved_own, small_other)
+                count = saved_own.shape[0]
+                saved_other = small_other[:count]
+                active_other = small_other[count : count + units]
+                ids_other = small_other[count + units].astype(jnp.int32)
+                pick_other = (ids_other[None, :] == places).astype(bf16)
+                last_own = dot(saved_own, picked(ticks - 1)).astype(bf16)
+                last_other = dot(saved_other, pick_other).astype(bf16)
         else:
             spread = dot(jnp.concatenate(hiddens, axis=1), pick, 1, 1).astype(bf16)
             spread_other = swap(spread[units:])

time: 240 us -> 236 us (0.983)
  the two profiles are of different devices: /device:TPU:354 before, /device:TPU:96 now
where the time goes in v8:
time: 236 us; the launch traced here: 234 us
  starting transfers between devices  73.2 us (31%)
  waiting for transfers between devices  67.1 us (28%)
  blocking collectives  54.9 us (23%)
  matrix products  24.3 us (10%)
  local copies, waits for them, and re-layouts  8.78 us (4%)
  other arithmetic  4.31 us (2%)
    all_to_all x3, blocking collectives, gather(): return lax.all_to_all(spread, axes, 0, 0)  34.2 us
    ppermute x8, starting transfers between devices, swap(): return lax.ppermute(x, 'replica', [(0, 1), (1, 0)])  31.1 us
    ppermute x8, waiting for transfers between devices, swap(): return lax.ppermute(x, 'replica', [(0, 1), (1, 0)])  26.6 us
    dot_general x27, matrix products, dot(): lax.dot_general(a, b, (((ca,), (cb,)), ((), ())), preferred_element_type=...  24.3 us
    all_to_all x5, starting transfers between devices, gather(): return lax.all_to_all(spread, axes, 0, 0)  23.8 us
    all_to_all x5, waiting for transfers between devices, gather(): return lax.all_to_all(spread, axes, 0, 0)  23.1 us
    all_to_all x2, blocking collectives, body(): lax.all_to_all(partial.reshape(parts, chunk_rows, rows), 'tensor', 0, 0)  20.7 us
    ppermute x3, waiting for transfers between devices, body(): lax.ppermute(skip_grad, 'section', [(i, sections - 1 - i) for i in range(...  14.4 us
  transfers between devices with their start and end apart: 21, of which 13 were waited for; matrix products, arithmetic and copies ran while one was open for 8% of the time, Pallas kernels for 0%

profile of v8, /device:TPU:96, one launch (start us, length us, event | category | flops | bytes accessed | tf_op | source)
XLA Modules:
  0.0 234.0 jit_solution(7951580866364295378)
XLA Ops:
  0.7 5.2 %collective-permute-start.1 = (bf16[1408,192]{0,1:T(8,128)(2,1)}, bf16[1408,192]{0,1:T(8,128)(2,1)S(1)}, u32[]{:S(2)}, u32[]{:S(2)}) collective-permute-start(bf16[1408,192]{0,1:T(8,128)(2,1)} %bitcast.131), channel_id=1, source_target_pairs={{0,1},{1,0},{2,3},{3,2},{4,5},{5,4},{6,7},{7,6},{8,9},{9,8},{10,11... | collective-permute-start | bytes 1622024 | tf_op jit(solution)/shard_map/ppermute | solution.py:27
  5.9 2.2 collective-permute-start.2
  8.2 1.6 broadcast_in_dim.24
  9.7 5.3 %all-to-all-start = ((bf16[8,176,128]{2,1,0:T(8,128)(2,1)}), bf16[8,176,128]{2,1,0:T(8,128)(2,1)S(1)}, u32[]{:S(2)}, u32[]{:S(2)}) async-start(bf16[8,176,128]{2,1,0:T(8,128)(2,1)} %broadcast_in_dim.24), calls=%async_computation | async-start | bytes 720896 | tf_op jit(solution)/shard_map/all_to_all | solution.py:37
  15.0 6.7 %collective-permute-done.1 = bf16[1408,192]{0,1:T(8,128)(2,1)S(1)} collective-permute-done((bf16[1408,192]{0,1:T(8,128)(2,1)}, bf16[1408,192]{0,1:T(8,128)(2,1)S(1)}, u32[]{:S(2)}, u32[]{:S(2)}) %collective-permute-start.1) | collective-permute-done | bytes 540704 | tf_op jit(solution)/shard_map/ppermute | solution.py:27
  23.2 10.2 %collective-permute-done.2 = bf16[192,1408]{1,0:T(8,128)(2,1)S(1)} collective-permute-done((bf16[192,1408]{1,0:T(8,128)(2,1)}, bf16[192,1408]{1,0:T(8,128)(2,1)S(1)}, u32[]{:S(2)}, u32[]{:S(2)}) %collective-permute-start.2) | collective-permute-done | bytes 540704 | tf_op jit(solution)/shard_map/ppermute | solution.py:27
  35.5 1.2 convolution_convert_fusion.8
  36.8 5.2 %all-to-all-start.1 = ((bf16[8,176,128]{2,1,0:T(8,128)(2,1)}), bf16[8,176,128]{2,1,0:T(8,128)(2,1)S(1)}, u32[]{:S(2)}, u32[]{:S(2)}) async-start(bf16[8,176,128]{2,1,0:T(8,128)(2,1)} %bitcast.15), calls=%async_computation.1 | async-start | bytes 720896 | tf_op jit(solution)/shard_map/all_to_all | solution.py:104
  42.0 4.3 %collective-permute-start = (bf16[2,88,1408]{2,1,0:T(8,128)(2,1)S(1)}, bf16[2,88,1408]{2,1,0:T(8,128)(2,1)}, u32[]{:S(2)}, u32[]{:S(2)}) collective-permute-start(bf16[2,88,1408]{2,1,0:T(8,128)(2,1)S(1)} %bitcast.111), channel_id=1, source_target_pairs={{0,1},{1,0},{2,3},{3,2},{4,5},{5,4},{6,7},{7,6},{8,9},{9,8},{10,11... | collective-permute-start | bytes 1486856 | tf_op jit(solution)/shard_map/ppermute | solution.py:27
  46.3 3.0 %all-to-all-done.1 = bf16[8,176,128]{2,1,0:T(8,128)(2,1)S(1)} async-done(((bf16[8,176,128]{2,1,0:T(8,128)(2,1)}), bf16[8,176,128]{2,1,0:T(8,128)(2,1)S(1)}, u32[]{:S(2)}, u32[]{:S(2)}) %all-to-all-start.1) | async-done | bytes 360480 | tf_op jit(solution)/shard_map/all_to_all | solution.py:104
  50.2 4.1 %all-to-all-start.2 = ((bf16[8,176,128]{2,1,0:T(8,128)(2,1)}), bf16[8,176,128]{2,1,0:T(8,128)(2,1)}, u32[]{:S(2)}, u32[]{:S(2)}) async-start(bf16[8,176,128]{2,1,0:T(8,128)(2,1)} %broadcast_in_dim.25), calls=%async_computation.2 | async-start | bytes 720896 | tf_op jit(solution)/shard_map/all_to_all | solution.py:37
  54.3 8.8 %collective-permute-done = bf16[2,88,1408]{2,1,0:T(8,128)(2,1)} collective-permute-done((bf16[2,88,1408]{2,1,0:T(8,128)(2,1)S(1)}, bf16[2,88,1408]{2,1,0:T(8,128)(2,1)}, u32[]{:S(2)}, u32[]{:S(2)}) %collective-permute-start) | collective-permute-done | bytes 495648 | tf_op jit(solution)/shard_map/ppermute | solution.py:27
  63.0 1.1 broadcast_select_fusion
  64.2 1.5 convolution_convert_fusion.17
  65.7 1.3 convolution_convert_fusion.16
  67.0 1.9 collective-permute-start.3
  68.9 1.3 collective-permute-start.4
  70.2 3.5 %collective-permute-start.5 = (bf16[128,1408]{1,0:T(8,128)(2,1)}, bf16[128,1408]{1,0:T(8,128)(2,1)S(1)}, u32[]{:S(2)}, u32[]{:S(2)}) collective-permute-start(bf16[128,1408]{1,0:T(8,128)(2,1)} %bitcast.137), channel_id=1, source_target_pairs={{0,1},{1,0},{2,3},{3,2},{4,5},{5,4},{6,7},{7,6},{8,9},{9,8},{10,11... | collective-permute-start | bytes 1081352 | tf_op jit(solution)/shard_map/ppermute | solution.py:27
  73.7 8.3 %collective-permute-done.4 = bf16[176,128]{1,0:T(8,128)(2,1)S(1)} collective-permute-done((bf16[176,128]{1,0:T(8,128)(2,1)S(1)}, bf16[176,128]{1,0:T(8,128)(2,1)S(1)}, u32[]{:S(2)}, u32[]{:S(2)}) %collective-permute-start.4) | collective-permute-done | bytes 45088 | tf_op jit(solution)/shard_map/ppermute | solution.py:112
  82.1 12.6 %all_to_all.60 = bf16[8,176,128]{2,1,0:T(8,128)(2,1)S(1)} all-to-all(bf16[8,176,128]{2,1,0:T(8,128)(2,1)S(1)} %broadcast_in_dim.26), channel_id=1, replica_groups=mesh['section'=32,'tensor'=8,'replica'=2] {'tensor'}, dimensions={0} | all-to-all | bytes 720896 | tf_op jit(solution)/shard_map/all_to_all | solution.py:37
  96.7 10.3 %all_to_all.61 = bf16[8,176,128]{2,1,0:T(8,128)(2,1)S(1)} all-to-all(bf16[8,176,128]{2,1,0:T(8,128)(2,1)S(1)} %bitcast.118), channel_id=1, replica_groups=mesh['section'=32,'tensor'=8,'replica'=2] {'tensor'}, dimensions={0} | all-to-all | bytes 720896 | tf_op jit(solution)/shard_map/all_to_all | solution.py:104
  107.9 3.6 %all-to-all-start.5 = ((bf16[8,176,128]{2,1,0:T(8,128)(2,1)}), bf16[8,176,128]{2,1,0:T(8,128)(2,1)S(1)}, u32[]{:S(2)}, u32[]{:S(2)}) async-start(bf16[8,176,128]{2,1,0:T(8,128)(2,1)} %broadcast_in_dim.27), calls=%async_computation.5 | async-start | bytes 720896 | tf_op jit(solution)/shard_map/all_to_all | solution.py:37
  111.6 7.2 %all-to-all-done.5 = bf16[8,176,128]{2,1,0:T(8,128)(2,1)S(1)} async-done(((bf16[8,176,128]{2,1,0:T(8,128)(2,1)}), bf16[8,176,128]{2,1,0:T(8,128)(2,1)S(1)}, u32[]{:S(2)}, u32[]{:S(2)}) %all-to-all-start.5) | async-done | bytes 360480 | tf_op jit(solution)/shard_map/all_to_all | solution.py:37
  119.1 1.3 collective-permute-start.7
  120.8 1.9 collective-permute-start.6
  122.8 4.2 %collective-permute-start.8 = (bf16[384,128]{1,0:T(8,128)(2,1)S(1)}, bf16[384,128]{1,0:T(8,128)(2,1)S(1)}, u32[]{:S(2)}, u32[]{:S(2)}) collective-permute-start(bf16[384,128]{1,0:T(8,128)(2,1)S(1)} %pad_maximum_fusion.3), channel_id=1, source_target_pairs={{0,1},{1,0},{2,3},{3,2},{4,5},{5,4},{6,7},{7,6},{8,9},{9,8},{10,11... | collective-permute-start | bytes 294920 | tf_op jit(solution)/shard_map/ppermute | solution.py:27
  127.1 4.0 %collective-permute-done.7 = bf16[176,128]{1,0:T(8,128)(2,1)S(1)} collective-permute-done((bf16[176,128]{1,0:T(8,128)(2,1)S(1)}, bf16[176,128]{1,0:T(8,128)(2,1)S(1)}, u32[]{:S(2)}, u32[]{:S(2)}) %collective-permute-start.7) | collective-permute-done | bytes 45088 | tf_op jit(solution)/shard_map/ppermute | solution.py:112
  131.5 11.2 %all_to_all.62 = bf16[8,176,128]{2,1,0:T(8,128)(2,1)S(1)} all-to-all(bf16[8,176,128]{2,1,0:T(8,128)(2,1)S(1)} %broadcast_in_dim.29), channel_id=1, replica_groups=mesh['section'=32,'tensor'=8,'replica'=2] {'tensor'}, dimensions={0} | all-to-all | bytes 720896 | tf_op jit(solution)/shard_map/all_to_all | solution.py:37
  144.6 10.3 %all_to_all.63 = bf16[8,176,128]{2,1,0:T(8,128)(2,1)S(1)} all-to-all(bf16[8,176,128]{2,1,0:T(8,128)(2,1)S(1)} %bitcast.119), channel_id=1, replica_groups=mesh['section'=32,'tensor'=8,'replica'=2] {'tensor'}, dimensions={0} | all-to-all | bytes 720896 | tf_op jit(solution)/shard_map/all_to_all | solution.py:104
  155.0 10.3 %all_to_all.64 = bf16[8,176,128]{2,1,0:T(8,128)(2,1)S(1)} all-to-all(bf16[8,176,128]{2,1,0:T(8,128)(2,1)S(1)} %broadcast_in_dim.30), channel_id=1, replica_groups=mesh['section'=32,'tensor'=8,'replica'=2] {'tensor'}, dimensions={0} | all-to-all | bytes 720896 | tf_op jit(solution)/shard_map/all_to_all | solution.py:37
  165.7 1.3 collective-permute-start.10
  167.3 1.9 collective-permute-start.9
  169.2 2.2 convolution_convert_fusion.5
  171.4 4.2 %collective-permute-start.11 = (bf16[1408,128]{0,1:T(8,128)(2,1)}, bf16[1408,128]{0,1:T(8,128)(2,1)}, u32[]{:S(2)}, u32[]{:S(2)}) collective-permute-start(bf16[1408,128]{0,1:T(8,128)(2,1)} %convolution_convert_fusion.5), channel_id=1, source_target_pairs={{0,1},{1,0},{2,3},{3,2},{4,5},{5,4},{6,7},{7,6},{8,9},{9,8},{10,11... | collective-permute-start | bytes 1081352 | tf_op jit(solution)/shard_map/ppermute | solution.py:27
  175.6 2.1 collective-permute-done.10
  179.3 4.1 %all-to-all-start.9 = ((bf16[8,176,128]{2,1,0:T(8,128)(2,1)}), bf16[8,176,128]{2,1,0:T(8,128)(2,1)}, u32[]{:S(2)}, u32[]{:S(2)}) async-start(bf16[8,176,128]{2,1,0:T(8,128)(2,1)} %broadcast_in_dim.31), calls=%async_computation.9 | async-start | bytes 720896 | tf_op jit(solution)/shard_map/all_to_all | solution.py:37
  185.9 6.2 %all-to-all-done.9 = bf16[8,176,128]{2,1,0:T(8,128)(2,1)} async-done(((bf16[8,176,128]{2,1,0:T(8,128)(2,1)}), bf16[8,176,128]{2,1,0:T(8,128)(2,1)}, u32[]{:S(2)}, u32[]{:S(2)}) %all-to-all-start.9) | async-done | bytes 360480 | tf_op jit(solution)/shard_map/all_to_all | solution.py:37
  192.1 1.5 multiply_convert_fusion
  193.7 1.2 convolution_convert_fusion.4
  194.9 3.4 %all-to-all-start.10 = ((bf16[8,176,128]{2,1,0:T(8,128)(2,1)}), bf16[8,176,128]{2,1,0:T(8,128)(2,1)S(1)}, u32[]{:S(2)}, u32[]{:S(2)}) async-start(bf16[8,176,128]{2,1,0:T(8,128)(2,1)} %bitcast.34), calls=%async_computation.10 | async-start | bytes 720896 | tf_op jit(solution)/shard_map/all_to_all | solution.py:104
  198.4 2.4 %convolution_convert_fusion.3 = bf16[1408,128]{0,1:T(8,128)(2,1)} fusion(bf16[1408,128]{1,0:T(8,128)(2,1)} %bitcast.30, bf16[1408,128]{1,0:T(8,128)(2,1)S(1)} %bitcast.108, bf16[1408,128]{1,0:T(8,128)(2,1)S(1)} %bitcast.106, bf16[1408,128]{1,0:T(8,128)(2,1)S(1)} %bitcast.104, s32[512]{0:T(512)S(1)} %bitcast.129), kind=kOutput, calls=%fused_computation.5 | convolution fusion | flops 190562304 | bytes 1804288 | tf_op jit(solution)/shard_map/dot_general | solution.py:23
  201.1 4.2 %collective-permute-start.13 = (bf16[1408,128]{0,1:T(8,128)(2,1)}, bf16[1408,128]{0,1:T(8,128)(2,1)S(1)}, u32[]{:S(2)}, u32[]{:S(2)}) collective-permute-start(bf16[1408,128]{0,1:T(8,128)(2,1)} %convolution_convert_fusion.3), channel_id=1, source_target_pairs={{0,1},{1,0},{2,3},{3,2},{4,5},{5,4},{6,7},{7,6},{8,9},{9,8},{10,11... | collective-permute-start | bytes 1081352 | tf_op jit(solution)/shard_map/ppermute | solution.py:27
  205.3 3.1 %collective-permute-start.12 = (bf16[192,128]{1,0:T(8,128)(2,1)S(1)}, bf16[192,128]{1,0:T(8,128)(2,1)S(1)}, u32[]{:S(2)}, u32[]{:S(2)}) collective-permute-start(bf16[192,128]{1,0:T(8,128)(2,1)S(1)} %get-tuple-element.51), channel_id=1, source_target_pairs={{0,1},{1,0},{2,3},{3,2},{4,5},{5,4},{6,7},{7,6},{8,9},{9,8},{10,11... | collective-permute-start | bytes 147464 | tf_op jit(solution)/shard_map/ppermute | solution.py:27
  209.5 6.7 %all-to-all-start.11 = ((bf16[16,176,128]{2,1,0:T(8,128)(2,1)}), bf16[16,176,128]{2,1,0:T(8,128)(2,1)S(1)}, u32[]{:S(2)}, u32[]{:S(2)}) async-start(bf16[16,176,128]{2,1,0:T(8,128)(2,1)} %broadcast_in_dim.32), calls=%async_computation.11 | async-start | bytes 1441792 | tf_op jit(solution)/shard_map/all_to_all | solution.py:37
  217.4 1.1 fusion.1
  218.5 2.1 fusion
  220.7 9.1 %all-to-all-done.11 = bf16[16,176,128]{2,1,0:T(8,128)(2,1)S(1)} async-done(((bf16[16,176,128]{2,1,0:T(8,128)(2,1)}), bf16[16,176,128]{2,1,0:T(8,128)(2,1)S(1)}, u32[]{:S(2)}, u32[]{:S(2)}) %all-to-all-start.11) | async-done | bytes 720928 | tf_op jit(solution)/shard_map/all_to_all | solution.py:37
  231.7 2.3 convolution_convert_fusion.2
  (140 shorter events, 19.6 us)
Async XLA Ops:
  0.6 21.1 %copy-start.22 = (bf16[1,1408,192]{1,2,0:T(8,128)(2,1)S(1)}, bf16[1,1408,192]{1,2,0:T(8,128)(2,1)}, u32[]{:S(2)}) copy-start(bf16[1,1408,192]{1,2,0:T(8,128)(2,1)} %param.14) | copy-start | bytes 1622020
  0.6 21.1 %copy-start.32 = (bf16[1,128,1408]{2,1,0:T(8,128)(2,1)S(1)}, bf16[1,128,1408]{2,1,0:T(8,128)(2,1)}, u32[]{:S(2)}) copy-start(bf16[1,128,1408]{2,1,0:T(8,128)(2,1)} %param.9) | copy-start | bytes 1081348
  0.7 21.1 %collective-permute-start.1 = (bf16[1408,192]{0,1:T(8,128)(2,1)}, bf16[1408,192]{0,1:T(8,128)(2,1)S(1)}, u32[]{:S(2)}, u32[]{:S(2)}) collective-permute-start(bf16[1408,192]{0,1:T(8,128)(2,1)} %bitcast.131), channel_id=1, source_target_pairs={{0,1},{1,0},{2,3},{3,2},{4,5},{5,4},{6,7},{7,6},{8,9},{9,8},{10,11... | collective-permute-start | bytes 1622024 | tf_op jit(solution)/shard_map/ppermute | solution.py:27
  5.9 27.5 %collective-permute-start.2 = (bf16[192,1408]{1,0:T(8,128)(2,1)}, bf16[192,1408]{1,0:T(8,128)(2,1)S(1)}, u32[]{:S(2)}, u32[]{:S(2)}) collective-permute-start(bf16[192,1408]{1,0:T(8,128)(2,1)} %bitcast.109), channel_id=1, source_target_pairs={{0,1},{1,0},{2,3},{3,2},{4,5},{5,4},{6,7},{7,6},{8,9},{9,8},{10,11... | collective-permute-start | bytes 1622024 | tf_op jit(solution)/shard_map/ppermute | solution.py:27
  9.7 24.5 %all-to-all-start = ((bf16[8,176,128]{2,1,0:T(8,128)(2,1)}), bf16[8,176,128]{2,1,0:T(8,128)(2,1)S(1)}, u32[]{:S(2)}, u32[]{:S(2)}) async-start(bf16[8,176,128]{2,1,0:T(8,128)(2,1)} %broadcast_in_dim.24), calls=%async_computation | async-start | bytes 720896 | tf_op jit(solution)/shard_map/all_to_all | solution.py:37
  15.0 7.5 %copy-start.21 = (s32[1,4,128]{2,1,0:T(4,128)S(1)}, s32[1,4,128]{2,1,0:T(4,128)}, u32[]{:S(2)}) copy-start(s32[1,4,128]{2,1,0:T(4,128)} %param.10) | copy-start | bytes 6148
  22.6 97.9 %copy-start.12 = (bf16[384,128]{1,0:T(8,128)(2,1)}, bf16[384,128]{1,0:T(8,128)(2,1)S(1)}, u32[]{:S(2)}) copy-start(bf16[384,128]{1,0:T(8,128)(2,1)S(1)} %get-tuple-element.33) | copy-start | bytes 294916
  22.9 10.5 %copy-start.7 = (bf16[1,192,1408]{2,1,0:T(8,128)(2,1)S(1)}, bf16[1,192,1408]{2,1,0:T(8,128)(2,1)}, u32[]{:S(2)}) copy-start(bf16[1,192,1408]{2,1,0:T(8,128)(2,1)} %param.15) | copy-start | bytes 1622020
  34.2 2.6 %copy-start.1 = (bf16[8,176,128]{2,1,0:T(8,128)(2,1)}, bf16[8,176,128]{2,1,0:T(8,128)(2,1)S(1)}, u32[]{:S(2)}) copy-start(bf16[8,176,128]{2,1,0:T(8,128)(2,1)S(1)} %all-to-all-done) | copy-start | bytes 1081348
  35.5 6.4 %copy-start.8 = (bf16[1,2,88,1408]{3,2,1,0:T(8,128)(2,1)S(1)}, bf16[1,2,88,1408]{3,2,1,0:T(8,128)(2,1)}, u32[]{:S(2)}) copy-start(bf16[1,2,88,1408]{3,2,1,0:T(8,128)(2,1)} %param.13) | copy-start | bytes 1486852
  36.8 12.6 %copy-start.10 = (bf16[1,128,176]{1,2,0:T(8,128)(2,1)S(1)}, bf16[1,128,176]{1,2,0:T(8,128)(2,1)}, u32[]{:S(2)}) copy-start(bf16[1,128,176]{1,2,0:T(8,128)(2,1)} %param.11) | copy-start | bytes 135172
  36.8 12.6 %all-to-all-start.1 = ((bf16[8,176,128]{2,1,0:T(8,128)(2,1)}), bf16[8,176,128]{2,1,0:T(8,128)(2,1)S(1)}, u32[]{:S(2)}, u32[]{:S(2)}) async-start(bf16[8,176,128]{2,1,0:T(8,128)(2,1)} %bitcast.15), calls=%async_computation.1 | async-start | bytes 720896 | tf_op jit(solution)/shard_map/all_to_all | solution.py:104
  42.0 21.1 %collective-permute-start = (bf16[2,88,1408]{2,1,0:T(8,128)(2,1)S(1)}, bf16[2,88,1408]{2,1,0:T(8,128)(2,1)}, u32[]{:S(2)}, u32[]{:S(2)}) collective-permute-start(bf16[2,88,1408]{2,1,0:T(8,128)(2,1)S(1)} %bitcast.111), channel_id=1, source_target_pairs={{0,1},{1,0},{2,3},{3,2},{4,5},{5,4},{6,7},{7,6},{8,9},{9,8},{10,11... | collective-permute-start | bytes 1486856 | tf_op jit(solution)/shard_map/ppermute | solution.py:27
  50.2 14.0 %all-to-all-start.2 = ((bf16[8,176,128]{2,1,0:T(8,128)(2,1)}), bf16[8,176,128]{2,1,0:T(8,128)(2,1)}, u32[]{:S(2)}, u32[]{:S(2)}) async-start(bf16[8,176,128]{2,1,0:T(8,128)(2,1)} %broadcast_in_dim.25), calls=%async_computation.2 | async-start | bytes 720896 | tf_op jit(solution)/shard_map/all_to_all | solution.py:37
  64.2 102.8 %copy-start = (bf16[2,88,1408]{2,1,0:T(8,128)(2,1)}, bf16[2,88,1408]{2,1,0:T(8,128)(2,1)S(1)}, u32[]{:S(2)}) copy-start(bf16[2,88,1408]{2,1,0:T(8,128)(2,1)S(1)} %get-tuple-element.47) | copy-start | bytes 1486852
  65.7 16.3 %copy-start.11 = (bf16[3,128,176]{1,2,0:T(8,128)(2,1)S(1)}, bf16[3,128,176]{1,2,0:T(8,128)(2,1)}, u32[]{:S(2)}) copy-start(bf16[3,128,176]{1,2,0:T(8,128)(2,1)} %param.12) | copy-start | bytes 405508
  67.0 6.7 %collective-permute-start.3 = (bf16[176,128]{1,0:T(8,128)(2,1)S(1)}, bf16[176,128]{1,0:T(8,128)(2,1)S(1)}, u32[]{:S(2)}, u32[]{:S(2)}) collective-permute-start(bf16[176,128]{1,0:T(8,128)(2,1)S(1)} %convolution_convert_fusion.16), channel_id=1, source_target_pairs={{16,0},{32,16},{48,32},{64,48},{80,64},{96,80},{112,96},{128,112},... | collective-permute-start | bytes 135176 | tf_op jit(solution)/shard_map/ppermute | solution.py:118
  68.9 13.1 %collective-permute-start.4 = (bf16[176,128]{1,0:T(8,128)(2,1)S(1)}, bf16[176,128]{1,0:T(8,128)(2,1)S(1)}, u32[]{:S(2)}, u32[]{:S(2)}) collective-permute-start(bf16[176,128]{1,0:T(8,128)(2,1)S(1)} %convolution_convert_fusion.17), channel_id=1, source_target_pairs={{256,240},{272,224},{288,208},{304,192},{320,176},{336,160},{352,1... | collective-permute-start | bytes 135176 | tf_op jit(solution)/shard_map/ppermute | solution.py:112
  70.2 24.5 %collective-permute-start.5 = (bf16[128,1408]{1,0:T(8,128)(2,1)}, bf16[128,1408]{1,0:T(8,128)(2,1)S(1)}, u32[]{:S(2)}, u32[]{:S(2)}) collective-permute-start(bf16[128,1408]{1,0:T(8,128)(2,1)} %bitcast.137), channel_id=1, source_target_pairs={{0,1},{1,0},{2,3},{3,2},{4,5},{5,4},{6,7},{7,6},{8,9},{9,8},{10,11... | collective-permute-start | bytes 1081352 | tf_op jit(solution)/shard_map/ppermute | solution.py:27
  82.1 14.0 %copy-start.24 = (bf16[1,1408,192]{1,2,0:T(8,128)(2,1)S(1)}, bf16[1,1408,192]{1,2,0:T(8,128)(2,1)}, u32[]{:S(2)}) copy-start(bf16[1,1408,192]{1,2,0:T(8,128)(2,1)} %param.14) | copy-start | bytes 1622020
  82.1 14.0 %copy-start.29 = (bf16[1408,192]{0,1:T(8,128)(2,1)S(1)}, bf16[1408,192]{0,1:T(8,128)(2,1)}, u32[]{:S(2)}) copy-start(bf16[1408,192]{0,1:T(8,128)(2,1)} %copy-done.27) | copy-start | bytes 1622020
  107.9 12.5 %copy-start.20 = (bf16[1,128,2,176]{1,3,2,0:T(8,128)(2,1)S(1)}, bf16[1,128,2,176]{1,3,2,0:T(8,128)(2,1)}, u32[]{:S(2)}) copy-start(bf16[1,128,2,176]{1,3,2,0:T(8,128)(2,1)} %param.8) | copy-start | bytes 270340
  107.9 10.8 %all-to-all-start.5 = ((bf16[8,176,128]{2,1,0:T(8,128)(2,1)}), bf16[8,176,128]{2,1,0:T(8,128)(2,1)S(1)}, u32[]{:S(2)}, u32[]{:S(2)}) async-start(bf16[8,176,128]{2,1,0:T(8,128)(2,1)} %broadcast_in_dim.27), calls=%async_computation.5 | async-start | bytes 720896 | tf_op jit(solution)/shard_map/all_to_all | solution.py:37
  119.1 12.0 %collective-permute-start.7 = (bf16[176,128]{1,0:T(8,128)(2,1)S(1)}, bf16[176,128]{1,0:T(8,128)(2,1)S(1)}, u32[]{:S(2)}, u32[]{:S(2)}) collective-permute-start(bf16[176,128]{1,0:T(8,128)(2,1)S(1)} %convolution_convert_fusion.15), channel_id=1, source_target_pairs={{256,240},{272,224},{288,208},{304,192},{320,176},{336,160},{352,1... | collective-permute-start | bytes 135176 | tf_op jit(solution)/shard_map/ppermute | solution.py:112
  120.8 6.2 %collective-permute-start.6 = (bf16[176,128]{1,0:T(8,128)(2,1)S(1)}, bf16[176,128]{1,0:T(8,128)(2,1)S(1)}, u32[]{:S(2)}, u32[]{:S(2)}) collective-permute-start(bf16[176,128]{1,0:T(8,128)(2,1)S(1)} %convolution_convert_fusion.14), channel_id=1, source_target_pairs={{16,0},{32,16},{48,32},{64,48},{80,64},{96,80},{112,96},{128,112},... | collective-permute-start | bytes 135176 | tf_op jit(solution)/shard_map/ppermute | solution.py:118
  122.8 8.6 %collective-permute-start.8 = (bf16[384,128]{1,0:T(8,128)(2,1)S(1)}, bf16[384,128]{1,0:T(8,128)(2,1)S(1)}, u32[]{:S(2)}, u32[]{:S(2)}) collective-permute-start(bf16[384,128]{1,0:T(8,128)(2,1)S(1)} %pad_maximum_fusion.3), channel_id=1, source_target_pairs={{0,1},{1,0},{2,3},{3,2},{4,5},{5,4},{6,7},{7,6},{8,9},{9,8},{10,11... | collective-permute-start | bytes 294920 | tf_op jit(solution)/shard_map/ppermute | solution.py:27
  131.4 86.0 %copy-start.9 = (bf16[384,128]{1,0:T(8,128)(2,1)}, bf16[384,128]{1,0:T(8,128)(2,1)S(1)}, u32[]{:S(2)}) copy-start(bf16[384,128]{1,0:T(8,128)(2,1)S(1)} %collective-permute-done.8) | copy-start | bytes 294916
  131.4 12.5 %copy-start.25 = (bf16[1,1408,192]{1,2,0:T(8,128)(2,1)S(1)}, bf16[1,1408,192]{1,2,0:T(8,128)(2,1)}, u32[]{:S(2)}) copy-start(bf16[1,1408,192]{1,2,0:T(8,128)(2,1)} %param.14) | copy-start | bytes 1622020
  131.5 12.5 %copy-start.30 = (bf16[1408,192]{0,1:T(8,128)(2,1)S(1)}, bf16[1408,192]{0,1:T(8,128)(2,1)}, u32[]{:S(2)}) copy-start(bf16[1408,192]{0,1:T(8,128)(2,1)} %copy-done.27) | copy-start | bytes 1622020
  165.7 12.1 %collective-permute-start.10 = (bf16[176,128]{1,0:T(8,128)(2,1)S(1)}, bf16[176,128]{1,0:T(8,128)(2,1)S(1)}, u32[]{:S(2)}, u32[]{:S(2)}) collective-permute-start(bf16[176,128]{1,0:T(8,128)(2,1)S(1)} %convolution_convert_fusion.13), channel_id=1, source_target_pairs={{256,240},{272,224},{288,208},{304,192},{320,176},{336,160},{352,1... | collective-permute-start | bytes 135176 | tf_op jit(solution)/shard_map/ppermute | solution.py:112
  167.3 8.4 %collective-permute-start.9 = (bf16[176,128]{1,0:T(8,128)(2,1)S(1)}, bf16[176,128]{1,0:T(8,128)(2,1)S(1)}, u32[]{:S(2)}, u32[]{:S(2)}) collective-permute-start(bf16[176,128]{1,0:T(8,128)(2,1)S(1)} %convolution_convert_fusion.12), channel_id=1, source_target_pairs={{16,0},{32,16},{48,32},{64,48},{80,64},{96,80},{112,96},{128,112},... | collective-permute-start | bytes 135176 | tf_op jit(solution)/shard_map/ppermute | solution.py:118
  171.4 14.5 %collective-permute-start.11 = (bf16[1408,128]{0,1:T(8,128)(2,1)}, bf16[1408,128]{0,1:T(8,128)(2,1)}, u32[]{:S(2)}, u32[]{:S(2)}) collective-permute-start(bf16[1408,128]{0,1:T(8,128)(2,1)} %convolution_convert_fusion.5), channel_id=1, source_target_pairs={{0,1},{1,0},{2,3},{3,2},{4,5},{5,4},{6,7},{7,6},{8,9},{9,8},{10,11... | collective-permute-start | bytes 1081352 | tf_op jit(solution)/shard_map/ppermute | solution.py:27
  179.3 12.8 %all-to-all-start.9 = ((bf16[8,176,128]{2,1,0:T(8,128)(2,1)}), bf16[8,176,128]{2,1,0:T(8,128)(2,1)}, u32[]{:S(2)}, u32[]{:S(2)}) async-start(bf16[8,176,128]{2,1,0:T(8,128)(2,1)} %broadcast_in_dim.31), calls=%async_computation.9 | async-start | bytes 720896 | tf_op jit(solution)/shard_map/all_to_all | solution.py:37
  183.4 1.8 copy-start.13
  192.1 1.5 copy-start.26
  192.1 1.5 copy-start.31
  193.6 4.7 %copy-start.2 = (bf16[8,176,128]{2,1,0:T(8,128)(2,1)S(1)}, bf16[8,176,128]{2,1,0:T(8,128)(2,1)}, u32[]{:S(2)}) copy-start(bf16[8,176,128]{2,1,0:T(8,128)(2,1)} %copy-done.1) | copy-start | bytes 1081348
  193.6 4.7 %copy-start.4 = (bf16[8,176,128]{2,1,0:T(8,128)(2,1)S(1)}, bf16[8,176,128]{2,1,0:T(8,128)(2,1)}, u32[]{:S(2)}) copy-start(bf16[8,176,128]{2,1,0:T(8,128)(2,1)} %copy-done.3) | copy-start | bytes 1081348
  193.7 4.7 %copy-start.6 = (bf16[8,176,128]{2,1,0:T(8,128)(2,1)S(1)}, bf16[8,176,128]{2,1,0:T(8,128)(2,1)}, u32[]{:S(2)}) copy-start(bf16[8,176,128]{2,1,0:T(8,128)(2,1)} %copy-done.5) | copy-start | bytes 1081348
  194.9 13.6 %all-to-all-start.10 = ((bf16[8,176,128]{2,1,0:T(8,128)(2,1)}), bf16[8,176,128]{2,1,0:T(8,128)(2,1)S(1)}, u32[]{:S(2)}, u32[]{:S(2)}) async-start(bf16[8,176,128]{2,1,0:T(8,128)(2,1)} %bitcast.34), calls=%async_computation.10 | async-start | bytes 720896 | tf_op jit(solution)/shard_map/all_to_all | solution.py:104
  198.4 2.4 %copy-start.15 = (bf16[384,128]{1,0:T(8,128)(2,1)S(1)}, bf16[384,128]{1,0:T(8,128)(2,1)}, u32[]{:S(2)}) copy-start(bf16[384,128]{1,0:T(8,128)(2,1)} %copy-done.14) | copy-start | bytes 294916
  198.4 2.4 %copy-start.17 = (bf16[384,128]{1,0:T(8,128)(2,1)S(1)}, bf16[384,128]{1,0:T(8,128)(2,1)}, u32[]{:S(2)}) copy-start(bf16[384,128]{1,0:T(8,128)(2,1)} %copy-done.16) | copy-start | bytes 294916
  198.4 2.4 %copy-start.19 = (bf16[384,128]{1,0:T(8,128)(2,1)S(1)}, bf16[384,128]{1,0:T(8,128)(2,1)}, u32[]{:S(2)}) copy-start(bf16[384,128]{1,0:T(8,128)(2,1)} %copy-done.18) | copy-start | bytes 294916
  201.1 17.5 %collective-permute-start.13 = (bf16[1408,128]{0,1:T(8,128)(2,1)}, bf16[1408,128]{0,1:T(8,128)(2,1)S(1)}, u32[]{:S(2)}, u32[]{:S(2)}) collective-permute-start(bf16[1408,128]{0,1:T(8,128)(2,1)} %convolution_convert_fusion.3), channel_id=1, source_target_pairs={{0,1},{1,0},{2,3},{3,2},{4,5},{5,4},{6,7},{7,6},{8,9},{9,8},{10,11... | collective-permute-start | bytes 1081352 | tf_op jit(solution)/shard_map/ppermute | solution.py:27
  205.3 12.0 %collective-permute-start.12 = (bf16[192,128]{1,0:T(8,128)(2,1)S(1)}, bf16[192,128]{1,0:T(8,128)(2,1)S(1)}, u32[]{:S(2)}, u32[]{:S(2)}) collective-permute-start(bf16[192,128]{1,0:T(8,128)(2,1)S(1)} %get-tuple-element.51), channel_id=1, source_target_pairs={{0,1},{1,0},{2,3},{3,2},{4,5},{5,4},{6,7},{7,6},{8,9},{9,8},{10,11... | collective-permute-start | bytes 147464 | tf_op jit(solution)/shard_map/ppermute | solution.py:27
  209.5 7.8 %copy-start.33 = (bf16[1,128,1408]{2,1,0:T(8,128)(2,1)S(1)}, bf16[1,128,1408]{2,1,0:T(8,128)(2,1)}, u32[]{:S(2)}) copy-start(bf16[1,128,1408]{2,1,0:T(8,128)(2,1)} %param.9) | copy-start | bytes 1081348
  209.5 7.9 %copy-start.35 = (bf16[128,1408]{1,0:T(8,128)(2,1)S(1)}, bf16[128,1408]{1,0:T(8,128)(2,1)}, u32[]{:S(2)}) copy-start(bf16[128,1408]{1,0:T(8,128)(2,1)} %copy-done.34) | copy-start | bytes 1081348
  209.5 20.2 %all-to-all-start.11 = ((bf16[16,176,128]{2,1,0:T(8,128)(2,1)}), bf16[16,176,128]{2,1,0:T(8,128)(2,1)S(1)}, u32[]{:S(2)}, u32[]{:S(2)}) async-start(bf16[16,176,128]{2,1,0:T(8,128)(2,1)} %broadcast_in_dim.32), calls=%async_computation.11 | async-start | bytes 1441792 | tf_op jit(solution)/shard_map/all_to_all | solution.py:37
  (11 other events, 10.1 us)

commit v9 on v8

--- a/solution.py
+++ b/solution.py
@@ -77,13 +77,12 @@
     high = slope.astype(bf16)
     low = (slope - high.astype(f32)).astype(bf16)
     slopes = dot(high, pick) + dot(low, pick)
-    down_own, down_other, slopes = tied(w_down[0], down_other, slopes)
-    (down,) = tied(jnp.concatenate([down_own, down_other], axis=0))
+    down = jnp.concatenate([w_down[0], down_other], axis=0)
 
     def small_of(inputs, active_sent, ids_sent):
+        saved = inputs.transpose(1, 2, 0)
         decoder = jnp.where(section < half, 0.0, 1.0).astype(bf16)
-        mask = jnp.stack([jnp.ones((), bf16), decoder])[:, None, None]
-        saved = inputs.transpose(1, 2, 0) * mask
+        saved = jnp.stack([saved[0], saved[1] * decoder])
         saved_first, saved_second = saved[:, :own_in], saved[:, own_in:]
         saved_own = jnp.where(first, saved_first, saved_second).reshape(-1, pool)
         saved_sent = jnp.where(first, saved_second, saved_first).reshape(-1, pool)
@@ -121,9 +120,10 @@
                 [(i, i - 1) for i in range(1, sections)],
             )
             if t == 0:
+                down_own, down_late, _ = tied(w_down[0], down_other, skip_grad)
+                (down,) = tied(jnp.concatenate([down_own, down_late], axis=0))
                 mixed_sent, _ = tied(pool_mixed[0], skip_grad)
                 sent = swap(mixed_sent)
-            elif t + 3 == ticks:
                 inputs, active_late, ids_late, _ = tied(
                     pool_inputs[0], active, crop_ids, skip_grad
                 )
@@ -139,11 +139,9 @@
                 sent = swap(early)
             summed = (above.astype(f32) + mirrored.astype(f32)).astype(bf16)
             chunk = jnp.where(is_top, loss_grads[t].T, summed)
-            if t + 3 == ticks:
-                chunk, small_other = tied(chunk, small_other)
             upstream = gather(chunk).reshape(width, rows)
             if t == 0:
-                upstream, mixed_other = tied(upstream, sent)
+                upstream, mixed_other, small_other = tied(upstream, sent, small_other)
             elif t + 2 == ticks:
                 upstream, early_other = tied(upstream, sent)
                 upstream, saved_own, small_other = tied(upstream, saved_own, small_other)

time: 236 us -> 231 us (0.979)
  the two profiles are of different devices: /device:TPU:96 before, /device:TPU:352 now
where the time goes in v9:
time: 231 us; the launch traced here: 229 us
  starting transfers between devices  84.6 us (37%)
  blocking collectives  53 us (23%)
  waiting for transfers between devices  52.1 us (23%)
  matrix products  24.9 us (11%)
  local copies, waits for them, and re-layouts  8.21 us (4%)
  other arithmetic  4.97 us (2%)
    all_to_all x3, blocking collectives, gather(): return lax.all_to_all(spread, axes, 0, 0)  31.2 us
    ppermute x8, starting transfers between devices, swap(): return lax.ppermute(x, 'replica', [(0, 1), (1, 0)])  30.3 us
    dot_general x27, matrix products, dot(): lax.dot_general(a, b, (((ca,), (cb,)), ((), ())), preferred_element_type=...  24.9 us
    all_to_all x5, waiting for transfers between devices, gather(): return lax.all_to_all(spread, axes, 0, 0)  23.8 us
    all_to_all x5, starting transfers between devices, gather(): return lax.all_to_all(spread, axes, 0, 0)  23.1 us
    ppermute x8, waiting for transfers between devices, swap(): return lax.ppermute(x, 'replica', [(0, 1), (1, 0)])  23 us
    all_to_all x2, blocking collectives, body(): lax.all_to_all(partial.reshape(parts, chunk_rows, rows), 'tensor', 0, 0)  21.8 us
    ppermute x3, starting transfers between devices, body(): lax.ppermute(skip_grad, 'section', [(i, sections - 1 - i) for i in range(...  13.6 us
  transfers between devices with their start and end apart: 21, of which 11 were waited for; matrix products, arithmetic and copies ran while one was open for 10% of the time, Pallas kernels for 0%

profile of v9, /device:TPU:352, one launch (start us, length us, event | category | flops | bytes accessed | tf_op | source)
XLA Modules:
  0.0 229.2 jit_solution(4897232651949789145)
XLA Ops:
  0.6 5.2 %collective-permute-start.1 = (bf16[1408,192]{0,1:T(8,128)(2,1)}, bf16[1408,192]{0,1:T(8,128)(2,1)S(1)}, u32[]{:S(2)}, u32[]{:S(2)}) collective-permute-start(bf16[1408,192]{0,1:T(8,128)(2,1)} %bitcast.129), channel_id=1, source_target_pairs={{0,1},{1,0},{2,3},{3,2},{4,5},{5,4},{6,7},{7,6},{8,9},{9,8},{10,11... | collective-permute-start | bytes 1622024 | tf_op jit(solution)/shard_map/ppermute | solution.py:27
  5.9 2.2 collective-permute-start.2
  8.1 1.6 broadcast_in_dim.24
  9.7 5.3 %all-to-all-start = ((bf16[8,176,128]{2,1,0:T(8,128)(2,1)}), bf16[8,176,128]{2,1,0:T(8,128)(2,1)S(1)}, u32[]{:S(2)}, u32[]{:S(2)}) async-start(bf16[8,176,128]{2,1,0:T(8,128)(2,1)} %broadcast_in_dim.24), calls=%async_computation | async-start | bytes 720896 | tf_op jit(solution)/shard_map/all_to_all | solution.py:37
  15.0 6.7 %collective-permute-done.1 = bf16[1408,192]{0,1:T(8,128)(2,1)S(1)} collective-permute-done((bf16[1408,192]{0,1:T(8,128)(2,1)}, bf16[1408,192]{0,1:T(8,128)(2,1)S(1)}, u32[]{:S(2)}, u32[]{:S(2)}) %collective-permute-start.1) | collective-permute-done | bytes 540704 | tf_op jit(solution)/shard_map/ppermute | solution.py:27
  21.8 1.7 multiply_convert_fusion
  24.2 10.0 %all-to-all-done = bf16[8,176,128]{2,1,0:T(8,128)(2,1)S(1)} async-done(((bf16[8,176,128]{2,1,0:T(8,128)(2,1)}), bf16[8,176,128]{2,1,0:T(8,128)(2,1)S(1)}, u32[]{:S(2)}, u32[]{:S(2)}) %all-to-all-start) | async-done | bytes 360480 | tf_op jit(solution)/shard_map/all_to_all | solution.py:37
  36.0 1.2 convolution_convert_fusion.8
  37.2 5.2 %all-to-all-start.1 = ((bf16[8,176,128]{2,1,0:T(8,128)(2,1)}), bf16[8,176,128]{2,1,0:T(8,128)(2,1)S(1)}, u32[]{:S(2)}, u32[]{:S(2)}) async-start(bf16[8,176,128]{2,1,0:T(8,128)(2,1)} %bitcast.12), calls=%async_computation.1 | async-start | bytes 720896 | tf_op jit(solution)/shard_map/all_to_all | solution.py:103
  42.4 3.7 %collective-permute-start = (bf16[2,88,1408]{2,1,0:T(8,128)(2,1)S(1)}, bf16[2,88,1408]{2,1,0:T(8,128)(2,1)S(1)}, u32[]{:S(2)}, u32[]{:S(2)}) collective-permute-start(bf16[2,88,1408]{2,1,0:T(8,128)(2,1)S(1)} %bitcast.107), channel_id=1, source_target_pairs={{0,1},{1,0},{2,3},{3,2},{4,5},{5,4},{6,7},{7,6},{8,9},{9,8},{10,11... | collective-permute-start | bytes 1486856 | tf_op jit(solution)/shard_map/ppermute | solution.py:27
  46.1 3.6 %all-to-all-done.1 = bf16[8,176,128]{2,1,0:T(8,128)(2,1)S(1)} async-done(((bf16[8,176,128]{2,1,0:T(8,128)(2,1)}), bf16[8,176,128]{2,1,0:T(8,128)(2,1)S(1)}, u32[]{:S(2)}, u32[]{:S(2)}) %all-to-all-start.1) | async-done | bytes 360480 | tf_op jit(solution)/shard_map/all_to_all | solution.py:103
  50.6 4.1 %all-to-all-start.2 = ((bf16[8,176,128]{2,1,0:T(8,128)(2,1)}), bf16[8,176,128]{2,1,0:T(8,128)(2,1)}, u32[]{:S(2)}, u32[]{:S(2)}) async-start(bf16[8,176,128]{2,1,0:T(8,128)(2,1)} %broadcast_in_dim.25), calls=%async_computation.2 | async-start | bytes 720896 | tf_op jit(solution)/shard_map/all_to_all | solution.py:37
  54.7 8.3 %collective-permute-done = bf16[2,88,1408]{2,1,0:T(8,128)(2,1)S(1)} collective-permute-done((bf16[2,88,1408]{2,1,0:T(8,128)(2,1)S(1)}, bf16[2,88,1408]{2,1,0:T(8,128)(2,1)S(1)}, u32[]{:S(2)}, u32[]{:S(2)}) %collective-permute-start) | collective-permute-done | bytes 495648 | tf_op jit(solution)/shard_map/ppermute | solution.py:27
  63.7 1.3 convolution_convert_fusion.17
  65.0 1.4 collective-permute-start.4
  66.5 1.3 convolution_convert_fusion.16
  67.8 3.3 %collective-permute-start.3 = (bf16[176,128]{1,0:T(8,128)(2,1)S(1)}, bf16[176,128]{1,0:T(8,128)(2,1)S(1)}, u32[]{:S(2)}, u32[]{:S(2)}) collective-permute-start(bf16[176,128]{1,0:T(8,128)(2,1)S(1)} %convolution_convert_fusion.16), channel_id=1, source_target_pairs={{16,0},{32,16},{48,32},{64,48},{80,64},{96,80},{112,96},{128,112},... | collective-permute-start | bytes 135176 | tf_op jit(solution)/shard_map/ppermute | solution.py:117
  71.1 3.6 %collective-permute-start.5 = (bf16[128,1408]{1,0:T(8,128)(2,1)}, bf16[128,1408]{1,0:T(8,128)(2,1)}, u32[]{:S(2)}, u32[]{:S(2)}) collective-permute-start(bf16[128,1408]{1,0:T(8,128)(2,1)} %bitcast.10), channel_id=1, source_target_pairs={{0,1},{1,0},{2,3},{3,2},{4,5},{5,4},{6,7},{7,6},{8,9},{9,8},{10,11... | collective-permute-start | bytes 1081352 | tf_op jit(solution)/shard_map/ppermute | solution.py:27
  77.1 3.9 %all-to-all-start.3 = ((bf16[8,176,128]{2,1,0:T(8,128)(2,1)}), bf16[8,176,128]{2,1,0:T(8,128)(2,1)S(1)}, u32[]{:S(2)}, u32[]{:S(2)}) async-start(bf16[8,176,128]{2,1,0:T(8,128)(2,1)} %broadcast_in_dim.26), calls=%async_computation.3 | async-start | bytes 720896 | tf_op jit(solution)/shard_map/all_to_all | solution.py:37
  81.1 3.9 %collective-permute-start.6 = (bf16[384,128]{1,0:T(8,128)(2,1)S(1)}, bf16[384,128]{1,0:T(8,128)(2,1)S(1)}, u32[]{:S(2)}, u32[]{:S(2)}) collective-permute-start(bf16[384,128]{1,0:T(8,128)(2,1)S(1)} %pad_maximum_fusion.3), channel_id=1, source_target_pairs={{0,1},{1,0},{2,3},{3,2},{4,5},{5,4},{6,7},{7,6},{8,9},{9,8},{10,11... | collective-permute-start | bytes 294920 | tf_op jit(solution)/shard_map/ppermute | solution.py:27
  85.0 1.3 pad_maximum_fusion.2
  86.3 4.5 %collective-permute-done.6 = bf16[384,128]{1,0:T(8,128)(2,1)S(1)} collective-permute-done((bf16[384,128]{1,0:T(8,128)(2,1)S(1)}, bf16[384,128]{1,0:T(8,128)(2,1)S(1)}, u32[]{:S(2)}, u32[]{:S(2)}) %collective-permute-start.6) | collective-permute-done | bytes 98336 | tf_op jit(solution)/shard_map/ppermute | solution.py:27
  92.8 11.5 %all_to_all.60 = bf16[8,176,128]{2,1,0:T(8,128)(2,1)S(1)} all-to-all(bf16[8,176,128]{2,1,0:T(8,128)(2,1)S(1)} %bitcast.116), channel_id=1, replica_groups=mesh['section'=32,'tensor'=8,'replica'=2] {'tensor'}, dimensions={0} | all-to-all | bytes 720896 | tf_op jit(solution)/shard_map/all_to_all | solution.py:103
  104.4 10.3 %all_to_all.61 = bf16[8,176,128]{2,1,0:T(8,128)(2,1)S(1)} all-to-all(bf16[8,176,128]{2,1,0:T(8,128)(2,1)S(1)} %broadcast_in_dim.28), channel_id=1, replica_groups=mesh['section'=32,'tensor'=8,'replica'=2] {'tensor'}, dimensions={0} | all-to-all | bytes 720896 | tf_op jit(solution)/shard_map/all_to_all | solution.py:37
  115.4 1.9 collective-permute-start.7
  117.3 4.7 %collective-permute-start.8 = (bf16[176,128]{1,0:T(8,128)(2,1)S(1)}, bf16[176,128]{1,0:T(8,128)(2,1)S(1)}, u32[]{:S(2)}, u32[]{:S(2)}) collective-permute-start(bf16[176,128]{1,0:T(8,128)(2,1)S(1)} %convolution_convert_fusion.15), channel_id=1, source_target_pairs={{256,240},{272,224},{288,208},{304,192},{320,176},{336,160},{352,1... | collective-permute-start | bytes 135176 | tf_op jit(solution)/shard_map/ppermute | solution.py:111
  122.0 1.7 collective-permute-done.8
  123.8 10.5 %all_to_all.62 = bf16[8,176,128]{2,1,0:T(8,128)(2,1)S(1)} all-to-all(bf16[8,176,128]{2,1,0:T(8,128)(2,1)S(1)} %broadcast_in_dim.29), channel_id=1, replica_groups=mesh['section'=32,'tensor'=8,'replica'=2] {'tensor'}, dimensions={0} | all-to-all | bytes 720896 | tf_op jit(solution)/shard_map/all_to_all | solution.py:37
  135.4 10.3 %all_to_all.63 = bf16[8,176,128]{2,1,0:T(8,128)(2,1)S(1)} all-to-all(bf16[8,176,128]{2,1,0:T(8,128)(2,1)S(1)} %bitcast.117), channel_id=1, replica_groups=mesh['section'=32,'tensor'=8,'replica'=2] {'tensor'}, dimensions={0} | all-to-all | bytes 720896 | tf_op jit(solution)/shard_map/all_to_all | solution.py:103
  145.8 10.3 %all_to_all.64 = bf16[8,176,128]{2,1,0:T(8,128)(2,1)S(1)} all-to-all(bf16[8,176,128]{2,1,0:T(8,128)(2,1)S(1)} %broadcast_in_dim.30), channel_id=1, replica_groups=mesh['section'=32,'tensor'=8,'replica'=2] {'tensor'}, dimensions={0} | all-to-all | bytes 720896 | tf_op jit(solution)/shard_map/all_to_all | solution.py:37
  156.5 7.5 %collective-permute-start.10 = (bf16[176,128]{1,0:T(8,128)(2,1)S(1)}, bf16[176,128]{1,0:T(8,128)(2,1)S(1)}, u32[]{:S(2)}, u32[]{:S(2)}) collective-permute-start(bf16[176,128]{1,0:T(8,128)(2,1)S(1)} %convolution_convert_fusion.13), channel_id=1, source_target_pairs={{256,240},{272,224},{288,208},{304,192},{320,176},{336,160},{352,1... | collective-permute-start | bytes 135176 | tf_op jit(solution)/shard_map/ppermute | solution.py:111
  164.3 3.7 %collective-permute-start.9 = (bf16[176,128]{1,0:T(8,128)(2,1)S(1)}, bf16[176,128]{1,0:T(8,128)(2,1)S(1)}, u32[]{:S(2)}, u32[]{:S(2)}) collective-permute-start(bf16[176,128]{1,0:T(8,128)(2,1)S(1)} %convolution_convert_fusion.12), channel_id=1, source_target_pairs={{16,0},{32,16},{48,32},{64,48},{80,64},{96,80},{112,96},{128,112},... | collective-permute-start | bytes 135176 | tf_op jit(solution)/shard_map/ppermute | solution.py:117
  168.0 2.2 convolution_convert_fusion.5
  170.2 4.2 %collective-permute-start.11 = (bf16[1408,128]{0,1:T(8,128)(2,1)}, bf16[1408,128]{0,1:T(8,128)(2,1)}, u32[]{:S(2)}, u32[]{:S(2)}) collective-permute-start(bf16[1408,128]{0,1:T(8,128)(2,1)} %convolution_convert_fusion.5), channel_id=1, source_target_pairs={{0,1},{1,0},{2,3},{3,2},{4,5},{5,4},{6,7},{7,6},{8,9},{9,8},{10,11... | collective-permute-start | bytes 1081352 | tf_op jit(solution)/shard_map/ppermute | solution.py:27
  175.2 4.1 %all-to-all-start.9 = ((bf16[8,176,128]{2,1,0:T(8,128)(2,1)}), bf16[8,176,128]{2,1,0:T(8,128)(2,1)}, u32[]{:S(2)}, u32[]{:S(2)}) async-start(bf16[8,176,128]{2,1,0:T(8,128)(2,1)} %broadcast_in_dim.31), calls=%async_computation.9 | async-start | bytes 720896 | tf_op jit(solution)/shard_map/all_to_all | solution.py:37
  181.1 3.3 %collective-permute-done.11 = bf16[1408,128]{0,1:T(8,128)(2,1)} collective-permute-done((bf16[1408,128]{0,1:T(8,128)(2,1)}, bf16[1408,128]{0,1:T(8,128)(2,1)}, u32[]{:S(2)}, u32[]{:S(2)}) %collective-permute-start.11) | collective-permute-done | bytes 360480 | tf_op jit(solution)/shard_map/ppermute | solution.py:27
  184.4 3.5 %all-to-all-done.9 = bf16[8,176,128]{2,1,0:T(8,128)(2,1)} async-done(((bf16[8,176,128]{2,1,0:T(8,128)(2,1)}), bf16[8,176,128]{2,1,0:T(8,128)(2,1)}, u32[]{:S(2)}, u32[]{:S(2)}) %all-to-all-start.9) | async-done | bytes 360480 | tf_op jit(solution)/shard_map/all_to_all | solution.py:37
  187.9 1.5 fusion.19
  189.6 1.2 convolution_convert_fusion.4
  190.8 3.4 %all-to-all-start.10 = ((bf16[8,176,128]{2,1,0:T(8,128)(2,1)}), bf16[8,176,128]{2,1,0:T(8,128)(2,1)S(1)}, u32[]{:S(2)}, u32[]{:S(2)}) async-start(bf16[8,176,128]{2,1,0:T(8,128)(2,1)} %bitcast.33), calls=%async_computation.10 | async-start | bytes 720896 | tf_op jit(solution)/shard_map/all_to_all | solution.py:103
  194.3 1.7 convolution_convert_fusion.3
  196.3 3.1 %collective-permute-start.13 = (bf16[1408,128]{0,1:T(8,128)(2,1)S(1)}, bf16[1408,128]{0,1:T(8,128)(2,1)S(1)}, u32[]{:S(2)}, u32[]{:S(2)}) collective-permute-start(bf16[1408,128]{0,1:T(8,128)(2,1)S(1)} %convolution_convert_fusion.3), channel_id=1, source_target_pairs={{0,1},{1,0},{2,3},{3,2},{4,5},{5,4},{6,7},{7,6},{8,9},{9,8},{10,11... | collective-permute-start | bytes 1081352 | tf_op jit(solution)/shard_map/ppermute | solution.py:27
  199.4 4.2 %collective-permute-start.12 = (bf16[192,128]{1,0:T(8,128)(2,1)S(1)}, bf16[192,128]{1,0:T(8,128)(2,1)S(1)}, u32[]{:S(2)}, u32[]{:S(2)}) collective-permute-start(bf16[192,128]{1,0:T(8,128)(2,1)S(1)} %get-tuple-element.47), channel_id=1, source_target_pairs={{0,1},{1,0},{2,3},{3,2},{4,5},{5,4},{6,7},{7,6},{8,9},{9,8},{10,11... | collective-permute-start | bytes 147464 | tf_op jit(solution)/shard_map/ppermute | solution.py:27
  204.8 5.7 %all-to-all-start.11 = ((bf16[16,176,128]{2,1,0:T(8,128)(2,1)}), bf16[16,176,128]{2,1,0:T(8,128)(2,1)S(1)}, u32[]{:S(2)}, u32[]{:S(2)}) async-start(bf16[16,176,128]{2,1,0:T(8,128)(2,1)} %broadcast_in_dim.32), calls=%async_computation.11 | async-start | bytes 1441792 | tf_op jit(solution)/shard_map/all_to_all | solution.py:37
  211.8 2.2 fusion.1
  214.0 1.1 fusion
  215.1 9.7 %all-to-all-done.11 = bf16[16,176,128]{2,1,0:T(8,128)(2,1)S(1)} async-done(((bf16[16,176,128]{2,1,0:T(8,128)(2,1)}), bf16[16,176,128]{2,1,0:T(8,128)(2,1)S(1)}, u32[]{:S(2)}, u32[]{:S(2)}) %all-to-all-start.11) | async-done | bytes 720928 | tf_op jit(solution)/shard_map/all_to_all | solution.py:37
  226.8 2.3 %convolution_convert_fusion.2 = bf16[176,1408]{1,0:T(8,128)(2,1)} fusion(bf16[1408,128]{0,1:T(8,128)(2,1)S(1)} %copy.18, bf16[1408,128]{0,1:T(8,128)(2,1)S(1)} %copy.17, bf16[1408,128]{0,1:T(8,128)(2,1)} %collective-permute-done.11, bf16[1408,128]{0,1:T(8,128)(2,1)} %convolution_convert_fusion.5, bf16[176,128]{1,0:T(8,128)(2,1)S(1)} %get-tuple-element.49, ...), kind=kOutput, calls=%fused_computation.2 | convolution fusion | flops 260491264 | bytes 2117632 | tf_op jit(solution)/shard_map/dot_general | solution.py:23
  (133 shorter events, 18.3 us)
Async XLA Ops:
  0.6 21.1 %copy-start.24 = (bf16[1,1408,192]{1,2,0:T(8,128)(2,1)S(1)}, bf16[1,1408,192]{1,2,0:T(8,128)(2,1)}, u32[]{:S(2)}) copy-start(bf16[1,1408,192]{1,2,0:T(8,128)(2,1)} %param.14) | copy-start | bytes 1622020
  0.6 21.1 %collective-permute-start.1 = (bf16[1408,192]{0,1:T(8,128)(2,1)}, bf16[1408,192]{0,1:T(8,128)(2,1)S(1)}, u32[]{:S(2)}, u32[]{:S(2)}) collective-permute-start(bf16[1408,192]{0,1:T(8,128)(2,1)} %bitcast.129), channel_id=1, source_target_pairs={{0,1},{1,0},{2,3},{3,2},{4,5},{5,4},{6,7},{7,6},{8,9},{9,8},{10,11... | collective-permute-start | bytes 1622024 | tf_op jit(solution)/shard_map/ppermute | solution.py:27
  5.9 28.3 %collective-permute-start.2 = (bf16[192,1408]{1,0:T(8,128)(2,1)}, bf16[192,1408]{1,0:T(8,128)(2,1)S(1)}, u32[]{:S(2)}, u32[]{:S(2)}) collective-permute-start(bf16[192,1408]{1,0:T(8,128)(2,1)} %bitcast.104), channel_id=1, source_target_pairs={{0,1},{1,0},{2,3},{3,2},{4,5},{5,4},{6,7},{7,6},{8,9},{9,8},{10,11... | collective-permute-start | bytes 1622024 | tf_op jit(solution)/shard_map/ppermute | solution.py:27
  9.7 24.5 %all-to-all-start = ((bf16[8,176,128]{2,1,0:T(8,128)(2,1)}), bf16[8,176,128]{2,1,0:T(8,128)(2,1)S(1)}, u32[]{:S(2)}, u32[]{:S(2)}) async-start(bf16[8,176,128]{2,1,0:T(8,128)(2,1)} %broadcast_in_dim.24), calls=%async_computation | async-start | bytes 720896 | tf_op jit(solution)/shard_map/all_to_all | solution.py:37
  15.0 8.4 %copy-start.23 = (s32[1,4,128]{2,1,0:T(4,128)S(1)}, s32[1,4,128]{2,1,0:T(4,128)}, u32[]{:S(2)}) copy-start(s32[1,4,128]{2,1,0:T(4,128)} %param.10) | copy-start | bytes 6148
  21.8 1.7 copy-start.27
  23.4 52.0 %copy-start.13 = (bf16[384,128]{1,0:T(8,128)(2,1)}, bf16[384,128]{1,0:T(8,128)(2,1)S(1)}, u32[]{:S(2)}) copy-start(bf16[384,128]{1,0:T(8,128)(2,1)S(1)} %get-tuple-element.28) | copy-start | bytes 294916
  23.8 11.1 %copy-start.5 = (bf16[1,192,1408]{2,1,0:T(8,128)(2,1)S(1)}, bf16[1,192,1408]{2,1,0:T(8,128)(2,1)}, u32[]{:S(2)}) copy-start(bf16[1,192,1408]{2,1,0:T(8,128)(2,1)} %param.15) | copy-start | bytes 1622020
  34.2 16.5 %copy-start.6 = (bf16[192,1408]{1,0:T(8,128)(2,1)}, bf16[192,1408]{1,0:T(8,128)(2,1)S(1)}, u32[]{:S(2)}) copy-start(bf16[192,1408]{1,0:T(8,128)(2,1)S(1)} %collective-permute-done.2) | copy-start | bytes 1622020
  36.0 6.4 %copy-start.7 = (bf16[1,2,88,1408]{3,2,1,0:T(8,128)(2,1)S(1)}, bf16[1,2,88,1408]{3,2,1,0:T(8,128)(2,1)}, u32[]{:S(2)}) copy-start(bf16[1,2,88,1408]{3,2,1,0:T(8,128)(2,1)} %param.13) | copy-start | bytes 1486852
  37.2 12.6 %copy-start.11 = (bf16[1,128,176]{1,2,0:T(8,128)(2,1)S(1)}, bf16[1,128,176]{1,2,0:T(8,128)(2,1)}, u32[]{:S(2)}) copy-start(bf16[1,128,176]{1,2,0:T(8,128)(2,1)} %param.11) | copy-start | bytes 135172
  37.2 12.6 %all-to-all-start.1 = ((bf16[8,176,128]{2,1,0:T(8,128)(2,1)}), bf16[8,176,128]{2,1,0:T(8,128)(2,1)S(1)}, u32[]{:S(2)}, u32[]{:S(2)}) async-start(bf16[8,176,128]{2,1,0:T(8,128)(2,1)} %bitcast.12), calls=%async_computation.1 | async-start | bytes 720896 | tf_op jit(solution)/shard_map/all_to_all | solution.py:103
  42.4 20.6 %collective-permute-start = (bf16[2,88,1408]{2,1,0:T(8,128)(2,1)S(1)}, bf16[2,88,1408]{2,1,0:T(8,128)(2,1)S(1)}, u32[]{:S(2)}, u32[]{:S(2)}) collective-permute-start(bf16[2,88,1408]{2,1,0:T(8,128)(2,1)S(1)} %bitcast.107), channel_id=1, source_target_pairs={{0,1},{1,0},{2,3},{3,2},{4,5},{5,4},{6,7},{7,6},{8,9},{9,8},{10,11... | collective-permute-start | bytes 1486856 | tf_op jit(solution)/shard_map/ppermute | solution.py:27
  50.6 13.1 %all-to-all-start.2 = ((bf16[8,176,128]{2,1,0:T(8,128)(2,1)}), bf16[8,176,128]{2,1,0:T(8,128)(2,1)}, u32[]{:S(2)}, u32[]{:S(2)}) async-start(bf16[8,176,128]{2,1,0:T(8,128)(2,1)} %broadcast_in_dim.25), calls=%async_computation.2 | async-start | bytes 720896 | tf_op jit(solution)/shard_map/all_to_all | solution.py:37
  63.1 100.9 %copy-start = (bf16[2,88,1408]{2,1,0:T(8,128)(2,1)}, bf16[2,88,1408]{2,1,0:T(8,128)(2,1)S(1)}, u32[]{:S(2)}) copy-start(bf16[2,88,1408]{2,1,0:T(8,128)(2,1)S(1)} %get-tuple-element.43) | copy-start | bytes 1486852
  65.0 9.7 %copy-start.21 = (bf16[1,128,2,176]{1,3,2,0:T(8,128)(2,1)S(1)}, bf16[1,128,2,176]{1,3,2,0:T(8,128)(2,1)}, u32[]{:S(2)}) copy-start(bf16[1,128,2,176]{1,3,2,0:T(8,128)(2,1)} %param.8) | copy-start | bytes 270340
  65.0 10.4 %collective-permute-start.4 = (bf16[176,128]{1,0:T(8,128)(2,1)S(1)}, bf16[176,128]{1,0:T(8,128)(2,1)S(1)}, u32[]{:S(2)}, u32[]{:S(2)}) collective-permute-start(bf16[176,128]{1,0:T(8,128)(2,1)S(1)} %convolution_convert_fusion.17), channel_id=1, source_target_pairs={{256,240},{272,224},{288,208},{304,192},{320,176},{336,160},{352,1... | collective-permute-start | bytes 135176 | tf_op jit(solution)/shard_map/ppermute | solution.py:111
  67.8 7.7 %collective-permute-start.3 = (bf16[176,128]{1,0:T(8,128)(2,1)S(1)}, bf16[176,128]{1,0:T(8,128)(2,1)S(1)}, u32[]{:S(2)}, u32[]{:S(2)}) collective-permute-start(bf16[176,128]{1,0:T(8,128)(2,1)S(1)} %convolution_convert_fusion.16), channel_id=1, source_target_pairs={{16,0},{32,16},{48,32},{64,48},{80,64},{96,80},{112,96},{128,112},... | collective-permute-start | bytes 135176 | tf_op jit(solution)/shard_map/ppermute | solution.py:117
  71.1 19.7 %collective-permute-start.5 = (bf16[128,1408]{1,0:T(8,128)(2,1)}, bf16[128,1408]{1,0:T(8,128)(2,1)}, u32[]{:S(2)}, u32[]{:S(2)}) collective-permute-start(bf16[128,1408]{1,0:T(8,128)(2,1)} %bitcast.10), channel_id=1, source_target_pairs={{0,1},{1,0},{2,3},{3,2},{4,5},{5,4},{6,7},{7,6},{8,9},{9,8},{10,11... | collective-permute-start | bytes 1081352 | tf_op jit(solution)/shard_map/ppermute | solution.py:27
  77.1 13.7 %all-to-all-start.3 = ((bf16[8,176,128]{2,1,0:T(8,128)(2,1)}), bf16[8,176,128]{2,1,0:T(8,128)(2,1)S(1)}, u32[]{:S(2)}, u32[]{:S(2)}) async-start(bf16[8,176,128]{2,1,0:T(8,128)(2,1)} %broadcast_in_dim.26), calls=%async_computation.3 | async-start | bytes 720896 | tf_op jit(solution)/shard_map/all_to_all | solution.py:37
  81.1 9.7 %collective-permute-start.6 = (bf16[384,128]{1,0:T(8,128)(2,1)S(1)}, bf16[384,128]{1,0:T(8,128)(2,1)S(1)}, u32[]{:S(2)}, u32[]{:S(2)}) collective-permute-start(bf16[384,128]{1,0:T(8,128)(2,1)S(1)} %pad_maximum_fusion.3), channel_id=1, source_target_pairs={{0,1},{1,0},{2,3},{3,2},{4,5},{5,4},{6,7},{7,6},{8,9},{9,8},{10,11... | collective-permute-start | bytes 294920 | tf_op jit(solution)/shard_map/ppermute | solution.py:27
  90.8 120.8 %copy-start.10 = (bf16[384,128]{1,0:T(8,128)(2,1)}, bf16[384,128]{1,0:T(8,128)(2,1)S(1)}, u32[]{:S(2)}) copy-start(bf16[384,128]{1,0:T(8,128)(2,1)S(1)} %collective-permute-done.6) | copy-start | bytes 294916
  90.8 1.9 copy-start.1
  90.8 1.4 copy-start.29
  115.1 8.6 %copy-start.12 = (bf16[3,128,176]{1,2,0:T(8,128)(2,1)S(1)}, bf16[3,128,176]{1,2,0:T(8,128)(2,1)}, u32[]{:S(2)}) copy-start(bf16[3,128,176]{1,2,0:T(8,128)(2,1)} %param.12) | copy-start | bytes 405508
  115.4 6.6 %collective-permute-start.7 = (bf16[176,128]{1,0:T(8,128)(2,1)S(1)}, bf16[176,128]{1,0:T(8,128)(2,1)S(1)}, u32[]{:S(2)}, u32[]{:S(2)}) collective-permute-start(bf16[176,128]{1,0:T(8,128)(2,1)S(1)} %convolution_convert_fusion.14), channel_id=1, source_target_pairs={{16,0},{32,16},{48,32},{64,48},{80,64},{96,80},{112,96},{128,112},... | collective-permute-start | bytes 135176 | tf_op jit(solution)/shard_map/ppermute | solution.py:117
  117.3 6.4 %collective-permute-start.8 = (bf16[176,128]{1,0:T(8,128)(2,1)S(1)}, bf16[176,128]{1,0:T(8,128)(2,1)S(1)}, u32[]{:S(2)}, u32[]{:S(2)}) collective-permute-start(bf16[176,128]{1,0:T(8,128)(2,1)S(1)} %convolution_convert_fusion.15), channel_id=1, source_target_pairs={{256,240},{272,224},{288,208},{304,192},{320,176},{336,160},{352,1... | collective-permute-start | bytes 135176 | tf_op jit(solution)/shard_map/ppermute | solution.py:111
  156.5 17.9 %collective-permute-start.10 = (bf16[176,128]{1,0:T(8,128)(2,1)S(1)}, bf16[176,128]{1,0:T(8,128)(2,1)S(1)}, u32[]{:S(2)}, u32[]{:S(2)}) collective-permute-start(bf16[176,128]{1,0:T(8,128)(2,1)S(1)} %convolution_convert_fusion.13), channel_id=1, source_target_pairs={{256,240},{272,224},{288,208},{304,192},{320,176},{336,160},{352,1... | collective-permute-start | bytes 135176 | tf_op jit(solution)/shard_map/ppermute | solution.py:111
  164.3 10.1 %collective-permute-start.9 = (bf16[176,128]{1,0:T(8,128)(2,1)S(1)}, bf16[176,128]{1,0:T(8,128)(2,1)S(1)}, u32[]{:S(2)}, u32[]{:S(2)}) collective-permute-start(bf16[176,128]{1,0:T(8,128)(2,1)S(1)} %convolution_convert_fusion.12), channel_id=1, source_target_pairs={{16,0},{32,16},{48,32},{64,48},{80,64},{96,80},{112,96},{128,112},... | collective-permute-start | bytes 135176 | tf_op jit(solution)/shard_map/ppermute | solution.py:117
  170.2 14.2 %collective-permute-start.11 = (bf16[1408,128]{0,1:T(8,128)(2,1)}, bf16[1408,128]{0,1:T(8,128)(2,1)}, u32[]{:S(2)}, u32[]{:S(2)}) collective-permute-start(bf16[1408,128]{0,1:T(8,128)(2,1)} %convolution_convert_fusion.5), channel_id=1, source_target_pairs={{0,1},{1,0},{2,3},{3,2},{4,5},{5,4},{6,7},{7,6},{8,9},{9,8},{10,11... | collective-permute-start | bytes 1081352 | tf_op jit(solution)/shard_map/ppermute | solution.py:27
  175.2 12.7 %all-to-all-start.9 = ((bf16[8,176,128]{2,1,0:T(8,128)(2,1)}), bf16[8,176,128]{2,1,0:T(8,128)(2,1)}, u32[]{:S(2)}, u32[]{:S(2)}) async-start(bf16[8,176,128]{2,1,0:T(8,128)(2,1)} %broadcast_in_dim.31), calls=%async_computation.9 | async-start | bytes 720896 | tf_op jit(solution)/shard_map/all_to_all | solution.py:37
  179.3 1.8 copy-start.14
  187.9 1.6 copy-start.26
  187.9 1.6 copy-start.30
  189.5 4.7 %copy-start.2 = (bf16[8,176,128]{2,1,0:T(8,128)(2,1)S(1)}, bf16[8,176,128]{2,1,0:T(8,128)(2,1)}, u32[]{:S(2)}) copy-start(bf16[8,176,128]{2,1,0:T(8,128)(2,1)} %copy-done.1) | copy-start | bytes 1081348
  189.5 4.7 %copy-start.4 = (bf16[8,176,128]{2,1,0:T(8,128)(2,1)S(1)}, bf16[8,176,128]{2,1,0:T(8,128)(2,1)}, u32[]{:S(2)}) copy-start(bf16[8,176,128]{2,1,0:T(8,128)(2,1)} %copy-done.3) | copy-start | bytes 1081348
  189.5 4.7 %copy-start.9 = (bf16[8,176,128]{2,1,0:T(8,128)(2,1)S(1)}, bf16[8,176,128]{2,1,0:T(8,128)(2,1)}, u32[]{:S(2)}) copy-start(bf16[8,176,128]{2,1,0:T(8,128)(2,1)} %copy-done.8) | copy-start | bytes 1081348
  190.8 12.9 %all-to-all-start.10 = ((bf16[8,176,128]{2,1,0:T(8,128)(2,1)}), bf16[8,176,128]{2,1,0:T(8,128)(2,1)S(1)}, u32[]{:S(2)}, u32[]{:S(2)}) async-start(bf16[8,176,128]{2,1,0:T(8,128)(2,1)} %bitcast.33), calls=%async_computation.10 | async-start | bytes 720896 | tf_op jit(solution)/shard_map/all_to_all | solution.py:103
  194.3 1.7 copy-start.16
  194.3 1.7 copy-start.18
  194.3 1.7 copy-start.20
  194.3 1.7 copy-start.32
  196.3 17.7 %collective-permute-start.13 = (bf16[1408,128]{0,1:T(8,128)(2,1)S(1)}, bf16[1408,128]{0,1:T(8,128)(2,1)S(1)}, u32[]{:S(2)}, u32[]{:S(2)}) collective-permute-start(bf16[1408,128]{0,1:T(8,128)(2,1)S(1)} %convolution_convert_fusion.3), channel_id=1, source_target_pairs={{0,1},{1,0},{2,3},{3,2},{4,5},{5,4},{6,7},{7,6},{8,9},{9,8},{10,11... | collective-permute-start | bytes 1081352 | tf_op jit(solution)/shard_map/ppermute | solution.py:27
  199.4 12.3 %collective-permute-start.12 = (bf16[192,128]{1,0:T(8,128)(2,1)S(1)}, bf16[192,128]{1,0:T(8,128)(2,1)S(1)}, u32[]{:S(2)}, u32[]{:S(2)}) collective-permute-start(bf16[192,128]{1,0:T(8,128)(2,1)S(1)} %get-tuple-element.47), channel_id=1, source_target_pairs={{0,1},{1,0},{2,3},{3,2},{4,5},{5,4},{6,7},{7,6},{8,9},{9,8},{10,11... | collective-permute-start | bytes 147464 | tf_op jit(solution)/shard_map/ppermute | solution.py:27
  203.8 6.9 %copy-start.22 = (bf16[2,88,128]{2,1,0:T(8,128)(2,1)S(1)}, bf16[2,88,128]{2,1,0:T(8,128)(2,1)}, u32[]{:S(2)}) copy-start(bf16[2,88,128]{2,1,0:T(8,128)(2,1)} %get-tuple-element.50) | copy-start | bytes 135172
  204.8 20.1 %all-to-all-start.11 = ((bf16[16,176,128]{2,1,0:T(8,128)(2,1)}), bf16[16,176,128]{2,1,0:T(8,128)(2,1)S(1)}, u32[]{:S(2)}, u32[]{:S(2)}) async-start(bf16[16,176,128]{2,1,0:T(8,128)(2,1)} %broadcast_in_dim.32), calls=%async_computation.11 | async-start | bytes 1441792 | tf_op jit(solution)/shard_map/all_to_all | solution.py:37
  211.6 2.4 %slice-start = ((bf16[384,128]{1,0:T(8,128)(2,1)}), bf16[192,128]{1,0:T(8,128)(2,1)S(1)}, s32[]{:S(2)}) async-start(bf16[384,128]{1,0:T(8,128)(2,1)} %copy-done.10), calls=%async_computation.12 | async-start | bytes 98304 | tf_op jit(solution)/shard_map/slice | solution.py:150
  225.5 1.3 slice-start.1
  (8 other events, 7.7 us)

commit v10 on v9

--- a/solution.py
+++ b/solution.py
@@ -90,6 +90,13 @@
         return saved_own, jnp.concatenate([saved_sent, active_sent, ids], axis=0)
 
     hiddens, grads, upstreams = [], [], []
+
+    def scattered(parts_of, start):
+        ids_late, _ = tied(crop_ids, skip_grad)
+        ids_late = ids_late[0, start : start + len(parts_of)].reshape(1, -1)
+        picks = (ids_late == places).astype(bf16)
+        return dot(jnp.concatenate(parts_of, axis=1), picks, 1, 1)
+
     for t in range(ticks):
         upstreams.append(upstream)
         slope_now = slopes[:, t * rows : (t + 1) * rows]
@@ -131,14 +138,16 @@
                     inputs, active_late[units:], ids_late[0, ticks - 1]
                 )
                 small_other = swap(small)
+            elif t + 3 == ticks:
+                first_part = scattered(grads, 0)
             elif t + 2 == ticks:
-                ids_late, _ = tied(crop_ids, skip_grad)
-                picks = (ids_late[0, : t + 1].reshape(1, -1) == places).astype(bf16)
-                early = dot(jnp.concatenate(grads, axis=1), picks, 1, 1)
+                early = first_part + scattered(grads[t:], t)
                 early = early.astype(bf16)
                 sent = swap(early)
             summed = (above.astype(f32) + mirrored.astype(f32)).astype(bf16)
             chunk = jnp.where(is_top, loss_grads[t].T, summed)
+            if t + 3 == ticks:
+                chunk, first_part = tied(chunk, first_part)
             upstream = gather(chunk).reshape(width, rows)
             if t == 0:
                 upstream, mixed_other, small_other = tied(upstream, sent, small_other)

time: 231 us -> 226 us (0.978)
  the two profiles are of different devices: /device:TPU:352 before, /device:TPU:96 now
where the time goes in v10:
time: 226 us; the launch traced here: 224 us
  starting transfers between devices  71.2 us (32%)
  waiting for transfers between devices  62.7 us (28%)
  blocking collectives  53.8 us (24%)
  matrix products  22.2 us (10%)
  local copies, waits for them, and re-layouts  7.78 us (3%)
  other arithmetic  4.96 us (2%)
    all_to_all x3, blocking collectives, gather(): return lax.all_to_all(spread, axes, 0, 0)  31 us
    ppermute x8, starting transfers between devices, swap(): return lax.ppermute(x, 'replica', [(0, 1), (1, 0)])  30.3 us
    all_to_all x2, blocking collectives, body(): lax.all_to_all(partial.reshape(parts, chunk_rows, rows), 'tensor', 0, 0)  22.7 us
    ppermute x8, waiting for transfers between devices, swap(): return lax.ppermute(x, 'replica', [(0, 1), (1, 0)])  22.7 us
    all_to_all x5, starting transfers between devices, gather(): return lax.all_to_all(spread, axes, 0, 0)  22.2 us
    dot_general x28, matrix products, dot(): lax.dot_general(a, b, (((ca,), (cb,)), ((), ())), preferred_element_type=...  22.2 us
    all_to_all x5, waiting for transfers between devices, gather(): return lax.all_to_all(spread, axes, 0, 0)  20.4 us
    ppermute x3, waiting for transfers between devices, body(): lax.ppermute(skip_grad, 'section', [(i, sections - 1 - i) for i in range(...  14.7 us
  transfers between devices with their start and end apart: 21, of which 13 were waited for; matrix products, arithmetic and copies ran while one was open for 9% of the time, Pallas kernels for 0%

profile of v10, /device:TPU:96, one launch (start us, length us, event | category | flops | bytes accessed | tf_op | source)
XLA Modules:
  0.0 224.1 jit_solution(6588821219097752185)
XLA Ops:
  0.6 5.2 %collective-permute-start.1 = (bf16[1408,192]{0,1:T(8,128)(2,1)}, bf16[1408,192]{0,1:T(8,128)(2,1)S(1)}, u32[]{:S(2)}, u32[]{:S(2)}) collective-permute-start(bf16[1408,192]{0,1:T(8,128)(2,1)} %bitcast.135), channel_id=1, source_target_pairs={{0,1},{1,0},{2,3},{3,2},{4,5},{5,4},{6,7},{7,6},{8,9},{9,8},{10,11... | collective-permute-start | bytes 1622024 | tf_op jit(solution)/shard_map/ppermute | solution.py:27
  5.9 2.2 %collective-permute-start.2 = (bf16[192,1408]{1,0:T(8,128)(2,1)}, bf16[192,1408]{1,0:T(8,128)(2,1)S(1)}, u32[]{:S(2)}, u32[]{:S(2)}) collective-permute-start(bf16[192,1408]{1,0:T(8,128)(2,1)} %bitcast.116), channel_id=1, source_target_pairs={{0,1},{1,0},{2,3},{3,2},{4,5},{5,4},{6,7},{7,6},{8,9},{9,8},{10,11... | collective-permute-start | bytes 1622024 | tf_op jit(solution)/shard_map/ppermute | solution.py:27
  8.1 1.6 broadcast_in_dim.24
  9.7 5.3 %all-to-all-start = ((bf16[8,176,128]{2,1,0:T(8,128)(2,1)}), bf16[8,176,128]{2,1,0:T(8,128)(2,1)S(1)}, u32[]{:S(2)}, u32[]{:S(2)}) async-start(bf16[8,176,128]{2,1,0:T(8,128)(2,1)} %broadcast_in_dim.24), calls=%async_computation | async-start | bytes 720896 | tf_op jit(solution)/shard_map/all_to_all | solution.py:37
  15.0 6.7 %collective-permute-done.1 = bf16[1408,192]{0,1:T(8,128)(2,1)S(1)} collective-permute-done((bf16[1408,192]{0,1:T(8,128)(2,1)}, bf16[1408,192]{0,1:T(8,128)(2,1)S(1)}, u32[]{:S(2)}, u32[]{:S(2)}) %collective-permute-start.1) | collective-permute-done | bytes 540704 | tf_op jit(solution)/shard_map/ppermute | solution.py:27
  21.8 1.7 multiply_convert_fusion
  24.2 10.0 %all-to-all-done = bf16[8,176,128]{2,1,0:T(8,128)(2,1)S(1)} async-done(((bf16[8,176,128]{2,1,0:T(8,128)(2,1)}), bf16[8,176,128]{2,1,0:T(8,128)(2,1)S(1)}, u32[]{:S(2)}, u32[]{:S(2)}) %all-to-all-start) | async-done | bytes 360480 | tf_op jit(solution)/shard_map/all_to_all | solution.py:37
  36.0 1.2 convolution_convert_fusion.7
  37.2 5.2 %all-to-all-start.1 = ((bf16[8,176,128]{2,1,0:T(8,128)(2,1)}), bf16[8,176,128]{2,1,0:T(8,128)(2,1)S(1)}, u32[]{:S(2)}, u32[]{:S(2)}) async-start(bf16[8,176,128]{2,1,0:T(8,128)(2,1)} %bitcast.12), calls=%async_computation.1 | async-start | bytes 720896 | tf_op jit(solution)/shard_map/all_to_all | solution.py:110
  42.4 3.7 %collective-permute-start = (bf16[2,88,1408]{2,1,0:T(8,128)(2,1)S(1)}, bf16[2,88,1408]{2,1,0:T(8,128)(2,1)S(1)}, u32[]{:S(2)}, u32[]{:S(2)}) collective-permute-start(bf16[2,88,1408]{2,1,0:T(8,128)(2,1)S(1)} %bitcast.119), channel_id=1, source_target_pairs={{0,1},{1,0},{2,3},{3,2},{4,5},{5,4},{6,7},{7,6},{8,9},{9,8},{10,11... | collective-permute-start | bytes 1486856 | tf_op jit(solution)/shard_map/ppermute | solution.py:27
  46.1 3.6 %all-to-all-done.1 = bf16[8,176,128]{2,1,0:T(8,128)(2,1)S(1)} async-done(((bf16[8,176,128]{2,1,0:T(8,128)(2,1)}), bf16[8,176,128]{2,1,0:T(8,128)(2,1)S(1)}, u32[]{:S(2)}, u32[]{:S(2)}) %all-to-all-start.1) | async-done | bytes 360480 | tf_op jit(solution)/shard_map/all_to_all | solution.py:110
  50.6 3.4 %all-to-all-start.2 = ((bf16[8,176,128]{2,1,0:T(8,128)(2,1)}), bf16[8,176,128]{2,1,0:T(8,128)(2,1)S(1)}, u32[]{:S(2)}, u32[]{:S(2)}) async-start(bf16[8,176,128]{2,1,0:T(8,128)(2,1)} %broadcast_in_dim.25), calls=%async_computation.2 | async-start | bytes 720896 | tf_op jit(solution)/shard_map/all_to_all | solution.py:37
  54.1 8.9 %collective-permute-done = bf16[2,88,1408]{2,1,0:T(8,128)(2,1)S(1)} collective-permute-done((bf16[2,88,1408]{2,1,0:T(8,128)(2,1)S(1)}, bf16[2,88,1408]{2,1,0:T(8,128)(2,1)S(1)}, u32[]{:S(2)}, u32[]{:S(2)}) %collective-permute-start) | collective-permute-done | bytes 495648 | tf_op jit(solution)/shard_map/ppermute | solution.py:27
  63.9 1.4 collective-permute-start.4
  65.7 1.9 collective-permute-start.3
  67.6 3.6 %collective-permute-start.5 = (bf16[128,1408]{1,0:T(8,128)(2,1)}, bf16[128,1408]{1,0:T(8,128)(2,1)}, u32[]{:S(2)}, u32[]{:S(2)}) collective-permute-start(bf16[128,1408]{1,0:T(8,128)(2,1)} %bitcast.10), channel_id=1, source_target_pairs={{0,1},{1,0},{2,3},{3,2},{4,5},{5,4},{6,7},{7,6},{8,9},{9,8},{10,11... | collective-permute-start | bytes 1081352 | tf_op jit(solution)/shard_map/ppermute | solution.py:27
  72.0 4.1 %collective-permute-done.4 = bf16[176,128]{1,0:T(8,128)(2,1)S(1)} collective-permute-done((bf16[176,128]{1,0:T(8,128)(2,1)S(1)}, bf16[176,128]{1,0:T(8,128)(2,1)S(1)}, u32[]{:S(2)}, u32[]{:S(2)}) %collective-permute-start.4) | collective-permute-done | bytes 45088 | tf_op jit(solution)/shard_map/ppermute | solution.py:118
  77.7 3.6 %all-to-all-start.3 = ((bf16[8,176,128]{2,1,0:T(8,128)(2,1)}), bf16[8,176,128]{2,1,0:T(8,128)(2,1)S(1)}, u32[]{:S(2)}, u32[]{:S(2)}) async-start(bf16[8,176,128]{2,1,0:T(8,128)(2,1)} %broadcast_in_dim.26), calls=%async_computation.3 | async-start | bytes 720896 | tf_op jit(solution)/shard_map/all_to_all | solution.py:37
  81.3 4.6 %collective-permute-start.6 = (bf16[384,128]{1,0:T(8,128)(2,1)S(1)}, bf16[384,128]{1,0:T(8,128)(2,1)S(1)}, u32[]{:S(2)}, u32[]{:S(2)}) collective-permute-start(bf16[384,128]{1,0:T(8,128)(2,1)S(1)} %pad_maximum_fusion.3), channel_id=1, source_target_pairs={{0,1},{1,0},{2,3},{3,2},{4,5},{5,4},{6,7},{7,6},{8,9},{9,8},{10,11... | collective-permute-start | bytes 294920 | tf_op jit(solution)/shard_map/ppermute | solution.py:27
  86.0 1.3 pad_maximum_fusion.2
  87.3 4.7 %collective-permute-done.6 = bf16[384,128]{1,0:T(8,128)(2,1)S(1)} collective-permute-done((bf16[384,128]{1,0:T(8,128)(2,1)S(1)}, bf16[384,128]{1,0:T(8,128)(2,1)S(1)}, u32[]{:S(2)}, u32[]{:S(2)}) %collective-permute-start.6) | collective-permute-done | bytes 98336 | tf_op jit(solution)/shard_map/ppermute | solution.py:27
  94.0 12.4 %all_to_all.60 = bf16[8,176,128]{2,1,0:T(8,128)(2,1)S(1)} all-to-all(bf16[8,176,128]{2,1,0:T(8,128)(2,1)S(1)} %bitcast.122), channel_id=1, replica_groups=mesh['section'=32,'tensor'=8,'replica'=2] {'tensor'}, dimensions={0} | all-to-all | bytes 720896 | tf_op jit(solution)/shard_map/all_to_all | solution.py:110
  106.6 10.3 %all_to_all.61 = bf16[8,176,128]{2,1,0:T(8,128)(2,1)S(1)} all-to-all(bf16[8,176,128]{2,1,0:T(8,128)(2,1)S(1)} %broadcast_in_dim.28), channel_id=1, replica_groups=mesh['section'=32,'tensor'=8,'replica'=2] {'tensor'}, dimensions={0} | all-to-all | bytes 720896 | tf_op jit(solution)/shard_map/all_to_all | solution.py:37
  117.2 1.4 collective-permute-start.8
  119.0 2.1 collective-permute-start.7
  121.4 1.3 collective-permute-done.7
  122.7 6.6 %collective-permute-done.8 = bf16[176,128]{1,0:T(8,128)(2,1)S(1)} collective-permute-done((bf16[176,128]{1,0:T(8,128)(2,1)S(1)}, bf16[176,128]{1,0:T(8,128)(2,1)S(1)}, u32[]{:S(2)}, u32[]{:S(2)}) %collective-permute-start.8) | collective-permute-done | bytes 45088 | tf_op jit(solution)/shard_map/ppermute | solution.py:118
  129.4 10.3 %all_to_all.62 = bf16[8,176,128]{2,1,0:T(8,128)(2,1)S(1)} all-to-all(bf16[8,176,128]{2,1,0:T(8,128)(2,1)S(1)} %broadcast_in_dim.29), channel_id=1, replica_groups=mesh['section'=32,'tensor'=8,'replica'=2] {'tensor'}, dimensions={0} | all-to-all | bytes 720896 | tf_op jit(solution)/shard_map/all_to_all | solution.py:37
  140.9 10.3 %all_to_all.63 = bf16[8,176,128]{2,1,0:T(8,128)(2,1)S(1)} all-to-all(bf16[8,176,128]{2,1,0:T(8,128)(2,1)S(1)} %bitcast.123), channel_id=1, replica_groups=mesh['section'=32,'tensor'=8,'replica'=2] {'tensor'}, dimensions={0} | all-to-all | bytes 720896 | tf_op jit(solution)/shard_map/all_to_all | solution.py:110
  151.3 10.3 %all_to_all.64 = bf16[8,176,128]{2,1,0:T(8,128)(2,1)S(1)} all-to-all(bf16[8,176,128]{2,1,0:T(8,128)(2,1)S(1)} %broadcast_in_dim.30), channel_id=1, replica_groups=mesh['section'=32,'tensor'=8,'replica'=2] {'tensor'}, dimensions={0} | all-to-all | bytes 720896 | tf_op jit(solution)/shard_map/all_to_all | solution.py:37
  162.0 1.3 collective-permute-start.10
  163.6 1.9 collective-permute-start.9
  166.5 3.5 %collective-permute-start.11 = (bf16[1408,128]{1,0:T(8,128)(2,1)}, bf16[1408,128]{1,0:T(8,128)(2,1)}, u32[]{:S(2)}, u32[]{:S(2)}) collective-permute-start(bf16[1408,128]{1,0:T(8,128)(2,1)} %fusion.2), channel_id=1, source_target_pairs={{0,1},{1,0},{2,3},{3,2},{4,5},{5,4},{6,7},{7,6},{8,9},{9,8},{10,11... | collective-permute-start | bytes 1081352 | tf_op jit(solution)/shard_map/ppermute | solution.py:27
  170.0 3.9 %collective-permute-done.10 = bf16[176,128]{1,0:T(8,128)(2,1)S(1)} collective-permute-done((bf16[176,128]{1,0:T(8,128)(2,1)S(1)}, bf16[176,128]{1,0:T(8,128)(2,1)S(1)}, u32[]{:S(2)}, u32[]{:S(2)}) %collective-permute-start.10) | collective-permute-done | bytes 45088 | tf_op jit(solution)/shard_map/ppermute | solution.py:118
  174.7 4.1 %all-to-all-start.9 = ((bf16[8,176,128]{2,1,0:T(8,128)(2,1)}), bf16[8,176,128]{2,1,0:T(8,128)(2,1)}, u32[]{:S(2)}, u32[]{:S(2)}) async-start(bf16[8,176,128]{2,1,0:T(8,128)(2,1)} %broadcast_in_dim.31), calls=%async_computation.9 | async-start | bytes 720896 | tf_op jit(solution)/shard_map/all_to_all | solution.py:37
  180.6 2.2 %collective-permute-done.11 = bf16[1408,128]{1,0:T(8,128)(2,1)} collective-permute-done((bf16[1408,128]{1,0:T(8,128)(2,1)}, bf16[1408,128]{1,0:T(8,128)(2,1)}, u32[]{:S(2)}, u32[]{:S(2)}) %collective-permute-start.11) | collective-permute-done | bytes 360480 | tf_op jit(solution)/shard_map/ppermute | solution.py:27
  182.9 3.3 %all-to-all-done.9 = bf16[8,176,128]{2,1,0:T(8,128)(2,1)} async-done(((bf16[8,176,128]{2,1,0:T(8,128)(2,1)}), bf16[8,176,128]{2,1,0:T(8,128)(2,1)}, u32[]{:S(2)}, u32[]{:S(2)}) %all-to-all-start.9) | async-done | bytes 360480 | tf_op jit(solution)/shard_map/all_to_all | solution.py:37
  186.2 1.5 fusion.20
  187.8 1.2 convolution_convert_fusion.4
  189.0 3.4 %all-to-all-start.10 = ((bf16[8,176,128]{2,1,0:T(8,128)(2,1)}), bf16[8,176,128]{2,1,0:T(8,128)(2,1)S(1)}, u32[]{:S(2)}, u32[]{:S(2)}) async-start(bf16[8,176,128]{2,1,0:T(8,128)(2,1)} %bitcast.34), calls=%async_computation.10 | async-start | bytes 720896 | tf_op jit(solution)/shard_map/all_to_all | solution.py:110
  192.5 1.7 convolution_convert_fusion.3
  194.5 3.5 %collective-permute-start.13 = (bf16[1408,128]{0,1:T(8,128)(2,1)S(1)}, bf16[1408,128]{0,1:T(8,128)(2,1)S(1)}, u32[]{:S(2)}, u32[]{:S(2)}) collective-permute-start(bf16[1408,128]{0,1:T(8,128)(2,1)S(1)} %convolution_convert_fusion.3), channel_id=1, source_target_pairs={{0,1},{1,0},{2,3},{3,2},{4,5},{5,4},{6,7},{7,6},{8,9},{9,8},{10,11... | collective-permute-start | bytes 1081352 | tf_op jit(solution)/shard_map/ppermute | solution.py:27
  198.1 3.9 %collective-permute-start.12 = (bf16[192,128]{1,0:T(8,128)(2,1)S(1)}, bf16[192,128]{1,0:T(8,128)(2,1)S(1)}, u32[]{:S(2)}, u32[]{:S(2)}) collective-permute-start(bf16[192,128]{1,0:T(8,128)(2,1)S(1)} %get-tuple-element.53), channel_id=1, source_target_pairs={{0,1},{1,0},{2,3},{3,2},{4,5},{5,4},{6,7},{7,6},{8,9},{9,8},{10,11... | collective-permute-start | bytes 147464 | tf_op jit(solution)/shard_map/ppermute | solution.py:27
  203.0 5.8 %all-to-all-start.11 = ((bf16[16,176,128]{2,1,0:T(8,128)(2,1)}), bf16[16,176,128]{2,1,0:T(8,128)(2,1)S(1)}, u32[]{:S(2)}, u32[]{:S(2)}) async-start(bf16[16,176,128]{2,1,0:T(8,128)(2,1)} %broadcast_in_dim.32), calls=%async_computation.11 | async-start | bytes 1441792 | tf_op jit(solution)/shard_map/all_to_all | solution.py:37
  210.0 2.2 fusion.1
  212.2 1.1 fusion
  213.3 6.7 %all-to-all-done.11 = bf16[16,176,128]{2,1,0:T(8,128)(2,1)S(1)} async-done(((bf16[16,176,128]{2,1,0:T(8,128)(2,1)}), bf16[16,176,128]{2,1,0:T(8,128)(2,1)S(1)}, u32[]{:S(2)}, u32[]{:S(2)}) %all-to-all-start.11) | async-done | bytes 720928 | tf_op jit(solution)/shard_map/all_to_all | solution.py:37
  221.6 2.5 %convolution_convert_fusion.2 = bf16[176,1408]{1,0:T(8,128)(2,1)} fusion(bf16[1408,128]{1,0:T(8,128)(2,1)S(1)} %bitcast.115, bf16[1408,128]{1,0:T(8,128)(2,1)S(1)} %bitcast.113, bf16[1408,128]{1,0:T(8,128)(2,1)} %collective-permute-done.11, bf16[1408,128]{1,0:T(8,128)(2,1)} %fusion.2, bf16[176,128]{1,0:T(8,128)(2,1)S(1)} %get-tuple-element.55, ...), kind=kOutput, calls=%fused_computation.3 | convolution fusion | flops 260491264 | bytes 2117632 | tf_op jit(solution)/shard_map/dot_general | solution.py:23
  (137 shorter events, 19.4 us)
Async XLA Ops:
  0.6 21.1 %copy-start.26 = (bf16[1,1408,192]{1,2,0:T(8,128)(2,1)S(1)}, bf16[1,1408,192]{1,2,0:T(8,128)(2,1)}, u32[]{:S(2)}) copy-start(bf16[1,1408,192]{1,2,0:T(8,128)(2,1)} %param.14) | copy-start | bytes 1622020
  0.6 21.1 %collective-permute-start.1 = (bf16[1408,192]{0,1:T(8,128)(2,1)}, bf16[1408,192]{0,1:T(8,128)(2,1)S(1)}, u32[]{:S(2)}, u32[]{:S(2)}) collective-permute-start(bf16[1408,192]{0,1:T(8,128)(2,1)} %bitcast.135), channel_id=1, source_target_pairs={{0,1},{1,0},{2,3},{3,2},{4,5},{5,4},{6,7},{7,6},{8,9},{9,8},{10,11... | collective-permute-start | bytes 1622024 | tf_op jit(solution)/shard_map/ppermute | solution.py:27
  5.9 28.3 %collective-permute-start.2 = (bf16[192,1408]{1,0:T(8,128)(2,1)}, bf16[192,1408]{1,0:T(8,128)(2,1)S(1)}, u32[]{:S(2)}, u32[]{:S(2)}) collective-permute-start(bf16[192,1408]{1,0:T(8,128)(2,1)} %bitcast.116), channel_id=1, source_target_pairs={{0,1},{1,0},{2,3},{3,2},{4,5},{5,4},{6,7},{7,6},{8,9},{9,8},{10,11... | collective-permute-start | bytes 1622024 | tf_op jit(solution)/shard_map/ppermute | solution.py:27
  9.7 24.5 %all-to-all-start = ((bf16[8,176,128]{2,1,0:T(8,128)(2,1)}), bf16[8,176,128]{2,1,0:T(8,128)(2,1)S(1)}, u32[]{:S(2)}, u32[]{:S(2)}) async-start(bf16[8,176,128]{2,1,0:T(8,128)(2,1)} %broadcast_in_dim.24), calls=%async_computation | async-start | bytes 720896 | tf_op jit(solution)/shard_map/all_to_all | solution.py:37
  15.0 8.4 %copy-start.25 = (s32[1,4,128]{2,1,0:T(4,128)S(1)}, s32[1,4,128]{2,1,0:T(4,128)}, u32[]{:S(2)}) copy-start(s32[1,4,128]{2,1,0:T(4,128)} %param.10) | copy-start | bytes 6148
  21.8 1.7 copy-start.29
  23.4 48.5 %copy-start.15 = (bf16[384,128]{1,0:T(8,128)(2,1)}, bf16[384,128]{1,0:T(8,128)(2,1)S(1)}, u32[]{:S(2)}) copy-start(bf16[384,128]{1,0:T(8,128)(2,1)S(1)} %get-tuple-element.31) | copy-start | bytes 294916
  23.8 11.1 %copy-start.7 = (bf16[1,192,1408]{2,1,0:T(8,128)(2,1)S(1)}, bf16[1,192,1408]{2,1,0:T(8,128)(2,1)}, u32[]{:S(2)}) copy-start(bf16[1,192,1408]{2,1,0:T(8,128)(2,1)} %param.15) | copy-start | bytes 1622020
  34.2 16.4 %copy-start.8 = (bf16[192,1408]{1,0:T(8,128)(2,1)}, bf16[192,1408]{1,0:T(8,128)(2,1)S(1)}, u32[]{:S(2)}) copy-start(bf16[192,1408]{1,0:T(8,128)(2,1)S(1)} %collective-permute-done.2) | copy-start | bytes 1622020
  36.0 6.4 %copy-start.9 = (bf16[1,2,88,1408]{3,2,1,0:T(8,128)(2,1)S(1)}, bf16[1,2,88,1408]{3,2,1,0:T(8,128)(2,1)}, u32[]{:S(2)}) copy-start(bf16[1,2,88,1408]{3,2,1,0:T(8,128)(2,1)} %param.13) | copy-start | bytes 1486852
  37.2 12.6 %copy-start.13 = (bf16[1,128,176]{1,2,0:T(8,128)(2,1)S(1)}, bf16[1,128,176]{1,2,0:T(8,128)(2,1)}, u32[]{:S(2)}) copy-start(bf16[1,128,176]{1,2,0:T(8,128)(2,1)} %param.11) | copy-start | bytes 135172
  37.2 12.6 %all-to-all-start.1 = ((bf16[8,176,128]{2,1,0:T(8,128)(2,1)}), bf16[8,176,128]{2,1,0:T(8,128)(2,1)S(1)}, u32[]{:S(2)}, u32[]{:S(2)}) async-start(bf16[8,176,128]{2,1,0:T(8,128)(2,1)} %bitcast.12), calls=%async_computation.1 | async-start | bytes 720896 | tf_op jit(solution)/shard_map/all_to_all | solution.py:110
  42.4 20.6 %collective-permute-start = (bf16[2,88,1408]{2,1,0:T(8,128)(2,1)S(1)}, bf16[2,88,1408]{2,1,0:T(8,128)(2,1)S(1)}, u32[]{:S(2)}, u32[]{:S(2)}) collective-permute-start(bf16[2,88,1408]{2,1,0:T(8,128)(2,1)S(1)} %bitcast.119), channel_id=1, source_target_pairs={{0,1},{1,0},{2,3},{3,2},{4,5},{5,4},{6,7},{7,6},{8,9},{9,8},{10,11... | collective-permute-start | bytes 1486856 | tf_op jit(solution)/shard_map/ppermute | solution.py:27
  50.6 13.0 %all-to-all-start.2 = ((bf16[8,176,128]{2,1,0:T(8,128)(2,1)}), bf16[8,176,128]{2,1,0:T(8,128)(2,1)S(1)}, u32[]{:S(2)}, u32[]{:S(2)}) async-start(bf16[8,176,128]{2,1,0:T(8,128)(2,1)} %broadcast_in_dim.25), calls=%async_computation.2 | async-start | bytes 720896 | tf_op jit(solution)/shard_map/all_to_all | solution.py:37
  63.1 100.1 %copy-start = (bf16[2,88,1408]{2,1,0:T(8,128)(2,1)}, bf16[2,88,1408]{2,1,0:T(8,128)(2,1)S(1)}, u32[]{:S(2)}) copy-start(bf16[2,88,1408]{2,1,0:T(8,128)(2,1)S(1)} %get-tuple-element.49) | copy-start | bytes 1486852
  63.6 2.1 copy-start.3
  63.9 7.4 %copy-start.23 = (bf16[1,128,2,176]{1,3,2,0:T(8,128)(2,1)S(1)}, bf16[1,128,2,176]{1,3,2,0:T(8,128)(2,1)}, u32[]{:S(2)}) copy-start(bf16[1,128,2,176]{1,3,2,0:T(8,128)(2,1)} %param.8) | copy-start | bytes 270340
  63.9 12.2 %collective-permute-start.4 = (bf16[176,128]{1,0:T(8,128)(2,1)S(1)}, bf16[176,128]{1,0:T(8,128)(2,1)S(1)}, u32[]{:S(2)}, u32[]{:S(2)}) collective-permute-start(bf16[176,128]{1,0:T(8,128)(2,1)S(1)} %convolution_convert_fusion.16), channel_id=1, source_target_pairs={{256,240},{272,224},{288,208},{304,192},{320,176},{336,160},{352,1... | collective-permute-start | bytes 135176 | tf_op jit(solution)/shard_map/ppermute | solution.py:118
  65.7 6.3 %collective-permute-start.3 = (bf16[176,128]{1,0:T(8,128)(2,1)S(1)}, bf16[176,128]{1,0:T(8,128)(2,1)S(1)}, u32[]{:S(2)}, u32[]{:S(2)}) collective-permute-start(bf16[176,128]{1,0:T(8,128)(2,1)S(1)} %convolution_convert_fusion.15), channel_id=1, source_target_pairs={{16,0},{32,16},{48,32},{64,48},{80,64},{96,80},{112,96},{128,112},... | collective-permute-start | bytes 135176 | tf_op jit(solution)/shard_map/ppermute | solution.py:124
  67.6 24.4 %collective-permute-start.5 = (bf16[128,1408]{1,0:T(8,128)(2,1)}, bf16[128,1408]{1,0:T(8,128)(2,1)}, u32[]{:S(2)}, u32[]{:S(2)}) collective-permute-start(bf16[128,1408]{1,0:T(8,128)(2,1)} %bitcast.10), channel_id=1, source_target_pairs={{0,1},{1,0},{2,3},{3,2},{4,5},{5,4},{6,7},{7,6},{8,9},{9,8},{10,11... | collective-permute-start | bytes 1081352 | tf_op jit(solution)/shard_map/ppermute | solution.py:27
  77.7 14.3 %all-to-all-start.3 = ((bf16[8,176,128]{2,1,0:T(8,128)(2,1)}), bf16[8,176,128]{2,1,0:T(8,128)(2,1)S(1)}, u32[]{:S(2)}, u32[]{:S(2)}) async-start(bf16[8,176,128]{2,1,0:T(8,128)(2,1)} %broadcast_in_dim.26), calls=%async_computation.3 | async-start | bytes 720896 | tf_op jit(solution)/shard_map/all_to_all | solution.py:37
  81.3 10.7 %collective-permute-start.6 = (bf16[384,128]{1,0:T(8,128)(2,1)S(1)}, bf16[384,128]{1,0:T(8,128)(2,1)S(1)}, u32[]{:S(2)}, u32[]{:S(2)}) collective-permute-start(bf16[384,128]{1,0:T(8,128)(2,1)S(1)} %pad_maximum_fusion.3), channel_id=1, source_target_pairs={{0,1},{1,0},{2,3},{3,2},{4,5},{5,4},{6,7},{7,6},{8,9},{9,8},{10,11... | collective-permute-start | bytes 294920 | tf_op jit(solution)/shard_map/ppermute | solution.py:27
  92.0 117.9 %copy-start.12 = (bf16[384,128]{1,0:T(8,128)(2,1)}, bf16[384,128]{1,0:T(8,128)(2,1)S(1)}, u32[]{:S(2)}) copy-start(bf16[384,128]{1,0:T(8,128)(2,1)S(1)} %collective-permute-done.6) | copy-start | bytes 294916
  92.0 1.9 copy-start.1
  117.2 3.8 %copy-start.4 = (bf16[8,176,128]{2,1,0:T(8,128)(2,1)S(1)}, bf16[8,176,128]{2,1,0:T(8,128)(2,1)}, u32[]{:S(2)}) copy-start(bf16[8,176,128]{2,1,0:T(8,128)(2,1)} %copy-done.3) | copy-start | bytes 1081348
  117.2 12.1 %collective-permute-start.8 = (bf16[176,128]{1,0:T(8,128)(2,1)S(1)}, bf16[176,128]{1,0:T(8,128)(2,1)S(1)}, u32[]{:S(2)}, u32[]{:S(2)}) collective-permute-start(bf16[176,128]{1,0:T(8,128)(2,1)S(1)} %convolution_convert_fusion.14), channel_id=1, source_target_pairs={{256,240},{272,224},{288,208},{304,192},{320,176},{336,160},{352,1... | collective-permute-start | bytes 135176 | tf_op jit(solution)/shard_map/ppermute | solution.py:118
  119.0 10.4 %copy-start.14 = (bf16[3,128,176]{1,2,0:T(8,128)(2,1)S(1)}, bf16[3,128,176]{1,2,0:T(8,128)(2,1)}, u32[]{:S(2)}) copy-start(bf16[3,128,176]{1,2,0:T(8,128)(2,1)} %param.12) | copy-start | bytes 405508
  119.0 3.8 %collective-permute-start.7 = (bf16[176,128]{1,0:T(8,128)(2,1)S(1)}, bf16[176,128]{1,0:T(8,128)(2,1)S(1)}, u32[]{:S(2)}, u32[]{:S(2)}) collective-permute-start(bf16[176,128]{1,0:T(8,128)(2,1)S(1)} %convolution_convert_fusion.13), channel_id=1, source_target_pairs={{16,0},{32,16},{48,32},{64,48},{80,64},{96,80},{112,96},{128,112},... | collective-permute-start | bytes 135176 | tf_op jit(solution)/shard_map/ppermute | solution.py:124
  162.0 12.0 %collective-permute-start.10 = (bf16[176,128]{1,0:T(8,128)(2,1)S(1)}, bf16[176,128]{1,0:T(8,128)(2,1)S(1)}, u32[]{:S(2)}, u32[]{:S(2)}) collective-permute-start(bf16[176,128]{1,0:T(8,128)(2,1)S(1)} %convolution_convert_fusion.12), channel_id=1, source_target_pairs={{256,240},{272,224},{288,208},{304,192},{320,176},{336,160},{352,1... | collective-permute-start | bytes 135176 | tf_op jit(solution)/shard_map/ppermute | solution.py:118
  163.6 6.4 %collective-permute-start.9 = (bf16[176,128]{1,0:T(8,128)(2,1)S(1)}, bf16[176,128]{1,0:T(8,128)(2,1)S(1)}, u32[]{:S(2)}, u32[]{:S(2)}) collective-permute-start(bf16[176,128]{1,0:T(8,128)(2,1)S(1)} %convolution_convert_fusion.11), channel_id=1, source_target_pairs={{16,0},{32,16},{48,32},{64,48},{80,64},{96,80},{112,96},{128,112},... | collective-permute-start | bytes 135176 | tf_op jit(solution)/shard_map/ppermute | solution.py:124
  166.5 16.4 %collective-permute-start.11 = (bf16[1408,128]{1,0:T(8,128)(2,1)}, bf16[1408,128]{1,0:T(8,128)(2,1)}, u32[]{:S(2)}, u32[]{:S(2)}) collective-permute-start(bf16[1408,128]{1,0:T(8,128)(2,1)} %fusion.2), channel_id=1, source_target_pairs={{0,1},{1,0},{2,3},{3,2},{4,5},{5,4},{6,7},{7,6},{8,9},{9,8},{10,11... | collective-permute-start | bytes 1081352 | tf_op jit(solution)/shard_map/ppermute | solution.py:27
  174.7 11.4 %all-to-all-start.9 = ((bf16[8,176,128]{2,1,0:T(8,128)(2,1)}), bf16[8,176,128]{2,1,0:T(8,128)(2,1)}, u32[]{:S(2)}, u32[]{:S(2)}) async-start(bf16[8,176,128]{2,1,0:T(8,128)(2,1)} %broadcast_in_dim.31), calls=%async_computation.9 | async-start | bytes 720896 | tf_op jit(solution)/shard_map/all_to_all | solution.py:37
  178.8 1.8 copy-start.16
  186.2 1.6 copy-start.28
  186.2 1.6 copy-start.32
  187.8 4.7 %copy-start.2 = (bf16[8,176,128]{2,1,0:T(8,128)(2,1)S(1)}, bf16[8,176,128]{2,1,0:T(8,128)(2,1)}, u32[]{:S(2)}) copy-start(bf16[8,176,128]{2,1,0:T(8,128)(2,1)} %copy-done.1) | copy-start | bytes 1081348
  187.8 4.7 %copy-start.6 = (bf16[8,176,128]{2,1,0:T(8,128)(2,1)S(1)}, bf16[8,176,128]{2,1,0:T(8,128)(2,1)}, u32[]{:S(2)}) copy-start(bf16[8,176,128]{2,1,0:T(8,128)(2,1)} %copy-done.5) | copy-start | bytes 1081348
  187.8 4.7 %copy-start.11 = (bf16[8,176,128]{2,1,0:T(8,128)(2,1)S(1)}, bf16[8,176,128]{2,1,0:T(8,128)(2,1)}, u32[]{:S(2)}) copy-start(bf16[8,176,128]{2,1,0:T(8,128)(2,1)} %copy-done.10) | copy-start | bytes 1081348
  189.0 12.9 %all-to-all-start.10 = ((bf16[8,176,128]{2,1,0:T(8,128)(2,1)}), bf16[8,176,128]{2,1,0:T(8,128)(2,1)S(1)}, u32[]{:S(2)}, u32[]{:S(2)}) async-start(bf16[8,176,128]{2,1,0:T(8,128)(2,1)} %bitcast.34), calls=%async_computation.10 | async-start | bytes 720896 | tf_op jit(solution)/shard_map/all_to_all | solution.py:110
  192.5 1.7 copy-start.18
  192.5 1.7 copy-start.20
  192.5 1.7 copy-start.22
  192.5 1.7 copy-start.34
  194.5 17.7 %collective-permute-start.13 = (bf16[1408,128]{0,1:T(8,128)(2,1)S(1)}, bf16[1408,128]{0,1:T(8,128)(2,1)S(1)}, u32[]{:S(2)}, u32[]{:S(2)}) collective-permute-start(bf16[1408,128]{0,1:T(8,128)(2,1)S(1)} %convolution_convert_fusion.3), channel_id=1, source_target_pairs={{0,1},{1,0},{2,3},{3,2},{4,5},{5,4},{6,7},{7,6},{8,9},{9,8},{10,11... | collective-permute-start | bytes 1081352 | tf_op jit(solution)/shard_map/ppermute | solution.py:27
  198.1 11.9 %collective-permute-start.12 = (bf16[192,128]{1,0:T(8,128)(2,1)S(1)}, bf16[192,128]{1,0:T(8,128)(2,1)S(1)}, u32[]{:S(2)}, u32[]{:S(2)}) collective-permute-start(bf16[192,128]{1,0:T(8,128)(2,1)S(1)} %get-tuple-element.53), channel_id=1, source_target_pairs={{0,1},{1,0},{2,3},{3,2},{4,5},{5,4},{6,7},{7,6},{8,9},{9,8},{10,11... | collective-permute-start | bytes 147464 | tf_op jit(solution)/shard_map/ppermute | solution.py:27
  202.0 7.0 %copy-start.24 = (bf16[2,88,128]{2,1,0:T(8,128)(2,1)S(1)}, bf16[2,88,128]{2,1,0:T(8,128)(2,1)}, u32[]{:S(2)}) copy-start(bf16[2,88,128]{2,1,0:T(8,128)(2,1)} %get-tuple-element.56) | copy-start | bytes 135172
  203.0 17.0 %all-to-all-start.11 = ((bf16[16,176,128]{2,1,0:T(8,128)(2,1)}), bf16[16,176,128]{2,1,0:T(8,128)(2,1)S(1)}, u32[]{:S(2)}, u32[]{:S(2)}) async-start(bf16[16,176,128]{2,1,0:T(8,128)(2,1)} %broadcast_in_dim.32), calls=%async_computation.11 | async-start | bytes 1441792 | tf_op jit(solution)/shard_map/all_to_all | solution.py:37
  209.9 2.3 %slice-start = ((bf16[384,128]{1,0:T(8,128)(2,1)}), bf16[192,128]{1,0:T(8,128)(2,1)S(1)}, s32[]{:S(2)}) async-start(bf16[384,128]{1,0:T(8,128)(2,1)} %copy-done.12), calls=%async_computation.12 | async-start | bytes 98304 | tf_op jit(solution)/shard_map/slice | solution.py:159
  (10 other events, 10.2 us)
